TPU v7x, 32 devices: a whole 2x2x4 slice. The times are simulated.
32 devices in a mesh: seq: 8 (over z, x), head: 4 (over y, core).
Axes of the slice: x: 2, y: 2, z: 4, core: 2. Of those that a mesh axis runs over, the one named last changes fastest.
Arguments:
- tokens: bfloat16 [3, 1024, 2048], P(None, 'seq'), may hold values from -6 to 6
- lengths: int32 [3], replicated, may hold values from 256 to 1024, as said below
- norm_first: float32 [2048], replicated, may hold values from 0.5 to 1.5
- mix_weight: bfloat16 [4, 2048, 2048], P(None, None, 'head'), may hold values from -0.125 to 0.125
- lower_bound: float32 [2048], P('head'), may hold values from 0.9 to 1, as said below
- out_gain: float32 [2048], P('head'), may hold values from 0.5 to 1.5
- w_out: bfloat16 [2048, 2048], P('head'), may hold values from -0.25 to 0.25
- norm_second: float32 [2048], replicated, may hold values from 0.5 to 1.5
- ffn_in: bfloat16 [2, 2048, 5632], P(None, None, 'head'), may hold values from -0.125 to 0.125
- ffn_out: bfloat16 [5632, 2048], P('head'), may hold values from -0.078125 to 0.078125
- cotangent: bfloat16 [3, 1024, 2048], P(None, 'seq'), may hold values from -6 to 6
Outputs:
- output: bfloat16 [3, 1024, 2048], P(None, 'seq')
- grad_tokens: bfloat16 [3, 1024, 2048], P(None, 'seq')
- grad_norm_first: float32 [2048], replicated
- grad_mix: float32 [4, 2048, 2048], P(None, 'seq', 'head')
- grad_bound: float32 [2048], P('head')
- grad_out_gain: float32 [2048], P('head')
- grad_w_out: float32 [2048, 2048], P('head', 'seq')
- grad_norm_second: float32 [2048], replicated
- grad_ffn_in: float32 [2, 2048, 5632], P(None, 'seq', 'head')
- grad_ffn_out: float32 [5632, 2048], P('head', 'seq')
Inputs may be any that keep to these rules, and one draw needn't show every extreme that they name: `lengths`: positions at or past a slot's length are padding; some slot is full. `lower_bound`: channel-wise lower bounds below one.
All inputs are finite; a program needn't handle non-finite values.
Results may differ from a plain program's by a relative error of at most 0.01.
Values sent between devices are 32-bit elements; how exact they have to be, the bound alone decides.
No kernel may reach another device: no remote copies, remote signals or barrier semaphores. Data moves between devices by JAX's collectives and lax.ppermute only.
A program may use at most 320 MiB of HBM per device.

v0:
```python
import jax
import jax.numpy as jnp
from jax import lax
from jax.sharding import PartitionSpec as P

HD = 128


EPS = 1e-06
HIGHEST_ACCURACY = lax.Precision.HIGHEST


def entering(value, axis, join, neutral, backward):
    count, mine = (lax.axis_size(axis), lax.axis_index(axis))
    pieces = jax.tree.map(lambda part: lax.all_gather(part, axis), value)
    if backward:
        pieces = jax.tree.map(lambda part: part[::-1], pieces)
        mine = count - 1 - mine
    subtotal = jax.tree.map(
        lambda part, zero: jnp.full_like(part, 0) + jnp.asarray(zero, part.dtype), value, neutral
    )

    def step(position, subtotal):
        longer = join(subtotal, jax.tree.map(lambda part: part[position], pieces))
        return jax.tree.map(lambda new, old: jnp.where(position < mine, new, old), longer, subtotal)

    return lax.fori_loop(0, count - 1, step, subtotal)


def rms_scale(v):
    return lax.rsqrt(jnp.mean(v * v, axis=-1, keepdims=True) + EPS)


def block_step(hidden_state, inputs):
    query_vectors, logf, key_vectors, value_vectors = inputs
    running_total = jnp.cumsum(logf, axis=1)
    cross_segment = jnp.einsum(
        "raf,rfj->raj",
        query_vectors * jnp.exp(running_total),
        hidden_state,
        precision=HIGHEST_ACCURACY,
    )
    size = query_vectors.shape[1]
    lower = (jnp.arange(size)[:, None] >= jnp.arange(size)[None, :])[None, :, :, None]
    diff = running_total[:, :, None, :] - running_total[:, None, :, :]
    rel = jnp.where(lower, jnp.exp(jnp.where(lower, diff, 0.0)), 0.0)
    scores = jnp.einsum(
        "htk,hsk,htsk->hts", query_vectors, key_vectors, rel, precision=HIGHEST_ACCURACY
    )
    intra = jnp.einsum("hts,hsv->htv", scores, value_vectors, precision=HIGHEST_ACCURACY)
    final_position = running_total[:, -1:, :]
    hidden_state = jnp.exp(final_position[:, 0, :])[:, :, None] * hidden_state + jnp.einsum(
        "ndp,ndi->npi",
        key_vectors * jnp.exp(final_position - running_total),
        value_vectors,
        precision=HIGHEST_ACCURACY,
    )
    return (hidden_state, cross_segment + intra)


def recurrence(query_vectors, logf, key_vectors, value_vectors, incoming):
    slots, heads, length, width = query_vectors.shape
    size = min(64, length)
    count = length // size

    def cut(a):
        return jnp.moveaxis(a.reshape(slots * heads, count, size, width), 1, 0)

    final, outs = lax.scan(
        jax.checkpoint(block_step),
        incoming.reshape(slots * heads, width, width),
        (cut(query_vectors), cut(logf), cut(key_vectors), cut(value_vectors)),
    )
    return jnp.moveaxis(outs, 0, 1).reshape(slots, heads, length, width)


def state_summary(logf, key_vectors, value_vectors):
    running_total = jnp.cumsum(logf, axis=2)
    final_position = running_total[:, :, -1:, :]
    local = jnp.einsum(
        "shtk,shtv->shkv",
        key_vectors * jnp.exp(final_position - running_total),
        value_vectors,
        precision=HIGHEST_ACCURACY,
    )
    return (jnp.exp(final_position[:, :, 0, :]), local)


def to_heads(a, heads):
    slots, length, width = a.shape
    return a.reshape(slots, length, heads, width // heads).transpose(0, 2, 1, 3)


def gate_norm(mixed, gate_pre, gain):
    joined = mixed.transpose(0, 2, 1, 3)
    normed = (joined * rms_scale(joined)).reshape(gate_pre.shape)
    return normed * gain * jax.nn.silu(gate_pre)


def forward_combine(earlier, later):
    return (earlier[0] * later[0], later[0][..., None] * earlier[1] + later[1])


def norm_back(grad_normed, gain, scale, normed_hat):
    scaled = grad_normed * gain
    return scale * (scaled - normed_hat * jnp.mean(scaled * normed_hat, axis=-1, keepdims=True))


def body(
    tokens,
    lengths,
    norm_first,
    mix_weight,
    lower_bound,
    out_gain,
    w_out,
    norm_second,
    ffn_in,
    ffn_out,
    cotangent,
):
    slots, length, width = tokens.shape
    heads = lower_bound.shape[0] // HD
    position = lax.axis_index("seq")
    valid = (position * length + jnp.arange(length, dtype=jnp.int32))[None, :] < lengths[:, None]
    x = tokens.astype(jnp.float32)
    scale_one = rms_scale(x)
    hat_one = x * scale_one
    xn1 = (hat_one * norm_first).astype(jnp.bfloat16)
    proj = jnp.einsum("std,cde->cste", xn1, mix_weight, preferred_element_type=jnp.float32)

    def open_gates(pre_query, pre_forget, pre_values, bound):
        forget = bound + (1.0 - bound) * jax.nn.sigmoid(pre_forget)
        forget = jnp.where(valid[:, :, None], forget, 1.0)
        return (
            to_heads(jax.nn.silu(pre_query), heads),
            to_heads(jnp.log(forget), heads),
            to_heads(1.0 - forget, heads),
            to_heads(pre_values, heads),
        )

    (query_vectors, logf, key_vectors, value_vectors), pull_gates = jax.vjp(
        open_gates, proj[0], proj[1], proj[2], lower_bound
    )
    (decay, local), pull_summary = jax.vjp(state_summary, logf, key_vectors, value_vectors)
    identity = (jnp.ones_like(decay), jnp.zeros_like(local))
    incoming = entering((decay, local), "seq", forward_combine, identity, False)[1]
    mixed, pull_recur = jax.vjp(
        recurrence, query_vectors, logf, key_vectors, value_vectors, incoming
    )
    gated, pull_norm = jax.vjp(gate_norm, mixed, proj[3], out_gain)
    gated_low = gated.astype(jnp.bfloat16)
    branch = lax.psum(
        jnp.einsum("std,de->ste", gated_low, w_out, preferred_element_type=jnp.float32), "head"
    )
    hidden = x + branch
    scale_two = rms_scale(hidden)
    hat_two = hidden * scale_two
    xn2 = (hat_two * norm_second).astype(jnp.bfloat16)
    gate_up = jnp.einsum("std,cdf->cstf", xn2, ffn_in, preferred_element_type=jnp.float32)
    sig = jax.nn.sigmoid(gate_up[0])
    swish = gate_up[0] * sig
    act = (swish * gate_up[1]).astype(jnp.bfloat16)
    ffn = lax.psum(
        jnp.einsum("stf,fd->std", act, ffn_out, preferred_element_type=jnp.float32), "head"
    )
    output = (hidden + ffn).astype(jnp.bfloat16)
    grad_ffn_out = jnp.einsum("stf,std->fd", act, cotangent, preferred_element_type=jnp.float32)
    dact = jnp.einsum("std,fd->stf", cotangent, ffn_out, preferred_element_type=jnp.float32)
    dswish = sig * (1.0 + gate_up[0] * (1.0 - sig))
    dgate_up = jnp.stack([dact * gate_up[1] * dswish, dact * swish]).astype(jnp.bfloat16)
    grad_ffn_in = jnp.einsum("std,cstf->cdf", xn2, dgate_up, preferred_element_type=jnp.float32)
    dxn2 = lax.psum(
        jnp.einsum("cstf,cdf->std", dgate_up, ffn_in, preferred_element_type=jnp.float32), "head"
    )
    part_norm_second = jnp.sum(dxn2 * hat_two, axis=(0, 1))
    dhidden = cotangent.astype(jnp.float32) + norm_back(dxn2, norm_second, scale_two, hat_two)
    dbranch = dhidden.astype(jnp.bfloat16)
    grad_w_out = jnp.einsum("std,ste->de", gated_low, dbranch, preferred_element_type=jnp.float32)
    dgated = jnp.einsum("ste,de->std", dbranch, w_out, preferred_element_type=jnp.float32)
    dmixed, dgate_pre, part_out_gain = pull_norm(dgated)
    dquery, dlogf, dkeys, dvalues, direct = pull_recur(dmixed)

    def backward_combine(earlier, later):
        return (earlier[0] * later[0], later[1] + later[0][..., None] * earlier[1])

    identity = (jnp.ones_like(decay), jnp.zeros_like(direct))
    carried = entering((decay, direct), "seq", backward_combine, identity, True)[1]
    ddecay = jnp.sum(carried * incoming, axis=-1)
    dlogf_sum, dkeys_sum, dvalues_sum = pull_summary((ddecay, carried))
    dpre_query, dpre_forget, dpre_values, part_bound = pull_gates(
        (dquery, dlogf + dlogf_sum, dkeys + dkeys_sum, dvalues + dvalues_sum)
    )
    dproj = jnp.stack([dpre_query, dpre_forget, dpre_values, dgate_pre]).astype(jnp.bfloat16)
    grad_mix = jnp.einsum("std,cste->cde", xn1, dproj, preferred_element_type=jnp.float32)
    dxn1 = lax.psum(
        jnp.einsum("cste,cde->std", dproj, mix_weight, preferred_element_type=jnp.float32), "head"
    )
    part_norm_first = jnp.sum(dxn1 * hat_one, axis=(0, 1))
    grad_tokens = (dhidden + norm_back(dxn1, norm_first, scale_one, hat_one)).astype(jnp.bfloat16)
    summed = (
        lax.psum_scatter(grad_mix, "seq", scatter_dimension=1, tiled=True),
        lax.psum_scatter(grad_w_out, "seq", scatter_dimension=1, tiled=True),
        lax.psum_scatter(grad_ffn_in, "seq", scatter_dimension=1, tiled=True),
        lax.psum_scatter(grad_ffn_out, "seq", scatter_dimension=1, tiled=True),
    )
    small = lax.psum((part_norm_first, part_bound, part_out_gain, part_norm_second), "seq")
    return (
        output,
        grad_tokens,
        small[0],
        summed[0],
        small[1],
        small[2],
        summed[1],
        small[3],
        summed[2],
        summed[3],
    )


def solution(mesh):
    in_specs = (
        P(None, "seq", None),
        P(),
        P(),
        P(None, None, "head"),
        P("head"),
        P("head"),
        P("head", None),
        P(),
        P(None, None, "head"),
        P("head", None),
        P(None, "seq", None),
    )
    out_specs = (
        P(None, "seq", None),
        P(None, "seq", None),
        P(),
        P(None, "seq", "head"),
        P("head"),
        P("head"),
        P("head", "seq"),
        P(),
        P(None, "seq", "head"),
        P("head", "seq"),
    )
    return jax.shard_map(body, mesh=mesh, in_specs=in_specs, out_specs=out_specs, check_vma=False)
```

profile of v0, /device:TPU:0, one launch (start us, length us, event | category | flops | bytes accessed | tf_op | source)
XLA Modules:
  0.0 1766.8 jit_solution(11519585510255518585)
XLA Ops:
  9.2 6.4 fusion.81
  22.4 2.7 reduce_window_sum.62
  26.8 3.4 fusion.120
  31.6 3.7 fusion.109
  46.1 33.5 %all-gather = f32[24,4,1,128]{3,1,2,0:T(4,128)S(1)} all-gather(f32[3,4,1,128]{3,1,2,0:T(4,128)S(1)} %get-tuple-element.954), channel_id=2, replica_groups=mesh['seq'=8,'head'=4] {'seq'}, dimensions={0}, use_global_device_ids=true | all-gather | bytes 55296 | tf_op jit(solution)/shard_map/all_gather | solution.py:15
  79.6 58.2 %all-gather.7.cloned.1.call-done = f32[24,4,128,128]{3,2,1,0:T(8,128)} async-done(((f32[3,4,128,128]{3,2,1,0:T(8,128)}), f32[24,4,128,128]{3,2,1,0:T(8,128)}) %all-gather.7.cloned.1.call-update) | async-done | bytes 6291472 | tf_op jit(solution)/shard_map/all_gather | solution.py:15
  137.8 11.6 while.70
  152.5 67.5 %while.69 = (s32[]{:T(128)}, f32[12,128,128]{2,1,0:T(8,128)S(1)}, f32[2,12,64,128]{3,2,0,1:T(8,128)}, f32[2,12,128,128]{3,2,1,0:T(8,128)}, f32[2,12,64,128]{3,1,...) while((s32[]{:T(128)}, f32[12,128,128]{2,1,0:T(8,128)S(1)}, ...), condition=%wide.region_6.7_spmd.clone.clone, body=%wide.region_4.6_spmd.clone.clone.sunk | while | flops 422166528 | bytes 76916968 | solution.py:69
  154.7 5.3 exponential_select_fusion.2
  161.1 21.1 %fusion.214 = f32[12,64,64]{1,2,0:T(8,128)S(1)} fusion(f32[12,64,64,128]{3,2,1,0:T(8,128)S(1)} %exponential_select_fusion.2, f32[12,128,64]{1,2,0:T(8,128)S(1)} %bitcast.483, f32[12,128,64]{1,2,0:T(8,128)S(1)} %bitcast.484), kind=kLoop, calls=%fused_computation.8.clone.1 | loop fusion | flops 18825216 | bytes 26148864 | tf_op jit(solution)/shard_map/jvp()/while/body/eval_jaxpr/htk,hsk,htsk->hts/dot_general | solution.py:47
  188.5 5.3 exponential_select_fusion.2
  194.9 21.1 %fusion.214 = f32[12,64,64]{1,2,0:T(8,128)S(1)} fusion(f32[12,64,64,128]{3,2,1,0:T(8,128)S(1)} %exponential_select_fusion.2, f32[12,128,64]{1,2,0:T(8,128)S(1)} %bitcast.483, f32[12,128,64]{1,2,0:T(8,128)S(1)} %bitcast.484), kind=kLoop, calls=%fused_computation.8.clone.1 | loop fusion | flops 18825216 | bytes 26148864 | tf_op jit(solution)/shard_map/jvp()/while/body/eval_jaxpr/htk,hsk,htsk->hts/dot_general | solution.py:47
  226.9 66.5 %all-reduce.8.cloned.1.call-done = f32[3,128,2048]{2,1,0:T(8,128)} async-done(((f32[3,128,2048]{2,1,0:T(8,128)}), f32[3,128,2048]{2,1,0:T(8,128)}) %all-reduce.8.cloned.1.call-update) | async-done | bytes 3145744 | tf_op jit(solution)/shard_map/psum | solution.py:153
  293.4 3.0 multiply_reduce_fusion.3
  298.1 8.1 fusion.59
  306.3 5.5 fusion.92
  311.9 7.9 fusion.73
  319.9 68.6 %all-reduce.10.cloned.1.call-done = f32[3,128,2048]{2,1,0:T(8,128)} async-done(((f32[3,128,2048]{2,1,0:T(8,128)}), f32[3,128,2048]{2,1,0:T(8,128)}) %all-reduce.10.cloned.1.call-update) | async-done | bytes 3145744 | tf_op jit(solution)/shard_map/psum | solution.py:173
  388.5 4.4 multiply_reduce_fusion.1
  395.7 4.5 fusion.101
  405.9 117.4 %while.71 = (s32[]{:T(128)}, f32[12,128,128]{2,1,0:T(8,128)}, f32[2,12,64,128]{3,2,0,1:T(8,128)}, f32[2,12,64,128]{3,2,0,1:T(8,128)}, f32[2,12,64,128]{3,2,0,1:T...) while((s32[]{:T(128)}, f32[12,128,128]{2,1,0:T(8,128)}, ...), condition=%wide.region_21.22_spmd.clone, body=%wide.region_14.21_spmd.clone.sunk | while | flops 921260032 | bytes 65536476 | solution.py:69
  415.2 8.3 fusion.235
  425.2 9.8 fusion.237
  436.6 23.0 %fusion.238 = (f32[12,64,128]{2,1,0:T(8,128)S(1)}, f32[12,64,128]{2,1,0:T(8,128)S(1)}, f32[12,64,64]{2,1,0:T(8,128)S(1)}) fusion(f32[12,128,64]{1,2,0:T(8,128)S(1)} %bitcast.482, f32[12,128,64]{1,2,0:T(8,128)S(1)} %bitcast.486, f32[12,64,128]{2,1,0:T(8,128)S(1)} %copy.478, f32[12,64,64]{2,1,0:T(8,128)S(1)} %fusion.234, ...), kind=kLoop, calls=%fused_computation.50.clone.1 | loop fusion | flops 75251712 | bytes 2363392 | tf_op jit(solution)/shard_map/transpose(jvp())/while/body/eval_jaxpr/checkpoint/reduce_sum | solution.py:45
  474.1 8.3 fusion.235
  484.1 9.8 fusion.237
  495.6 23.0 %fusion.238 = (f32[12,64,128]{2,1,0:T(8,128)S(1)}, f32[12,64,128]{2,1,0:T(8,128)S(1)}, f32[12,64,64]{2,1,0:T(8,128)S(1)}) fusion(f32[12,128,64]{1,2,0:T(8,128)S(1)} %bitcast.482, f32[12,128,64]{1,2,0:T(8,128)S(1)} %bitcast.486, f32[12,64,128]{2,1,0:T(8,128)S(1)} %copy.478, f32[12,64,64]{2,1,0:T(8,128)S(1)} %fusion.234, ...), kind=kLoop, calls=%fused_computation.50.clone.1 | loop fusion | flops 75251712 | bytes 2363392 | tf_op jit(solution)/shard_map/transpose(jvp())/while/body/eval_jaxpr/checkpoint/reduce_sum | solution.py:45
  523.4 7.4 fusion.53
  533.6 88.9 %all-gather.5.cloned.1.call-done = f32[8,3,4,128,128]{4,3,2,1,0:T(8,128)} async-done(((f32[1,3,4,128,128]{4,3,2,1,0:T(8,128)}), f32[8,3,4,128,128]{4,3,2,1,0:T(8,128)}) %all-gather.5.cloned.1.call-update) | async-done | bytes 6291472 | tf_op jit(solution)/shard_map/all_gather | solution.py:15
  622.6 6.2 rev.6
  628.8 11.7 while.72
  651.3 15.5 reduce_window_sum.63
  666.8 6.4 add_select_fusion
  679.5 8.5 fusion.70
  689.4 9.7 convolution_bitcast_fusion.2
  699.2 13.2 convolution_bitcast_fusion
  713.4 5.2 convolution_bitcast_fusion.3
  718.8 9.2 convolution_bitcast_fusion.1
  729.7 76.5 %all-reduce.12.cloned.1.call-done = (f32[3,128,2048]{2,1,0:T(8,128)}, f32[3,128,2048]{2,1,0:T(8,128)}) async-done(((f32[3,128,2048]{2,1,0:T(8,128)}, f32[3,128,2048]{2,1,0:T(8,128)}), (f32[3,128,2048]{2,1,0:T(8,128)}, f32[3,128,2048]{2,1,0:T(8,128)})) %all-reduce.12.cloned.1.call-update) | async-done | bytes 6291472 | tf_op jit(solution)/shard_map/psum | solution.py:164
  806.2 2.8 fusion.68
  809.0 39.5 %all-reduce.2 = (f32[2048]{0:T(1024)}, f32[512]{0:T(512)}, f32[512]{0:T(512)}, f32[2048]{0:T(1024)}) all-reduce(f32[2048]{0:T(1024)S(1)} %get-tuple-element.853, f32[512]{0:T(512)S(1)} %add_bitcast_fusion.1, f32[512]{0:T(512)S(1)} %copy-done.60, f32[2048]{0:T(1024)S(1)} %copy-done.56), channel_id=1, replica_groups=mesh['seq'=8,'head'=4] {'seq'}, use_global_device_ids=true, to_apply=%region_30.31 | all-reduce | flops 5120 | bytes 40960 | tf_op jit(solution)/shard_map/psum | solution.py:207
  848.5 7.4 fusion.67
  855.9 237.3 %reduce-scatter.5.cloned.1.call-done = f32[4,256,512]{1,2,0:T(8,128)} async-done(((f32[4,2048,512]{1,2,0:T(8,128)}), f32[4,256,512]{1,2,0:T(8,128)}) %reduce-scatter.5.cloned.1.call-update) | async-done | bytes 2097168 | tf_op jit(solution)/shard_map/reduce_scatter | solution.py:202
  1093.2 3.0 copy.316
  1096.2 374.6 %reduce-scatter.9.cloned.1.call-done = f32[2,256,1408]{1,2,0:T(8,128)} async-done(((f32[2,2048,1408]{1,2,0:T(8,128)}), f32[2,256,1408]{1,2,0:T(8,128)}) %reduce-scatter.9.cloned.1.call-update) | async-done | bytes 2883600 | tf_op jit(solution)/shard_map/reduce_scatter | solution.py:204
  1470.9 3.4 copy.317
  1474.3 88.9 %reduce-scatter.7.cloned.1.call-done = f32[512,256]{1,0:T(8,128)} async-done(((f32[512,2048]{1,0:T(8,128)}), f32[512,256]{1,0:T(8,128)}) %reduce-scatter.7.cloned.1.call-update) | async-done | bytes 524304 | tf_op jit(solution)/shard_map/reduce_scatter | solution.py:203
  1563.2 196.9 %reduce-scatter.11.cloned.1.call-done = f32[1408,256]{1,0:T(8,128)} async-done(((f32[1408,2048]{1,0:T(8,128)}), f32[1408,256]{1,0:T(8,128)}) %reduce-scatter.11.cloned.1.call-update) | async-done | bytes 1441808 | tf_op jit(solution)/shard_map/reduce_scatter | solution.py:205
  (340 shorter events, 138.1 us)
Async XLA Ops:
  7.2 216.8 %copy-start = (bf16[512,2048]{1,0:T(8,128)(2,1)S(1)}, bf16[512,2048]{1,0:T(8,128)(2,1)}, u32[]{:S(2)}) copy-start(bf16[512,2048]{1,0:T(8,128)(2,1)} %param.25) | copy-start | bytes 6291460
  7.2 130.6 %all-gather.7.cloned.1.call-start = ((), (), s32[]{:S(2)}) async-start(), calls=%async_computation.11 | async-start | bytes 7077888 | tf_op jit(solution)/shard_map/all_gather | solution.py:15
  9.2 6.4 copy-start.54
  20.1 6.6 copy-start.12
  20.8 6.0 copy-start.52
  20.9 5.9 copy-start.57
  35.3 258.1 %all-reduce.8.cloned.1.call-start = ((), (), s32[]{:S(2)}) async-start(), calls=%async_computation.4 | async-start | bytes 6291456 | tf_op jit(solution)/shard_map/psum | solution.py:153
  152.5 69.0 %copy-start.61 = (f32[512]{0:T(512)S(1)}, f32[512]{0:T(512)}, u32[]{:S(2)}) copy-start(f32[512]{0:T(512)} %param.24) | copy-start | bytes 6148
  154.7 5.4 copy-start.9
  161.1 21.1 %copy-start.4 = (f32[2,12,64,128]{3,2,1,0:T(8,128)S(1)}, f32[2,12,64,128]{3,2,1,0:T(8,128)}, u32[]{:S(2)}) copy-start(f32[2,12,64,128]{3,2,1,0:T(8,128)} %get-tuple-element.1234) | copy-start | bytes 2359300 | tf_op jit(solution)/shard_map/jvp()/while
  188.4 5.4 copy-start.9
  194.9 21.1 %copy-start.4 = (f32[2,12,64,128]{3,2,1,0:T(8,128)S(1)}, f32[2,12,64,128]{3,2,1,0:T(8,128)}, u32[]{:S(2)}) copy-start(f32[2,12,64,128]{3,2,1,0:T(8,128)} %get-tuple-element.1234) | copy-start | bytes 2359300 | tf_op jit(solution)/shard_map/jvp()/while
  226.6 71.5 %copy-start.46 = (f32[2048]{0:T(1024)S(1)}, f32[2048]{0:T(1024)}, u32[]{:S(2)}) copy-start(f32[2048]{0:T(1024)} %param.26) | copy-start | bytes 24580
  226.7 161.9 %all-reduce.10.cloned.1.call-start = ((), (), s32[]{:S(2)}) async-start(), calls=%async_computation.5 | async-start | bytes 6291456 | tf_op jit(solution)/shard_map/psum | solution.py:173
  293.4 12.9 slice-start.3
  298.1 8.2 copy-start.40
  298.1 8.2 slice-start.4
  298.1 13.8 slice-start
  298.1 13.8 slice-start.1
  306.3 5.6 slice-start.2
  319.8 302.7 %all-gather.5.cloned.1.call-start = ((), (), s32[]{:S(2)}) async-start(), calls=%async_computation.6 | async-start | bytes 7077888 | tf_op jit(solution)/shard_map/all_gather | solution.py:15
  400.5 5.4 copy-start.5
  405.9 117.5 %copy-start.45 = (f32[8,3,4,128]{3,2,1,0:T(4,128)S(1)}, f32[8,3,4,128]{3,2,1,0:T(4,128)}, u32[]{:S(2)}) copy-start(f32[8,3,4,128]{3,2,1,0:T(4,128)} %copy-done.44) | copy-start | bytes 147460
  425.1 9.8 copy-start.28
  425.2 9.8 copy-start.33
  436.6 23.1 %copy-start.29 = (f32[2,12,64,128]{3,2,0,1:T(8,128)}, f32[2,12,64,128]{3,2,0,1:T(8,128)S(1)}, u32[]{:S(2)}) copy-start(f32[2,12,64,128]{3,2,0,1:T(8,128)S(1)} %get-tuple-element.1268) | copy-start | bytes 2359300 | tf_op jit(solution)/shard_map/transpose(jvp())/while
  436.6 23.1 %copy-start.34 = (f32[2,12,64,128]{3,2,0,1:T(8,128)}, f32[2,12,64,128]{3,2,0,1:T(8,128)S(1)}, u32[]{:S(2)}) copy-start(f32[2,12,64,128]{3,2,0,1:T(8,128)S(1)} %get-tuple-element.1270) | copy-start | bytes 2359300 | tf_op jit(solution)/shard_map/transpose(jvp())/while
  484.1 9.8 copy-start.28
  484.1 9.8 copy-start.33
  495.6 23.1 %copy-start.29 = (f32[2,12,64,128]{3,2,0,1:T(8,128)}, f32[2,12,64,128]{3,2,0,1:T(8,128)S(1)}, u32[]{:S(2)}) copy-start(f32[2,12,64,128]{3,2,0,1:T(8,128)S(1)} %get-tuple-element.1268) | copy-start | bytes 2359300 | tf_op jit(solution)/shard_map/transpose(jvp())/while
  495.6 23.1 %copy-start.34 = (f32[2,12,64,128]{3,2,0,1:T(8,128)}, f32[2,12,64,128]{3,2,0,1:T(8,128)S(1)}, u32[]{:S(2)}) copy-start(f32[2,12,64,128]{3,2,0,1:T(8,128)S(1)} %get-tuple-element.1270) | copy-start | bytes 2359300 | tf_op jit(solution)/shard_map/transpose(jvp())/while
  523.3 282.9 %all-reduce.12.cloned.1.call-start = ((), (), s32[]{:S(2)}) async-start(), calls=%async_computation.12 | async-start | bytes 12582912 | tf_op jit(solution)/shard_map/psum | solution.py:164
  523.4 7.4 copy-start.37
  523.4 8.5 copy-start.30
  628.8 11.8 copy-start.20
  628.8 14.4 copy-start.8
  649.3 17.5 copy-start.13
  649.3 17.5 copy-start.15
  649.3 17.5 copy-start.51
  649.3 17.5 copy-start.53
  649.3 17.5 copy-start.58
  688.0 405.2 %reduce-scatter.5.cloned.1.call-start = ((), (), s32[]{:S(2)}) async-start(), calls=%async_computation.7 | async-start | bytes 18874368 | tf_op jit(solution)/shard_map/reduce_scatter | solution.py:202
  699.1 771.8 %reduce-scatter.9.cloned.1.call-start = ((), (), s32[]{:S(2)}) async-start(), calls=%async_computation.9 | async-start | bytes 25952256 | tf_op jit(solution)/shard_map/reduce_scatter | solution.py:204
  712.4 850.8 %reduce-scatter.7.cloned.1.call-start = ((), (), s32[]{:S(2)}) async-start(), calls=%async_computation.8 | async-start | bytes 4718592 | tf_op jit(solution)/shard_map/reduce_scatter | solution.py:203
  718.6 1041.4 %reduce-scatter.11.cloned.1.call-start = ((), (), s32[]{:S(2)}) async-start(), calls=%async_computation.10 | async-start | bytes 12976128 | tf_op jit(solution)/shard_map/reduce_scatter | solution.py:205
  728.1 80.9 %copy-start.56 = (f32[2048]{0:T(1024)S(1)}, f32[2048]{0:T(1024)}, u32[]{:S(2)}) copy-start(f32[2048]{0:T(1024)} %get-tuple-element.851) | copy-start | bytes 24580
  728.1 80.9 %copy-start.60 = (f32[512]{0:T(512)S(1)}, f32[512]{0:T(512)}, u32[]{:S(2)}) copy-start(f32[512]{0:T(512)} %get-tuple-element.945) | copy-start | bytes 6148
  1093.2 666.8 %copy-start.1 = (bf16[512,2048]{1,0:T(8,128)(2,1)S(1)}, bf16[512,2048]{1,0:T(8,128)(2,1)}, u32[]{:S(2)}) copy-start(bf16[512,2048]{1,0:T(8,128)(2,1)} %param.25) | copy-start | bytes 6291460
  (43 other events, 115.9 us)
Sparse Core Ops, SparseCore 0:
  35.5 102.2 all-gather.6
  226.8 66.6 all-reduce.7
  319.9 68.5 all-reduce.9
  523.4 99.1 all-gather.4
  688.2 117.9 all-reduce.11
  809.8 283.3 reduce-scatter.4
  1097.6 373.2 reduce-scatter.8
  1475.5 87.5 reduce-scatter.6
  1567.4 192.6 reduce-scatter.10
where the time goes:
time: 1780 us; the launch traced here: 1770 us
  waiting for transfers between devices  1260 us (71%)
  other arithmetic  234 us (13%)
  matrix products  119 us (7%)
  blocking collectives  73.1 us (4%)
  local copies, waits for them, and re-layouts  66.5 us (4%)
    reduce_scatter x1, waiting for transfers between devices, body(): lax.psum_scatter(grad_ffn_in, 'seq', scatter_dimension=1, tiled=True)  375 us
    reduce_scatter x1, waiting for transfers between devices, body(): lax.psum_scatter(grad_mix, 'seq', scatter_dimension=1, tiled=True)  237 us
    reduce_scatter x1, waiting for transfers between devices, body(): lax.psum_scatter(grad_ffn_out, 'seq', scatter_dimension=1, tiled=True)  197 us
    all_gather x2, waiting for transfers between devices, entering(): pieces = jax.tree.map(lambda part: lax.all_gather(part, axis), value)  147 us
    reduce_scatter x1, waiting for transfers between devices, body(): lax.psum_scatter(grad_w_out, 'seq', scatter_dimension=1, tiled=True)  88.9 us
    dot_general x6, other arithmetic, block_step(): jnp.einsum('htk,hsk,htsk->hts', query_vectors, key_vectors, rel, precisio...  78.3 us
    psum x1, waiting for transfers between devices, body(): lax.psum(jnp.einsum('stf,fd->std', act, ffn_out, preferred_element_type=j...  76.5 us
    psum x1, waiting for transfers between devices, body(): lax.psum(jnp.einsum('cstf,cdf->std', dgate_up, ffn_in, preferred_element_...  68.6 us
  transfers between devices with their start and end apart: 9, of which 9 were waited for; matrix products, arithmetic and copies ran while one was open for 4% of the time, Pallas kernels for 0%

commit v1 on v0

v1 whole, which is shorter than its diff:
```python
import jax
import jax.numpy as jnp
from jax import lax
from jax.experimental import pallas as pl
from jax.experimental.pallas import tpu as pltpu
from jax.sharding import PartitionSpec as P

HD = 128
EPS = 1e-06
F32 = jnp.float32
BF16 = jnp.bfloat16
MIB = 1 << 20
PACKED = HD + 8

X_SWAP = [(p, p ^ 1) for p in range(8)]
CORE_SWAP = [(h, h ^ 1) for h in range(4)]
Y_SWAP = [(h, h ^ 2) for h in range(4)]


def z_shift(k):
    return [(p, (p + 2 * k) % 8) for p in range(8)]


def z_line(k):
    return [(p, p + 2 * k) for p in range(8) if 0 <= p + 2 * k < 8]


def flip(bit):
    return [(p, p ^ bit) for p in range(8)]


def rms_scale(v):
    return lax.rsqrt(jnp.mean(v * v, axis=-1, keepdims=True) + EPS)


def norm_back(grad_normed, gain, scale, normed_hat):
    scaled = grad_normed * gain
    return scale * (scaled - normed_hat * jnp.mean(scaled * normed_hat, axis=-1, keepdims=True))


def dot(a, b, dims=((1,), (0,))):
    return lax.dot_general(a, b, (dims, ((), ())), preferred_element_type=F32)


NT = ((1,), (1,))
TN = ((0,), (0,))


def sigmoid(v):
    return 1.0 / (1.0 + jnp.exp(-v))


def triangle(kind):
    row = lax.broadcasted_iota(jnp.int32, (HD, HD), 0)
    col = lax.broadcasted_iota(jnp.int32, (HD, HD), 1)
    return {"lower": row >= col, "strict": row > col, "upper": row <= col}[kind]


def exact_dot(ones, v):
    total = None
    for _ in range(3):
        part = v.astype(BF16)
        v = v - part.astype(F32)
        term = dot(ones, part)
        total = term if total is None else total + term
    return total


def valid_rows(pos, length):
    row = lax.broadcasted_iota(jnp.int32, (HD, 1), 0)
    return (pos * HD + row) < length


def open_forget(pre, bound, ok):
    sig = sigmoid(pre)
    return sig, jnp.where(ok, bound + (1.0 - bound) * sig, 1.0)


def project_kernel(pos, lengths, x_ref, gain_ref, w_ref, bound_ref, xn_ref, away_ref, proj_ref, c_ref, qe_ref, ke_ref, intra_ref, sum_ref):
    @pl.when(pl.program_id(0) == 0)
    def _():
        x = x_ref[...].astype(F32)
        xn_ref[...] = (x * rms_scale(x) * gain_ref[...]).astype(BF16)
        n = away_ref.shape[1] // 4
        for z in range(4):
            at = pl.multiple_of((2 * z + 1 - pos[0] % 2) * n, n)
            away_ref[:, pl.ds(z * n, n)] = xn_ref[:, pl.ds(at, n)].astype(F32)

    xn = xn_ref[...]
    for c in range(4):
        proj_ref[c] = dot(xn, w_ref[c])
    slots, heads = sum_ref.shape[:2]
    lower = triangle("lower")
    ones = lower.astype(BF16)
    for s in range(slots):
        rows = pl.ds(s * HD, HD)
        ok = valid_rows(pos[0], lengths[s])
        for h in range(heads):
            cols = pl.ds(h * HD, HD)
            pre_q, pre_f, v = (proj_ref[c, rows, cols] for c in range(3))
            _, forget = open_forget(pre_f, bound_ref[:, cols], ok)
            cum = exact_dot(ones, jnp.log(forget))
            c_ref[rows, cols] = cum
            keys = 1.0 - forget
            qe = (pre_q * sigmoid(pre_q) * jnp.exp(cum)).astype(BF16)
            ke = (keys * jnp.exp(-cum)).astype(BF16)
            qe_ref[rows, cols] = qe
            ke_ref[rows, cols] = ke
            vb = v.astype(BF16)
            scores = jnp.where(lower, dot(qe, ke, NT), 0.0).astype(BF16)
            intra_ref[rows, cols] = dot(scores, vb)
            last = cum[HD - 1 :, :]
            to_end = (keys * jnp.exp(last - cum)).astype(BF16)
            sum_ref[s, h, pl.ds(0, HD), :] = dot(vb, to_end, TN)
            sum_ref[s, h, pl.ds(HD, 8), :] = jnp.broadcast_to(jnp.exp(last), (8, HD))


def split_store(keep_ref, send_ref, core, make):
    half = keep_ref.shape[1]
    keep_ref[...] = make(pl.multiple_of(core * half, half), half)
    send_ref[...] = make(pl.multiple_of((1 - core) * half, half), half)


def mixer_out_kernel(core, qe_ref, state_ref, intra_ref, pre_ref, gain_ref, w_ref, mixed_ref, gated_ref, keep_ref, send_ref):
    slots, heads = state_ref.shape[:2]
    for s in range(slots):
        rows = pl.ds(s * HD, HD)
        for h in range(heads):
            cols = pl.ds(h * HD, HD)
            mixed = intra_ref[rows, cols] + dot(qe_ref[rows, cols], state_ref[s, h].astype(BF16), NT)
            mixed_ref[rows, cols] = mixed
            pre = pre_ref[0, rows, cols]
            gated = mixed * rms_scale(mixed) * gain_ref[:, cols] * (pre * sigmoid(pre))
            gated_ref[rows, cols] = gated.astype(BF16)
    split_store(keep_ref, send_ref, core[0], lambda at, n: dot(gated_ref[...], w_ref[:, pl.ds(at, n)]))


def ffn_unit(xn, dy, w_gate, w_up, w_out):
    gate, up = dot(xn, w_gate), dot(xn, w_up)
    dact = dot(dy, w_out, NT)
    sig = sigmoid(gate)
    swish = gate * sig
    act = (swish * up).astype(BF16)
    dgate = (dact * up * (sig * (1.0 + gate * (1.0 - sig)))).astype(BF16)
    dup = (dact * swish).astype(BF16)
    return act, dgate, dup


def ffn_own_kernel(core, xn_ref, dy_ref, in_ref, in_tail, out_ref, out_tail, f_keep, f_send, d_keep, d_send, f_acc, d_acc):
    step = pl.program_id(0)

    @pl.when(step == 0)
    def _():
        f_acc[...] = jnp.zeros_like(f_acc)
        d_acc[...] = jnp.zeros_like(d_acc)

    def add(w_in, w_out):
        act, dgate, dup = ffn_unit(xn_ref[...], dy_ref[...], w_in[0], w_in[1], w_out[...])
        f_acc[...] += dot(act, w_out[...])
        d_acc[...] += dot(dgate, w_in[0], NT) + dot(dup, w_in[1], NT)

    add(in_ref, out_ref)

    @pl.when(step == pl.num_programs(0) - 1)
    def _():
        add(in_tail, out_tail)
        split_store(f_keep, f_send, core[0], lambda at, n: f_acc[:, pl.ds(at, n)])
        split_store(d_keep, d_send, core[0], lambda at, n: d_acc[:, pl.ds(at, n)])


def widen_kernel(at, a_ref, out_ref):
    n = out_ref.shape[1]
    out_ref[...] = a_ref[:, pl.ds(pl.multiple_of(at[0] * n, n), n)].astype(F32)


def assemble_kernel(at, *refs):
    out_ref = refs[-1]
    for k, piece in enumerate(refs[:-1]):
        n = piece.shape[1]
        out_ref[:, pl.ds(pl.multiple_of(at[k] * n, n), n)] = piece[...].astype(BF16)


def ffn_grad_kernel(rows, xn_ref, xn_line, dy_ref, dy_line, in_ref, in_tail, out_ref, out_tail, in_mine, in_other, out_mine, out_other, tail_in_mine, tail_in_other, tail_out_mine, tail_out_other):
    step = pl.program_id(0)
    n = in_mine.shape[1]
    count = xn_ref.shape[0]

    def put(w_in, w_out, targets):
        blocks = [(xn_ref, dy_ref, pl.ds(0, count))]
        blocks += [(xn_line, dy_line, pl.ds(k * count, count)) for k in range(xn_line.shape[0] // count)]
        for k, (xs, dys, tokens) in enumerate(blocks):
            act, dgate, dup = ffn_unit(xs[tokens, :], dys[tokens, :], w_in[0], w_in[1], w_out[...])
            for which, (gin, gout) in enumerate(targets):
                at = pl.ds(pl.multiple_of(rows[which] * n, n), n)
                x = xs[tokens, at]
                sums = dot(x, dgate, TN), dot(x, dup, TN), dot(act, dys[tokens, at], TN)
                if k == 0:
                    gin[0], gin[1], gout[...] = sums
                else:
                    gin[0] += sums[0]
                    gin[1] += sums[1]
                    gout[...] += sums[2]

    put(in_ref, out_ref, ((in_mine, out_mine), (in_other, out_other)))

    @pl.when(step == pl.num_programs(0) - 1)
    def _():
        put(in_tail, out_tail, ((tail_in_mine, tail_out_mine), (tail_in_other, tail_out_other)))


def mix_grad_kernel(place, xn_ref, xn_got, *refs):
    keep_ref, send_ref = refs[-2:]
    n = keep_ref.shape[2]
    z, x = place[0] // 2, place[0] % 2
    for c in range(keep_ref.shape[0]):
        own, got = refs[2 * c][...].astype(BF16), refs[2 * c + 1][...].astype(BF16)
        for high in range(2):
            for out, low in ((keep_ref, z % 2), (send_ref, 1 - z % 2)):
                row = 2 * high + low
                a = xn_ref[:, pl.ds(pl.multiple_of((2 * row + x) * n, n), n)]
                b = xn_got[:, pl.ds(pl.multiple_of(row * n, n), n)].astype(BF16)
                out[c, high] = dot(a, own, TN) + dot(b, got, TN)


def norm_back_kernel(db_ref, w_ref, mixed_ref, pre_ref, gain_ref, qe_ref, sum_ref, dpre_ref, dm_ref, dgain_ref, back_ref, dg_ref):
    dg_ref[...] = dot(db_ref[...], w_ref[...], NT)
    slots, heads = sum_ref.shape[:2]
    for h in range(heads):
        cols = pl.ds(h * HD, HD)
        gain = gain_ref[:, cols]
        total = jnp.zeros((1, HD), F32)
        for s in range(slots):
            rows = pl.ds(s * HD, HD)
            mixed, pre, dgated = mixed_ref[rows, cols], pre_ref[0, rows, cols], dg_ref[rows, cols]
            scale = rms_scale(mixed)
            hat = mixed * scale
            sig = sigmoid(pre)
            swish = pre * sig
            total += jnp.sum(dgated * hat * swish, axis=0, keepdims=True)
            dpre_ref[rows, cols] = (dgated * hat * gain * (sig * (1.0 + pre * (1.0 - sig)))).astype(BF16).astype(F32)
            dm = norm_back(dgated * swish, gain, scale, hat).astype(BF16)
            dm_ref[rows, cols] = dm
            back_ref[s, h, pl.ds(0, HD), :] = dot(dm, qe_ref[rows, cols], TN)
            back_ref[s, h, pl.ds(HD, 8), :] = sum_ref[s, h, pl.ds(HD, 8), :]
        dgain_ref[:, cols] = total


def intra_back_kernel(dm_ref, qe_ref, ke_ref, proj_ref, c_ref, state_ref, dq_ref, dk_ref, dv_ref, dl_ref):
    slots, heads = state_ref.shape[:2]
    lower = triangle("lower")
    upper = triangle("upper").astype(BF16)
    for s in range(slots):
        rows = pl.ds(s * HD, HD)
        for h in range(heads):
            cols = pl.ds(h * HD, HD)
            dm, qe, ke, cum = (r[rows, cols] for r in (dm_ref, qe_ref, ke_ref, c_ref))
            vb = proj_ref[2, rows, cols].astype(BF16)
            dscores = jnp.where(lower, dot(dm, vb, NT), 0.0).astype(BF16)
            to_q = dot(dscores, ke) + dot(dm, state_ref[s, h].astype(BF16))
            to_k = dot(dscores, qe, TN)
            pre = proj_ref[0, rows, cols]
            sig = sigmoid(pre)
            dq_ref[rows, cols] = (jnp.exp(cum) * to_q * (sig * (1.0 + pre * (1.0 - sig)))).astype(BF16).astype(F32)
            dk_ref[rows, cols] = jnp.exp(-cum) * to_k
            scores = jnp.where(lower, dot(qe, ke, NT), 0.0).astype(BF16)
            dv_ref[rows, cols] = dot(scores, dm, TN)
            dl_ref[rows, cols] = exact_dot(upper, qe.astype(F32) * to_q - ke.astype(F32) * to_k)


def state_back_kernel(pos, lengths, carried_ref, state_ref, ke_ref, forget_ref, value_ref, c_ref, bound_ref, dk_ref, dv_ref, dl_ref, df_ref, dval_ref, dbound_ref):
    slots, heads = state_ref.shape[:2]
    strict = triangle("strict").astype(BF16)
    for h in range(heads):
        cols = pl.ds(h * HD, HD)
        bound = bound_ref[:, cols]
        total = jnp.zeros((1, HD), F32)
        for s in range(slots):
            rows = pl.ds(s * HD, HD)
            ok = valid_rows(pos[0], lengths[s])
            cum, ke = c_ref[rows, cols], ke_ref[rows, cols]
            ending = carried_ref[s, h] * jnp.exp(cum[HD - 1 :, :])
            ending_low = ending.astype(BF16)
            to_k = dot(value_ref[0, rows, cols].astype(BF16), ending_low)
            dval_ref[rows, cols] = (dv_ref[rows, cols] + dot(ke, ending_low, NT)).astype(BF16).astype(F32)
            through = jnp.sum(ending * state_ref[s, h], axis=0, keepdims=True)
            dlogf = dl_ref[rows, cols] + exact_dot(strict, ke.astype(F32) * to_k) + through
            dkeys = dk_ref[rows, cols] + jnp.exp(-cum) * to_k
            sig, forget = open_forget(forget_ref[0, rows, cols], bound, ok)
            dforget = jnp.where(ok, dlogf / forget - dkeys, 0.0)
            total += jnp.sum(dforget * (1.0 - sig), axis=0, keepdims=True)
            df_ref[rows, cols] = (dforget * (1.0 - bound) * sig * (1.0 - sig)).astype(BF16).astype(F32)
        dbound_ref[:, cols] = total


SMEM = pl.BlockSpec(memory_space=pltpu.SMEM)


def whole(shape, *index):
    index = index or (0,) * len(shape)
    return pl.BlockSpec(shape, lambda *_: index)


def sds(shape, dtype=F32):
    return jax.ShapeDtypeStruct(shape, dtype)


def call(kernel, name, outs, in_specs, out_specs, flops, moved, grid=(1,), scratch=(), vmem=48):
    return pl.pallas_call(
        kernel,
        name=name,
        grid=grid,
        out_shape=outs,
        in_specs=in_specs,
        out_specs=out_specs,
        scratch_shapes=list(scratch),
        compiler_params=pltpu.CompilerParams(vmem_limit_bytes=vmem * MIB),
        cost_estimate=pl.CostEstimate(flops=int(flops), bytes_accessed=int(moved), transcendentals=0),
    )


def entering_all(packed, backward):
    count, mine = lax.axis_size("seq"), lax.axis_index("seq")
    pieces = lax.all_gather(packed, "seq")
    if backward:
        pieces, mine = pieces[::-1], count - 1 - mine

    def step(position, state):
        piece = pieces[position]
        longer = piece[:, :, HD : HD + 1] * state + piece[:, :, :HD]
        return jnp.where(position < mine, longer, state)

    return lax.fori_loop(0, count - 1, step, jnp.zeros_like(packed[:, :, :HD]))


def entering_lines(packed, backward):
    shape = packed.shape
    packed = packed.reshape(-1, PACKED, HD)
    half = packed.shape[0] // 2
    is_low = lax.axis_index("seq") % 2 == 0
    first = ~is_low if backward else is_low
    step = -1 if backward else 1
    mine = jnp.where(is_low, packed[:half], packed[half:])
    other = lax.ppermute(jnp.where(is_low, packed[half:], packed[:half]), "seq", X_SWAP)
    early, late = jnp.where(first, mine, other), jnp.where(first, other, mine)

    def decay(a):
        return a[:, HD : HD + 1]

    def state(a):
        return a[:, :HD]

    def join(a, b):
        both = decay(b) * state(a) + state(b)
        return jnp.concatenate([both, jnp.broadcast_to(decay(a) * decay(b), (half, 8, HD))], axis=1)

    pair = join(early, late)
    before = lax.ppermute(pair, "seq", z_line(step))
    further = lax.ppermute(join(before, pair), "seq", z_line(2 * step))
    into_first = decay(before) * state(further) + state(before)
    into_second = decay(early) * into_first + state(early)
    kept = jnp.where(first, into_first, into_second)
    given = lax.ppermute(jnp.where(first, into_second, into_first), "seq", X_SWAP)
    low, high = jnp.where(is_low, kept, given), jnp.where(is_low, given, kept)
    return jnp.concatenate([low, high]).reshape(*shape[:2], HD, HD)


def sum_heads(keep, send, fast):
    if not fast:
        return lax.psum(jnp.concatenate([keep, send], axis=1), "head")
    half = keep + lax.ppermute(send, "head", CORE_SWAP)
    half = half + lax.ppermute(half, "head", Y_SWAP)
    other = lax.ppermute(half, "head", CORE_SWAP)
    low = lax.axis_index("head") % 2 == 0
    return jnp.concatenate([jnp.where(low, half, other), jnp.where(low, other, half)], axis=1)


def gather_line(piece):
    rows, quarter = piece.shape
    head = lax.axis_index("head")
    own = jnp.concatenate([lax.ppermute(piece, "seq", z_shift(k)) for k in (1, 2, 3)])
    over = lax.ppermute(own, "head", Y_SWAP)
    pieces = [own, lax.ppermute(own, "head", CORE_SWAP), over, lax.ppermute(over, "head", CORE_SWAP)]
    return call(
        assemble_kernel,
        "assemble",
        sds((3 * rows, 4 * quarter), BF16),
        [SMEM] + [pl.BlockSpec((rows, quarter), lambda i: (i, 0))] * 4,
        pl.BlockSpec((rows, 4 * quarter), lambda i: (i, 0)),
        0,
        18 * rows * 4 * quarter,
        grid=(3,),
    )(jnp.stack([head ^ k for k in range(4)]).astype(jnp.int32), *pieces)


def sum_line(keep, send, axis):
    high = lax.axis_index("seq") // 4

    def take(a, at):
        return lax.dynamic_index_in_dim(a, at, axis, keepdims=False)

    near = keep + lax.ppermute(send, "seq", flip(2))
    return take(near, high) + lax.ppermute(take(near, 1 - high), "seq", flip(4))


def sum_small(v, fast):
    if not fast:
        return lax.psum(v, "seq")
    for bit in (1, 2, 4):
        v = v + lax.ppermute(v, "seq", flip(bit))
    return v


def body(tokens, lengths, norm_first, mix_weight, lower_bound, out_gain, w_out, norm_second, ffn_in, ffn_out, cotangent):
    slots, length, width = tokens.shape
    count = slots * length
    local = lower_bound.shape[0]
    heads = local // HD
    units = ffn_out.shape[0]
    fast = lax.axis_size("seq") == 8 and lax.axis_size("head") == 4
    entering = entering_lines if fast else entering_all
    seq = lax.axis_index("seq")
    pos = seq.astype(jnp.int32).reshape(1)
    core = (lax.axis_index("head") % 2 if fast else jnp.int32(0)).astype(jnp.int32).reshape(1)
    tokens = tokens.reshape(count, width)
    dy = cotangent.reshape(count, width)
    bound, gain = lower_bound.reshape(1, local), out_gain.reshape(1, local)
    norm_first, norm_second = norm_first.reshape(1, width), norm_second.reshape(1, width)

    pair = 2 * HD
    tall = whole((count, width))
    channel = whole((count, local))
    state_shape = (slots, heads, HD, HD)
    packed_shape = (slots, heads, PACKED, HD)
    state_spec, packed_spec, row_spec = whole(state_shape), whole(packed_shape), whole((1, local))
    w_spec = whole((local, width))
    half_out, half_spec = sds((count, width // 2)), whole((count, width // 2))

    def block(rows):
        return pl.BlockSpec((rows, pair), lambda i: (0, i))

    xn1, xn1_away, proj, cum, qe, ke, intra, packed = call(
        project_kernel,
        "project",
        [sds((count, width), BF16), sds((count, width // 2)), sds((4, count, local)), sds((count, local)), sds((count, local), BF16), sds((count, local), BF16), sds((count, local)), sds(packed_shape)],
        [SMEM, SMEM, tall, whole((1, width)), pl.BlockSpec((4, width, pair), lambda i: (0, 0, i)), block(1)],
        [tall, half_spec, pl.BlockSpec((4, count, pair), lambda i: (0, 0, i)), block(count), block(count), block(count), block(count), pl.BlockSpec((slots, 2, PACKED, HD), lambda i: (0, i, 0, 0))],
        8 * count * width * local,
        20e6,
        grid=(local // pair,),
    )(pos, lengths, tokens, norm_first, mix_weight, bound)

    state = entering(packed, False)

    gate_spec = whole((1, count, local), 3, 0, 0)
    mixed, gated, keep, send = call(
        mixer_out_kernel,
        "mixer_out",
        [sds((count, local)), sds((count, local), BF16), half_out, half_out],
        [SMEM, channel, state_spec, channel, gate_spec, row_spec, w_spec],
        [channel, channel, half_spec, half_spec],
        2 * count * width * local,
        10e6,
    )(core, qe, state, intra, proj, gain, w_out)
    hidden = tokens.astype(F32) + sum_heads(keep, send, fast)
    scale_two = rms_scale(hidden)
    hat_two = hidden * scale_two
    xn2 = (hat_two * norm_second).astype(BF16)

    steps = units // pair
    rest = units - steps * pair
    in_specs = [
        pl.BlockSpec((2, width, pair), lambda i: (0, 0, i)),
        whole((2, width, rest), 0, 0, steps * pair // rest),
        pl.BlockSpec((pair, width), lambda i: (i, 0)),
        whole((rest, width), steps * pair // rest, 0),
    ]
    keep, send, dkeep, dsend = call(
        ffn_own_kernel,
        "ffn_own",
        [half_out] * 4,
        [SMEM, tall, tall, *in_specs],
        [half_spec] * 4,
        12 * count * width * units,
        30e6,
        grid=(steps,),
        scratch=[pltpu.VMEM((count, width), F32)] * 2,
        vmem=60,
    )(core, xn2, dy, ffn_in, ffn_in, ffn_out, ffn_out)
    dxn2 = sum_heads(dkeep, dsend, fast)
    output = (hidden + sum_heads(keep, send, fast)).astype(BF16)
    part_norm_second = jnp.sum(dxn2 * hat_two, axis=0)
    dhidden = dy.astype(F32) + norm_back(dxn2, norm_second, scale_two, hat_two)
    dbranch = dhidden.astype(BF16)

    dpre_gate, dmixed, part_gain, back = call(
        norm_back_kernel,
        "norm_back",
        [sds((count, local)), sds((count, local), BF16), sds((1, local)), sds(packed_shape)],
        [tall, w_spec, channel, gate_spec, row_spec, channel, packed_spec],
        [channel, channel, row_spec, packed_spec],
        2 * count * width * local,
        10e6,
        scratch=[pltpu.VMEM((count, local), F32)],
    )(dbranch, w_out, mixed, proj, gain, qe, packed)

    carried = entering(back, True)

    three, two = whole((3, count, local)), whole((1, count, local), 1, 0, 0)
    dpre_query, dkeys, dvalues, dlogf = call(
        intra_back_kernel,
        "intra_back",
        [sds((count, local))] * 4,
        [channel, channel, channel, three, channel, state_spec],
        [channel] * 4,
        14 * count * local * HD,
        10e6,
    )(dmixed, qe, ke, proj, cum, state)
    dpre_forget, dpre_values, part_bound = call(
        state_back_kernel,
        "state_back",
        [sds((count, local)), sds((count, local)), sds((1, local))],
        [SMEM, SMEM, state_spec, state_spec, channel, two, whole((1, count, local), 2, 0, 0), channel, row_spec, channel, channel, channel],
        [channel, channel, row_spec],
        8 * count * local * HD,
        10e6,
    )(pos, lengths, carried, state, ke, proj, proj, cum, bound, dkeys, dvalues, dlogf)
    dproj = (dpre_query, dpre_forget, dpre_values, dpre_gate)

    x = tokens.astype(F32)
    scale_one = rms_scale(x)
    hat_one = x * scale_one
    dxn1 = sum(dot(d.astype(BF16), mix_weight[c], NT) for c, d in enumerate(dproj))
    if fast:
        at = core[0] * (width // 2)
        keep = lax.dynamic_slice_in_dim(dxn1, at, width // 2, 1)
        send = lax.dynamic_slice_in_dim(dxn1, width // 2 - at, width // 2, 1)
    else:
        keep, send = jnp.split(dxn1, 2, axis=1)
    dxn1 = sum_heads(keep, send, fast)
    part_norm_first = jnp.sum(dxn1 * hat_one, axis=0)
    grad_tokens = (dhidden + norm_back(dxn1, norm_first, scale_one, hat_one)).astype(BF16)

    if fast:
        weights = weight_grads(xn1, xn1_away, dproj, gated, dbranch, xn2, hat_two * norm_second, dy, ffn_in, ffn_out, in_specs, steps)
    else:
        weights = weight_grads_whole(xn1, dproj, gated, dbranch, xn2, dy, ffn_in, ffn_out)
    sizes = (width, width, local, local)
    small = jnp.concatenate([part_norm_first, part_norm_second, part_bound[0], part_gain[0]])
    small = sum_small(small, fast)
    first, second, bound_sum, gain_sum = jnp.split(small, [sum(sizes[: i + 1]) for i in range(3)])
    shape = (slots, length, width)
    return (output.reshape(shape), grad_tokens.reshape(shape), first, weights[0], bound_sum, gain_sum, weights[1], second, weights[2], weights[3])


def weight_grads_whole(xn1, dproj, gated, dbranch, xn2, dy, ffn_in, ffn_out):
    gate, up = dot(xn2, ffn_in[0]), dot(xn2, ffn_in[1])
    dact = dot(dy, ffn_out, NT)
    sig = sigmoid(gate)
    swish = gate * sig
    act = (swish * up).astype(BF16)
    dgate = (dact * up * (sig * (1.0 + gate * (1.0 - sig)))).astype(BF16)
    dup = (dact * swish).astype(BF16)

    def scatter(a, axis):
        return lax.psum_scatter(a, "seq", scatter_dimension=axis, tiled=True)

    return (
        jnp.stack([scatter(dot(xn1, d.astype(BF16), TN), 0) for d in dproj]),
        scatter(dot(gated, dbranch, TN), 1),
        jnp.stack([scatter(dot(xn2, d, TN), 0) for d in (dgate, dup)]),
        scatter(dot(act, dy, TN), 1),
    )


def weight_grads(xn1, xn1_away, dproj, gated, dbranch, xn2, xn2_wide, dy, ffn_in, ffn_out, in_specs, steps):
    count, width = xn1.shape
    units = ffn_out.shape[0]
    local = gated.shape[1]
    n = width // 8
    seq, head = lax.axis_index("seq"), lax.axis_index("head")
    x, z = seq % 2, seq // 2
    place = seq.astype(jnp.int32).reshape(1)
    tall, channel = whole((count, width)), whole((count, local))

    def swap(a):
        return lax.ppermute(a, "seq", X_SWAP)

    xn1_got = swap(xn1_away)

    def mix_pair(*grads):
        shape = (len(grads), 2, n, local)
        keep, send = call(
            mix_grad_kernel,
            "mix_grad",
            [sds(shape)] * 2,
            [SMEM, tall, whole((count, width // 2))] + [channel] * (2 * len(grads)),
            [whole(shape)] * 2,
            2 * len(grads) * 2 * count * width // 2 * local,
            10e6,
        )(place, xn1, xn1_got, *(a for d in grads for a in (d, swap(d))))
        return sum_line(keep, send, 1)

    early, late = mix_pair(dproj[0], dproj[3]), mix_pair(dproj[1], dproj[2])
    mix = jnp.stack([early[0], late[0], late[1], early[1]])

    blocks = dbranch.reshape(count, 2, 2, 2, n)

    def columns(at):
        return jnp.einsum("td,thln->lhdn", gated, lax.dynamic_index_in_dim(blocks, at, 3, keepdims=False), preferred_element_type=F32)

    two = columns(x) + swap(columns(1 - x))
    keep, send = (lax.dynamic_index_in_dim(two, at, 0, keepdims=False) for at in (z % 2, 1 - z % 2))
    grad_w_out = sum_line(keep, send, 0)

    quarter = width // 4
    dy_wide = call(widen_kernel, "widen", sds((count, quarter)), [SMEM, tall], whole((count, quarter)), 0, 4e6)(
        head.astype(jnp.int32).reshape(1), dy
    )
    dy_line = gather_line(dy_wide)
    xn_line = gather_line(lax.dynamic_slice_in_dim(xn2_wide, head * quarter, quarter, 1))
    pair = 2 * HD
    rest = units - steps * pair
    line = whole(xn_line.shape)
    rows = jnp.stack([seq, seq ^ 1]).astype(jnp.int32)
    main = steps * pair
    outs = [sds((2, n, main))] * 2 + [sds((main, n))] * 2 + [sds((2, n, rest))] * 2 + [sds((rest, n))] * 2
    gin, gout = pl.BlockSpec((2, n, pair), lambda i: (0, 0, i)), pl.BlockSpec((pair, n), lambda i: (i, 0))
    got = call(
        ffn_grad_kernel,
        "ffn_grad",
        outs,
        [SMEM, tall, line, tall, line, *in_specs],
        [gin, gin, gout, gout] + [whole(o.shape) for o in outs[4:]],
        6 * 4 * count * width * units + 6 * 4 * count * 2 * n * units,
        40e6,
        grid=(steps,),
        vmem=60,
    )(rows, xn2, xn_line, dy, dy_line, ffn_in, ffn_in, ffn_out, ffn_out)
    in_mine, in_other, out_mine, out_other, tin_mine, tin_other, tout_mine, tout_other = got

    def finish(mine, other):
        return mine + lax.ppermute(other, "seq", X_SWAP)

    grad_in = jnp.concatenate([finish(in_mine, in_other), finish(tin_mine, tin_other)], axis=2)
    grad_out = jnp.concatenate([finish(out_mine, out_other), finish(tout_mine, tout_other)], axis=0)
    return mix, grad_w_out, grad_in, grad_out


def solution(mesh):
    in_specs = (
        P(None, "seq", None),
        P(),
        P(),
        P(None, None, "head"),
        P("head"),
        P("head"),
        P("head", None),
        P(),
        P(None, None, "head"),
        P("head", None),
        P(None, "seq", None),
    )
    out_specs = (
        P(None, "seq", None),
        P(None, "seq", None),
        P(),
        P(None, "seq", "head"),
        P("head"),
        P("head"),
        P("head", "seq"),
        P(),
        P(None, "seq", "head"),
        P("head", "seq"),
    )
    return jax.shard_map(body, mesh=mesh, in_specs=in_specs, out_specs=out_specs, check_vma=False)
```

time: 1780 us -> 827 us (0.46)
  waiting for transfers between devices: 1260 us -> 466 us
  other arithmetic: 234 us -> 71.5 us
  Pallas kernels: 0 us -> 134 us
  matrix products: 119 us -> 18 us
  starting transfers between devices: 0.72 us -> 77.2 us
  blocking collectives: 73.1 us -> 0 us
    reduce_scatter x4 -> x0, waiting for transfers between devices: 898 us -> none  [the longest x1 375 us: body(): lax.psum_scatter(grad_ffn_in, 'seq', scatter_dimension=1, tiled=True)]
    ppermute x0 -> x51, waiting for transfers between devices: none -> 466 us  [the longest x4 82.2 us: finish(): return mine + lax.ppermute(other, 'seq', X_SWAP)]
    psum x3 -> x0, waiting for transfers between devices: 212 us -> none  [the longest x1 76.5 us: body(): lax.psum(jnp.einsum('stf,fd->std', act, ffn_out, preferred_element_type=j...]
    all_gather x2 -> x0, waiting for transfers between devices: 147 us -> none  [entering(): pieces = jax.tree.map(lambda part: lax.all_gather(part, axis), value)]
    pallas_call x0 -> x12, Pallas kernels: none -> 134 us  [the longest x1 56.4 us: weight_grads(): call(ffn_grad_kernel, 'ffn_grad', outs, [SMEM, tall, line, tall, line, *i...]
    dot_general x33 -> x6, matrix products: 119 us -> 18 us  [the longest x4 13.3 us: dot(): return lax.dot_general(a, b, (dims, ((), ())), preferred_element_type=F32)]
    dot_general x6 -> x0, other arithmetic: 78.3 us -> none  [block_step(): jnp.einsum('htk,hsk,htsk->hts', query_vectors, key_vectors, rel, precisio...]
    ppermute x0 -> x51, starting transfers between devices: none -> 77.2 us  [the longest x6 36 us: gather_line(): lax.ppermute(piece, 'seq', z_shift(k))]
  transfers between devices with their start and end apart: 9 -> 51, of which waited for: 9 -> 25; matrix products, arithmetic and copies ran while one was open for 4% -> 15% of each run, Pallas kernels for 0% -> 11%
where the time goes in v1:
time: 827 us; the launch traced here: 822 us
  waiting for transfers between devices  466 us (56%)
  Pallas kernels  134 us (16%)
  starting transfers between devices  77.2 us (9%)
  other arithmetic  71.5 us (9%)
  local copies, waits for them, and re-layouts  52.9 us (6%)
  matrix products  18 us (2%)
    ppermute x4, waiting for transfers between devices, finish(): return mine + lax.ppermute(other, 'seq', X_SWAP)  82.2 us
    ppermute x3, waiting for transfers between devices, sum_line(): near = keep + lax.ppermute(send, 'seq', flip(2))  73 us
    ppermute x6, waiting for transfers between devices, gather_line(): lax.ppermute(piece, 'seq', z_shift(k))  66.1 us
    ppermute x2, waiting for transfers between devices, gather_line(): over = lax.ppermute(own, 'head', Y_SWAP)  56.7 us
    pallas_call x1, Pallas kernels, weight_grads(): call(ffn_grad_kernel, 'ffn_grad', outs, [SMEM, tall, line, tall, line, *i...  56.4 us
    ppermute x3, waiting for transfers between devices, sum_line(): return take(near, high) + lax.ppermute(take(near, 1 - high), 'seq', flip(4))  48.2 us
    ppermute x4, waiting for transfers between devices, sum_heads(): half = half + lax.ppermute(half, 'head', Y_SWAP)  38.7 us
    ppermute x6, starting transfers between devices, gather_line(): lax.ppermute(piece, 'seq', z_shift(k))  36 us
  transfers between devices with their start and end apart: 51, of which 25 were waited for; matrix products, arithmetic and copies ran while one was open for 15% of the time, Pallas kernels for 11%

profile of v1, /device:TPU:0, one launch (start us, length us, event | category | flops | bytes accessed | tf_op | source)
XLA Modules:
  0.0 822.0 jit_solution(15226553458118288702)
XLA Ops:
  2.7 12.6 %project.1 = (bf16[384,2048]{1,0:T(8,128)(2,1)S(1)}, f32[384,1024]{1,0:T(8,128)}, f32[4,384,512]{2,1,0:T(8,128)}, f32[384,512]{1,0:T(8,128)S(1)}, bf16[384,512]{...) custom-call(s32[1]{0:T(128)} %bitcast.1.pos.place, ...), custom_call_target="tpu_custom_call" | custom-call | flops 3221225472 | bytes 20000000 | tf_op jit(solution)/shard_map/project/pallas_call | solution.py:441
  18.4 9.6 %collective-permute-done = f32[6,136,128]{2,1,0:T(8,128)S(1)} collective-permute-done((f32[6,136,128]{2,1,0:T(8,128)S(1)}, f32[6,136,128]{2,1,0:T(8,128)S(1)}, u32[]{:S(2)}, u32[]{:S(2)}) %collective-permute-start) | collective-permute-done | bytes 417824 | tf_op jit(solution)/shard_map/ppermute | solution.py:343
  28.3 3.8 collective-permute-start.1
  32.0 8.0 collective-permute-done.1
  40.1 5.6 collective-permute-start.2
  45.8 6.9 collective-permute-done.2
  55.0 7.0 collective-permute-done.3
  63.2 4.5 mixer_out.1
  67.7 3.6 collective-permute-done.4
  73.3 34.9 %collective-permute-done.5 = f32[384,1024]{1,0:T(8,128)S(1)} collective-permute-done((f32[384,1024]{1,0:T(8,128)S(1)}, f32[384,1024]{1,0:T(8,128)S(1)}, u32[]{:S(2)}, u32[]{:S(2)}) %collective-permute-start.5) | collective-permute-done | bytes 1572896 | tf_op jit(solution)/shard_map/ppermute | solution.py:371
  109.7 3.7 collective-permute-done.6
  119.9 23.2 %ffn_own.1 = (f32[384,1024]{1,0:T(8,128)}, f32[384,1024]{1,0:T(8,128)}, f32[384,1024]{1,0:T(8,128)}, f32[384,1024]{1,0:T(8,128)}) custom-call(s32[1]{0:T(128)} %bitcast.core, bf16[384,2048]{1,0:T(8,128)(2,1)} %get-tuple-element.95.xn_ref, bf16[384,2048]{1,0:T(8,128)(2,1)} %bitcast.106, bf16[2,2048,1408]{2,1,0:T(8,128)(2,1)} %in_tail.3, ...), custom_call_target="tpu_custom_call" | custom-call | flops 13287555072 | bytes 30000000 | tf_op jit(solution)/shard_map/ffn_own/pallas_call | solution.py:477
  143.3 13.3 %collective-permute-start.41 = (f32[384,512]{1,0:T(8,128)S(1)}, f32[384,512]{1,0:T(8,128)S(1)}, u32[]{:S(2)}, u32[]{:S(2)}) collective-permute-start(f32[384,512]{1,0:T(8,128)S(1)} %widen.1), channel_id=1, source_target_pairs={{0,8},{4,12},{8,16},{12,20},{16,24},{20,28},{24,0},{28,4},{1,9},{5... | collective-permute-start | bytes 2359304 | tf_op jit(solution)/shard_map/ppermute | solution.py:380
  156.6 3.4 collective-permute-start.42
  161.9 16.0 %collective-permute-done.41 = f32[384,512]{1,0:T(8,128)S(1)} collective-permute-done((f32[384,512]{1,0:T(8,128)S(1)}, f32[384,512]{1,0:T(8,128)S(1)}, u32[]{:S(2)}, u32[]{:S(2)}) %collective-permute-start.41) | collective-permute-done | bytes 786464 | tf_op jit(solution)/shard_map/ppermute | solution.py:380
  178.9 32.4 %collective-permute-done.42 = f32[384,512]{1,0:T(8,128)S(1)} collective-permute-done((f32[384,512]{1,0:T(8,128)S(1)}, f32[384,512]{1,0:T(8,128)S(1)}, u32[]{:S(2)}, u32[]{:S(2)}) %collective-permute-start.42) | collective-permute-done | bytes 786464 | tf_op jit(solution)/shard_map/ppermute | solution.py:380
  217.4 16.5 %collective-permute-start.35 = (f32[384,512]{1,0:T(8,128)S(1)}, f32[384,512]{1,0:T(8,128)S(1)}, u32[]{:S(2)}, u32[]{:S(2)}) collective-permute-start(f32[384,512]{1,0:T(8,128)S(1)} %constant_dynamic-slice_fusion), channel_id=1, source_target_pairs={{0,8},{4,12},{8,16},{12,20},{16,24},{20,28},{24,0},{28,4},{1,9},{5... | collective-permute-start | bytes 2359304 | tf_op jit(solution)/shard_map/ppermute | solution.py:380
  236.7 29.9 %collective-permute-done.45.refs_2_ = f32[1152,512]{1,0:T(8,128)} collective-permute-done((f32[1152,512]{1,0:T(8,128)}, f32[1152,512]{1,0:T(8,128)}, u32[]{:S(2)}, u32[]{:S(2)}) %collective-permute-start.45) | collective-permute-done | bytes 2359328 | tf_op jit(solution)/shard_map/ppermute | solution.py:381
  268.1 17.7 %collective-permute-done.36 = f32[384,512]{1,0:T(8,128)S(1)} collective-permute-done((f32[384,512]{1,0:T(8,128)S(1)}, f32[384,512]{1,0:T(8,128)S(1)}, u32[]{:S(2)}, u32[]{:S(2)}) %collective-permute-start.36) | collective-permute-done | bytes 786464 | tf_op jit(solution)/shard_map/ppermute | solution.py:380
  294.7 4.2 norm_back.1
  302.9 8.2 collective-permute-done.13
  315.2 26.8 %collective-permute-done.39.refs_2_ = f32[1152,512]{1,0:T(8,128)} collective-permute-done((f32[1152,512]{1,0:T(8,128)}, f32[1152,512]{1,0:T(8,128)}, u32[]{:S(2)}, u32[]{:S(2)}) %collective-permute-start.39) | collective-permute-done | bytes 2359328 | tf_op jit(solution)/shard_map/ppermute | solution.py:381
  342.0 4.1 reshape.243
  346.1 5.5 reshape.244
  354.5 6.5 assemble.3.dy_line
  361.0 3.5 concatenate.116
  371.5 3.8 collective-permute-done.8
  375.3 3.4 add.217
  378.7 3.5 concatenate.113
  392.1 3.8 fusion.9
  398.1 27.8 %collective-permute-done.15 = f32[6,136,128]{2,1,0:T(8,128)S(1)} collective-permute-done((f32[6,136,128]{2,1,0:T(8,128)S(1)}, f32[6,136,128]{2,1,0:T(8,128)S(1)}, u32[]{:S(2)}, u32[]{:S(2)}) %collective-permute-start.15) | collective-permute-done | bytes 417824 | tf_op jit(solution)/shard_map/ppermute | solution.py:358
  428.5 5.3 intra_back.1
  433.9 4.8 fusion.17
  440.8 6.5 assemble.2.xn_line
  465.0 56.4 %ffn_grad.1 = (f32[2,256,1280]{2,1,0:T(8,128)}, f32[2,256,1280]{2,1,0:T(8,128)}, f32[1280,256]{1,0:T(8,128)}, f32[1280,256]{1,0:T(8,128)}, f32[2,256,128]{2,1,0:...) custom-call(s32[2]{0:T(128)} %pad_add_fusion.rows, ...), custom_call_target="tpu_custom_call" | custom-call | flops 33218887680 | bytes 40000000 | tf_op jit(solution)/shard_map/ffn_grad/pallas_call | solution.py:628
  525.1 6.0 mix_grad.2
  531.1 6.9 collective-permute-done.28.refs_1_
  541.1 13.7 %collective-permute-done.29.refs_3_ = f32[384,512]{1,0:T(8,128)} collective-permute-done((f32[384,512]{1,0:T(8,128)S(1)}, f32[384,512]{1,0:T(8,128)}, u32[]{:S(2)}, u32[]{:S(2)}) %collective-permute-start.29) | collective-permute-done | bytes 786464 | tf_op jit(solution)/shard_map/ppermute | solution.py:586
  555.4 6.2 mix_grad.3
  561.6 78.7 %collective-permute-done.50 = f32[128,256]{1,0:T(8,128)S(1)} collective-permute-done((f32[128,256]{1,0:T(8,128)S(1)}, f32[128,256]{1,0:T(8,128)S(1)}, u32[]{:S(2)}, u32[]{:S(2)}) %collective-permute-start.50) | collective-permute-done | bytes 131104 | tf_op jit(solution)/shard_map/ppermute | solution.py:642
  643.7 3.5 collective-permute-done.48
  649.4 4.2 broadcast_select_fusion.5
  659.1 73.0 %collective-permute-done.33 = f32[2,512,256]{1,2,0:T(8,128)} collective-permute-done((f32[2,512,256]{1,2,0:T(8,128)}, f32[2,512,256]{1,2,0:T(8,128)}, u32[]{:S(2)}, u32[]{:S(2)}) %collective-permute-start.33) | collective-permute-done | bytes 1048608 | tf_op jit(solution)/shard_map/ppermute | solution.py:401
  736.6 3.4 add.234
  752.6 29.4 %collective-permute-done.34 = f32[512,256]{1,0:T(8,128)} collective-permute-done((f32[512,256]{1,0:T(8,128)}, f32[512,256]{1,0:T(8,128)}, u32[]{:S(2)}, u32[]{:S(2)}) %collective-permute-start.34) | collective-permute-done | bytes 524320 | tf_op jit(solution)/shard_map/ppermute | solution.py:402
  785.4 18.9 %collective-permute-done.31 = f32[2,256,512]{2,1,0:T(8,128)S(1)} collective-permute-done((f32[2,256,512]{2,1,0:T(8,128)S(1)}, f32[2,256,512]{2,1,0:T(8,128)S(1)}, u32[]{:S(2)}, u32[]{:S(2)}) %collective-permute-start.31) | collective-permute-done | bytes 1048608 | tf_op jit(solution)/shard_map/ppermute | solution.py:402
  812.0 3.8 collective-permute-done.21
  815.8 4.0 add_convert_fusion
  (346 shorter events, 141.3 us)
Async XLA Ops:
  15.4 12.6 %collective-permute-start = (f32[6,136,128]{2,1,0:T(8,128)S(1)}, f32[6,136,128]{2,1,0:T(8,128)S(1)}, u32[]{:S(2)}, u32[]{:S(2)}) collective-permute-start(f32[6,136,128]{2,1,0:T(8,128)S(1)} %slice_select_fusion.3), channel_id=1, source_target_pairs={{0,4},{4,0},{8,12},{12,8},{16,20},{20,16},{24,28},{28,24},{1,5},{5... | collective-permute-start | bytes 1253384 | tf_op jit(solution)/shard_map/ppermute | solution.py:343
  28.3 11.7 %collective-permute-start.1 = (f32[6,136,128]{2,1,0:T(8,128)S(1)}, f32[6,136,128]{2,1,0:T(8,128)S(1)}, u32[]{:S(2)}, u32[]{:S(2)}) collective-permute-start(f32[6,136,128]{2,1,0:T(8,128)S(1)} %pad_maximum_fusion.7), channel_id=1, source_target_pairs={{0,8},{4,12},{8,16},{12,20},{16,24},{20,28},{1,9},{5,13},{9,17},{1... | collective-permute-start | bytes 1253384 | tf_op jit(solution)/shard_map/ppermute | solution.py:357
  40.1 12.5 %collective-permute-start.2 = (f32[6,136,128]{2,1,0:T(8,128)S(1)}, f32[6,136,128]{2,1,0:T(8,128)S(1)}, u32[]{:S(2)}, u32[]{:S(2)}) collective-permute-start(f32[6,136,128]{2,1,0:T(8,128)S(1)} %pad_maximum_fusion.8), channel_id=1, source_target_pairs={{0,16},{4,20},{8,24},{12,28},{1,17},{5,21},{9,25},{13,29},{2,18},{... | collective-permute-start | bytes 1253384 | tf_op jit(solution)/shard_map/ppermute | solution.py:358
  53.5 8.5 %collective-permute-start.3 = (f32[6,128,128]{2,1,0:T(8,128)}, f32[6,128,128]{2,1,0:T(8,128)}, u32[]{:S(2)}, u32[]{:S(2)}) collective-permute-start(f32[6,128,128]{2,1,0:T(8,128)} %get-tuple-element.97), channel_id=1, source_target_pairs={{0,4},{4,0},{8,12},{12,8},{16,20},{20,16},{24,28},{28,24},{1,5},{5... | collective-permute-start | bytes 1179656 | tf_op jit(solution)/shard_map/ppermute | solution.py:362
  71.7 36.5 %collective-permute-start.5 = (f32[384,1024]{1,0:T(8,128)S(1)}, f32[384,1024]{1,0:T(8,128)S(1)}, u32[]{:S(2)}, u32[]{:S(2)}) collective-permute-start(f32[384,1024]{1,0:T(8,128)S(1)} %add.211), channel_id=1, source_target_pairs={{0,2},{1,3},{2,0},{3,1},{4,6},{5,7},{6,4},{7,5},{8,10},{9,11},{10,... | collective-permute-start | bytes 4718600 | tf_op jit(solution)/shard_map/ppermute | solution.py:371
  143.1 16.9 %collective-permute-start.10 = (f32[384,1024]{1,0:T(8,128)}, f32[384,1024]{1,0:T(8,128)S(1)}, u32[]{:S(2)}, u32[]{:S(2)}) collective-permute-start(f32[384,1024]{1,0:T(8,128)} %get-tuple-element.58), channel_id=1, source_target_pairs={{0,1},{1,0},{2,3},{3,2},{4,5},{5,4},{6,7},{7,6},{8,9},{9,8},{10,11... | collective-permute-start | bytes 4718600 | tf_op jit(solution)/shard_map/ppermute | solution.py:370
  143.3 34.6 %collective-permute-start.41 = (f32[384,512]{1,0:T(8,128)S(1)}, f32[384,512]{1,0:T(8,128)S(1)}, u32[]{:S(2)}, u32[]{:S(2)}) collective-permute-start(f32[384,512]{1,0:T(8,128)S(1)} %widen.1), channel_id=1, source_target_pairs={{0,8},{4,12},{8,16},{12,20},{16,24},{20,28},{24,0},{28,4},{1,9},{5... | collective-permute-start | bytes 2359304 | tf_op jit(solution)/shard_map/ppermute | solution.py:380
  156.6 54.7 %collective-permute-start.42 = (f32[384,512]{1,0:T(8,128)S(1)}, f32[384,512]{1,0:T(8,128)S(1)}, u32[]{:S(2)}, u32[]{:S(2)}) collective-permute-start(f32[384,512]{1,0:T(8,128)S(1)} %widen.1), channel_id=1, source_target_pairs={{0,16},{4,20},{8,24},{12,28},{16,0},{20,4},{24,8},{28,12},{1,17},{... | collective-permute-start | bytes 2359304 | tf_op jit(solution)/shard_map/ppermute | solution.py:380
  160.0 52.3 %collective-permute-start.43 = (f32[384,512]{1,0:T(8,128)S(1)}, f32[384,512]{1,0:T(8,128)S(1)}, u32[]{:S(2)}, u32[]{:S(2)}) collective-permute-start(f32[384,512]{1,0:T(8,128)S(1)} %widen.1), channel_id=1, source_target_pairs={{0,24},{4,28},{8,0},{12,4},{16,8},{20,12},{24,16},{28,20},{1,25},{... | collective-permute-start | bytes 2359304 | tf_op jit(solution)/shard_map/ppermute | solution.py:380
  160.3 54.4 %collective-permute-start.11 = (f32[384,1024]{1,0:T(8,128)S(1)}, f32[384,1024]{1,0:T(8,128)S(1)}, u32[]{:S(2)}, u32[]{:S(2)}) collective-permute-start(f32[384,1024]{1,0:T(8,128)S(1)} %add.219), channel_id=1, source_target_pairs={{0,2},{1,3},{2,0},{3,1},{4,6},{5,7},{6,4},{7,5},{8,10},{9,11},{10,... | collective-permute-start | bytes 4718600 | tf_op jit(solution)/shard_map/ppermute | solution.py:371
  213.2 53.5 %collective-permute-start.45 = (f32[1152,512]{1,0:T(8,128)}, f32[1152,512]{1,0:T(8,128)}, u32[]{:S(2)}, u32[]{:S(2)}) collective-permute-start(f32[1152,512]{1,0:T(8,128)} %constant_dynamic-update-slice_fusion.3.refs_0_), channel_id=1, source_target_pairs={{0,2},{1,3},{2,0},{3,1},{4,6},{5,7},{6,4},{7,5},{8,10},{9,11},{10,... | collective-permute-start | bytes 7077896 | tf_op jit(solution)/shard_map/ppermute | solution.py:381
  216.2 72.0 %collective-permute-start.12 = (f32[384,1024]{1,0:T(8,128)}, f32[384,1024]{1,0:T(8,128)}, u32[]{:S(2)}, u32[]{:S(2)}) collective-permute-start(f32[384,1024]{1,0:T(8,128)} %add.220), channel_id=1, source_target_pairs={{0,1},{1,0},{2,3},{3,2},{4,5},{5,4},{6,7},{7,6},{8,9},{9,8},{10,11... | collective-permute-start | bytes 4718600 | tf_op jit(solution)/shard_map/ppermute | solution.py:372
  217.4 49.2 %collective-permute-start.35 = (f32[384,512]{1,0:T(8,128)S(1)}, f32[384,512]{1,0:T(8,128)S(1)}, u32[]{:S(2)}, u32[]{:S(2)}) collective-permute-start(f32[384,512]{1,0:T(8,128)S(1)} %constant_dynamic-slice_fusion), channel_id=1, source_target_pairs={{0,8},{4,12},{8,16},{12,20},{16,24},{20,28},{24,0},{28,4},{1,9},{5... | collective-permute-start | bytes 2359304 | tf_op jit(solution)/shard_map/ppermute | solution.py:380
  233.9 51.9 %collective-permute-start.36 = (f32[384,512]{1,0:T(8,128)S(1)}, f32[384,512]{1,0:T(8,128)S(1)}, u32[]{:S(2)}, u32[]{:S(2)}) collective-permute-start(f32[384,512]{1,0:T(8,128)S(1)} %constant_dynamic-slice_fusion), channel_id=1, source_target_pairs={{0,16},{4,20},{8,24},{12,28},{16,0},{20,4},{24,8},{28,12},{1,17},{... | collective-permute-start | bytes 2359304 | tf_op jit(solution)/shard_map/ppermute | solution.py:380
  234.3 52.4 %collective-permute-start.37 = (f32[384,512]{1,0:T(8,128)S(1)}, f32[384,512]{1,0:T(8,128)S(1)}, u32[]{:S(2)}, u32[]{:S(2)}) collective-permute-start(f32[384,512]{1,0:T(8,128)S(1)} %constant_dynamic-slice_fusion), channel_id=1, source_target_pairs={{0,24},{4,28},{8,0},{12,4},{16,8},{20,12},{24,16},{28,20},{1,25},{... | collective-permute-start | bytes 2359304 | tf_op jit(solution)/shard_map/ppermute | solution.py:380
  266.6 48.5 %collective-permute-start.44 = (f32[1152,512]{1,0:T(8,128)}, f32[1152,512]{1,0:T(8,128)}, u32[]{:S(2)}, u32[]{:S(2)}) collective-permute-start(f32[1152,512]{1,0:T(8,128)} %constant_dynamic-update-slice_fusion.3.refs_0_), channel_id=1, source_target_pairs={{0,1},{1,0},{2,3},{3,2},{4,5},{5,4},{6,7},{7,6},{8,9},{9,8},{10,11... | collective-permute-start | bytes 7077896 | tf_op jit(solution)/shard_map/ppermute | solution.py:382
  266.6 86.3 %collective-permute-start.46 = (f32[1152,512]{1,0:T(8,128)}, f32[1152,512]{1,0:T(8,128)}, u32[]{:S(2)}, u32[]{:S(2)}) collective-permute-start(f32[1152,512]{1,0:T(8,128)} %collective-permute-done.45.refs_2_), channel_id=1, source_target_pairs={{0,1},{1,0},{2,3},{3,2},{4,5},{5,4},{6,7},{7,6},{8,9},{9,8},{10,11... | collective-permute-start | bytes 7077896 | tf_op jit(solution)/shard_map/ppermute | solution.py:382
  285.8 14.7 %collective-permute-start.7 = (f32[384,1024]{1,0:T(8,128)}, f32[384,1024]{1,0:T(8,128)S(1)}, u32[]{:S(2)}, u32[]{:S(2)}) collective-permute-start(f32[384,1024]{1,0:T(8,128)} %get-tuple-element.56), channel_id=1, source_target_pairs={{0,1},{1,0},{2,3},{3,2},{4,5},{5,4},{6,7},{7,6},{8,9},{9,8},{10,11... | collective-permute-start | bytes 4718600 | tf_op jit(solution)/shard_map/ppermute | solution.py:370
  287.7 54.4 %collective-permute-start.39 = (f32[1152,512]{1,0:T(8,128)}, f32[1152,512]{1,0:T(8,128)}, u32[]{:S(2)}, u32[]{:S(2)}) collective-permute-start(f32[1152,512]{1,0:T(8,128)} %constant_dynamic-update-slice_fusion.refs_0_), channel_id=1, source_target_pairs={{0,2},{1,3},{2,0},{3,1},{4,6},{5,7},{6,4},{7,5},{8,10},{9,11},{10,... | collective-permute-start | bytes 7077896 | tf_op jit(solution)/shard_map/ppermute | solution.py:381
  298.9 12.1 %collective-permute-start.13 = (f32[6,136,128]{2,1,0:T(8,128)S(1)}, f32[6,136,128]{2,1,0:T(8,128)S(1)}, u32[]{:S(2)}, u32[]{:S(2)}) collective-permute-start(f32[6,136,128]{2,1,0:T(8,128)S(1)} %slice_select_fusion.1), channel_id=1, source_target_pairs={{0,4},{4,0},{8,12},{12,8},{16,20},{20,16},{24,28},{28,24},{1,5},{5... | collective-permute-start | bytes 1253384 | tf_op jit(solution)/shard_map/ppermute | solution.py:343
  301.9 73.5 %collective-permute-start.8 = (f32[384,1024]{1,0:T(8,128)}, f32[384,1024]{1,0:T(8,128)}, u32[]{:S(2)}, u32[]{:S(2)}) collective-permute-start(f32[384,1024]{1,0:T(8,128)} %add.216), channel_id=1, source_target_pairs={{0,2},{1,3},{2,0},{3,1},{4,6},{5,7},{6,4},{7,5},{8,10},{9,11},{10,... | collective-permute-start | bytes 4718600 | tf_op jit(solution)/shard_map/ppermute | solution.py:371
  313.9 74.7 %collective-permute-start.14 = (f32[6,136,128]{2,1,0:T(8,128)}, f32[6,136,128]{2,1,0:T(8,128)}, u32[]{:S(2)}, u32[]{:S(2)}) collective-permute-start(f32[6,136,128]{2,1,0:T(8,128)} %pad_maximum_fusion.9), channel_id=1, source_target_pairs={{8,0},{12,4},{16,8},{20,12},{24,16},{28,20},{9,1},{13,5},{17,9},{2... | collective-permute-start | bytes 1253384 | tf_op jit(solution)/shard_map/ppermute | solution.py:357
  315.2 123.5 %collective-permute-start.38 = (f32[1152,512]{1,0:T(8,128)}, f32[1152,512]{1,0:T(8,128)}, u32[]{:S(2)}, u32[]{:S(2)}) collective-permute-start(f32[1152,512]{1,0:T(8,128)} %constant_dynamic-update-slice_fusion.refs_0_), channel_id=1, source_target_pairs={{0,1},{1,0},{2,3},{3,2},{4,5},{5,4},{6,7},{7,6},{8,9},{9,8},{10,11... | collective-permute-start | bytes 7077896 | tf_op jit(solution)/shard_map/ppermute | solution.py:382
  342.0 97.3 %collective-permute-start.40 = (f32[1152,512]{1,0:T(8,128)}, f32[1152,512]{1,0:T(8,128)}, u32[]{:S(2)}, u32[]{:S(2)}) collective-permute-start(f32[1152,512]{1,0:T(8,128)} %collective-permute-done.39.refs_2_), channel_id=1, source_target_pairs={{0,1},{1,0},{2,3},{3,2},{4,5},{5,4},{6,7},{7,6},{8,9},{9,8},{10,11... | collective-permute-start | bytes 7077896 | tf_op jit(solution)/shard_map/ppermute | solution.py:382
  353.0 109.1 %collective-permute-start.23 = (f32[384,1024]{1,0:T(8,128)}, f32[384,1024]{1,0:T(8,128)}, u32[]{:S(2)}, u32[]{:S(2)}) collective-permute-start(f32[384,1024]{1,0:T(8,128)} %get-tuple-element.74), channel_id=1, source_target_pairs={{0,4},{4,0},{8,12},{12,8},{16,20},{20,16},{24,28},{28,24},{1,5},{5... | collective-permute-start | bytes 4718600 | tf_op jit(solution)/shard_map/ppermute | solution.py:586
  378.7 84.8 %collective-permute-start.9 = (f32[384,1024]{1,0:T(8,128)}, f32[384,1024]{1,0:T(8,128)}, u32[]{:S(2)}, u32[]{:S(2)}) collective-permute-start(f32[384,1024]{1,0:T(8,128)} %add.217), channel_id=1, source_target_pairs={{0,1},{1,0},{2,3},{3,2},{4,5},{5,4},{6,7},{7,6},{8,9},{9,8},{10,11... | collective-permute-start | bytes 4718600 | tf_op jit(solution)/shard_map/ppermute | solution.py:372
  390.4 35.5 %collective-permute-start.15 = (f32[6,136,128]{2,1,0:T(8,128)S(1)}, f32[6,136,128]{2,1,0:T(8,128)S(1)}, u32[]{:S(2)}, u32[]{:S(2)}) collective-permute-start(f32[6,136,128]{2,1,0:T(8,128)S(1)} %pad_maximum_fusion.10), channel_id=1, source_target_pairs={{16,0},{20,4},{24,8},{28,12},{17,1},{21,5},{25,9},{29,13},{18,2},{... | collective-permute-start | bytes 1253384 | tf_op jit(solution)/shard_map/ppermute | solution.py:358
  427.0 20.3 %collective-permute-start.16 = (f32[6,128,128]{2,1,0:T(8,128)S(1)}, f32[6,128,128]{2,1,0:T(8,128)S(1)}, u32[]{:S(2)}, u32[]{:S(2)}) collective-permute-start(f32[6,128,128]{2,1,0:T(8,128)S(1)} %fusion.34), channel_id=1, source_target_pairs={{0,4},{4,0},{8,12},{12,8},{16,20},{20,16},{24,28},{28,24},{1,5},{5... | collective-permute-start | bytes 1179656 | tf_op jit(solution)/shard_map/ppermute | solution.py:362
  438.7 25.4 %collective-permute-start.24 = (f32[384,512]{1,0:T(8,128)S(1)}, f32[384,512]{1,0:T(8,128)S(1)}, u32[]{:S(2)}, u32[]{:S(2)}) collective-permute-start(f32[384,512]{1,0:T(8,128)S(1)} %get-tuple-element.63.refs_0_), channel_id=1, source_target_pairs={{0,4},{4,0},{8,12},{12,8},{16,20},{20,16},{24,28},{28,24},{1,5},{5... | collective-permute-start | bytes 2359304 | tf_op jit(solution)/shard_map/ppermute | solution.py:586
  439.3 82.1 %collective-permute-start.25 = (f32[384,512]{1,0:T(8,128)}, f32[384,512]{1,0:T(8,128)}, u32[]{:S(2)}, u32[]{:S(2)}) collective-permute-start(f32[384,512]{1,0:T(8,128)} %get-tuple-element.70.refs_2_), channel_id=1, source_target_pairs={{0,4},{4,0},{8,12},{12,8},{16,20},{20,16},{24,28},{28,24},{1,5},{5... | collective-permute-start | bytes 2359304 | tf_op jit(solution)/shard_map/ppermute | solution.py:586
  447.3 83.8 %collective-permute-start.32 = (f32[2,2,512,256]{2,3,0,1:T(8,128)}, f32[2,2,512,256]{2,3,0,1:T(8,128)}, u32[]{:S(2)}, u32[]{:S(2)}) collective-permute-start(f32[2,2,512,256]{2,3,0,1:T(8,128)} %convolution_bitcast_fusion), channel_id=1, source_target_pairs={{0,4},{4,0},{8,12},{12,8},{16,20},{20,16},{24,28},{28,24},{1,5},{5... | collective-permute-start | bytes 6291464 | tf_op jit(solution)/shard_map/ppermute | solution.py:586
  462.1 75.9 %collective-permute-start.28 = (f32[384,512]{1,0:T(8,128)S(1)}, f32[384,512]{1,0:T(8,128)}, u32[]{:S(2)}, u32[]{:S(2)}) collective-permute-start(f32[384,512]{1,0:T(8,128)S(1)} %get-tuple-element.68.refs_0_), channel_id=1, source_target_pairs={{0,4},{4,0},{8,12},{12,8},{16,20},{20,16},{24,28},{28,24},{1,5},{5... | collective-permute-start | bytes 2359304 | tf_op jit(solution)/shard_map/ppermute | solution.py:586
  463.6 91.3 %collective-permute-start.29 = (f32[384,512]{1,0:T(8,128)S(1)}, f32[384,512]{1,0:T(8,128)}, u32[]{:S(2)}, u32[]{:S(2)}) collective-permute-start(f32[384,512]{1,0:T(8,128)S(1)} %get-tuple-element.69.refs_2_), channel_id=1, source_target_pairs={{0,4},{4,0},{8,12},{12,8},{16,20},{20,16},{24,28},{28,24},{1,5},{5... | collective-permute-start | bytes 2359304 | tf_op jit(solution)/shard_map/ppermute | solution.py:586
  465.0 175.9 %collective-permute-start.17 = (f32[384,1024]{1,0:T(8,128)}, f32[384,1024]{1,0:T(8,128)}, u32[]{:S(2)}, u32[]{:S(2)}) collective-permute-start(f32[384,1024]{1,0:T(8,128)} %constant_dynamic-slice_fusion.3), channel_id=1, source_target_pairs={{0,1},{1,0},{2,3},{3,2},{4,5},{5,4},{6,7},{7,6},{8,9},{9,8},{10,11... | collective-permute-start | bytes 4718600 | tf_op jit(solution)/shard_map/ppermute | solution.py:370
  521.4 127.4 %collective-permute-start.49 = (f32[1280,256]{1,0:T(8,128)}, f32[1280,256]{1,0:T(8,128)}, u32[]{:S(2)}, u32[]{:S(2)}) collective-permute-start(f32[1280,256]{1,0:T(8,128)} %get-tuple-element.85), channel_id=1, source_target_pairs={{0,4},{4,0},{8,12},{12,8},{16,20},{20,16},{24,28},{28,24},{1,5},{5... | collective-permute-start | bytes 3932168 | tf_op jit(solution)/shard_map/ppermute | solution.py:642
  531.1 124.8 %collective-permute-start.26 = (f32[2,2,256,512]{3,2,1,0:T(8,128)}, f32[2,2,256,512]{3,2,1,0:T(8,128)}, u32[]{:S(2)}, u32[]{:S(2)}) collective-permute-start(f32[2,2,256,512]{3,2,1,0:T(8,128)} %get-tuple-element.76), channel_id=1, source_target_pairs={{0,8},{4,12},{8,0},{12,4},{16,24},{20,28},{24,16},{28,20},{1,9},{5... | collective-permute-start | bytes 6291464 | tf_op jit(solution)/shard_map/ppermute | solution.py:401
  538.0 204.5 %collective-permute-start.47 = (f32[2,256,1280]{2,1,0:T(8,128)}, f32[2,256,1280]{2,1,0:T(8,128)}, u32[]{:S(2)}, u32[]{:S(2)}) collective-permute-start(f32[2,256,1280]{2,1,0:T(8,128)} %get-tuple-element.81), channel_id=1, source_target_pairs={{0,4},{4,0},{8,12},{12,8},{16,20},{20,16},{24,28},{28,24},{1,5},{5... | collective-permute-start | bytes 7864328 | tf_op jit(solution)/shard_map/ppermute | solution.py:642
  554.8 85.5 %collective-permute-start.50 = (f32[128,256]{1,0:T(8,128)S(1)}, f32[128,256]{1,0:T(8,128)S(1)}, u32[]{:S(2)}, u32[]{:S(2)}) collective-permute-start(f32[128,256]{1,0:T(8,128)S(1)} %copy-done.83), channel_id=1, source_target_pairs={{0,4},{4,0},{8,12},{12,8},{16,20},{20,16},{24,28},{28,24},{1,5},{5... | collective-permute-start | bytes 393224 | tf_op jit(solution)/shard_map/ppermute | solution.py:642
  640.3 6.9 collective-permute-start.48
  640.9 104.6 %collective-permute-start.30 = (f32[2,2,256,512]{3,2,1,0:T(8,128)}, f32[2,2,256,512]{3,2,1,0:T(8,128)}, u32[]{:S(2)}, u32[]{:S(2)}) collective-permute-start(f32[2,2,256,512]{3,2,1,0:T(8,128)} %get-tuple-element.78), channel_id=1, source_target_pairs={{0,8},{4,12},{8,0},{12,4},{16,24},{20,28},{24,16},{28,20},{1,9},{5... | collective-permute-start | bytes 6291464 | tf_op jit(solution)/shard_map/ppermute | solution.py:401
  647.2 89.4 %collective-permute-start.18 = (f32[384,1024]{1,0:T(8,128)}, f32[384,1024]{1,0:T(8,128)}, u32[]{:S(2)}, u32[]{:S(2)}) collective-permute-start(f32[384,1024]{1,0:T(8,128)} %dynamic-slice_add_fusion), channel_id=1, source_target_pairs={{0,2},{1,3},{2,0},{3,1},{4,6},{5,7},{6,4},{7,5},{8,10},{9,11},{10,... | collective-permute-start | bytes 4718600 | tf_op jit(solution)/shard_map/ppermute | solution.py:371
  648.8 83.3 %collective-permute-start.33 = (f32[2,512,256]{1,2,0:T(8,128)}, f32[2,512,256]{1,2,0:T(8,128)}, u32[]{:S(2)}, u32[]{:S(2)}) collective-permute-start(f32[2,512,256]{1,2,0:T(8,128)} %dynamic-slice_bitcast_fusion), channel_id=1, source_target_pairs={{0,8},{4,12},{8,0},{12,4},{16,24},{20,28},{24,16},{28,20},{1,9},{5... | collective-permute-start | bytes 3145736 | tf_op jit(solution)/shard_map/ppermute | solution.py:401
  659.1 124.8 %collective-permute-start.27 = (f32[2,256,512]{2,1,0:T(8,128)}, f32[2,256,512]{2,1,0:T(8,128)}, u32[]{:S(2)}, u32[]{:S(2)}) collective-permute-start(f32[2,256,512]{2,1,0:T(8,128)} %dynamic-slice_bitcast_fusion.2), channel_id=1, source_target_pairs={{0,16},{4,20},{8,24},{12,28},{16,0},{20,4},{24,8},{28,12},{1,17},{... | collective-permute-start | bytes 3145736 | tf_op jit(solution)/shard_map/ppermute | solution.py:402
  736.6 45.3 %collective-permute-start.34 = (f32[512,256]{1,0:T(8,128)}, f32[512,256]{1,0:T(8,128)}, u32[]{:S(2)}, u32[]{:S(2)}) collective-permute-start(f32[512,256]{1,0:T(8,128)} %bitcast.143), channel_id=1, source_target_pairs={{0,16},{4,20},{8,24},{12,28},{16,0},{20,4},{24,8},{28,12},{1,17},{... | collective-permute-start | bytes 1572872 | tf_op jit(solution)/shard_map/ppermute | solution.py:402
  740.0 64.5 %collective-permute-start.19 = (f32[384,1024]{1,0:T(8,128)}, f32[384,1024]{1,0:T(8,128)}, u32[]{:S(2)}, u32[]{:S(2)}) collective-permute-start(f32[384,1024]{1,0:T(8,128)} %add.234), channel_id=1, source_target_pairs={{0,1},{1,0},{2,3},{3,2},{4,5},{5,4},{6,7},{7,6},{8,9},{9,8},{10,11... | collective-permute-start | bytes 4718600 | tf_op jit(solution)/shard_map/ppermute | solution.py:372
  747.8 56.4 %collective-permute-start.31 = (f32[2,256,512]{2,1,0:T(8,128)S(1)}, f32[2,256,512]{2,1,0:T(8,128)S(1)}, u32[]{:S(2)}, u32[]{:S(2)}) collective-permute-start(f32[2,256,512]{2,1,0:T(8,128)S(1)} %dynamic-slice_bitcast_fusion.1), channel_id=1, source_target_pairs={{0,16},{4,20},{8,24},{12,28},{16,0},{20,4},{24,8},{28,12},{1,17},{... | collective-permute-start | bytes 3145736 | tf_op jit(solution)/shard_map/ppermute | solution.py:402
  808.0 3.8 collective-permute-start.20
  815.7 4.7 collective-permute-start.22
  (87 other events, 1442.8 us)

commit v2 on v1

v2 whole, which is shorter than its diff:
```python
import functools

import jax
import jax.numpy as jnp
from jax import lax
from jax.experimental import pallas as pl
from jax.experimental.pallas import tpu as pltpu
from jax.sharding import PartitionSpec as P

HD = 128
EPS = 1e-06
F32 = jnp.float32
BF16 = jnp.bfloat16
MIB = 1 << 20
PACKED = HD + 8

X_SWAP = [(p, p ^ 1) for p in range(8)]
CORE_SWAP = [(h, h ^ 1) for h in range(4)]
Y_SWAP = [(h, h ^ 2) for h in range(4)]


def z_shift(k):
    return [(p, (p + 2 * k) % 8) for p in range(8)]


def z_line(k):
    return [(p, p + 2 * k) for p in range(8) if 0 <= p + 2 * k < 8]


def flip(bit):
    return [(p, p ^ bit) for p in range(8)]


def rms_scale(v):
    return lax.rsqrt(jnp.mean(v * v, axis=-1, keepdims=True) + EPS)


def norm_back(grad_normed, gain, scale, normed_hat):
    scaled = grad_normed * gain
    return scale * (scaled - normed_hat * jnp.mean(scaled * normed_hat, axis=-1, keepdims=True))


def dot(a, b, dims=((1,), (0,))):
    return lax.dot_general(a, b, (dims, ((), ())), preferred_element_type=F32)


NT = ((1,), (1,))
TN = ((0,), (0,))


def sigmoid(v):
    return 1.0 / (1.0 + jnp.exp(-v))


def triangle(kind):
    row = lax.broadcasted_iota(jnp.int32, (HD, HD), 0)
    col = lax.broadcasted_iota(jnp.int32, (HD, HD), 1)
    return {"lower": row >= col, "strict": row > col, "upper": row <= col}[kind]


def exact_dot(ones, v):
    total = None
    for _ in range(3):
        part = v.astype(BF16)
        v = v - part.astype(F32)
        term = dot(ones, part)
        total = term if total is None else total + term
    return total


def valid_rows(pos, length):
    row = lax.broadcasted_iota(jnp.int32, (HD, 1), 0)
    return (pos * HD + row) < length


def open_forget(pre, bound, ok):
    sig = sigmoid(pre)
    return sig, jnp.where(ok, bound + (1.0 - bound) * sig, 1.0)


def project_kernel(pos, lengths, x_ref, gain_ref, w_ref, bound_ref, xn_ref, away_ref, proj_ref, c_ref, qe_ref, ke_ref, intra_ref, sum_ref):
    @pl.when(pl.program_id(0) == 0)
    def _():
        x = x_ref[...].astype(F32)
        xn_ref[...] = (x * rms_scale(x) * gain_ref[...]).astype(BF16)
        n = away_ref.shape[1] // 4
        for z in range(4):
            at = pl.multiple_of((2 * z + 1 - pos[0] % 2) * n, n)
            away_ref[:, pl.ds(z * n, n)] = xn_ref[:, pl.ds(at, n)].astype(F32)

    xn = xn_ref[...]
    for c in range(4):
        proj_ref[c] = dot(xn, w_ref[c])
    slots, heads = sum_ref.shape[:2]
    lower = triangle("lower")
    ones = lower.astype(BF16)
    for s in range(slots):
        rows = pl.ds(s * HD, HD)
        ok = valid_rows(pos[0], lengths[s])
        for h in range(heads):
            cols = pl.ds(h * HD, HD)
            pre_q, pre_f, v = (proj_ref[c, rows, cols] for c in range(3))
            _, forget = open_forget(pre_f, bound_ref[:, cols], ok)
            cum = exact_dot(ones, jnp.log(forget))
            c_ref[rows, cols] = cum
            keys = 1.0 - forget
            qe = (pre_q * sigmoid(pre_q) * jnp.exp(cum)).astype(BF16)
            ke = (keys * jnp.exp(-cum)).astype(BF16)
            qe_ref[rows, cols] = qe
            ke_ref[rows, cols] = ke
            vb = v.astype(BF16)
            scores = jnp.where(lower, dot(qe, ke, NT), 0.0).astype(BF16)
            intra_ref[rows, cols] = dot(scores, vb)
            last = cum[HD - 1 :, :]
            to_end = (keys * jnp.exp(last - cum)).astype(BF16)
            sum_ref[s, h, pl.ds(0, HD), :] = dot(vb, to_end, TN)
            sum_ref[s, h, pl.ds(HD, 8), :] = jnp.broadcast_to(jnp.exp(last), (8, HD))


def split_store(keep_ref, send_ref, core, make):
    half = keep_ref.shape[1]
    keep_ref[...] = make(pl.multiple_of(core * half, half), half)
    send_ref[...] = make(pl.multiple_of((1 - core) * half, half), half)


def mixer_out_kernel(core, qe_ref, state_ref, intra_ref, pre_ref, gain_ref, w_ref, mixed_ref, gated_ref, wide_ref, keep_ref, send_ref):
    slots, heads = state_ref.shape[:2]
    for s in range(slots):
        rows = pl.ds(s * HD, HD)
        for h in range(heads):
            cols = pl.ds(h * HD, HD)
            mixed = intra_ref[rows, cols] + dot(qe_ref[rows, cols], state_ref[s, h].astype(BF16), NT)
            mixed_ref[rows, cols] = mixed
            pre = pre_ref[0, rows, cols]
            gated = mixed * rms_scale(mixed) * gain_ref[:, cols] * (pre * sigmoid(pre))
            gated_ref[rows, cols] = gated.astype(BF16)
            wide_ref[rows, cols] = gated_ref[rows, cols].astype(F32)
    split_store(keep_ref, send_ref, core[0], lambda at, n: dot(gated_ref[...], w_ref[:, pl.ds(at, n)]))


def ffn_unit(xn, dy, w_gate, w_up, w_out):
    gate, up = dot(xn, w_gate), dot(xn, w_up)
    dact = dot(dy, w_out, NT)
    sig = sigmoid(gate)
    swish = gate * sig
    act = (swish * up).astype(BF16)
    dgate = (dact * up * (sig * (1.0 + gate * (1.0 - sig)))).astype(BF16)
    dup = (dact * swish).astype(BF16)
    return act, dgate, dup


def ffn_own_kernel(core, xn_ref, dy_ref, in_ref, out_ref, in_tail, out_tail, f_keep, f_send, d_keep, d_send, f_acc, d_acc):
    step = pl.program_id(0)

    @pl.when(step == 0)
    def _():
        f_acc[...] = jnp.zeros_like(f_acc)
        d_acc[...] = jnp.zeros_like(d_acc)

    def add(w_in, w_out):
        act, dgate, dup = ffn_unit(xn_ref[...], dy_ref[...], w_in[0], w_in[1], w_out[...])
        f_acc[...] += dot(act, w_out[...])
        d_acc[...] += dot(dgate, w_in[0], NT) + dot(dup, w_in[1], NT)

    add(in_ref, out_ref)

    @pl.when(step == pl.num_programs(0) - 1)
    def _():
        add(in_tail, out_tail)
        split_store(f_keep, f_send, core[0], lambda at, n: f_acc[:, pl.ds(at, n)])
        split_store(d_keep, d_send, core[0], lambda at, n: d_acc[:, pl.ds(at, n)])


def widen_kernel(at, a_ref, out_ref):
    n = out_ref.shape[1]
    out_ref[...] = a_ref[:, pl.ds(pl.multiple_of(at[0] * n, n), n)].astype(F32)


def assemble_kernel(at, *refs):
    out_ref = refs[-1]
    for k, piece in enumerate(refs[:-1]):
        n = piece.shape[1]
        out_ref[:, pl.ds(pl.multiple_of(at[k], n), n)] = piece[...].astype(BF16)


def ffn_grad_kernel(lines, tail, rows, *refs):
    step = pl.program_id(0)
    tokens, refs = refs[: 2 * lines], refs[2 * lines :]
    weights, outs = (refs[:4], refs[4:]) if tail else (refs[:2], refs[2:])
    n = outs[0].shape[1]

    def put(w_in, w_out, targets):
        for k in range(lines):
            xs, dys = tokens[2 * k], tokens[2 * k + 1]
            act, dgate, dup = ffn_unit(xs[...], dys[...], w_in[0], w_in[1], w_out[...])
            for which in range(2):
                gin, gout = targets[which], targets[2 + which]
                at = pl.ds(pl.multiple_of(rows[which] * n, n), n)
                x = xs[:, at]
                sums = dot(x, dgate, TN), dot(x, dup, TN), dot(act, dys[:, at], TN)
                if k == 0:
                    gin[0], gin[1], gout[...] = sums
                else:
                    gin[0] += sums[0]
                    gin[1] += sums[1]
                    gout[...] += sums[2]

    put(weights[0], weights[1], outs[:4])
    if tail:

        @pl.when(step == pl.num_programs(0) - 1)
        def _():
            put(weights[2], weights[3], outs[4:])


def mix_grad_kernel(turned, place, xn_ref, xn_got, *refs):
    keep_ref, send_ref = refs[-2:]
    n = xn_ref.shape[1] // 8
    z, x = place[0] // 2, place[0] % 2
    for c in range(keep_ref.shape[0]):
        own, got = refs[2 * c][...].astype(BF16), refs[2 * c + 1][...].astype(BF16)
        for high in range(2):
            for out, low in ((keep_ref, z % 2), (send_ref, 1 - z % 2)):
                row = 2 * high + low
                a = xn_ref[:, pl.ds(pl.multiple_of((2 * row + x) * n, n), n)]
                b = xn_got[:, pl.ds(pl.multiple_of(row * n, n), n)].astype(BF16)
                out[c, high] = dot(own, a, TN) + dot(got, b, TN) if turned else dot(a, own, TN) + dot(b, got, TN)


def norm_back_kernel(db_ref, w_ref, mixed_ref, pre_ref, gain_ref, qe_ref, sum_ref, dpre_ref, dm_ref, dgain_ref, back_ref, dg_ref):
    dg_ref[...] = dot(db_ref[...], w_ref[...], NT)
    slots, heads = sum_ref.shape[:2]
    for h in range(heads):
        cols = pl.ds(h * HD, HD)
        gain = gain_ref[:, cols]
        total = jnp.zeros((1, HD), F32)
        for s in range(slots):
            rows = pl.ds(s * HD, HD)
            mixed, pre, dgated = mixed_ref[rows, cols], pre_ref[0, rows, cols], dg_ref[rows, cols]
            scale = rms_scale(mixed)
            hat = mixed * scale
            sig = sigmoid(pre)
            swish = pre * sig
            total += jnp.sum(dgated * hat * swish, axis=0, keepdims=True)
            dpre_ref[rows, cols] = (dgated * hat * gain * (sig * (1.0 + pre * (1.0 - sig)))).astype(BF16).astype(F32)
            dm = norm_back(dgated * swish, gain, scale, hat).astype(BF16)
            dm_ref[rows, cols] = dm
            back_ref[s, h, pl.ds(0, HD), :] = dot(dm, qe_ref[rows, cols], TN)
            back_ref[s, h, pl.ds(HD, 8), :] = sum_ref[s, h, pl.ds(HD, 8), :]
        dgain_ref[:, cols] = total


def intra_back_kernel(dm_ref, qe_ref, ke_ref, proj_ref, c_ref, state_ref, dq_ref, dk_ref, dv_ref, dl_ref):
    slots, heads = state_ref.shape[:2]
    lower = triangle("lower")
    upper = triangle("upper").astype(BF16)
    for s in range(slots):
        rows = pl.ds(s * HD, HD)
        for h in range(heads):
            cols = pl.ds(h * HD, HD)
            dm, qe, ke, cum = (r[rows, cols] for r in (dm_ref, qe_ref, ke_ref, c_ref))
            vb = proj_ref[2, rows, cols].astype(BF16)
            dscores = jnp.where(lower, dot(dm, vb, NT), 0.0).astype(BF16)
            to_q = dot(dscores, ke) + dot(dm, state_ref[s, h].astype(BF16))
            to_k = dot(dscores, qe, TN)
            pre = proj_ref[0, rows, cols]
            sig = sigmoid(pre)
            dq_ref[rows, cols] = (jnp.exp(cum) * to_q * (sig * (1.0 + pre * (1.0 - sig)))).astype(BF16).astype(F32)
            dk_ref[rows, cols] = jnp.exp(-cum) * to_k
            scores = jnp.where(lower, dot(qe, ke, NT), 0.0).astype(BF16)
            dv_ref[rows, cols] = dot(scores, dm, TN)
            dl_ref[rows, cols] = exact_dot(upper, qe.astype(F32) * to_q - ke.astype(F32) * to_k)


def state_back_kernel(pos, lengths, carried_ref, state_ref, ke_ref, forget_ref, value_ref, c_ref, bound_ref, dk_ref, dv_ref, dl_ref, df_ref, dval_ref, dbound_ref):
    slots, heads = state_ref.shape[:2]
    strict = triangle("strict").astype(BF16)
    for h in range(heads):
        cols = pl.ds(h * HD, HD)
        bound = bound_ref[:, cols]
        total = jnp.zeros((1, HD), F32)
        for s in range(slots):
            rows = pl.ds(s * HD, HD)
            ok = valid_rows(pos[0], lengths[s])
            cum, ke = c_ref[rows, cols], ke_ref[rows, cols]
            ending = carried_ref[s, h] * jnp.exp(cum[HD - 1 :, :])
            ending_low = ending.astype(BF16)
            to_k = dot(value_ref[0, rows, cols].astype(BF16), ending_low)
            dval_ref[rows, cols] = (dv_ref[rows, cols] + dot(ke, ending_low, NT)).astype(BF16).astype(F32)
            through = jnp.sum(ending * state_ref[s, h], axis=0, keepdims=True)
            dlogf = dl_ref[rows, cols] + exact_dot(strict, ke.astype(F32) * to_k) + through
            dkeys = dk_ref[rows, cols] + jnp.exp(-cum) * to_k
            sig, forget = open_forget(forget_ref[0, rows, cols], bound, ok)
            dforget = jnp.where(ok, dlogf / forget - dkeys, 0.0)
            total += jnp.sum(dforget * (1.0 - sig), axis=0, keepdims=True)
            df_ref[rows, cols] = (dforget * (1.0 - bound) * sig * (1.0 - sig)).astype(BF16).astype(F32)
        dbound_ref[:, cols] = total


SMEM = pl.BlockSpec(memory_space=pltpu.SMEM)


def whole(shape, *index):
    index = index or (0,) * len(shape)
    return pl.BlockSpec(shape, lambda *_: index)


def sds(shape, dtype=F32):
    return jax.ShapeDtypeStruct(shape, dtype)


def call(kernel, name, outs, in_specs, out_specs, flops, moved, grid=(1,), scratch=(), vmem=48):
    return pl.pallas_call(
        kernel,
        name=name,
        grid=grid,
        out_shape=outs,
        in_specs=in_specs,
        out_specs=out_specs,
        scratch_shapes=list(scratch),
        compiler_params=pltpu.CompilerParams(vmem_limit_bytes=vmem * MIB),
        cost_estimate=pl.CostEstimate(flops=int(flops), bytes_accessed=int(moved), transcendentals=0),
    )


def entering_all(packed, backward):
    count, mine = lax.axis_size("seq"), lax.axis_index("seq")
    pieces = lax.all_gather(packed, "seq")
    if backward:
        pieces, mine = pieces[::-1], count - 1 - mine

    def step(position, state):
        piece = pieces[position]
        longer = piece[:, :, HD : HD + 1] * state + piece[:, :, :HD]
        return jnp.where(position < mine, longer, state)

    return lax.fori_loop(0, count - 1, step, jnp.zeros_like(packed[:, :, :HD]))


def decay(a):
    return a[:, HD : HD + 1]


def state(a):
    return a[:, :HD]


def join(a, b):
    both = decay(b) * state(a) + state(b)
    return jnp.concatenate([both, jnp.broadcast_to(decay(a) * decay(b), (a.shape[0], 8, HD))], axis=1)


def is_first(backward):
    is_low = lax.axis_index("seq") % 2 == 0
    return is_low, (~is_low if backward else is_low)


def pair_states(packed, backward):
    packed = packed.reshape(-1, PACKED, HD)
    half = packed.shape[0] // 2
    is_low, first = is_first(backward)
    mine = jnp.where(is_low, packed[:half], packed[half:])
    other = lax.ppermute(jnp.where(is_low, packed[half:], packed[:half]), "seq", X_SWAP)
    return jnp.where(first, mine, other), jnp.where(first, other, mine)


def pass_states(pair, backward):
    step = -1 if backward else 1
    before = lax.ppermute(pair, "seq", z_line(step))
    further = lax.ppermute(join(before, pair), "seq", z_line(2 * step))
    return decay(before) * state(further) + state(before)


def enter_states(early, into_first, shape, backward):
    is_low, first = is_first(backward)
    into_second = decay(early) * into_first + state(early)
    kept = jnp.where(first, into_first, into_second)
    given = lax.ppermute(jnp.where(first, into_second, into_first), "seq", X_SWAP)
    low, high = jnp.where(is_low, kept, given), jnp.where(is_low, given, kept)
    return jnp.concatenate([low, high]).reshape(shape)


def tie(*values):
    return lax.optimization_barrier(values)


def core_swap(a):
    return lax.ppermute(a, "head", CORE_SWAP)


def y_swap(a):
    return lax.ppermute(a, "head", Y_SWAP)


def x_swap(a):
    return lax.ppermute(a, "seq", X_SWAP)


def join_halves(half):
    other = core_swap(half)
    low = lax.axis_index("head") % 2 == 0
    return jnp.concatenate([jnp.where(low, half, other), jnp.where(low, other, half)], axis=1)


def assemble(pieces, width):
    head = lax.axis_index("head")
    arrays, at = [], []
    for own, over, offset in pieces:
        for k, a in enumerate((own, core_swap(own), over, core_swap(over))):
            arrays.append(a)
            at.append((head ^ k) * (width // 4) + offset)
    tokens = arrays[0].shape[0]
    step = tokens // 3
    return call(
        assemble_kernel,
        "assemble",
        sds((tokens, width), BF16),
        [SMEM] + [pl.BlockSpec((step, a.shape[1]), lambda i: (i, 0)) for a in arrays],
        pl.BlockSpec((step, width), lambda i: (i, 0)),
        0,
        6 * tokens * width,
        grid=(3,),
    )(jnp.stack(at).astype(jnp.int32), *arrays)


class Calls:
    def __init__(self, slots, length, width, local, units):
        self.slots, self.count, self.width, self.local, self.units = slots, slots * length, width, local, units
        self.heads = local // HD
        self.pair = 2 * HD
        self.steps = units // self.pair
        self.rest = units - self.steps * self.pair
        self.tall, self.channel = whole((self.count, width)), whole((self.count, local))
        self.row, self.w_spec = whole((1, local)), whole((local, width))
        self.half, self.half_spec = sds((self.count, width // 2)), whole((self.count, width // 2))
        self.state_shape = (slots, self.heads, HD, HD)
        self.packed_shape = (slots, self.heads, PACKED, HD)
        self.state_spec, self.packed_spec = whole(self.state_shape), whole(self.packed_shape)
        self.low = sds((self.count, local), BF16)
        self.full = sds((self.count, local))

    def proj(self, *index):
        return whole((1, self.count, self.local), *index)

    def project(self, pos, lengths, tokens, norm, weight, bound):
        count, width, local, pair = self.count, self.width, self.local, self.pair
        block = pl.BlockSpec((count, pair), lambda i: (0, i))
        return call(
            project_kernel,
            "project",
            [sds((count, width), BF16), self.half, sds((4, count, local)), self.full, self.low, self.low, self.full, sds(self.packed_shape)],
            [SMEM, SMEM, self.tall, whole((1, width)), pl.BlockSpec((4, width, pair), lambda i: (0, 0, i)), pl.BlockSpec((1, pair), lambda i: (0, i))],
            [self.tall, self.half_spec, pl.BlockSpec((4, count, pair), lambda i: (0, 0, i))] + [block] * 4 + [pl.BlockSpec((self.slots, 2, PACKED, HD), lambda i: (0, i, 0, 0))],
            8 * count * width * local,
            20e6,
            grid=(local // pair,),
        )(pos, lengths, tokens, norm, weight, bound)

    def mixer_out(self, core, qe, states, intra, proj, gain, weight):
        return call(
            mixer_out_kernel,
            "mixer_out",
            [self.full, self.low, self.full, self.half, self.half],
            [SMEM, self.channel, self.state_spec, self.channel, self.proj(3, 0, 0), self.row, self.w_spec],
            [self.channel] * 3 + [self.half_spec] * 2,
            2 * self.count * self.width * self.local,
            10e6,
        )(core, qe, states, intra, proj, gain, weight)

    def ffn_specs(self, first=0, tail=True):
        width, pair, rest = self.width, self.pair, self.rest
        last = self.steps * pair // rest
        specs = [
            pl.BlockSpec((2, width, pair), lambda i: (0, 0, i + first)),
            pl.BlockSpec((pair, width), lambda i: (i + first, 0)),
            whole((2, width, rest), 0, 0, last),
            whole((rest, width), last, 0),
        ]
        return specs if tail else specs[:2]

    def ffn_own(self, core, xn2, dy, ffn_in, ffn_out):
        return call(
            ffn_own_kernel,
            "ffn_own",
            [self.half] * 4,
            [SMEM, self.tall, self.tall, *self.ffn_specs()],
            [self.half_spec] * 4,
            12 * self.count * self.width * self.units,
            30e6,
            grid=(self.steps,),
            scratch=[pltpu.VMEM((self.count, self.width), F32)] * 2,
            vmem=60,
        )(core, xn2, dy, ffn_in, ffn_out, ffn_in, ffn_out)

    def norm_back(self, dbranch, weight, mixed, proj, gain, qe, packed):
        return call(
            norm_back_kernel,
            "norm_back",
            [self.full, self.low, sds((1, self.local)), sds(self.packed_shape)],
            [self.tall, self.w_spec, self.channel, self.proj(3, 0, 0), self.row, self.channel, self.packed_spec],
            [self.channel, self.channel, self.row, self.packed_spec],
            2 * self.count * self.width * self.local,
            10e6,
            scratch=[pltpu.VMEM((self.count, self.local), F32)],
        )(dbranch, weight, mixed, proj, gain, qe, packed)

    def intra_back(self, dmixed, qe, ke, proj, cum, states):
        return call(
            intra_back_kernel,
            "intra_back",
            [self.full] * 4,
            [self.channel, self.channel, self.channel, whole((3, self.count, self.local)), self.channel, self.state_spec],
            [self.channel] * 4,
            14 * self.count * self.local * HD,
            10e6,
        )(dmixed, qe, ke, proj, cum, states)

    def state_back(self, pos, lengths, carried, states, ke, proj, cum, bound, dkeys, dvalues, dlogf):
        return call(
            state_back_kernel,
            "state_back",
            [self.full, self.full, sds((1, self.local))],
            [SMEM, SMEM, self.state_spec, self.state_spec, self.channel, self.proj(1, 0, 0), self.proj(2, 0, 0), self.channel, self.row] + [self.channel] * 3,
            [self.channel, self.channel, self.row],
            8 * self.count * self.local * HD,
            10e6,
        )(pos, lengths, carried, states, ke, proj, proj, cum, bound, dkeys, dvalues, dlogf)

    def widen(self, head, dy):
        quarter = self.width // 4
        return call(widen_kernel, "widen", sds((self.count, quarter)), [SMEM, self.tall], whole((self.count, quarter)), 0, 4e6)(head, dy)

    def mix_grad(self, place, xn, xn_got, *grads, turned=False):
        n = self.width // 8
        shape = (len(grads) // 2, 2, *((self.local, n) if turned else (n, self.local)))
        return call(
            functools.partial(mix_grad_kernel, turned),
            "mix_grad",
            [sds(shape)] * 2,
            [SMEM, self.tall, self.half_spec] + [self.channel] * len(grads),
            [whole(shape)] * 2,
            len(grads) * self.count * self.width * self.local,
            10e6,
        )(place, xn, xn_got, *grads)

    def ffn_grad(self, rows, lines, ffn_in, ffn_out, first, steps):
        n, pair, rest = self.width // 8, self.pair, self.rest
        tail = first + steps == self.steps and rest > 0
        main = steps * pair
        outs = [sds((2, n, main))] * 2 + [sds((main, n))] * 2
        gin, gout = pl.BlockSpec((2, n, pair), lambda i: (0, 0, i)), pl.BlockSpec((pair, n), lambda i: (i, 0))
        specs = [gin, gin, gout, gout]
        if tail:
            outs += [sds((2, n, rest))] * 2 + [sds((rest, n))] * 2
            specs += [whole(o.shape) for o in outs[4:]]
        tokens = [a for line in lines for a in line]
        return call(
            functools.partial(ffn_grad_kernel, len(lines), tail),
            "ffn_grad",
            outs,
            [SMEM] + [self.tall] * len(tokens) + self.ffn_specs(first, tail),
            specs,
            6 * len(lines) * self.count * (self.width + 2 * n) * (main + rest * tail),
            20e6,
            grid=(steps,),
            vmem=60,
        )(rows, *tokens, *([ffn_in, ffn_out] * (2 if tail else 1)))


def scalar(v):
    return jnp.asarray(v, jnp.int32).reshape(1)


def body(tokens, lengths, norm_first, mix_weight, lower_bound, out_gain, w_out, norm_second, ffn_in, ffn_out, cotangent):
    shape = tokens.shape
    slots, length, width = shape
    local = lower_bound.shape[0]
    do = Calls(slots, length, width, local, ffn_out.shape[0])
    fast = lax.axis_size("seq") == 8 and lax.axis_size("head") == 4
    run = run_lines if fast else run_any
    output, grad_tokens, small, weights = run(
        do,
        tokens.reshape(do.count, width),
        lengths,
        norm_first.reshape(1, width),
        mix_weight,
        lower_bound.reshape(1, local),
        out_gain.reshape(1, local),
        w_out,
        norm_second.reshape(1, width),
        ffn_in,
        ffn_out,
        cotangent.reshape(do.count, width),
    )
    first, second = small[:width], small[width : 2 * width]
    bound_sum, gain_sum = small[2 * width : 2 * width + local], small[2 * width + local :]
    return (output.reshape(shape), grad_tokens.reshape(shape), first, weights[0], bound_sum, gain_sum, weights[1], second, weights[2], weights[3])


def second_norm(tokens, branch, gain):
    hidden = tokens.astype(F32) + branch
    scale = rms_scale(hidden)
    hat = hidden * scale
    return hidden, scale, hat, hat * gain


def run_any(do, tokens, lengths, norm_first, mix_weight, bound, gain, w_out, norm_second, ffn_in, ffn_out, dy):
    def total(keep, send):
        return lax.psum(jnp.concatenate([keep, send], axis=1), "head")

    pos, core = scalar(lax.axis_index("seq")), scalar(0)
    xn1, _, proj, cum, qe, ke, intra, packed = do.project(pos, lengths, tokens, norm_first, mix_weight, bound)
    states = entering_all(packed, False)
    mixed, gated, _, keep, send = do.mixer_out(core, qe, states, intra, proj, gain, w_out)
    hidden, scale_two, hat_two, wide = second_norm(tokens, total(keep, send), norm_second)
    xn2 = wide.astype(BF16)
    keep, send, dkeep, dsend = do.ffn_own(core, xn2, dy, ffn_in, ffn_out)
    dxn2 = total(dkeep, dsend)
    output = (hidden + total(keep, send)).astype(BF16)
    part_norm_second = jnp.sum(dxn2 * hat_two, axis=0)
    dhidden = dy.astype(F32) + norm_back(dxn2, norm_second, scale_two, hat_two)
    dbranch = dhidden.astype(BF16)
    dpre_gate, dmixed, part_gain, back = do.norm_back(dbranch, w_out, mixed, proj, gain, qe, packed)
    carried = entering_all(back, True)
    dpre_query, dkeys, dvalues, dlogf = do.intra_back(dmixed, qe, ke, proj, cum, states)
    dpre_forget, dpre_values, part_bound = do.state_back(pos, lengths, carried, states, ke, proj, cum, bound, dkeys, dvalues, dlogf)
    dproj = (dpre_query, dpre_forget, dpre_values, dpre_gate)
    x = tokens.astype(F32)
    scale_one = rms_scale(x)
    hat_one = x * scale_one
    dxn1 = lax.psum(sum(dot(d.astype(BF16), mix_weight[c], NT) for c, d in enumerate(dproj)), "head")
    part_norm_first = jnp.sum(dxn1 * hat_one, axis=0)
    grad_tokens = (dhidden + norm_back(dxn1, norm_first, scale_one, hat_one)).astype(BF16)
    weights = weight_grads_whole(xn1, dproj, gated, dbranch, xn2, dy, ffn_in, ffn_out)
    small = lax.psum(jnp.concatenate([part_norm_first, part_norm_second, part_bound[0], part_gain[0]]), "seq")
    return output, grad_tokens, small, weights


def run_lines(do, tokens, lengths, norm_first, mix_weight, bound, gain, w_out, norm_second, ffn_in, ffn_out, dy):
    width, local, quarter = do.width, do.local, do.width // 4
    seq, head = lax.axis_index("seq"), lax.axis_index("head")
    x, z = seq % 2, seq // 2
    place, core = scalar(seq), scalar(head % 2)

    def shift(a, k):
        return lax.ppermute(a, "seq", z_shift(k))

    def head_quarter(a):
        n = a.shape[1] // 4
        return lax.dynamic_slice_in_dim(a, head * n, n, 1)

    dy_quarter = do.widen(scalar(head), dy)
    dy_left, dy_right = jnp.split(dy_quarter, 2, axis=1)
    dy1, dy3a = shift(dy_quarter, 1), shift(dy_left, 3)
    xn1, xn1_away, proj, cum, qe, ke, intra, packed = do.project(place, lengths, tokens, norm_first, mix_weight, bound)
    early, late = pair_states(packed, False)
    early, late, dy1, dy3a = tie(early, late, dy1, dy3a)

    into = pass_states(join(early, late), False)
    dy1_over = y_swap(dy1)
    early, into, dy1_over, dy3a, dy_right = tie(early, into, dy1_over, dy3a, dy_right)

    states = enter_states(early, into, do.state_shape, False)
    dy3b = shift(dy_right, 3)
    dy3a_over = y_swap(dy3a)
    states, dy3b, dy3a_over = tie(states, dy3b, dy3a_over)
    mixed, gated, gated_wide, keep, send = do.mixer_out(core, qe, states, intra, proj, gain, w_out)
    half = keep + core_swap(send)
    half, dy_quarter, dy3b, xn1_away = tie(half, dy_quarter, dy3b, xn1_away)

    half = half + y_swap(half)
    dy2 = shift(dy_quarter, 2)
    xn1_got = x_swap(xn1_away)
    half, dy2, dy3b, gated_wide, xn1_got = tie(half, dy2, dy3b, gated_wide, xn1_got)

    dy2_over, dy3b_over = y_swap(dy2), y_swap(dy3b)
    hidden, scale_two, hat_two, wide = second_norm(tokens, join_halves(half), norm_second)
    xn2 = wide.astype(BF16)
    xn_quarter = head_quarter(wide)
    xnl1 = shift(xn_quarter, 1)
    gated_got = x_swap(gated_wide)
    keep, send, dkeep, dsend = do.ffn_own(core, xn2, dy, ffn_in, ffn_out)
    dkeep, dsend, xn_quarter, dy2_over, dy3b_over, xnl1, gated_got, keep, send = tie(dkeep, dsend, xn_quarter, dy2_over, dy3b_over, xnl1, gated_got, keep, send)

    dhalf = dkeep + core_swap(dsend)
    dhalf, xn_quarter = tie(dhalf, xn_quarter)
    dhalf = dhalf + y_swap(dhalf)
    xnl2 = shift(xn_quarter, 2)
    dhalf, xnl2, xn_quarter, xnl1 = tie(dhalf, xnl2, xn_quarter, xnl1)

    dxn2 = join_halves(dhalf)
    xnl3 = shift(xn_quarter, 3)
    xnl1_over = y_swap(xnl1)
    part_norm_second = jnp.sum(dxn2 * hat_two, axis=0)
    dhidden = dy.astype(F32) + norm_back(dxn2, norm_second, scale_two, hat_two)
    dbranch = dhidden.astype(BF16)
    dbranch_away = lax.dynamic_index_in_dim(dhidden.reshape(do.count, 8, width // 8), 2 * head + 1 - x, 1, keepdims=False)
    dpre_gate, dmixed, part_gain, back = do.norm_back(dbranch, w_out, mixed, proj, gain, qe, packed)
    back, dpre_gate, xnl3, xnl1_over, dmixed, dbranch, xnl2, dbranch_away = tie(back, dpre_gate, xnl3, xnl1_over, dmixed, dbranch, xnl2, dbranch_away)

    early, late = pair_states(back, True)
    early, late, dpre_gate, dmixed, dbranch_away, xnl2 = tie(early, late, dpre_gate, dmixed, dbranch_away, xnl2)
    into = pass_states(join(early, late), True)
    dpre_query, dkeys, dvalues, dlogf = do.intra_back(dmixed, qe, ke, proj, cum, states)
    gate_got, dbranch_own = x_swap(dpre_gate), x_swap(dbranch_away)
    xnl2_over = y_swap(xnl2)
    early, into, gate_got, xnl2_over, dpre_query, dbranch_own, xnl3 = tie(early, into, gate_got, xnl2_over, dpre_query, dbranch_own, xnl3)

    carried = enter_states(early, into, do.state_shape, True)
    xnl3_over, dbranch_over = y_swap(xnl3), y_swap(dbranch_own)
    dpre_forget, dpre_values, part_bound = do.state_back(place, lengths, carried, states, ke, proj, cum, bound, dkeys, dvalues, dlogf)
    gate_keep, gate_send = do.mix_grad(place, xn1, xn1_got, dpre_gate, gate_got)
    dbranch_got = assemble([(dbranch_own, dbranch_over, 0)], width // 2)
    w_keep, w_send = do.mix_grad(place, dbranch, dbranch_got, gated, gated_got, turned=True)
    dpre_forget, dpre_values, dpre_query, gate_keep, gate_send, w_keep, w_send, xnl3_over = tie(
        dpre_forget, dpre_values, dpre_query, gate_keep, gate_send, w_keep, w_send, xnl3_over
    )

    forget_got, query_got, values_got = x_swap(dpre_forget), x_swap(dpre_query), x_swap(dpre_values)
    gate_near = gate_keep + lax.ppermute(gate_send, "seq", flip(2))
    w_near = w_keep + lax.ppermute(w_send, "seq", flip(2))
    lines = [
        (xn2, dy),
        (assemble([(xnl1, xnl1_over, 0)], width), assemble([(dy1, dy1_over, 0)], width)),
        (assemble([(xnl2, xnl2_over, 0)], width), assemble([(dy2, dy2_over, 0)], width)),
        (assemble([(xnl3, xnl3_over, 0)], width), assemble([(dy3a, dy3a_over, 0), (dy3b, dy3b_over, quarter // 2)], width)),
    ]
    rows = jnp.stack([seq, seq ^ 1]).astype(jnp.int32)
    cut = (do.steps + 1) // 2
    in_a, in_away_a, out_a, out_away_a = do.ffn_grad(rows, lines, ffn_in, ffn_out, 0, cut)
    dproj = (dpre_query, dpre_forget, dpre_values, dpre_gate)
    dxn1 = sum(dot(d.astype(BF16), mix_weight[c], NT) for c, d in enumerate(dproj))
    at = core[0] * (width // 2)
    half = lax.dynamic_slice_in_dim(dxn1, at, width // 2, 1) + core_swap(lax.dynamic_slice_in_dim(dxn1, width // 2 - at, width // 2, 1))
    forget_got, query_got, values_got, gate_near, w_near, in_away_a, out_away_a, half = tie(
        forget_got, query_got, values_got, gate_near, w_near, in_away_a, out_away_a, half
    )

    def high_bit(near):
        high = z // 2
        return (lax.dynamic_index_in_dim(near, at, 1, keepdims=False) for at in (high, 1 - high))

    gate_part, gate_far = high_bit(gate_near)
    w_part, w_far = high_bit(w_near)
    grad_gate = gate_part + lax.ppermute(gate_far, "seq", flip(4))
    grad_w_out = (w_part + lax.ppermute(w_far, "seq", flip(4)))[0]
    keep2, send2 = do.mix_grad(place, xn1, xn1_got, dpre_query, query_got, dpre_forget, forget_got)
    near2 = keep2 + lax.ppermute(send2, "seq", flip(2))
    v_keep, v_send = do.mix_grad(place, xn1, xn1_got, dpre_values, values_got)
    grad_in_a, grad_out_a = in_a + x_swap(in_away_a), out_a + x_swap(out_away_a)
    half = half + y_swap(half)
    in_b, in_away_b, out_b, out_away_b, tin, tin_away, tout, tout_away = do.ffn_grad(rows, lines, ffn_in, ffn_out, cut, do.steps - cut)
    grad_gate, grad_w_out, near2, v_send, grad_in_a, grad_out_a, half, in_away_b, out_away_b, tin_away, tout_away, send, keep = tie(
        grad_gate, grad_w_out, near2, v_send, grad_in_a, grad_out_a, half, in_away_b, out_away_b, tin_away, tout_away, send, keep
    )

    tokens_wide = tokens.astype(F32)
    scale_one = rms_scale(tokens_wide)
    hat_one = tokens_wide * scale_one
    dxn1 = join_halves(half)
    part_norm_first = jnp.sum(dxn1 * hat_one, axis=0)
    grad_tokens = (dhidden + norm_back(dxn1, norm_first, scale_one, hat_one)).astype(BF16)
    part2, far2 = high_bit(near2)
    grad2 = part2 + lax.ppermute(far2, "seq", flip(4))
    v_near = v_keep + lax.ppermute(v_send, "seq", flip(2))
    grad_in = jnp.concatenate([grad_in_a, in_b + x_swap(in_away_b), tin + x_swap(tin_away)], axis=2)
    grad_out = jnp.concatenate([grad_out_a, out_b + x_swap(out_away_b), tout + x_swap(tout_away)], axis=0)
    half = keep + core_swap(send)
    half = half + y_swap(half)
    v_near, half, part_norm_first, grad2 = tie(v_near, half, part_norm_first, grad2)

    output = (hidden + join_halves(half)).astype(BF16)
    v_part, v_far = high_bit(v_near)
    grad_v = v_part + lax.ppermute(v_far, "seq", flip(4))
    grad_mix = jnp.concatenate([grad2, grad_v, grad_gate])

    small = jnp.concatenate([part_norm_first, part_norm_second, part_bound[0], part_gain[0]])
    for bit in (1, 2, 4):
        small = small + lax.ppermute(small, "seq", flip(bit))
    return output, grad_tokens, small, (grad_mix, grad_w_out, grad_in, grad_out)


def weight_grads_whole(xn1, dproj, gated, dbranch, xn2, dy, ffn_in, ffn_out):
    gate, up = dot(xn2, ffn_in[0]), dot(xn2, ffn_in[1])
    dact = dot(dy, ffn_out, NT)
    sig = sigmoid(gate)
    swish = gate * sig
    act = (swish * up).astype(BF16)
    dgate = (dact * up * (sig * (1.0 + gate * (1.0 - sig)))).astype(BF16)
    dup = (dact * swish).astype(BF16)

    def scatter(a, axis):
        return lax.psum_scatter(a, "seq", scatter_dimension=axis, tiled=True)

    return (
        jnp.stack([scatter(dot(xn1, d.astype(BF16), TN), 0) for d in dproj]),
        scatter(dot(gated, dbranch, TN), 1),
        jnp.stack([scatter(dot(xn2, d, TN), 0) for d in (dgate, dup)]),
        scatter(dot(act, dy, TN), 1),
    )


def solution(mesh):
    in_specs = (
        P(None, "seq", None),
        P(),
        P(),
        P(None, None, "head"),
        P("head"),
        P("head"),
        P("head", None),
        P(),
        P(None, None, "head"),
        P("head", None),
        P(None, "seq", None),
    )
    out_specs = (
        P(None, "seq", None),
        P(None, "seq", None),
        P(),
        P(None, "seq", "head"),
        P("head"),
        P("head"),
        P("head", "seq"),
        P(),
        P(None, "seq", "head"),
        P("head", "seq"),
    )
    return jax.shard_map(body, mesh=mesh, in_specs=in_specs, out_specs=out_specs, check_vma=False)
```

time: 827 us -> 604 us (0.73)
  waiting for transfers between devices: 466 us -> 236 us
  Pallas kernels: 134 us -> 145 us
  other arithmetic: 71.5 us -> 62.1 us
    ppermute x51 -> x75, waiting for transfers between devices: 466 us -> 236 us  [the longest x12 73.1 us: y_swap(): return lax.ppermute(a, 'head', Y_SWAP)]
    unnamed x181 -> x260, local copies, waits for them, and re-layouts: 10.2 us -> 29.4 us
    concatenate x10 -> x4, local copies, waits for them, and re-layouts: 22.1 us -> 11.5 us  [join_halves(): jnp.concatenate([jnp.where(low, half, other), jnp.where(low, other, half)...]
    pallas_call x12 -> x20, Pallas kernels: 134 us -> 145 us  [the longest x2 63 us: ffn_grad(): call(functools.partial(ffn_grad_kernel, len(lines), tail), 'ffn_grad', ou...]
    convert_element_type x2 -> x0, local copies, waits for them, and re-layouts: 9.61 us -> none  [the longest x1 5.52 us: body(): hidden = tokens.astype(F32) + sum_heads(keep, send, fast)]
    ppermute x51 -> x75, starting transfers between devices: 77.2 us -> 84 us  [the longest x7 24.4 us: shift(): return lax.ppermute(a, 'seq', z_shift(k))]
    select_n x13 -> x12, other arithmetic: 16.8 us -> 10.6 us  [the longest x4 7.03 us: join_halves(): jnp.where(low, half, other)]
    add x21 -> x27, other arithmetic: 29.1 us -> 27 us  [the longest x1 5.71 us: run_lines(): dhidden = dy.astype(F32) + norm_back(dxn2, norm_second, scale_two, hat_two)]
  transfers between devices with their start and end apart: 51 -> 75, of which waited for: 25 -> 29; matrix products, arithmetic and copies ran while one was open for 15% -> 16% of each run, Pallas kernels for 11% -> 24%
where the time goes in v2:
time: 604 us; the launch traced here: 596 us
  waiting for transfers between devices  236 us (39%)
  Pallas kernels  145 us (24%)
  starting transfers between devices  84 us (14%)
  other arithmetic  62.1 us (10%)
  local copies, waits for them, and re-layouts  49.7 us (8%)
  matrix products  15.9 us (3%)
    ppermute x12, waiting for transfers between devices, y_swap(): return lax.ppermute(a, 'head', Y_SWAP)  73.1 us
    pallas_call x2, Pallas kernels, ffn_grad(): call(functools.partial(ffn_grad_kernel, len(lines), tail), 'ffn_grad', ou...  63 us
    ppermute x13, waiting for transfers between devices, x_swap(): return lax.ppermute(a, 'seq', X_SWAP)  37 us
    unnamed x260, local copies, waits for them, and re-layouts  29.4 us
    ppermute x7, starting transfers between devices, shift(): return lax.ppermute(a, 'seq', z_shift(k))  24.4 us
    ppermute x3, waiting for transfers between devices, run_lines(): small = small + lax.ppermute(small, 'seq', flip(bit))  24 us
    pallas_call x1, Pallas kernels, ffn_own(): call(ffn_own_kernel, 'ffn_own', [self.half] * 4, [SMEM, self.tall, self.t...  23.2 us
    ppermute x2, waiting for transfers between devices, pair_states(): lax.ppermute(jnp.where(is_low, packed[half:], packed[:half]), 'seq', X_SWAP)  16.2 us
  transfers between devices with their start and end apart: 75, of which 29 were waited for; matrix products, arithmetic and copies ran while one was open for 16% of the time, Pallas kernels for 24%

profile of v2, /device:TPU:0, one launch (start us, length us, event | category | flops | bytes accessed | tf_op | source)
XLA Modules:
  0.0 595.9 jit_solution(18216143597586845541)
XLA Ops:
  2.1 3.1 collective-permute-start.1
  5.2 12.6 %project.1 = (bf16[384,2048]{1,0:T(8,128)(2,1)S(1)}, f32[384,1024]{1,0:T(8,128)}, f32[4,384,512]{2,1,0:T(8,128)}, f32[384,512]{1,0:T(8,128)S(1)}, bf16[384,512]{...) custom-call(s32[1]{0:T(128)} %bitcast.1.pos.place, ...), custom_call_target="tpu_custom_call" | custom-call | flops 3221225472 | bytes 20000000 | tf_op jit(solution)/shard_map/project/pallas_call | solution.py:448
  22.9 6.2 %collective-permute-done = f32[6,136,128]{2,1,0:T(8,128)S(1)} collective-permute-done((f32[6,136,128]{2,1,0:T(8,128)S(1)}, f32[6,136,128]{2,1,0:T(8,128)S(1)}, u32[]{:S(2)}, u32[]{:S(2)}) %collective-permute-start) | collective-permute-done | bytes 417824 | tf_op jit(solution)/shard_map/ppermute | solution.py:363
  29.2 4.0 collective-permute-done.2.refs_0_
  37.4 7.2 %collective-permute-done.3 = f32[6,136,128]{2,1,0:T(8,128)S(1)} collective-permute-done((f32[6,136,128]{2,1,0:T(8,128)S(1)}, f32[6,136,128]{2,1,0:T(8,128)S(1)}, u32[]{:S(2)}, u32[]{:S(2)}) %collective-permute-start.3) | collective-permute-done | bytes 417824 | tf_op jit(solution)/shard_map/ppermute | solution.py:369
  44.8 4.1 collective-permute-start.4
  48.9 7.7 %collective-permute-done.4 = f32[6,136,128]{2,1,0:T(8,128)S(1)} collective-permute-done((f32[6,136,128]{2,1,0:T(8,128)S(1)}, f32[6,136,128]{2,1,0:T(8,128)S(1)}, u32[]{:S(2)}, u32[]{:S(2)}) %collective-permute-start.4) | collective-permute-done | bytes 417824 | tf_op jit(solution)/shard_map/ppermute | solution.py:370
  60.1 12.1 %collective-permute-start.7 = (f32[384,256]{1,0:T(8,128)}, f32[384,256]{1,0:T(8,128)S(1)}, u32[]{:S(2)}, u32[]{:S(2)}) collective-permute-start(f32[384,256]{1,0:T(8,128)} %get-tuple-element.156), channel_id=1, source_target_pairs={{0,24},{4,28},{8,0},{12,4},{16,8},{20,12},{24,16},{28,20},{1,25},{... | collective-permute-start | bytes 1179656 | tf_op jit(solution)/shard_map/ppermute | solution.py:646
  75.1 4.5 collective-permute-done.7.refs_4_
  82.5 4.6 mixer_out.1
  87.2 3.6 collective-permute-done.9
  93.1 34.6 %collective-permute-done.10 = f32[384,1024]{1,0:T(8,128)S(1)} collective-permute-done((f32[384,1024]{1,0:T(8,128)S(1)}, f32[384,1024]{1,0:T(8,128)S(1)}, u32[]{:S(2)}, u32[]{:S(2)}) %collective-permute-start.10) | collective-permute-done | bytes 1572896 | tf_op jit(solution)/shard_map/ppermute | solution.py:392
  140.5 23.2 %ffn_own.1 = (f32[384,1024]{1,0:T(8,128)}, f32[384,1024]{1,0:T(8,128)}, f32[384,1024]{1,0:T(8,128)}, f32[384,1024]{1,0:T(8,128)}) custom-call(s32[1]{0:T(128)} %bitcast.core, bf16[384,2048]{1,0:T(8,128)(2,1)} %get-tuple-element.291.xn_ref.refs_0_, bf16[384,2048]{1,0:T(8,128)(2,1)} %bitcast.114, bf16[2,2048,1408]{2,1,0:T(8,128)(2,1)} %refs_10_.1, ...), custom_call_target="tpu_custom_call" | custom-call | flops 13287555072 | bytes 30000000 | tf_op jit(solution)/shard_map/ffn_own/pallas_call | solution.py:482
  163.8 3.6 collective-permute-done.18
  173.1 32.5 %collective-permute-done.19 = f32[384,1024]{1,0:T(8,128)S(1)} collective-permute-done((f32[384,1024]{1,0:T(8,128)S(1)}, f32[384,1024]{1,0:T(8,128)S(1)}, u32[]{:S(2)}, u32[]{:S(2)}) %collective-permute-start.19) | collective-permute-done | bytes 1572896 | tf_op jit(solution)/shard_map/ppermute | solution.py:392
  214.5 2.9 concatenate.102
  217.4 2.9 concatenate.103
  220.4 3.7 collective-permute-start.22
  224.7 4.1 broadcast_select_fusion.5
  228.8 2.8 concatenate.100
  234.5 5.2 multiply_reduce_fusion
  240.4 5.7 dynamic-slice_add_fusion.1
  248.3 4.1 norm_back.1
  255.9 10.0 %collective-permute-done.24 = f32[6,136,128]{2,1,0:T(8,128)} collective-permute-done((f32[6,136,128]{2,1,0:T(8,128)S(1)}, f32[6,136,128]{2,1,0:T(8,128)}, u32[]{:S(2)}, u32[]{:S(2)}) %collective-permute-start.24) | collective-permute-done | bytes 417824 | tf_op jit(solution)/shard_map/ppermute | solution.py:363
  271.4 8.4 %collective-permute-done.25 = f32[6,136,128]{2,1,0:T(8,128)S(1)} collective-permute-done((f32[6,136,128]{2,1,0:T(8,128)S(1)}, f32[6,136,128]{2,1,0:T(8,128)S(1)}, u32[]{:S(2)}, u32[]{:S(2)}) %collective-permute-start.25) | collective-permute-done | bytes 417824 | tf_op jit(solution)/shard_map/ppermute | solution.py:369
  302.9 5.4 intra_back.1
  313.5 4.3 fusion.6
  321.6 3.9 mix_grad.4
  326.5 3.9 state_back.1
  334.3 3.9 collective-permute-done.34.refs_2_
  339.3 4.3 fusion.11
  346.9 3.2 fusion.9
  350.1 4.1 add_add_fusion
  359.8 9.0 %collective-permute-done.39 = f32[1,2,512,256]{3,2,1,0:T(8,128)S(1)} collective-permute-done((f32[1,2,512,256]{3,2,1,0:T(8,128)S(1)}, f32[1,2,512,256]{3,2,1,0:T(8,128)S(1)}, u32[]{:S(2)}, u32[]{:S(2)}) %collective-permute-start.39) | collective-permute-done | bytes 1048608 | tf_op jit(solution)/shard_map/ppermute | solution.py:721
  370.1 30.7 %ffn_grad.2 = (f32[2,256,768]{2,1,0:T(8,128)}, f32[2,256,768]{2,1,0:T(8,128)}, f32[768,256]{1,0:T(8,128)}, f32[768,256]{1,0:T(8,128)}) custom-call(s32[2]{0:T(128)} %pad_add_fusion.1.rows, bf16[384,2048]{1,0:T(8,128)(2,1)} %get-tuple-element.291.xn_ref.refs_0_, bf16[384,2048]{1,0:T(8,128)(2,1)} %bitcast.115, bf16[384,2048]{1,0:T(8,128)(2,1)} %copy-done.18, ...), custom_call_target="tpu_custom_call" | custom-call | flops 18119393280 | bytes 20000000 | tf_op jit(solution)/shard_map/ffn_grad/pallas_call | solution.py:557
  409.2 4.1 collective-permute-start.56
  416.5 6.0 %mix_grad.7 = (f32[2,2,256,512]{3,2,1,0:T(8,128)}, f32[2,2,256,512]{3,2,1,0:T(8,128)}) custom-call(s32[1]{0:T(128)} %bitcast.1.pos.place, bf16[384,2048]{1,0:T(8,128)(2,1)S(1)} %get-tuple-element.171.xn_ref, f32[384,1024]{1,0:T(8,128)} %collective-permute-done.12.xn_got, f32[384,512]{1,0:T(8,128)S(1)} %get-tuple-element.229.refs_0_, ...), custom_call_target="tpu_custom_call" | custom-call | flops 1610612736 | bytes 10000000 | tf_op jit(solution)/shard_map/mix_grad/pallas_call | solution.py:536
  425.2 11.4 %collective-permute-done.56 = f32[1,512,256]{2,1,0:T(8,128)} collective-permute-done((f32[1,512,256]{2,1,0:T(8,128)}, f32[1,512,256]{2,1,0:T(8,128)}, u32[]{:S(2)}, u32[]{:S(2)}) %collective-permute-start.56) | collective-permute-done | bytes 524320 | tf_op jit(solution)/shard_map/ppermute | solution.py:746
  436.6 32.3 %ffn_grad.3 = (f32[2,256,512]{2,1,0:T(8,128)}, f32[2,256,512]{2,1,0:T(8,128)}, f32[512,256]{1,0:T(8,128)}, f32[512,256]{1,0:T(8,128)}, f32[2,256,128]{2,1,0:T(8,...) custom-call(s32[2]{0:T(128)} %pad_add_fusion.1.rows, ...), custom_call_target="tpu_custom_call" | custom-call | flops 15099494400 | bytes 20000000 | tf_op jit(solution)/shard_map/ffn_grad/pallas_call | solution.py:557
  468.9 3.3 mix_grad.6
  474.2 6.5 %collective-permute-done.55 = f32[1,256,512]{2,1,0:T(8,128)} collective-permute-done((f32[1,256,512]{2,1,0:T(8,128)}, f32[1,256,512]{2,1,0:T(8,128)}, u32[]{:S(2)}, u32[]{:S(2)}) %collective-permute-start.55) | collective-permute-done | bytes 524320 | tf_op jit(solution)/shard_map/ppermute | solution.py:745
  486.7 3.4 collective-permute-done.57
  494.0 9.5 %collective-permute-done.74 = f32[128,256]{1,0:T(8,128)S(1)} collective-permute-done((f32[128,256]{1,0:T(8,128)S(1)}, f32[128,256]{1,0:T(8,128)S(1)}, u32[]{:S(2)}, u32[]{:S(2)}) %collective-permute-start.74) | collective-permute-done | bytes 131104 | tf_op jit(solution)/shard_map/ppermute | solution.py:396
  507.1 7.6 %collective-permute-done.73 = f32[512,256]{1,0:T(8,128)S(1)} collective-permute-done((f32[512,256]{1,0:T(8,128)S(1)}, f32[512,256]{1,0:T(8,128)S(1)}, u32[]{:S(2)}, u32[]{:S(2)}) %collective-permute-start.73) | collective-permute-done | bytes 524320 | tf_op jit(solution)/shard_map/ppermute | solution.py:396
  516.9 19.9 %collective-permute-done.71 = f32[2,256,512]{2,1,0:T(8,128)S(1)} collective-permute-done((f32[2,256,512]{2,1,0:T(8,128)S(1)}, f32[2,256,512]{2,1,0:T(8,128)S(1)}, u32[]{:S(2)}, u32[]{:S(2)}) %collective-permute-start.71) | collective-permute-done | bytes 1048608 | tf_op jit(solution)/shard_map/ppermute | solution.py:396
  537.0 12.8 %collective-permute-done.61 = f32[1,2,256,512]{3,2,1,0:T(8,128)S(1)} collective-permute-done((f32[1,2,256,512]{3,2,1,0:T(8,128)S(1)}, f32[1,2,256,512]{3,2,1,0:T(8,128)S(1)}, u32[]{:S(2)}, u32[]{:S(2)}) %collective-permute-start.61) | collective-permute-done | bytes 1048608 | tf_op jit(solution)/shard_map/ppermute | solution.py:765
  563.2 22.6 %collective-permute-done.69 = f32[5120]{0:T(1024)S(1)} collective-permute-done((f32[5120]{0:T(1024)S(1)}, f32[5120]{0:T(1024)S(1)}, u32[]{:S(2)}, u32[]{:S(2)}) %collective-permute-start.69) | collective-permute-done | bytes 20512 | tf_op jit(solution)/shard_map/ppermute | solution.py:779
  591.6 3.9 add_convert_fusion
  (479 shorter events, 163.5 us)
Async XLA Ops:
  2.1 31.1 %collective-permute-start.1 = (f32[384,512]{1,0:T(8,128)S(1)}, f32[384,512]{1,0:T(8,128)S(1)}, u32[]{:S(2)}, u32[]{:S(2)}) collective-permute-start(f32[384,512]{1,0:T(8,128)S(1)} %widen.1), channel_id=1, source_target_pairs={{0,8},{4,12},{8,16},{12,20},{16,24},{20,28},{24,0},{28,4},{1,9},{5... | collective-permute-start | bytes 2359304 | tf_op jit(solution)/shard_map/ppermute | solution.py:646
  35.9 20.9 %collective-permute-start.5 = (f32[384,512]{1,0:T(8,128)S(1)}, f32[384,512]{1,0:T(8,128)S(1)}, u32[]{:S(2)}, u32[]{:S(2)}) collective-permute-start(f32[384,512]{1,0:T(8,128)S(1)} %collective-permute-done.1.refs_0_), channel_id=1, source_target_pairs={{0,2},{1,3},{2,0},{3,1},{4,6},{5,7},{6,4},{7,5},{8,10},{9,11},{10,... | collective-permute-start | bytes 2359304 | tf_op jit(solution)/shard_map/ppermute | solution.py:392
  60.1 19.6 %collective-permute-start.7 = (f32[384,256]{1,0:T(8,128)}, f32[384,256]{1,0:T(8,128)S(1)}, u32[]{:S(2)}, u32[]{:S(2)}) collective-permute-start(f32[384,256]{1,0:T(8,128)} %get-tuple-element.156), channel_id=1, source_target_pairs={{0,24},{4,28},{8,0},{12,4},{16,8},{20,12},{24,16},{28,20},{1,25},{... | collective-permute-start | bytes 1179656 | tf_op jit(solution)/shard_map/ppermute | solution.py:646
  91.2 36.5 %collective-permute-start.10 = (f32[384,1024]{1,0:T(8,128)S(1)}, f32[384,1024]{1,0:T(8,128)S(1)}, u32[]{:S(2)}, u32[]{:S(2)}) collective-permute-start(f32[384,1024]{1,0:T(8,128)S(1)} %add.224), channel_id=1, source_target_pairs={{0,2},{1,3},{2,0},{3,1},{4,6},{5,7},{6,4},{7,5},{8,10},{9,11},{10,... | collective-permute-start | bytes 4718600 | tf_op jit(solution)/shard_map/ppermute | solution.py:392
  92.8 36.6 %collective-permute-start.12 = (f32[384,1024]{1,0:T(8,128)S(1)}, f32[384,1024]{1,0:T(8,128)}, u32[]{:S(2)}, u32[]{:S(2)}) collective-permute-start(f32[384,1024]{1,0:T(8,128)S(1)} %copy-done.119), channel_id=1, source_target_pairs={{0,4},{4,0},{8,12},{12,8},{16,20},{20,16},{24,28},{28,24},{1,5},{5... | collective-permute-start | bytes 4718600 | tf_op jit(solution)/shard_map/ppermute | solution.py:396
  93.1 36.4 %collective-permute-start.11 = (f32[384,512]{1,0:T(8,128)S(1)}, f32[384,512]{1,0:T(8,128)S(1)}, u32[]{:S(2)}, u32[]{:S(2)}) collective-permute-start(f32[384,512]{1,0:T(8,128)S(1)} %widen.1), channel_id=1, source_target_pairs={{0,16},{4,20},{8,24},{12,28},{16,0},{20,4},{24,8},{28,12},{1,17},{... | collective-permute-start | bytes 2359304 | tf_op jit(solution)/shard_map/ppermute | solution.py:646
  129.5 34.2 %collective-permute-start.14 = (f32[384,512]{1,0:T(8,128)S(1)}, f32[384,512]{1,0:T(8,128)}, u32[]{:S(2)}, u32[]{:S(2)}) collective-permute-start(f32[384,512]{1,0:T(8,128)S(1)} %collective-permute-done.11.refs_0_), channel_id=1, source_target_pairs={{0,2},{1,3},{2,0},{3,1},{4,6},{5,7},{6,4},{7,5},{8,10},{9,11},{10,... | collective-permute-start | bytes 2359304 | tf_op jit(solution)/shard_map/ppermute | solution.py:392
  130.9 32.8 %collective-permute-start.17 = (f32[384,512]{1,0:T(8,128)}, f32[384,512]{1,0:T(8,128)}, u32[]{:S(2)}, u32[]{:S(2)}) collective-permute-start(f32[384,512]{1,0:T(8,128)} %copy-done.67), channel_id=1, source_target_pairs={{0,4},{4,0},{8,12},{12,8},{16,20},{20,16},{24,28},{28,24},{1,5},{5... | collective-permute-start | bytes 2359304 | tf_op jit(solution)/shard_map/ppermute | solution.py:396
  132.5 31.2 %collective-permute-start.15 = (f32[384,256]{1,0:T(8,128)}, f32[384,256]{1,0:T(8,128)}, u32[]{:S(2)}, u32[]{:S(2)}) collective-permute-start(f32[384,256]{1,0:T(8,128)} %copy-done.47), channel_id=1, source_target_pairs={{0,2},{1,3},{2,0},{3,1},{4,6},{5,7},{6,4},{7,5},{8,10},{9,11},{10,... | collective-permute-start | bytes 1179656 | tf_op jit(solution)/shard_map/ppermute | solution.py:392
  140.3 23.4 %collective-permute-start.16 = (f32[384,512]{1,0:T(8,128)}, f32[384,512]{1,0:T(8,128)S(1)}, u32[]{:S(2)}, u32[]{:S(2)}) collective-permute-start(f32[384,512]{1,0:T(8,128)} %constant_dynamic-slice_fusion.2), channel_id=1, source_target_pairs={{0,8},{4,12},{8,16},{12,20},{16,24},{20,28},{24,0},{28,4},{1,9},{5... | collective-permute-start | bytes 2359304 | tf_op jit(solution)/shard_map/ppermute | solution.py:646
  169.1 36.5 %collective-permute-start.19 = (f32[384,1024]{1,0:T(8,128)S(1)}, f32[384,1024]{1,0:T(8,128)S(1)}, u32[]{:S(2)}, u32[]{:S(2)}) collective-permute-start(f32[384,1024]{1,0:T(8,128)S(1)} %add.230), channel_id=1, source_target_pairs={{0,2},{1,3},{2,0},{3,1},{4,6},{5,7},{6,4},{7,5},{8,10},{9,11},{10,... | collective-permute-start | bytes 4718600 | tf_op jit(solution)/shard_map/ppermute | solution.py:392
  170.4 37.5 %collective-permute-start.20 = (f32[384,512]{1,0:T(8,128)}, f32[384,512]{1,0:T(8,128)}, u32[]{:S(2)}, u32[]{:S(2)}) collective-permute-start(f32[384,512]{1,0:T(8,128)} %constant_dynamic-slice_fusion.2), channel_id=1, source_target_pairs={{0,16},{4,20},{8,24},{12,28},{16,0},{20,4},{24,8},{28,12},{1,17},{... | collective-permute-start | bytes 2359304 | tf_op jit(solution)/shard_map/ppermute | solution.py:646
  207.8 16.8 %collective-permute-start.21 = (f32[384,1024]{1,0:T(8,128)}, f32[384,1024]{1,0:T(8,128)}, u32[]{:S(2)}, u32[]{:S(2)}) collective-permute-start(f32[384,1024]{1,0:T(8,128)} %add.231), channel_id=1, source_target_pairs={{0,1},{1,0},{2,3},{3,2},{4,5},{5,4},{6,7},{7,6},{8,9},{9,8},{10,11... | collective-permute-start | bytes 4718600 | tf_op jit(solution)/shard_map/ppermute | solution.py:388
  220.4 33.8 %collective-permute-start.22 = (f32[384,512]{1,0:T(8,128)}, f32[384,512]{1,0:T(8,128)}, u32[]{:S(2)}, u32[]{:S(2)}) collective-permute-start(f32[384,512]{1,0:T(8,128)} %constant_dynamic-slice_fusion.2), channel_id=1, source_target_pairs={{0,24},{4,28},{8,0},{12,4},{16,8},{20,12},{24,16},{28,20},{1,25},{... | collective-permute-start | bytes 2359304 | tf_op jit(solution)/shard_map/ppermute | solution.py:646
  224.1 30.1 %collective-permute-start.23 = (f32[384,512]{1,0:T(8,128)}, f32[384,512]{1,0:T(8,128)}, u32[]{:S(2)}, u32[]{:S(2)}) collective-permute-start(f32[384,512]{1,0:T(8,128)} %copy-done.29), channel_id=1, source_target_pairs={{0,2},{1,3},{2,0},{3,1},{4,6},{5,7},{6,4},{7,5},{8,10},{9,11},{10,... | collective-permute-start | bytes 2359304 | tf_op jit(solution)/shard_map/ppermute | solution.py:392
  269.1 16.6 %collective-permute-start.46 = (f32[384,512]{1,0:T(8,128)S(1)}, f32[384,512]{1,0:T(8,128)S(1)}, u32[]{:S(2)}, u32[]{:S(2)}) collective-permute-start(f32[384,512]{1,0:T(8,128)S(1)} %copy-done.32), channel_id=1, source_target_pairs={{0,1},{1,0},{2,3},{3,2},{4,5},{5,4},{6,7},{7,6},{8,9},{9,8},{10,11... | collective-permute-start | bytes 2359304 | tf_op jit(solution)/shard_map/ppermute | solution.py:388
  279.8 19.4 %collective-permute-start.47 = (f32[384,512]{1,0:T(8,128)}, f32[384,512]{1,0:T(8,128)}, u32[]{:S(2)}, u32[]{:S(2)}) collective-permute-start(f32[384,512]{1,0:T(8,128)} %collective-permute-done.14.refs_2_), channel_id=1, source_target_pairs={{0,1},{1,0},{2,3},{3,2},{4,5},{5,4},{6,7},{7,6},{8,9},{9,8},{10,11... | collective-permute-start | bytes 2359304 | tf_op jit(solution)/shard_map/ppermute | solution.py:388
  281.7 28.2 %collective-permute-start.27 = (f32[384,512]{1,0:T(8,128)S(1)}, f32[384,512]{1,0:T(8,128)}, u32[]{:S(2)}, u32[]{:S(2)}) collective-permute-start(f32[384,512]{1,0:T(8,128)S(1)} %copy-done.12), channel_id=1, source_target_pairs={{0,4},{4,0},{8,12},{12,8},{16,20},{20,16},{24,28},{28,24},{1,5},{5... | collective-permute-start | bytes 2359304 | tf_op jit(solution)/shard_map/ppermute | solution.py:396
  284.1 25.8 %collective-permute-start.28 = (f32[384,512]{1,0:T(8,128)}, f32[384,512]{1,0:T(8,128)}, u32[]{:S(2)}, u32[]{:S(2)}) collective-permute-start(f32[384,512]{1,0:T(8,128)} %collective-permute-done.20.refs_0_), channel_id=1, source_target_pairs={{0,2},{1,3},{2,0},{3,1},{4,6},{5,7},{6,4},{7,5},{8,10},{9,11},{10,... | collective-permute-start | bytes 2359304 | tf_op jit(solution)/shard_map/ppermute | solution.py:392
  286.6 22.1 %collective-permute-start.26 = (f32[6,136,128]{2,1,0:T(8,128)}, f32[6,136,128]{2,1,0:T(8,128)}, u32[]{:S(2)}, u32[]{:S(2)}) collective-permute-start(f32[6,136,128]{2,1,0:T(8,128)} %pad_maximum_fusion.10), channel_id=1, source_target_pairs={{16,0},{20,4},{24,8},{28,12},{17,1},{21,5},{25,9},{29,13},{18,2},{... | collective-permute-start | bytes 1253384 | tf_op jit(solution)/shard_map/ppermute | solution.py:370
  289.2 20.7 %collective-permute-start.29 = (f32[384,256]{1,0:T(8,128)}, f32[384,256]{1,0:T(8,128)S(1)}, u32[]{:S(2)}, u32[]{:S(2)}) collective-permute-start(f32[384,256]{1,0:T(8,128)} %bitcast.156), channel_id=1, source_target_pairs={{0,4},{4,0},{8,12},{12,8},{16,20},{20,16},{24,28},{28,24},{1,5},{5... | collective-permute-start | bytes 1179656 | tf_op jit(solution)/shard_map/ppermute | solution.py:396
  310.0 15.6 %collective-permute-start.32 = (f32[384,256]{1,0:T(8,128)S(1)}, f32[384,256]{1,0:T(8,128)S(1)}, u32[]{:S(2)}, u32[]{:S(2)}) collective-permute-start(f32[384,256]{1,0:T(8,128)S(1)} %collective-permute-done.29.refs_0_), channel_id=1, source_target_pairs={{0,2},{1,3},{2,0},{3,1},{4,6},{5,7},{6,4},{7,5},{8,10},{9,11},{10,... | collective-permute-start | bytes 1179656 | tf_op jit(solution)/shard_map/ppermute | solution.py:392
  312.4 25.8 %collective-permute-start.34 = (f32[384,512]{1,0:T(8,128)}, f32[384,512]{1,0:T(8,128)S(1)}, u32[]{:S(2)}, u32[]{:S(2)}) collective-permute-start(f32[384,512]{1,0:T(8,128)} %collective-permute-done.22.refs_0_), channel_id=1, source_target_pairs={{0,2},{1,3},{2,0},{3,1},{4,6},{5,7},{6,4},{7,5},{8,10},{9,11},{10,... | collective-permute-start | bytes 2359304 | tf_op jit(solution)/shard_map/ppermute | solution.py:392
  317.8 25.7 %collective-permute-start.44 = (f32[384,512]{1,0:T(8,128)}, f32[384,512]{1,0:T(8,128)S(1)}, u32[]{:S(2)}, u32[]{:S(2)}) collective-permute-start(f32[384,512]{1,0:T(8,128)} %collective-permute-done.20.refs_0_), channel_id=1, source_target_pairs={{0,1},{1,0},{2,3},{3,2},{4,5},{5,4},{6,7},{7,6},{8,9},{9,8},{10,11... | collective-permute-start | bytes 2359304 | tf_op jit(solution)/shard_map/ppermute | solution.py:388
  325.5 18.0 %collective-permute-start.45 = (f32[384,512]{1,0:T(8,128)}, f32[384,512]{1,0:T(8,128)S(1)}, u32[]{:S(2)}, u32[]{:S(2)}) collective-permute-start(f32[384,512]{1,0:T(8,128)} %collective-permute-done.28.refs_2_), channel_id=1, source_target_pairs={{0,1},{1,0},{2,3},{3,2},{4,5},{5,4},{6,7},{7,6},{8,9},{9,8},{10,11... | collective-permute-start | bytes 2359304 | tf_op jit(solution)/shard_map/ppermute | solution.py:388
  330.4 25.1 %collective-permute-start.48 = (f32[384,512]{1,0:T(8,128)}, f32[384,512]{1,0:T(8,128)S(1)}, u32[]{:S(2)}, u32[]{:S(2)}) collective-permute-start(f32[384,512]{1,0:T(8,128)} %collective-permute-done.22.refs_0_), channel_id=1, source_target_pairs={{0,1},{1,0},{2,3},{3,2},{4,5},{5,4},{6,7},{7,6},{8,9},{9,8},{10,11... | collective-permute-start | bytes 2359304 | tf_op jit(solution)/shard_map/ppermute | solution.py:388
  338.2 18.4 %collective-permute-start.49 = (f32[384,512]{1,0:T(8,128)S(1)}, f32[384,512]{1,0:T(8,128)S(1)}, u32[]{:S(2)}, u32[]{:S(2)}) collective-permute-start(f32[384,512]{1,0:T(8,128)S(1)} %collective-permute-done.34.refs_2_), channel_id=1, source_target_pairs={{0,1},{1,0},{2,3},{3,2},{4,5},{5,4},{6,7},{7,6},{8,9},{9,8},{10,11... | collective-permute-start | bytes 2359304 | tf_op jit(solution)/shard_map/ppermute | solution.py:388
  338.2 70.1 %collective-permute-start.36 = (f32[384,512]{1,0:T(8,128)S(1)}, f32[384,512]{1,0:T(8,128)}, u32[]{:S(2)}, u32[]{:S(2)}) collective-permute-start(f32[384,512]{1,0:T(8,128)S(1)} %get-tuple-element.229.refs_0_), channel_id=1, source_target_pairs={{0,4},{4,0},{8,12},{12,8},{16,20},{20,16},{24,28},{28,24},{1,5},{5... | collective-permute-start | bytes 2359304 | tf_op jit(solution)/shard_map/ppermute | solution.py:396
  343.5 25.3 %collective-permute-start.39 = (f32[1,2,512,256]{3,2,1,0:T(8,128)S(1)}, f32[1,2,512,256]{3,2,1,0:T(8,128)S(1)}, u32[]{:S(2)}, u32[]{:S(2)}) collective-permute-start(f32[1,2,512,256]{3,2,1,0:T(8,128)S(1)} %get-tuple-element.233), channel_id=1, source_target_pairs={{0,8},{4,12},{8,0},{12,4},{16,24},{20,28},{24,16},{28,20},{1,9},{5... | collective-permute-start | bytes 3145736 | tf_op jit(solution)/shard_map/ppermute | solution.py:721
  343.6 64.7 %collective-permute-start.35 = (f32[384,512]{1,0:T(8,128)S(1)}, f32[384,512]{1,0:T(8,128)}, u32[]{:S(2)}, u32[]{:S(2)}) collective-permute-start(f32[384,512]{1,0:T(8,128)S(1)} %get-tuple-element.228.refs_2_), channel_id=1, source_target_pairs={{0,4},{4,0},{8,12},{12,8},{16,20},{20,16},{24,28},{28,24},{1,5},{5... | collective-permute-start | bytes 2359304 | tf_op jit(solution)/shard_map/ppermute | solution.py:396
  355.6 52.8 %collective-permute-start.37 = (f32[384,512]{1,0:T(8,128)}, f32[384,512]{1,0:T(8,128)}, u32[]{:S(2)}, u32[]{:S(2)}) collective-permute-start(f32[384,512]{1,0:T(8,128)} %get-tuple-element.227.refs_0_), channel_id=1, source_target_pairs={{0,4},{4,0},{8,12},{12,8},{16,20},{20,16},{24,28},{28,24},{1,5},{5... | collective-permute-start | bytes 2359304 | tf_op jit(solution)/shard_map/ppermute | solution.py:396
  356.6 48.9 %collective-permute-start.54 = (f32[384,1024]{1,0:T(8,128)}, f32[384,1024]{1,0:T(8,128)}, u32[]{:S(2)}, u32[]{:S(2)}) collective-permute-start(f32[384,1024]{1,0:T(8,128)} %constant_dynamic-slice_fusion.1), channel_id=1, source_target_pairs={{0,1},{1,0},{2,3},{3,2},{4,5},{5,4},{6,7},{7,6},{8,9},{9,8},{10,11... | collective-permute-start | bytes 4718600 | tf_op jit(solution)/shard_map/ppermute | solution.py:388
  369.8 32.8 %collective-permute-start.38 = (f32[1,2,256,512]{3,2,1,0:T(8,128)}, f32[1,2,256,512]{3,2,1,0:T(8,128)}, u32[]{:S(2)}, u32[]{:S(2)}) collective-permute-start(f32[1,2,256,512]{3,2,1,0:T(8,128)} %get-tuple-element.231), channel_id=1, source_target_pairs={{0,8},{4,12},{8,0},{12,4},{16,24},{20,28},{24,16},{28,20},{1,9},{5... | collective-permute-start | bytes 3145736 | tf_op jit(solution)/shard_map/ppermute | solution.py:720
  409.2 27.4 %collective-permute-start.56 = (f32[1,512,256]{2,1,0:T(8,128)}, f32[1,512,256]{2,1,0:T(8,128)}, u32[]{:S(2)}, u32[]{:S(2)}) collective-permute-start(f32[1,512,256]{2,1,0:T(8,128)} %dynamic-slice_bitcast_fusion.2), channel_id=1, source_target_pairs={{0,16},{4,20},{8,24},{12,28},{16,0},{20,4},{24,8},{28,12},{1,17},{... | collective-permute-start | bytes 1572872 | tf_op jit(solution)/shard_map/ppermute | solution.py:746
  413.3 69.8 %collective-permute-start.60 = (f32[384,1024]{1,0:T(8,128)}, f32[384,1024]{1,0:T(8,128)}, u32[]{:S(2)}, u32[]{:S(2)}) collective-permute-start(f32[384,1024]{1,0:T(8,128)} %dynamic-slice_add_fusion), channel_id=1, source_target_pairs={{0,2},{1,3},{2,0},{3,1},{4,6},{5,7},{6,4},{7,5},{8,10},{9,11},{10,... | collective-permute-start | bytes 4718600 | tf_op jit(solution)/shard_map/ppermute | solution.py:392
  414.5 67.3 %collective-permute-start.59 = (f32[768,256]{1,0:T(8,128)}, f32[768,256]{1,0:T(8,128)}, u32[]{:S(2)}, u32[]{:S(2)}) collective-permute-start(f32[768,256]{1,0:T(8,128)} %get-tuple-element.255), channel_id=1, source_target_pairs={{0,4},{4,0},{8,12},{12,8},{16,20},{20,16},{24,28},{28,24},{1,5},{5... | collective-permute-start | bytes 2359304 | tf_op jit(solution)/shard_map/ppermute | solution.py:396
  414.9 70.0 %collective-permute-start.58 = (f32[2,256,768]{2,1,0:T(8,128)}, f32[2,256,768]{2,1,0:T(8,128)}, u32[]{:S(2)}, u32[]{:S(2)}) collective-permute-start(f32[2,256,768]{2,1,0:T(8,128)} %get-tuple-element.253), channel_id=1, source_target_pairs={{0,4},{4,0},{8,12},{12,8},{16,20},{20,16},{24,28},{28,24},{1,5},{5... | collective-permute-start | bytes 4718600 | tf_op jit(solution)/shard_map/ppermute | solution.py:396
  422.5 67.6 %collective-permute-start.57 = (f32[2,2,256,512]{3,2,1,0:T(8,128)}, f32[2,2,256,512]{3,2,1,0:T(8,128)S(1)}, u32[]{:S(2)}, u32[]{:S(2)}) collective-permute-start(f32[2,2,256,512]{3,2,1,0:T(8,128)} %get-tuple-element.250), channel_id=1, source_target_pairs={{0,8},{4,12},{8,0},{12,4},{16,24},{20,28},{24,16},{28,20},{1,9},{5... | collective-permute-start | bytes 6291464 | tf_op jit(solution)/shard_map/ppermute | solution.py:748
  436.6 44.1 %collective-permute-start.55 = (f32[1,256,512]{2,1,0:T(8,128)}, f32[1,256,512]{2,1,0:T(8,128)}, u32[]{:S(2)}, u32[]{:S(2)}) collective-permute-start(f32[1,256,512]{2,1,0:T(8,128)} %dynamic-slice_bitcast_fusion.3), channel_id=1, source_target_pairs={{0,16},{4,20},{8,24},{12,28},{16,0},{20,4},{24,8},{28,12},{1,17},{... | collective-permute-start | bytes 1572872 | tf_op jit(solution)/shard_map/ppermute | solution.py:745
  493.6 58.2 %collective-permute-start.64 = (f32[384,1024]{1,0:T(8,128)S(1)}, f32[384,1024]{1,0:T(8,128)S(1)}, u32[]{:S(2)}, u32[]{:S(2)}) collective-permute-start(f32[384,1024]{1,0:T(8,128)S(1)} %add.260), channel_id=1, source_target_pairs={{0,1},{1,0},{2,3},{3,2},{4,5},{5,4},{6,7},{7,6},{8,9},{9,8},{10,11... | collective-permute-start | bytes 4718600 | tf_op jit(solution)/shard_map/ppermute | solution.py:388
  493.6 21.1 %collective-permute-start.73 = (f32[512,256]{1,0:T(8,128)S(1)}, f32[512,256]{1,0:T(8,128)S(1)}, u32[]{:S(2)}, u32[]{:S(2)}) collective-permute-start(f32[512,256]{1,0:T(8,128)S(1)} %copy-done.121), channel_id=1, source_target_pairs={{0,4},{4,0},{8,12},{12,8},{16,20},{20,16},{24,28},{28,24},{1,5},{5... | collective-permute-start | bytes 1572872 | tf_op jit(solution)/shard_map/ppermute | solution.py:396
  503.5 33.3 %collective-permute-start.71 = (f32[2,256,512]{2,1,0:T(8,128)S(1)}, f32[2,256,512]{2,1,0:T(8,128)S(1)}, u32[]{:S(2)}, u32[]{:S(2)}) collective-permute-start(f32[2,256,512]{2,1,0:T(8,128)S(1)} %copy-done.120), channel_id=1, source_target_pairs={{0,4},{4,0},{8,12},{12,8},{16,20},{20,16},{24,28},{28,24},{1,5},{5... | collective-permute-start | bytes 3145736 | tf_op jit(solution)/shard_map/ppermute | solution.py:396
  503.9 45.9 %collective-permute-start.61 = (f32[1,2,256,512]{3,2,1,0:T(8,128)S(1)}, f32[1,2,256,512]{3,2,1,0:T(8,128)S(1)}, u32[]{:S(2)}, u32[]{:S(2)}) collective-permute-start(f32[1,2,256,512]{3,2,1,0:T(8,128)S(1)} %get-tuple-element.263), channel_id=1, source_target_pairs={{0,8},{4,12},{8,0},{12,4},{16,24},{20,28},{24,16},{28,20},{1,9},{5... | collective-permute-start | bytes 3145736 | tf_op jit(solution)/shard_map/ppermute | solution.py:765
  504.0 47.6 %collective-permute-start.65 = (f32[2,256,512]{2,1,0:T(8,128)S(1)}, f32[2,256,512]{2,1,0:T(8,128)S(1)}, u32[]{:S(2)}, u32[]{:S(2)}) collective-permute-start(f32[2,256,512]{2,1,0:T(8,128)S(1)} %dynamic-slice_bitcast_fusion), channel_id=1, source_target_pairs={{0,16},{4,20},{8,24},{12,28},{16,0},{20,4},{24,8},{28,12},{1,17},{... | collective-permute-start | bytes 3145736 | tf_op jit(solution)/shard_map/ppermute | solution.py:764
  514.7 39.5 %collective-permute-start.63 = (f32[384,1024]{1,0:T(8,128)S(1)}, f32[384,1024]{1,0:T(8,128)S(1)}, u32[]{:S(2)}, u32[]{:S(2)}) collective-permute-start(f32[384,1024]{1,0:T(8,128)S(1)} %add.262), channel_id=1, source_target_pairs={{0,2},{1,3},{2,0},{3,1},{4,6},{5,7},{6,4},{7,5},{8,10},{9,11},{10,... | collective-permute-start | bytes 4718600 | tf_op jit(solution)/shard_map/ppermute | solution.py:392
  556.5 32.2 %collective-permute-start.66 = (f32[384,1024]{1,0:T(8,128)S(1)}, f32[384,1024]{1,0:T(8,128)S(1)}, u32[]{:S(2)}, u32[]{:S(2)}) collective-permute-start(f32[384,1024]{1,0:T(8,128)S(1)} %add.263), channel_id=1, source_target_pairs={{0,1},{1,0},{2,3},{3,2},{4,5},{5,4},{6,7},{7,6},{8,9},{9,8},{10,11... | collective-permute-start | bytes 4718600 | tf_op jit(solution)/shard_map/ppermute | solution.py:388
  558.8 28.2 %collective-permute-start.70 = (f32[1,256,512]{2,1,0:T(8,128)S(1)}, f32[1,256,512]{2,1,0:T(8,128)S(1)}, u32[]{:S(2)}, u32[]{:S(2)}) collective-permute-start(f32[1,256,512]{2,1,0:T(8,128)S(1)} %dynamic-slice_bitcast_fusion.1), channel_id=1, source_target_pairs={{0,16},{4,20},{8,24},{12,28},{16,0},{20,4},{24,8},{28,12},{1,17},{... | collective-permute-start | bytes 1572872 | tf_op jit(solution)/shard_map/ppermute | solution.py:774
  562.5 23.3 %collective-permute-start.69 = (f32[5120]{0:T(1024)S(1)}, f32[5120]{0:T(1024)S(1)}, u32[]{:S(2)}, u32[]{:S(2)}) collective-permute-start(f32[5120]{0:T(1024)S(1)} %add.270), channel_id=1, source_target_pairs={{0,16},{4,20},{8,24},{12,28},{16,0},{20,4},{24,8},{28,12},{1,17},{... | collective-permute-start | bytes 61448 | tf_op jit(solution)/shard_map/ppermute | solution.py:779
  (151 other events, 1003.1 us)

commit v3 on v2

v3 whole, which is shorter than its diff:
```python
import functools

import jax
import jax.numpy as jnp
from jax import lax
from jax.experimental import pallas as pl
from jax.experimental.pallas import tpu as pltpu
from jax.sharding import PartitionSpec as P

HD = 128
EPS = 1e-06
F32 = jnp.float32
BF16 = jnp.bfloat16
MIB = 1 << 20
PACKED = HD + 8

X_SWAP = [(p, p ^ 1) for p in range(8)]
CORE_SWAP = [(h, h ^ 1) for h in range(4)]
Y_SWAP = [(h, h ^ 2) for h in range(4)]


def z_shift(k):
    return [(p, (p + 2 * k) % 8) for p in range(8)]


def z_line(k):
    return [(p, p + 2 * k) for p in range(8) if 0 <= p + 2 * k < 8]


def flip(bit):
    return [(p, p ^ bit) for p in range(8)]


def rms_scale(v):
    return lax.rsqrt(jnp.mean(v * v, axis=-1, keepdims=True) + EPS)


def norm_back(grad_normed, gain, scale, normed_hat):
    scaled = grad_normed * gain
    return scale * (scaled - normed_hat * jnp.mean(scaled * normed_hat, axis=-1, keepdims=True))


def dot(a, b, dims=((1,), (0,))):
    return lax.dot_general(a, b, (dims, ((), ())), preferred_element_type=F32)


NT = ((1,), (1,))
TN = ((0,), (0,))


def sigmoid(v):
    return 1.0 / (1.0 + jnp.exp(-v))


def triangle(kind):
    row = lax.broadcasted_iota(jnp.int32, (HD, HD), 0)
    col = lax.broadcasted_iota(jnp.int32, (HD, HD), 1)
    return {"lower": row >= col, "strict": row > col, "upper": row <= col}[kind]


def exact_dot(ones, v, parts=3):
    total = None
    for _ in range(parts):
        part = v.astype(BF16)
        v = v - part.astype(F32)
        term = dot(ones, part)
        total = term if total is None else total + term
    return total


def valid_rows(pos, length):
    row = lax.broadcasted_iota(jnp.int32, (HD, 1), 0)
    return (pos * HD + row) < length


def open_forget(pre, bound, ok):
    sig = sigmoid(pre)
    return sig, jnp.where(ok, bound + (1.0 - bound) * sig, 1.0)


def project_kernel(pos, lengths, x_ref, gain_ref, w_ref, bound_ref, xn_ref, away_ref, proj_ref, c_ref, qe_ref, ke_ref, intra_ref, sum_ref):
    @pl.when(pl.program_id(0) == 0)
    def _():
        x = x_ref[...].astype(F32)
        xn_ref[...] = (x * rms_scale(x) * gain_ref[...]).astype(BF16)
        n = away_ref.shape[1] // 4
        for z in range(4):
            at = pl.multiple_of((2 * z + 1 - pos[0] % 2) * n, n)
            away_ref[:, pl.ds(z * n, n)] = xn_ref[:, pl.ds(at, n)].astype(F32)

    xn = xn_ref[...]
    for c in range(4):
        proj_ref[c] = dot(xn, w_ref[c])
    slots, heads = sum_ref.shape[:2]
    lower = triangle("lower")
    ones = lower.astype(BF16)
    for s in range(slots):
        rows = pl.ds(s * HD, HD)
        ok = valid_rows(pos[0], lengths[s])
        _, forget = open_forget(proj_ref[1, rows, :], bound_ref[...], ok)
        c_ref[rows, :] = exact_dot(ones, jnp.log(forget), 2)
        for h in range(heads):
            cols = pl.ds(h * HD, HD)
            pre_q, v, cum = proj_ref[0, rows, cols], proj_ref[2, rows, cols], c_ref[rows, cols]
            keys = 1.0 - forget[:, h * HD : (h + 1) * HD]
            qe = (pre_q * sigmoid(pre_q) * jnp.exp(cum)).astype(BF16)
            ke = (keys * jnp.exp(-cum)).astype(BF16)
            qe_ref[rows, cols] = qe
            ke_ref[rows, cols] = ke
            vb = v.astype(BF16)
            scores = jnp.where(lower, dot(qe, ke, NT), 0.0).astype(BF16)
            intra_ref[rows, cols] = dot(scores, vb)
            last = cum[HD - 1 :, :]
            to_end = (keys * jnp.exp(last - cum)).astype(BF16)
            sum_ref[s, h, pl.ds(0, HD), :] = dot(vb, to_end, TN)
            sum_ref[s, h, pl.ds(HD, 8), :] = jnp.broadcast_to(jnp.exp(last), (8, HD))


def split_store(keep_ref, send_ref, core, make):
    half = keep_ref.shape[1]
    keep_ref[...] = make(pl.multiple_of(core * half, half), half)
    send_ref[...] = make(pl.multiple_of((1 - core) * half, half), half)


def mixer_out_kernel(core, qe_ref, state_ref, intra_ref, pre_ref, gain_ref, w_ref, mixed_ref, gated_ref, wide_ref, keep_ref, send_ref):
    slots, heads = state_ref.shape[:2]
    for s in range(slots):
        rows = pl.ds(s * HD, HD)
        for h in range(heads):
            cols = pl.ds(h * HD, HD)
            mixed = intra_ref[rows, cols] + dot(qe_ref[rows, cols], state_ref[s, h].astype(BF16), NT)
            mixed_ref[rows, cols] = mixed
            pre = pre_ref[0, rows, cols]
            gated = mixed * rms_scale(mixed) * gain_ref[:, cols] * (pre * sigmoid(pre))
            gated_ref[rows, cols] = gated.astype(BF16)
            wide_ref[rows, cols] = gated_ref[rows, cols].astype(F32)
    split_store(keep_ref, send_ref, core[0], lambda at, n: dot(gated_ref[...], w_ref[:, pl.ds(at, n)]))


def ffn_unit(xn, dy, w_gate, w_up, w_out):
    gate, up = dot(xn, w_gate), dot(xn, w_up)
    dact = dot(dy, w_out, NT)
    sig = sigmoid(gate)
    swish = gate * sig
    act = (swish * up).astype(BF16)
    dgate = (dact * up * (sig * (1.0 + gate * (1.0 - sig)))).astype(BF16)
    dup = (dact * swish).astype(BF16)
    return act, dgate, dup


def ffn_own_kernel(core, xn_ref, dy_ref, in_ref, out_ref, in_tail, out_tail, f_acc, d_keep, d_send, d_acc):
    step = pl.program_id(0)

    @pl.when(step == 0)
    def _():
        f_acc[...] = jnp.zeros_like(f_acc)
        d_acc[...] = jnp.zeros_like(d_acc)

    def add(w_in, w_out):
        act, dgate, dup = ffn_unit(xn_ref[...], dy_ref[...], w_in[0], w_in[1], w_out[...])
        f_acc[...] += dot(act, w_out[...])
        d_acc[...] += dot(dgate, w_in[0], NT) + dot(dup, w_in[1], NT)

    add(in_ref, out_ref)

    @pl.when(step == pl.num_programs(0) - 1)
    def _():
        add(in_tail, out_tail)
        split_store(d_keep, d_send, core[0], lambda at, n: d_acc[:, pl.ds(at, n)])


def widen_kernel(at, a_ref, out_ref, copy_ref):
    n = out_ref.shape[1]
    out_ref[...] = a_ref[:, pl.ds(pl.multiple_of(at[0] * n, n), n)].astype(F32)
    copy_ref[...] = a_ref[...]


def place_halves(out_ref, core, parts):
    n, terms = out_ref.shape[1] // 2, len(parts) // 2
    for k, which in ((0, core), (1, 1 - core)):
        mine = parts[k * terms : (k + 1) * terms]
        at = pl.ds(pl.multiple_of(which * n, n), n)
        out_ref[:, at] = mine[0][...] if terms == 1 else mine[0][...] + mine[1][...]


def second_norm_kernel(place, x_ref, p0, p1, p2, p3, gain_ref, hidden_ref, xn_ref, quarter_ref):
    core, head = place[0], place[1]
    place_halves(hidden_ref, core, (p0, p1, p2, p3))
    hidden = x_ref[...].astype(F32) + hidden_ref[...]
    hidden_ref[...] = hidden
    xn_ref[...] = (hidden * rms_scale(hidden) * gain_ref[...]).astype(BF16)
    n = quarter_ref.shape[1]
    quarter_ref[...] = xn_ref[:, pl.ds(pl.multiple_of(head * n, n), n)].astype(F32)


def first_back_kernel(d_ref, dhidden_ref, x_ref, gain_ref, grad_ref, part_ref):
    x, d = x_ref[...].astype(F32), d_ref[...]
    scale = rms_scale(x)
    hat = x * scale
    part_ref[...] = jnp.sum(d * hat, axis=0, keepdims=True)
    grad_ref[...] = (dhidden_ref[...] + norm_back(d, gain_ref[...], scale, hat)).astype(BF16)


def first_grad_kernel(d0, d1, d2, d3, w_ref, out_ref):
    out_ref[...] = sum(dot(d[...].astype(BF16), w_ref[c], NT) for c, d in enumerate((d0, d1, d2, d3)))


def assemble_kernel(at, here_ref, there_ref, *refs):
    out_ref = refs[-1]
    n = here_ref.shape[-1]
    for k, piece in enumerate((here_ref, there_ref)):
        for over in range(2):
            out_ref[:, pl.ds(pl.multiple_of(at[2 * over + k], n), n)] = piece[0, over].astype(BF16)


def join_kernel(parts_ref, _, out_ref):
    n = parts_ref.shape[2]
    for k in range(parts_ref.shape[0]):
        out_ref[:, pl.ds(k * n, n)] = parts_ref[k].astype(BF16)


def ffn_grad_kernel(tail, rows, xn_ref, dy_ref, *refs):
    weights, (mine_ref, away_ref, xt_ref, dyt_ref, act_ref, dgate_ref, dup_ref) = refs[:-7], refs[-7:]
    step = pl.program_id(0)
    n = mine_ref.shape[1]

    @pl.when(step == 0)
    def _():
        for which in range(2):
            at = pl.ds(pl.multiple_of(rows[which] * n, n), n)
            xt_ref[pl.ds(which * n, n), :] = xn_ref[:, at].T
            dyt_ref[pl.ds(which * n, n), :] = dy_ref[:, at].T

    def put(w_in, w_out, units):
        size = w_out.shape[0]
        block = xn_ref.shape[0] // 4
        for k in range(4):
            at = pl.ds(k * block, block)
            made = ffn_unit(xn_ref[at, :], dy_ref[at, :], w_in[0], w_in[1], w_out[...])
            act_ref[at, :size], dgate_ref[at, :size], dup_ref[at, :size] = made
        for k, (left, right) in enumerate(((xt_ref, dgate_ref), (xt_ref, dup_ref), (dyt_ref, act_ref))):
            both = dot(left[...], right[:, :size])
            mine_ref[k, :, units] = both[:n]
            away_ref[k, :, units] = both[n:]

    size = weights[1].shape[0]
    put(weights[0], weights[1], pl.ds(pl.multiple_of(step * size, size), size))
    if tail:

        @pl.when(step == pl.num_programs(0) - 1)
        def _():
            rest = weights[3].shape[0]
            put(weights[2], weights[3], pl.ds(mine_ref.shape[2] - rest, rest))


def turn_kernel(place, xn_ref, got_ref, out_ref):
    _, n, both = out_ref.shape
    z, x = place[0] // 2, place[0] % 2
    for k in range(4):
        high = z // 2 if k % 2 == 0 else 1 - z // 2
        row = 2 * high + (z % 2 if k < 2 else 1 - z % 2)
        a = xn_ref[:, pl.ds(pl.multiple_of((2 * row + x) * n, n), n)]
        b = got_ref[:, pl.ds(pl.multiple_of(row * n, n), n)].astype(BF16)
        out_ref[k, :, pl.ds(0, both // 2)] = a.T
        out_ref[k, :, pl.ds(both // 2, both // 2)] = b.T


def mix_grad_kernel(turned_ref, *refs):
    keep_ref, send_ref = refs[-2:]
    both = turned_ref.shape[2]
    for c in range(keep_ref.shape[0]):
        own, got = refs[2 * c][...].astype(BF16), refs[2 * c + 1][...].astype(BF16)
        for k in range(4):
            a = turned_ref[k]
            (keep_ref if k < 2 else send_ref)[c, k % 2] = dot(a[:, : both // 2], own) + dot(a[:, both // 2 :], got)


def norm_back_kernel(place, p0, p1, p2, p3, hidden_ref, dy_ref, norm_ref, w_ref, mixed_ref, pre_ref, gain_ref, qe_ref, sum_ref, dpre_ref, dm_ref, dgain_ref, back_ref, dhidden_ref, db_ref, away_ref, dnorm_ref, dg_ref):
    core, head, x = place[0], place[1], place[2]
    place_halves(dhidden_ref, core, (p0, p1, p2, p3))
    d, hidden = dhidden_ref[...], hidden_ref[...]
    scale = rms_scale(hidden)
    hat = hidden * scale
    dnorm_ref[...] = jnp.sum(d * hat, axis=0, keepdims=True)
    dhidden = dy_ref[...].astype(F32) + norm_back(d, norm_ref[...], scale, hat)
    dhidden_ref[...] = dhidden
    db_ref[...] = dhidden.astype(BF16)
    n = away_ref.shape[1]
    away_ref[...] = db_ref[:, pl.ds(pl.multiple_of((2 * head + 1 - x) * n, n), n)].astype(F32)
    dg_ref[...] = dot(db_ref[...], w_ref[...], NT)
    slots, heads = sum_ref.shape[:2]
    for h in range(heads):
        cols = pl.ds(h * HD, HD)
        gain = gain_ref[:, cols]
        total = jnp.zeros((1, HD), F32)
        for s in range(slots):
            rows = pl.ds(s * HD, HD)
            mixed, pre, dgated = mixed_ref[rows, cols], pre_ref[0, rows, cols], dg_ref[rows, cols]
            scale = rms_scale(mixed)
            hat = mixed * scale
            sig = sigmoid(pre)
            swish = pre * sig
            total += jnp.sum(dgated * hat * swish, axis=0, keepdims=True)
            dpre_ref[rows, cols] = (dgated * hat * gain * (sig * (1.0 + pre * (1.0 - sig)))).astype(BF16).astype(F32)
            dm = norm_back(dgated * swish, gain, scale, hat).astype(BF16)
            dm_ref[rows, cols] = dm
            back_ref[s, h, pl.ds(0, HD), :] = dot(dm, qe_ref[rows, cols], TN)
            back_ref[s, h, pl.ds(HD, 8), :] = sum_ref[s, h, pl.ds(HD, 8), :]
        dgain_ref[:, cols] = total


def intra_back_kernel(dm_ref, qe_ref, ke_ref, proj_ref, c_ref, state_ref, dq_ref, dk_ref, dv_ref, dl_ref):
    slots, heads = state_ref.shape[:2]
    lower = triangle("lower")
    upper = triangle("upper").astype(BF16)
    for s in range(slots):
        rows = pl.ds(s * HD, HD)
        for h in range(heads):
            cols = pl.ds(h * HD, HD)
            dm, qe, ke, cum = (r[rows, cols] for r in (dm_ref, qe_ref, ke_ref, c_ref))
            vb = proj_ref[2, rows, cols].astype(BF16)
            dscores = jnp.where(lower, dot(dm, vb, NT), 0.0).astype(BF16)
            to_q = dot(dscores, ke) + dot(dm, state_ref[s, h].astype(BF16))
            to_k = dot(dscores, qe, TN)
            pre = proj_ref[0, rows, cols]
            sig = sigmoid(pre)
            dq_ref[rows, cols] = (jnp.exp(cum) * to_q * (sig * (1.0 + pre * (1.0 - sig)))).astype(BF16).astype(F32)
            dk_ref[rows, cols] = jnp.exp(-cum) * to_k
            scores = jnp.where(lower, dot(qe, ke, NT), 0.0).astype(BF16)
            dv_ref[rows, cols] = dot(scores, dm, TN)
            dl_ref[rows, cols] = exact_dot(upper, qe.astype(F32) * to_q - ke.astype(F32) * to_k)


def state_back_kernel(pos, lengths, carried_ref, state_ref, ke_ref, forget_ref, value_ref, c_ref, bound_ref, dk_ref, dv_ref, dl_ref, dfv_ref, dbound_ref):
    slots, heads = state_ref.shape[:2]
    strict = triangle("strict").astype(BF16)
    for h in range(heads):
        cols = pl.ds(h * HD, HD)
        bound = bound_ref[:, cols]
        total = jnp.zeros((1, HD), F32)
        for s in range(slots):
            rows = pl.ds(s * HD, HD)
            ok = valid_rows(pos[0], lengths[s])
            cum, ke = c_ref[rows, cols], ke_ref[rows, cols]
            ending = carried_ref[s, h] * jnp.exp(cum[HD - 1 :, :])
            ending_low = ending.astype(BF16)
            to_k = dot(value_ref[0, rows, cols].astype(BF16), ending_low)
            dfv_ref[1, rows, cols] = (dv_ref[rows, cols] + dot(ke, ending_low, NT)).astype(BF16).astype(F32)
            through = jnp.sum(ending * state_ref[s, h], axis=0, keepdims=True)
            dlogf = dl_ref[rows, cols] + exact_dot(strict, ke.astype(F32) * to_k) + through
            dkeys = dk_ref[rows, cols] + jnp.exp(-cum) * to_k
            sig, forget = open_forget(forget_ref[0, rows, cols], bound, ok)
            dforget = jnp.where(ok, dlogf / forget - dkeys, 0.0)
            total += jnp.sum(dforget * (1.0 - sig), axis=0, keepdims=True)
            dfv_ref[0, rows, cols] = (dforget * (1.0 - bound) * sig * (1.0 - sig)).astype(BF16).astype(F32)
        dbound_ref[:, cols] = total


SMEM = pl.BlockSpec(memory_space=pltpu.SMEM)


def whole(shape, *index):
    index = index or (0,) * len(shape)
    return pl.BlockSpec(shape, lambda *_: index)


def sds(shape, dtype=F32):
    return jax.ShapeDtypeStruct(shape, dtype)


def call(kernel, name, outs, in_specs, out_specs, flops, moved, grid=(1,), scratch=(), vmem=48, aliases=None):
    return pl.pallas_call(
        kernel,
        name=name,
        grid=grid,
        out_shape=outs,
        in_specs=in_specs,
        out_specs=out_specs,
        scratch_shapes=list(scratch),
        input_output_aliases=aliases or {},
        compiler_params=pltpu.CompilerParams(vmem_limit_bytes=vmem * MIB),
        cost_estimate=pl.CostEstimate(flops=int(flops), bytes_accessed=int(moved), transcendentals=0),
    )


def entering_all(packed, backward):
    count, mine = lax.axis_size("seq"), lax.axis_index("seq")
    pieces = lax.all_gather(packed, "seq")
    if backward:
        pieces, mine = pieces[::-1], count - 1 - mine

    def step(position, state):
        piece = pieces[position]
        longer = piece[:, :, HD : HD + 1] * state + piece[:, :, :HD]
        return jnp.where(position < mine, longer, state)

    return lax.fori_loop(0, count - 1, step, jnp.zeros_like(packed[:, :, :HD]))


def decay(a):
    return a[:, HD : HD + 1]


def state(a):
    return a[:, :HD]


def join(a, b):
    both = decay(b) * state(a) + state(b)
    return jnp.concatenate([both, jnp.broadcast_to(decay(a) * decay(b), (a.shape[0], 8, HD))], axis=1)


def is_first(backward):
    is_low = lax.axis_index("seq") % 2 == 0
    return is_low, (~is_low if backward else is_low)


def pair_states(packed, backward):
    packed = packed.reshape(-1, PACKED, HD)
    half = packed.shape[0] // 2
    is_low, first = is_first(backward)
    mine = jnp.where(is_low, packed[:half], packed[half:])
    other = lax.ppermute(jnp.where(is_low, packed[half:], packed[:half]), "seq", X_SWAP)
    return jnp.where(first, mine, other), jnp.where(first, other, mine)


def pass_states(pair, backward):
    step = -1 if backward else 1
    before = lax.ppermute(pair, "seq", z_line(step))
    further = lax.ppermute(join(before, pair), "seq", z_line(2 * step))
    return decay(before) * state(further) + state(before)


def enter_states(early, into_first, shape, backward):
    is_low, first = is_first(backward)
    into_second = decay(early) * into_first + state(early)
    kept = jnp.where(first, into_first, into_second)
    given = lax.ppermute(jnp.where(first, into_second, into_first), "seq", X_SWAP)
    low, high = jnp.where(is_low, kept, given), jnp.where(is_low, given, kept)
    return jnp.concatenate([low, high]).reshape(shape)


def tie(*values):
    return lax.optimization_barrier(values)


def core_swap(a):
    return lax.ppermute(a, "head", CORE_SWAP)


def y_swap(a):
    return lax.ppermute(a, "head", Y_SWAP)


def x_swap(a):
    return lax.ppermute(a, "seq", X_SWAP)


def assemble(blocks, into=None, first=0):
    head = lax.axis_index("head")
    tokens, n = blocks[0][0].shape
    width = 4 * n
    here = jnp.stack([a for block in blocks for a in block]).reshape(len(blocks), 2, tokens, n)
    there = core_swap(here)
    at = jnp.stack([(head ^ k) * n for k in range(4)]).astype(jnp.int32)
    piece = pl.BlockSpec((1, 2, tokens, n), lambda i: (i, 0, 0, 0))
    out_spec = pl.BlockSpec((tokens, width), lambda i: (i + first, 0))
    grid = (len(blocks),)
    moved = 6 * len(blocks) * tokens * width
    if into is None:
        return call(assemble_kernel, "assemble", sds((len(blocks) * tokens, width), BF16), [SMEM, piece, piece], out_spec, 0, moved, grid=grid)(at, here, there)
    kept = pl.BlockSpec(memory_space=pl.ANY)
    return call(assemble_kernel, "assemble", sds(into.shape, BF16), [SMEM, piece, piece, kept], out_spec, 0, moved, grid=grid, aliases={3: 0})(at, here, there, into)


def join_heads(parts, into, first):
    heads, rows, n = parts.shape
    tokens = into.shape[0] // 4
    return call(
        join_kernel,
        "join",
        sds(into.shape, BF16),
        [pl.BlockSpec((heads, tokens, n), lambda i: (0, i, 0)), pl.BlockSpec(memory_space=pl.ANY)],
        pl.BlockSpec((tokens, heads * n), lambda i: (i + first, 0)),
        0,
        6 * rows * heads * n,
        grid=(rows // tokens,),
        aliases={1: 0},
    )(parts, into)


class Calls:
    def __init__(self, slots, length, width, local, units):
        self.slots, self.count, self.width, self.local, self.units = slots, slots * length, width, local, units
        self.heads = local // HD
        self.pair = 2 * HD
        self.steps = units // self.pair
        self.rest = units - self.steps * self.pair
        self.tall, self.channel = whole((self.count, width)), whole((self.count, local))
        self.row, self.w_spec = whole((1, local)), whole((local, width))
        self.half, self.half_spec = sds((self.count, width // 2)), whole((self.count, width // 2))
        self.state_shape = (slots, self.heads, HD, HD)
        self.packed_shape = (slots, self.heads, PACKED, HD)
        self.state_spec, self.packed_spec = whole(self.state_shape), whole(self.packed_shape)
        self.wide, self.norm_row = sds((self.count, width)), whole((1, width))
        self.low = sds((self.count, local), BF16)
        self.full = sds((self.count, local))

    def proj(self, *index):
        return whole((1, self.count, self.local), *index)

    def project(self, pos, lengths, tokens, norm, weight, bound):
        count, width, local, pair = self.count, self.width, self.local, self.pair
        block = pl.BlockSpec((count, pair), lambda i: (0, i))
        return call(
            project_kernel,
            "project",
            [sds((count, width), BF16), self.half, sds((4, count, local)), self.full, self.low, self.low, self.full, sds(self.packed_shape)],
            [SMEM, SMEM, self.tall, whole((1, width)), pl.BlockSpec((4, width, pair), lambda i: (0, 0, i)), pl.BlockSpec((1, pair), lambda i: (0, i))],
            [self.tall, self.half_spec, pl.BlockSpec((4, count, pair), lambda i: (0, 0, i))] + [block] * 4 + [pl.BlockSpec((self.slots, 2, PACKED, HD), lambda i: (0, i, 0, 0))],
            8 * count * width * local,
            20e6,
            grid=(local // pair,),
        )(pos, lengths, tokens, norm, weight, bound)

    def mixer_out(self, core, qe, states, intra, proj, gain, weight):
        return call(
            mixer_out_kernel,
            "mixer_out",
            [self.full, self.low, self.full, self.half, self.half],
            [SMEM, self.channel, self.state_spec, self.channel, self.proj(3, 0, 0), self.row, self.w_spec],
            [self.channel] * 3 + [self.half_spec] * 2,
            2 * self.count * self.width * self.local,
            10e6,
        )(core, qe, states, intra, proj, gain, weight)

    def ffn_specs(self, first=0, tail=True):
        width, pair, rest = self.width, self.pair, self.rest
        last = self.steps * pair // rest
        specs = [
            pl.BlockSpec((2, width, pair), lambda i: (0, 0, i + first)),
            pl.BlockSpec((pair, width), lambda i: (i + first, 0)),
            whole((2, width, rest), 0, 0, last),
            whole((rest, width), last, 0),
        ]
        return specs if tail else specs[:2]

    def ffn_own(self, core, xn2, dy, ffn_in, ffn_out):
        return call(
            ffn_own_kernel,
            "ffn_own",
            [self.wide, self.half, self.half],
            [SMEM, self.tall, self.tall, *self.ffn_specs()],
            [self.tall, self.half_spec, self.half_spec],
            12 * self.count * self.width * self.units,
            30e6,
            grid=(self.steps,),
            scratch=[pltpu.VMEM((self.count, self.width), F32)],
            vmem=60,
        )(core, xn2, dy, ffn_in, ffn_out, ffn_in, ffn_out)

    def norm_back(self, place, parts, hidden, dy, norm, weight, mixed, proj, gain, qe, packed):
        n = self.width // 8
        return call(
            norm_back_kernel,
            "norm_back",
            [self.full, self.low, sds((1, self.local)), sds(self.packed_shape), self.wide, sds((self.count, self.width), BF16), sds((self.count, n)), sds((1, self.width))],
            [SMEM] + [self.half_spec] * 4 + [self.tall, self.tall, self.norm_row, self.w_spec, self.channel, self.proj(3, 0, 0), self.row, self.channel, self.packed_spec],
            [self.channel, self.channel, self.row, self.packed_spec, self.tall, self.tall, whole((self.count, n)), self.norm_row],
            2 * self.count * self.width * self.local,
            10e6,
            scratch=[pltpu.VMEM((self.count, self.local), F32)],
        )(place, *parts, hidden, dy, norm, weight, mixed, proj, gain, qe, packed)

    def second_norm(self, place, tokens, parts, gain, lines):
        quarter = self.width // 4
        return call(
            second_norm_kernel,
            "second_norm",
            [self.wide, sds((lines * self.count, self.width), BF16), sds((self.count, quarter))],
            [SMEM, self.tall] + [self.half_spec] * 4 + [self.norm_row],
            [self.tall, self.tall, whole((self.count, quarter))],
            0,
            10e6,
        )(place, tokens, *parts, gain)

    def first_grad(self, dproj, weight):
        quarter = self.width // 4
        return call(
            first_grad_kernel,
            "first_grad",
            self.wide,
            [self.channel] * 4 + [pl.BlockSpec((4, quarter, self.local), lambda i: (0, i, 0))],
            pl.BlockSpec((self.count, quarter), lambda i: (0, i)),
            8 * self.count * self.width * self.local,
            15e6,
            grid=(4,),
        )(*dproj, weight)

    def first_back(self, dxn1, dhidden, tokens, gain):
        return call(
            first_back_kernel,
            "first_back",
            [sds((self.count, self.width), BF16), sds((1, self.width))],
            [self.tall, self.tall, self.tall, self.norm_row],
            [self.tall, self.norm_row],
            0,
            10e6,
        )(dxn1, dhidden, tokens, gain)

    def intra_back(self, dmixed, qe, ke, proj, cum, states):
        return call(
            intra_back_kernel,
            "intra_back",
            [self.full] * 4,
            [self.channel, self.channel, self.channel, whole((3, self.count, self.local)), self.channel, self.state_spec],
            [self.channel] * 4,
            14 * self.count * self.local * HD,
            10e6,
        )(dmixed, qe, ke, proj, cum, states)

    def state_back(self, pos, lengths, carried, states, ke, proj, cum, bound, dkeys, dvalues, dlogf):
        return call(
            state_back_kernel,
            "state_back",
            [sds((2, self.count, self.local)), sds((1, self.local))],
            [SMEM, SMEM, self.state_spec, self.state_spec, self.channel, self.proj(1, 0, 0), self.proj(2, 0, 0), self.channel, self.row] + [self.channel] * 3,
            [whole((2, self.count, self.local)), self.row],
            8 * self.count * self.local * HD,
            10e6,
        )(pos, lengths, carried, states, ke, proj, proj, cum, bound, dkeys, dvalues, dlogf)

    def widen(self, head, dy, lines):
        quarter = self.width // 4
        return call(
            widen_kernel,
            "widen",
            [sds((self.count, quarter)), sds((lines * self.count, self.width), BF16)],
            [SMEM, self.tall],
            [whole((self.count, quarter)), self.tall],
            0,
            4e6,
        )(head, dy)

    def turn(self, place, xn, got):
        shape = (4, self.width // 8, 2 * self.count)
        return call(turn_kernel, "turn", sds(shape, BF16), [SMEM, self.tall, self.half_spec], whole(shape), 0, 6e6)(place, xn, got)

    def mix_grad(self, turned, *grads):
        shape = (len(grads) // 2, 2, self.width // 8, self.local)
        return call(
            mix_grad_kernel,
            "mix_grad",
            [sds(shape)] * 2,
            [whole(turned.shape)] + [self.channel] * len(grads),
            [whole(shape)] * 2,
            len(grads) * self.count * self.width * self.local,
            10e6,
        )(turned, *grads)

    def ffn_grad(self, rows, xn, dy, ffn_in, ffn_out, first, steps):
        n, pair = self.width // 8, self.pair
        tail = first + steps == self.steps and self.rest > 0
        units = steps * pair + self.rest * tail
        out = sds((3, n, units))
        line = whole(xn.shape)
        return call(
            functools.partial(ffn_grad_kernel, tail),
            "ffn_grad",
            [out, out],
            [SMEM, line, line] + self.ffn_specs(first, tail),
            [whole(out.shape)] * 2,
            6 * xn.shape[0] * (self.width + 2 * n) * units,
            20e6,
            grid=(steps,),
            scratch=[pltpu.VMEM((2 * n, xn.shape[0]), BF16)] * 2 + [pltpu.VMEM((xn.shape[0], pair), BF16)] * 3,
            vmem=62,
        )(rows, xn, dy, *([ffn_in, ffn_out] * (2 if tail else 1)))


def scalar(v):
    return jnp.asarray(v, jnp.int32).reshape(1)


def body(tokens, lengths, norm_first, mix_weight, lower_bound, out_gain, w_out, norm_second, ffn_in, ffn_out, cotangent):
    shape = tokens.shape
    slots, length, width = shape
    local = lower_bound.shape[0]
    do = Calls(slots, length, width, local, ffn_out.shape[0])
    fast = lax.axis_size("seq") == 8 and lax.axis_size("head") == 4
    run = run_lines if fast else run_any
    output, grad_tokens, small, weights = run(
        do,
        tokens.reshape(do.count, width),
        lengths,
        norm_first.reshape(1, width),
        mix_weight,
        lower_bound.reshape(1, local),
        out_gain.reshape(1, local),
        w_out,
        norm_second.reshape(1, width),
        ffn_in,
        ffn_out,
        cotangent.reshape(do.count, width),
    )
    first, second = small[:width], small[width : 2 * width]
    bound_sum, gain_sum = small[2 * width : 2 * width + local], small[2 * width + local :]
    return (output.reshape(shape), grad_tokens.reshape(shape), first, weights[0], bound_sum, gain_sum, weights[1], second, weights[2], weights[3])


def run_any(do, tokens, lengths, norm_first, mix_weight, bound, gain, w_out, norm_second, ffn_in, ffn_out, dy):
    def total(halves):
        low, high = jnp.split(lax.psum(jnp.concatenate(halves, axis=1), "head"), 2, axis=1)
        return low, jnp.zeros_like(low), high, jnp.zeros_like(high)

    pos, core = scalar(lax.axis_index("seq")), scalar(0)
    nowhere = jnp.zeros((3,), jnp.int32)
    xn1, _, proj, cum, qe, ke, intra, packed = do.project(pos, lengths, tokens, norm_first, mix_weight, bound)
    states = entering_all(packed, False)
    mixed, gated, _, *halves = do.mixer_out(core, qe, states, intra, proj, gain, w_out)
    hidden, xn2, _ = do.second_norm(nowhere, tokens, total(halves), norm_second, 1)
    ffn, dkeep, dsend = do.ffn_own(core, xn2, dy, ffn_in, ffn_out)
    output = (hidden + lax.psum(ffn, "head")).astype(BF16)
    dpre_gate, dmixed, part_gain, back, dhidden, dbranch, _, part_norm_second = do.norm_back(
        nowhere, total((dkeep, dsend)), hidden, dy, norm_second, w_out, mixed, proj, gain, qe, packed
    )
    carried = entering_all(back, True)
    dpre_query, dkeys, dvalues, dlogf = do.intra_back(dmixed, qe, ke, proj, cum, states)
    dpre_fv, part_bound = do.state_back(pos, lengths, carried, states, ke, proj, cum, bound, dkeys, dvalues, dlogf)
    dproj = (dpre_query, dpre_fv[0], dpre_fv[1], dpre_gate)
    grad_tokens, part_norm_first = do.first_back(lax.psum(do.first_grad(dproj, mix_weight), "head"), dhidden, tokens, norm_first)
    weights = weight_grads_whole(xn1, dproj, gated, dbranch, xn2, dy, ffn_in, ffn_out)
    small = lax.psum(jnp.concatenate([part_norm_first[0], part_norm_second[0], part_bound[0], part_gain[0]]), "seq")
    return output, grad_tokens, small, weights


def run_lines(do, tokens, lengths, norm_first, mix_weight, bound, gain, w_out, norm_second, ffn_in, ffn_out, dy):
    width, local, quarter = do.width, do.local, do.width // 4
    seq, head = lax.axis_index("seq"), lax.axis_index("head")
    x, z = seq % 2, seq // 2
    seq_at, core = scalar(seq), scalar(head % 2)
    place = jnp.stack([head % 2, head, x]).astype(jnp.int32)

    def shift(a, k):
        return lax.ppermute(a, "seq", z_shift(k))

    def sum_cores(keep, send):
        return keep + core_swap(send)

    def sum_near(keep, send):
        got = lax.ppermute(send, "seq", flip(2))
        return (keep[:, 0], got[:, 0]), keep[:, 1] + got[:, 1]

    def sum_far(near):
        (a, b), far = near
        return a + b + lax.ppermute(far, "seq", flip(4))

    dy_quarter, dy_all = do.widen(scalar(head), dy, 4)
    dy1 = shift(dy_quarter, 1)
    xn1, xn1_away, proj, cum, qe, ke, intra, packed = do.project(seq_at, lengths, tokens, norm_first, mix_weight, bound)
    early, late = pair_states(packed, False)
    early, late, dy1 = tie(early, late, dy1)

    into = pass_states(join(early, late), False)
    dy1_over = y_swap(dy1)
    early, into, dy1_over, dy_quarter = tie(early, into, dy1_over, dy_quarter)

    states = enter_states(early, into, do.state_shape, False)
    mixed, gated, gated_wide, keep, send = do.mixer_out(core, qe, states, intra, proj, gain, w_out)
    half = sum_cores(keep, send)
    half, dy_quarter, xn1_away, dy1, dy1_over = tie(half, dy_quarter, xn1_away, dy1, dy1_over)

    over = y_swap(half)
    half_other = core_swap(half)
    dy2 = shift(dy_quarter, 2)
    xn1_got = x_swap(xn1_away)
    dy_all = assemble([(dy1, dy1_over)], dy_all, 1)
    half, half_other, over, dy2, gated_wide, xn1_got, dy_all = tie(half, half_other, over, dy2, gated_wide, xn1_got, dy_all)

    dy2_over = y_swap(dy2)
    hidden, xn_all, xn_quarter = do.second_norm(place, tokens, (half, over, half_other, core_swap(over)), norm_second, 4)
    xnl1 = shift(xn_quarter, 1)
    gated_got = x_swap(gated_wide)
    ffn, dkeep, dsend = do.ffn_own(core, xn_all, dy, ffn_in, ffn_out)
    dkeep, dsend, xn_quarter, dy2_over, xnl1, gated_got, ffn = tie(dkeep, dsend, xn_quarter, dy2_over, xnl1, gated_got, ffn)

    dhalf = sum_cores(dkeep, dsend)
    dhalf, xn_quarter, dy_all, xn1_got = tie(dhalf, xn_quarter, dy_all, xn1_got)
    dover = y_swap(dhalf)
    dhalf_other = core_swap(dhalf)
    xnl2 = shift(xn_quarter, 2)
    dy_all = assemble([(dy2, dy2_over)], dy_all, 2)
    xn1_turned = do.turn(seq_at, xn1, xn1_got)
    dhalf, dover, dhalf_other, xnl2, xn_quarter, xnl1, dy_all, xn1_turned = tie(dhalf, dover, dhalf_other, xnl2, xn_quarter, xnl1, dy_all, xn1_turned)

    xnl3 = shift(xn_quarter, 3)
    dpre_gate, dmixed, part_gain, back, dhidden, dbranch, dbranch_away, part_norm_second = do.norm_back(
        place, (dhalf, dover, dhalf_other, core_swap(dover)), hidden, dy, norm_second, w_out, mixed, proj, gain, qe, packed
    )
    back, dpre_gate, dmixed, dbranch, dbranch_away, dy_quarter = tie(back, dpre_gate, dmixed, dbranch, dbranch_away, dy_quarter)

    early, late = pair_states(back, True)
    dy3 = shift(dy_quarter, 3)
    early, late, dpre_gate, dmixed, dbranch_away, xnl3, dy3 = tie(early, late, dpre_gate, dmixed, dbranch_away, xnl3, dy3)
    xn_parts = lax.all_gather(jnp.concatenate([xnl1, xnl2, xnl3]), "head")
    into = pass_states(join(early, late), True)
    dbranch_own = x_swap(dbranch_away)
    dpre_query, dkeys, dvalues, dlogf = do.intra_back(dmixed, qe, ke, proj, cum, states)
    gate_got = x_swap(dpre_gate)
    dy3_over = y_swap(dy3)
    early, into, gate_got, dpre_query, dbranch_own, dy3_over = tie(early, into, gate_got, dpre_query, dbranch_own, dy3_over)

    dbranch_over = y_swap(dbranch_own)
    gate = do.mix_grad(xn1_turned, dpre_gate, gate_got)
    carried = enter_states(early, into, do.state_shape, True)
    dy_all = assemble([(dy3, dy3_over)], dy_all, 3)
    carried, gate = tie(carried, gate)
    dpre_fv, part_bound = do.state_back(seq_at, lengths, carried, states, ke, proj, cum, bound, dkeys, dvalues, dlogf)
    dpre_fv, dpre_query, gate, dbranch_over, dy_all = tie(dpre_fv, dpre_query, gate, dbranch_over, dy_all)

    fv_got = x_swap(dpre_fv)
    near_gate = sum_near(*gate)
    dxn1 = do.first_grad((dpre_query, dpre_fv[0], dpre_fv[1], dpre_gate), mix_weight)
    down = do.mix_grad(do.turn(seq_at, dbranch, assemble([(dbranch_own, dbranch_over)])), gated, gated_got)
    near_down = sum_near(*down)
    fv_got, near_gate, near_down, xn_all, dpre_query, xn_parts, dxn1, ffn = tie(fv_got, near_gate, near_down, xn_all, dpre_query, xn_parts, dxn1, ffn)
    dxn1, ffn = lax.psum((dxn1, ffn), "head")

    rows = jnp.stack([seq, seq ^ 1]).astype(jnp.int32)
    query_got = x_swap(dpre_query)
    grad_early = sum_far(tuple(jax.tree.map(lambda a, b: jnp.concatenate([a, b]), near_gate, near_down)))
    forget_values = do.mix_grad(xn1_turned, dpre_fv[0], fv_got[0], dpre_fv[1], fv_got[1])
    forget_values, xn_all, xn_parts = tie(forget_values, xn_all, xn_parts)
    near_fv = sum_near(*forget_values)
    xn_all = join_heads(xn_parts, xn_all, 1)
    mine_a, away_a = do.ffn_grad(rows, xn_all, dy_all, ffn_in, ffn_out, 0, 2)
    away_a, xn_all, query_got = tie(away_a, xn_all, query_got)
    got_a = x_swap(away_a)
    query = do.mix_grad(xn1_turned, dpre_query, query_got)
    mine_b, away_b = do.ffn_grad(rows, xn_all, dy_all, ffn_in, ffn_out, 2, 2)
    near_fv, grad_early, got_a, query, away_b, xn_all = tie(near_fv, grad_early, got_a, query, away_b, xn_all)

    got_b = x_swap(away_b)
    near_query, grad_fv = sum_near(*query), sum_far(near_fv)
    grad_tokens, part_norm_first = do.first_back(dxn1, dhidden, tokens, norm_first)
    mine_c, away_c = do.ffn_grad(rows, xn_all, dy_all, ffn_in, ffn_out, 4, do.steps - 4)
    small = jnp.concatenate([part_norm_first[0], part_norm_second[0], part_bound[0], part_gain[0]])
    got_b, near_query, grad_fv, small, away_c = tie(got_b, near_query, grad_fv, small, away_c)

    got_c = x_swap(away_c)
    grad_query = sum_far(near_query)
    for bit in (1, 2, 4):
        small = small + lax.ppermute(small, "seq", flip(bit))
    output = (hidden + ffn).astype(BF16)
    parts = ((mine_a, got_a), (mine_b, got_b), (mine_c, got_c))
    grad_in = jnp.concatenate([mine[:2] + got[:2] for mine, got in parts], axis=2)
    grad_out = jnp.concatenate([(mine[2] + got[2]).T for mine, got in parts], axis=0)
    grad_mix = jnp.concatenate([grad_query, grad_fv, grad_early[:1]])
    return output, grad_tokens, small, (grad_mix, grad_early[1].T, grad_in, grad_out)


def weight_grads_whole(xn1, dproj, gated, dbranch, xn2, dy, ffn_in, ffn_out):
    gate, up = dot(xn2, ffn_in[0]), dot(xn2, ffn_in[1])
    dact = dot(dy, ffn_out, NT)
    sig = sigmoid(gate)
    swish = gate * sig
    act = (swish * up).astype(BF16)
    dgate = (dact * up * (sig * (1.0 + gate * (1.0 - sig)))).astype(BF16)
    dup = (dact * swish).astype(BF16)

    def scatter(a, axis):
        return lax.psum_scatter(a, "seq", scatter_dimension=axis, tiled=True)

    return (
        jnp.stack([scatter(dot(xn1, d.astype(BF16), TN), 0) for d in dproj]),
        scatter(dot(gated, dbranch, TN), 1),
        jnp.stack([scatter(dot(xn2, d, TN), 0) for d in (dgate, dup)]),
        scatter(dot(act, dy, TN), 1),
    )


def solution(mesh):
    in_specs = (
        P(None, "seq", None),
        P(),
        P(),
        P(None, None, "head"),
        P("head"),
        P("head"),
        P("head", None),
        P(),
        P(None, None, "head"),
        P("head", None),
        P(None, "seq", None),
    )
    out_specs = (
        P(None, "seq", None),
        P(None, "seq", None),
        P(),
        P(None, "seq", "head"),
        P("head"),
        P("head"),
        P("head", "seq"),
        P(),
        P(None, "seq", "head"),
        P("head", "seq"),
    )
    return jax.shard_map(body, mesh=mesh, in_specs=in_specs, out_specs=out_specs, check_vma=False)
```

time: 604 us -> 556 us (0.921)
  Pallas kernels: 145 us -> 173 us
  local copies, waits for them, and re-layouts: 49.7 us -> 23 us
  waiting for transfers between devices: 236 us -> 214 us
  matrix products: 15.9 us -> 0 us
  other arithmetic: 62.1 us -> 46.8 us
  between operations: 2.85 us -> 15.4 us
  starting transfers between devices: 84 us -> 76.2 us
    ppermute x12 -> x6, waiting for transfers between devices: 73.1 us -> 3.22 us  [y_swap(): return lax.ppermute(a, 'head', Y_SWAP)]
    ppermute x7 -> x6, waiting for transfers between devices: 9.64 us -> 65.6 us  [shift(): return lax.ppermute(a, 'seq', z_shift(k))]
    ppermute x13 -> x9, waiting for transfers between devices: 37 us -> 0.32 us  [x_swap(): return lax.ppermute(a, 'seq', X_SWAP)]
    pallas_call x16 -> x20, Pallas kernels: 118 us -> 140 us  [the longest x3 62.4 us: ffn_grad(): call(functools.partial(ffn_grad_kernel, tail), 'ffn_grad', [out, out], [S...]
    psum x0 -> x1, waiting for transfers between devices: none -> 18.1 us  [run_lines(): dxn1, ffn = lax.psum((dxn1, ffn), 'head')]
    dot_general x4 -> x0, matrix products: 15.9 us -> none  [dot(): return lax.dot_general(a, b, (dims, ((), ())), preferred_element_type=F32)]
    unnamed x260 -> x137, local copies, waits for them, and re-layouts: 29.4 us -> 15.6 us
    ppermute x8 -> x7, waiting for transfers between devices: 44.7 us -> 30.9 us  [the longest x4 24.6 us: sum_near(): got = lax.ppermute(send, 'seq', flip(2))]
  transfers between devices with their start and end apart: 75 -> 51, of which waited for: 29 -> 23; matrix products, arithmetic and copies ran while one was open for 16% -> 8% of each run, Pallas kernels for 24% -> 30%
where the time goes in v3:
time: 556 us; the launch traced here: 548 us
  waiting for transfers between devices  214 us (38%)
  Pallas kernels  173 us (31%)
  starting transfers between devices  76.2 us (14%)
  other arithmetic  46.8 us (8%)
  local copies, waits for them, and re-layouts  23 us (4%)
  between operations  15.4 us (3%)
    ppermute x6, waiting for transfers between devices, shift(): return lax.ppermute(a, 'seq', z_shift(k))  65.6 us
    pallas_call x3, Pallas kernels, ffn_grad(): call(functools.partial(ffn_grad_kernel, tail), 'ffn_grad', [out, out], [S...  62.4 us
    ppermute x4, waiting for transfers between devices, sum_near(): got = lax.ppermute(send, 'seq', flip(2))  24.6 us
    ppermute x6, starting transfers between devices, shift(): return lax.ppermute(a, 'seq', z_shift(k))  23.7 us
    pallas_call x1, Pallas kernels, ffn_own(): call(ffn_own_kernel, 'ffn_own', [self.wide, self.half, self.half], [SMEM,...  22.9 us
    ppermute x2, waiting for transfers between devices, pass_states(): further = lax.ppermute(join(before, pair), 'seq', z_line(2 * step))  21.1 us
    ppermute x2, waiting for transfers between devices, pair_states(): lax.ppermute(jnp.where(is_low, packed[half:], packed[:half]), 'seq', X_SWAP)  20.7 us
    psum x1, waiting for transfers between devices, run_lines(): dxn1, ffn = lax.psum((dxn1, ffn), 'head')  18.1 us
  transfers between devices with their start and end apart: 51, of which 23 were waited for; matrix products, arithmetic and copies ran while one was open for 8% of the time, Pallas kernels for 30%

profile of v3, /device:TPU:0, one launch (start us, length us, event | category | flops | bytes accessed | tf_op | source)
XLA Modules:
  0.0 548.3 jit_solution(16425483197083996092)
XLA Ops:
  10.2 3.0 collective-permute-start.1
  13.2 11.8 %project.1 = (bf16[384,2048]{1,0:T(8,128)(2,1)S(1)}, f32[384,1024]{1,0:T(8,128)}, f32[4,384,512]{2,1,0:T(8,128)}, f32[384,512]{1,0:T(8,128)S(1)}, bf16[384,512]{...) custom-call(s32[1]{0:T(128)} %bitcast.4.pos.place, ...), custom_call_target="tpu_custom_call" | custom-call | flops 3221225472 | bytes 20000000 | tf_op jit(solution)/shard_map/project/pallas_call | solution.py:515
  26.6 9.6 %collective-permute-done = f32[6,136,128]{2,1,0:T(8,128)S(1)} collective-permute-done((f32[6,136,128]{2,1,0:T(8,128)S(1)}, f32[6,136,128]{2,1,0:T(8,128)S(1)}, u32[]{:S(2)}, u32[]{:S(2)}) %collective-permute-start) | collective-permute-done | bytes 417824 | tf_op jit(solution)/shard_map/ppermute | solution.py:423
  36.5 3.5 collective-permute-start.2
  41.6 6.1 %collective-permute-done.2 = f32[6,136,128]{2,1,0:T(8,128)S(1)} collective-permute-done((f32[6,136,128]{2,1,0:T(8,128)S(1)}, f32[6,136,128]{2,1,0:T(8,128)S(1)}, u32[]{:S(2)}, u32[]{:S(2)}) %collective-permute-start.2) | collective-permute-done | bytes 417824 | tf_op jit(solution)/shard_map/ppermute | solution.py:429
  47.8 5.4 collective-permute-start.3
  53.2 6.9 %collective-permute-done.3 = f32[6,136,128]{2,1,0:T(8,128)S(1)} collective-permute-done((f32[6,136,128]{2,1,0:T(8,128)S(1)}, f32[6,136,128]{2,1,0:T(8,128)S(1)}, u32[]{:S(2)}, u32[]{:S(2)}) %collective-permute-start.3) | collective-permute-done | bytes 417824 | tf_op jit(solution)/shard_map/ppermute | solution.py:430
  61.8 6.6 %collective-permute-done.5 = f32[6,128,128]{2,1,0:T(8,128)} collective-permute-done((f32[6,128,128]{2,1,0:T(8,128)S(1)}, f32[6,128,128]{2,1,0:T(8,128)}, u32[]{:S(2)}, u32[]{:S(2)}) %collective-permute-start.5) | collective-permute-done | bytes 393248 | tf_op jit(solution)/shard_map/ppermute | solution.py:438
  69.6 4.6 mixer_out.1
  74.2 3.6 collective-permute-done.6
  84.3 3.4 collective-permute-start.9
  87.8 2.8 assemble.4.refs_0_
  90.6 31.5 %collective-permute-done.9 = f32[384,512]{1,0:T(8,128)} collective-permute-done((f32[384,512]{1,0:T(8,128)}, f32[384,512]{1,0:T(8,128)}, u32[]{:S(2)}, u32[]{:S(2)}) %collective-permute-start.9) | collective-permute-done | bytes 786464 | tf_op jit(solution)/shard_map/ppermute | solution.py:745
  127.0 6.3 %second_norm.1 = (f32[384,2048]{1,0:T(8,128)}, bf16[1536,2048]{1,0:T(8,128)(2,1)}, f32[384,512]{1,0:T(8,128)}) custom-call(s32[3]{0:T(128)S(1)} %pad_add_fusion.place, bf16[384,2048]{1,0:T(8,128)(2,1)S(1)} %bitcast.133, f32[384,1024]{1,0:T(8,128)} %add.157.p0, f32[384,1024]{1,0:T(8,128)} %collective-permute-done.8.p1, ...), custom_call_target="tpu_custom_call" | custom-call | bytes 10000000 | tf_op jit(solution)/shard_map/second_norm/pallas_call | solution.py:577
  133.3 8.7 %collective-permute-start.14 = (f32[384,512]{1,0:T(8,128)}, f32[384,512]{1,0:T(8,128)S(1)}, u32[]{:S(2)}, u32[]{:S(2)}) collective-permute-start(f32[384,512]{1,0:T(8,128)} %get-tuple-element.220), channel_id=1, source_target_pairs={{0,8},{4,12},{8,16},{12,20},{16,24},{20,28},{24,0},{28,4},{1,9},{5... | collective-permute-start | bytes 2359304 | tf_op jit(solution)/shard_map/ppermute | solution.py:745
  141.9 22.9 %ffn_own.1 = (f32[384,2048]{1,0:T(8,128)}, f32[384,1024]{1,0:T(8,128)}, f32[384,1024]{1,0:T(8,128)}) custom-call(s32[1]{0:T(128)} %bitcast.core, bf16[1536,2048]{1,0:T(8,128)(2,1)} %get-tuple-element.280.xn_ref._, bf16[384,2048]{1,0:T(8,128)(2,1)} %bitcast.129, bf16[2,2048,1408]{2,1,0:T(8,128)(2,1)} %refs_2_.1, bf16[1408,2048]{1,0:T(8,128)(2,1)} %refs_3_.1, ...), custom_call_target="tpu_custom_call" | custom-call | flops 13287555072 | bytes 30000000 | tf_op jit(solution)/shard_map/ffn_own/pallas_call | solution.py:549
  170.5 3.4 collective-permute-start.19
  177.6 31.1 %collective-permute-done.19 = f32[384,512]{1,0:T(8,128)} collective-permute-done((f32[384,512]{1,0:T(8,128)}, f32[384,512]{1,0:T(8,128)}, u32[]{:S(2)}, u32[]{:S(2)}) %collective-permute-start.19) | collective-permute-done | bytes 786464 | tf_op jit(solution)/shard_map/ppermute | solution.py:745
  208.9 2.6 collective-permute-start.23
  213.3 10.4 %norm_back.1 = (f32[384,512]{1,0:T(8,128)S(1)}, bf16[384,512]{1,0:T(8,128)(2,1)S(1)}, f32[1,512]{1,0:T(1,128)S(1)}, f32[3,4,136,128]{3,2,1,0:T(8,128)S(1)}, f32[...) custom-call(s32[3]{0:T(128)S(1)} %pad_add_fusion.place, ...), custom_call_target="tpu_custom_call" | custom-call | flops 805306368 | bytes 10000000 | tf_op jit(solution)/shard_map/norm_back/pallas_call | solution.py:564
  225.7 2.6 collective-permute-start.24
  229.7 11.1 %collective-permute-done.22 = f32[6,136,128]{2,1,0:T(8,128)} collective-permute-done((f32[6,136,128]{2,1,0:T(8,128)}, f32[6,136,128]{2,1,0:T(8,128)}, u32[]{:S(2)}, u32[]{:S(2)}) %collective-permute-start.22) | collective-permute-done | bytes 417824 | tf_op jit(solution)/shard_map/ppermute | solution.py:423
  243.0 3.0 collective-permute-done.24
  246.1 3.0 pad_maximum_fusion.1
  255.2 9.2 %collective-permute-done.25 = f32[6,136,128]{2,1,0:T(8,128)S(1)} collective-permute-done((f32[6,136,128]{2,1,0:T(8,128)S(1)}, f32[6,136,128]{2,1,0:T(8,128)S(1)}, u32[]{:S(2)}, u32[]{:S(2)}) %collective-permute-start.25) | collective-permute-done | bytes 417824 | tf_op jit(solution)/shard_map/ppermute | solution.py:429
  266.5 5.9 %intra_back.1 = (f32[384,512]{1,0:T(8,128)}, f32[384,512]{1,0:T(8,128)S(1)}, f32[384,512]{1,0:T(8,128)S(1)}, f32[384,512]{1,0:T(8,128)S(1)}) custom-call(bf16[384,512]{1,0:T(8,128)(2,1)S(1)} %copy-done.26, bf16[384,512]{1,0:T(8,128)(2,1)S(1)} %get-tuple-element.162.qe_ref, bf16[384,512]{1,0:T(8,128)(2,1)S(1)} %get-tuple-element.226.ke_ref, ...), custom_call_target="tpu_custom_call" | custom-call | flops 352321536 | bytes 10000000 | tf_op jit(solution)/shard_map/intra_back/pallas_call | solution.py:612
  272.5 14.3 %collective-permute-done.26 = f32[6,136,128]{2,1,0:T(8,128)S(1)} collective-permute-done((f32[6,136,128]{2,1,0:T(8,128)S(1)}, f32[6,136,128]{2,1,0:T(8,128)S(1)}, u32[]{:S(2)}, u32[]{:S(2)}) %collective-permute-start.26) | collective-permute-done | bytes 417824 | tf_op jit(solution)/shard_map/ppermute | solution.py:430
  292.7 7.2 %collective-permute-done.30 = f32[6,128,128]{2,1,0:T(8,128)S(1)} collective-permute-done((f32[6,128,128]{2,1,0:T(8,128)S(1)}, f32[6,128,128]{2,1,0:T(8,128)S(1)}, u32[]{:S(2)}, u32[]{:S(2)}) %collective-permute-start.30) | collective-permute-done | bytes 393248 | tf_op jit(solution)/shard_map/ppermute | solution.py:438
  300.0 3.9 state_back.1
  305.8 3.2 collective-permute-done.31
  309.2 2.6 collective-permute-start.34
  322.0 8.0 %first_grad.1 = f32[384,2048]{1,0:T(8,128)} custom-call(f32[384,512]{1,0:T(8,128)} %get-tuple-element.283.d0.refs_0_, f32[384,512]{1,0:T(8,128)S(1)} %get-tuple-element.331.d1.refs_0_, f32[384,512]{1,0:T(8,128)S(1)} %get-tuple-element.330.d2.refs_2_, f32[384,512]{1,0:T(8,128)S(1)} %copy-done.8, bf16[4,2048,512]{2,1,0:T(8,128)(2,1)} %w_ref.7), custom_call_target="tpu_custom_call" | custom-call | flops 3221225472 | bytes 15000000 | tf_op jit(solution)/shard_map/first_grad/pallas_call | solution.py:589
  330.9 5.1 collective-permute-done.34
  336.1 2.7 fusion.4
  338.8 19.5 %collective-permute-done.36 = f32[1,2,256,512]{3,2,1,0:T(8,128)} collective-permute-done((f32[1,2,256,512]{3,2,1,0:T(8,128)}, f32[1,2,256,512]{3,2,1,0:T(8,128)}, u32[]{:S(2)}, u32[]{:S(2)}) %collective-permute-start.36) | collective-permute-done | bytes 1048608 | tf_op jit(solution)/shard_map/ppermute | solution.py:751
  362.3 3.8 mix_grad.6
  372.4 7.1 %join.1.xn_ref = bf16[1536,2048]{1,0:T(8,128)(2,1)} custom-call(f32[4,1152,512]{2,1,0:T(8,128)} %bitcast.150, bf16[1536,2048]{1,0:T(8,128)(2,1)} %get-tuple-element.280.xn_ref._), custom_call_target="tpu_custom_call", output_to_operand_aliasing={{}: (1, {})} | custom-call | bytes 14155776 | tf_op jit(solution)/shard_map/join/pallas_call | solution.py:479
  379.4 20.8 %ffn_grad.3 = (f32[3,256,512]{2,1,0:T(8,128)}, f32[3,256,512]{2,1,0:T(8,128)}) custom-call(s32[2]{0:T(128)} %pad_add_fusion.3.rows, bf16[1536,2048]{1,0:T(8,128)(2,1)} %join.1.xn_ref, bf16[1536,2048]{1,0:T(8,128)(2,1)} %assemble.6.dy_ref, bf16[2,2048,1408]{2,1,0:T(8,128)(2,1)} %refs_2_.1, bf16[1408,2048]{1,0:T(8,128)(2,1)} %refs_3_.1), custom_call_target="tpu_custom_call" | custom-call | flops 12079595520 | bytes 20000000 | tf_op jit(solution)/shard_map/ffn_grad/pallas_call | solution.py:667
  403.2 3.7 mix_grad.7
  407.8 21.1 %ffn_grad.4 = (f32[3,256,512]{2,1,0:T(8,128)}, f32[3,256,512]{2,1,0:T(8,128)}) custom-call(s32[2]{0:T(128)} %pad_add_fusion.3.rows, bf16[1536,2048]{1,0:T(8,128)(2,1)} %join.1.xn_ref, bf16[1536,2048]{1,0:T(8,128)(2,1)} %assemble.6.dy_ref, bf16[2,2048,1408]{2,1,0:T(8,128)(2,1)} %refs_2_.1, bf16[1408,2048]{1,0:T(8,128)(2,1)} %refs_3_.1), custom_call_target="tpu_custom_call" | custom-call | flops 12079595520 | bytes 20000000 | tf_op jit(solution)/shard_map/ffn_grad/pallas_call | solution.py:667
  429.0 6.3 %collective-permute-done.38 = f32[2,256,512]{2,1,0:T(8,128)} collective-permute-done((f32[2,256,512]{2,1,0:T(8,128)}, f32[2,256,512]{2,1,0:T(8,128)}, u32[]{:S(2)}, u32[]{:S(2)}) %collective-permute-start.38) | collective-permute-done | bytes 1048608 | tf_op jit(solution)/shard_map/ppermute | solution.py:756
  437.3 3.7 fusion
  442.0 3.2 collective-permute-start.42
  451.6 20.4 %ffn_grad.5 = (f32[3,256,384]{2,1,0:T(8,128)}, f32[3,256,384]{2,1,0:T(8,128)}) custom-call(s32[2]{0:T(128)} %pad_add_fusion.3.rows, bf16[1536,2048]{1,0:T(8,128)(2,1)} %join.1.xn_ref, bf16[1536,2048]{1,0:T(8,128)(2,1)} %assemble.6.dy_ref, bf16[2,2048,1408]{2,1,0:T(8,128)(2,1)} %refs_2_.1, bf16[1408,2048]{1,0:T(8,128)(2,1)} %refs_3_.1, ...), custom_call_target="tpu_custom_call" | custom-call | flops 9059696640 | bytes 20000000 | tf_op jit(solution)/shard_map/ffn_grad/pallas_call | solution.py:667
  472.0 18.1 %all-reduce.3.cloned.1.call-done = (f32[384,2048]{1,0:T(8,128)}, f32[384,2048]{1,0:T(8,128)}) async-done(((f32[384,2048]{1,0:T(8,128)}, f32[384,2048]{1,0:T(8,128)}), (f32[384,2048]{1,0:T(8,128)}, f32[384,2048]{1,0:T(8,128)})) %all-reduce.3.cloned.1.call-update) | async-done | bytes 6291472 | tf_op jit(solution)/shard_map/psum | solution.py:827
  491.9 5.9 %first_back.1 = (bf16[384,2048]{1,0:T(8,128)(2,1)}, f32[1,2048]{1,0:T(1,128)S(1)}) custom-call(f32[384,2048]{1,0:T(8,128)S(1)} %copy-done.11, f32[384,2048]{1,0:T(8,128)} %get-tuple-element.264.dhidden_ref, bf16[384,2048]{1,0:T(8,128)(2,1)S(1)} %bitcast.134, f32[1,2048]{1,0:T(1,128)S(1)} %bitcast.141), custom_call_target="tpu_custom_call" | custom-call | bytes 10000000 | tf_op jit(solution)/shard_map/first_back/pallas_call | solution.py:601
  510.5 7.6 %collective-permute-done.45 = f32[5120]{0:T(1024)S(1)} collective-permute-done((f32[5120]{0:T(1024)S(1)}, f32[5120]{0:T(1024)S(1)}, u32[]{:S(2)}, u32[]{:S(2)}) %collective-permute-start.45) | collective-permute-done | bytes 20512 | tf_op jit(solution)/shard_map/ppermute | solution.py:853
  521.7 9.0 %collective-permute-done.46 = f32[5120]{0:T(1024)S(1)} collective-permute-done((f32[5120]{0:T(1024)S(1)}, f32[5120]{0:T(1024)S(1)}, u32[]{:S(2)}, u32[]{:S(2)}) %collective-permute-start.46) | collective-permute-done | bytes 20512 | tf_op jit(solution)/shard_map/ppermute | solution.py:853
  (286 shorter events, 116.7 us)
Async XLA Ops:
  7.2 353.5 %all-gather.3.cloned.1.call-start = ((), (), s32[]{:S(2)}) async-start(), calls=%async_computation | async-start | bytes 11796480 | tf_op jit(solution)/shard_map/all_gather | solution.py:805
  10.2 26.2 %collective-permute-start.1 = (f32[384,512]{1,0:T(8,128)}, f32[384,512]{1,0:T(8,128)}, u32[]{:S(2)}, u32[]{:S(2)}) collective-permute-start(f32[384,512]{1,0:T(8,128)} %get-tuple-element.221), channel_id=1, source_target_pairs={{0,8},{4,12},{8,16},{12,20},{16,24},{20,28},{24,0},{28,4},{1,9},{5... | collective-permute-start | bytes 2359304 | tf_op jit(solution)/shard_map/ppermute | solution.py:745
  25.1 11.2 %collective-permute-start = (f32[6,136,128]{2,1,0:T(8,128)S(1)}, f32[6,136,128]{2,1,0:T(8,128)S(1)}, u32[]{:S(2)}, u32[]{:S(2)}) collective-permute-start(f32[6,136,128]{2,1,0:T(8,128)S(1)} %slice_select_fusion.2), channel_id=1, source_target_pairs={{0,4},{4,0},{8,12},{12,8},{16,20},{20,16},{24,28},{28,24},{1,5},{5... | collective-permute-start | bytes 1253384 | tf_op jit(solution)/shard_map/ppermute | solution.py:423
  36.5 11.2 %collective-permute-start.2 = (f32[6,136,128]{2,1,0:T(8,128)S(1)}, f32[6,136,128]{2,1,0:T(8,128)S(1)}, u32[]{:S(2)}, u32[]{:S(2)}) collective-permute-start(f32[6,136,128]{2,1,0:T(8,128)S(1)} %pad_maximum_fusion.7), channel_id=1, source_target_pairs={{0,8},{4,12},{8,16},{12,20},{16,24},{20,28},{1,9},{5,13},{9,17},{1... | collective-permute-start | bytes 1253384 | tf_op jit(solution)/shard_map/ppermute | solution.py:429
  40.0 20.2 %collective-permute-start.4 = (f32[384,512]{1,0:T(8,128)}, f32[384,512]{1,0:T(8,128)}, u32[]{:S(2)}, u32[]{:S(2)}) collective-permute-start(f32[384,512]{1,0:T(8,128)} %collective-permute-done.1), channel_id=1, source_target_pairs={{0,2},{1,3},{2,0},{3,1},{4,6},{5,7},{6,4},{7,5},{8,10},{9,11},{10,... | collective-permute-start | bytes 2359304 | tf_op jit(solution)/shard_map/ppermute | solution.py:452
  47.8 12.3 %collective-permute-start.3 = (f32[6,136,128]{2,1,0:T(8,128)S(1)}, f32[6,136,128]{2,1,0:T(8,128)S(1)}, u32[]{:S(2)}, u32[]{:S(2)}) collective-permute-start(f32[6,136,128]{2,1,0:T(8,128)S(1)} %pad_maximum_fusion.8), channel_id=1, source_target_pairs={{0,16},{4,20},{8,24},{12,28},{1,17},{5,21},{9,25},{13,29},{2,18},{... | collective-permute-start | bytes 1253384 | tf_op jit(solution)/shard_map/ppermute | solution.py:430
  60.3 8.1 %collective-permute-start.5 = (f32[6,128,128]{2,1,0:T(8,128)S(1)}, f32[6,128,128]{2,1,0:T(8,128)}, u32[]{:S(2)}, u32[]{:S(2)}) collective-permute-start(f32[6,128,128]{2,1,0:T(8,128)S(1)} %fusion.10), channel_id=1, source_target_pairs={{0,4},{4,0},{8,12},{12,8},{16,20},{20,16},{24,28},{28,24},{1,5},{5... | collective-permute-start | bytes 1179656 | tf_op jit(solution)/shard_map/ppermute | solution.py:438
  80.7 7.0 %collective-permute-start.11 = (f32[1,2,384,512]{3,2,1,0:T(8,128)S(1)}, f32[1,2,384,512]{3,2,1,0:T(8,128)}, u32[]{:S(2)}, u32[]{:S(2)}) collective-permute-start(f32[1,2,384,512]{3,2,1,0:T(8,128)S(1)} %maximum_bitcast_fusion.here_ref), channel_id=1, source_target_pairs={{0,1},{1,0},{2,3},{3,2},{4,5},{5,4},{6,7},{7,6},{8,9},{9,8},{10,11... | collective-permute-start | bytes 4718600 | tf_op jit(solution)/shard_map/ppermute | solution.py:448
  81.0 41.2 %collective-permute-start.7 = (f32[384,1024]{1,0:T(8,128)}, f32[384,1024]{1,0:T(8,128)}, u32[]{:S(2)}, u32[]{:S(2)}) collective-permute-start(f32[384,1024]{1,0:T(8,128)} %add.157.p0), channel_id=1, source_target_pairs={{0,1},{1,0},{2,3},{3,2},{4,5},{5,4},{6,7},{7,6},{8,9},{9,8},{10,11... | collective-permute-start | bytes 4718600 | tf_op jit(solution)/shard_map/ppermute | solution.py:448
  81.3 40.8 %collective-permute-start.8 = (f32[384,1024]{1,0:T(8,128)}, f32[384,1024]{1,0:T(8,128)}, u32[]{:S(2)}, u32[]{:S(2)}) collective-permute-start(f32[384,1024]{1,0:T(8,128)} %add.157.p0), channel_id=1, source_target_pairs={{0,2},{1,3},{2,0},{3,1},{4,6},{5,7},{6,4},{7,5},{8,10},{9,11},{10,... | collective-permute-start | bytes 4718600 | tf_op jit(solution)/shard_map/ppermute | solution.py:452
  82.8 39.3 %collective-permute-start.10 = (f32[384,1024]{1,0:T(8,128)}, f32[384,1024]{1,0:T(8,128)}, u32[]{:S(2)}, u32[]{:S(2)}) collective-permute-start(f32[384,1024]{1,0:T(8,128)} %get-tuple-element.180), channel_id=1, source_target_pairs={{0,4},{4,0},{8,12},{12,8},{16,20},{20,16},{24,28},{28,24},{1,5},{5... | collective-permute-start | bytes 4718600 | tf_op jit(solution)/shard_map/ppermute | solution.py:456
  84.3 37.8 %collective-permute-start.9 = (f32[384,512]{1,0:T(8,128)}, f32[384,512]{1,0:T(8,128)}, u32[]{:S(2)}, u32[]{:S(2)}) collective-permute-start(f32[384,512]{1,0:T(8,128)} %get-tuple-element.221), channel_id=1, source_target_pairs={{0,16},{4,20},{8,24},{12,28},{16,0},{20,4},{24,8},{28,12},{1,17},{... | collective-permute-start | bytes 2359304 | tf_op jit(solution)/shard_map/ppermute | solution.py:745
  122.2 3.7 collective-permute-start.12
  122.3 42.5 %collective-permute-start.13 = (f32[384,512]{1,0:T(8,128)}, f32[384,512]{1,0:T(8,128)}, u32[]{:S(2)}, u32[]{:S(2)}) collective-permute-start(f32[384,512]{1,0:T(8,128)} %collective-permute-done.9), channel_id=1, source_target_pairs={{0,2},{1,3},{2,0},{3,1},{4,6},{5,7},{6,4},{7,5},{8,10},{9,11},{10,... | collective-permute-start | bytes 2359304 | tf_op jit(solution)/shard_map/ppermute | solution.py:452
  122.8 42.0 %collective-permute-start.15 = (f32[384,512]{1,0:T(8,128)}, f32[384,512]{1,0:T(8,128)S(1)}, u32[]{:S(2)}, u32[]{:S(2)}) collective-permute-start(f32[384,512]{1,0:T(8,128)} %get-tuple-element.193), channel_id=1, source_target_pairs={{0,4},{4,0},{8,12},{12,8},{16,20},{20,16},{24,28},{28,24},{1,5},{5... | collective-permute-start | bytes 2359304 | tf_op jit(solution)/shard_map/ppermute | solution.py:456
  133.3 31.6 %collective-permute-start.14 = (f32[384,512]{1,0:T(8,128)}, f32[384,512]{1,0:T(8,128)S(1)}, u32[]{:S(2)}, u32[]{:S(2)}) collective-permute-start(f32[384,512]{1,0:T(8,128)} %get-tuple-element.220), channel_id=1, source_target_pairs={{0,8},{4,12},{8,16},{12,20},{16,24},{20,28},{24,0},{28,4},{1,9},{5... | collective-permute-start | bytes 2359304 | tf_op jit(solution)/shard_map/ppermute | solution.py:745
  167.0 8.7 %collective-permute-start.20 = (f32[1,2,384,512]{3,2,1,0:T(8,128)S(1)}, f32[1,2,384,512]{3,2,1,0:T(8,128)S(1)}, u32[]{:S(2)}, u32[]{:S(2)}) collective-permute-start(f32[1,2,384,512]{3,2,1,0:T(8,128)S(1)} %maximum_bitcast_fusion.1.here_ref), channel_id=1, source_target_pairs={{0,1},{1,0},{2,3},{3,2},{4,5},{5,4},{6,7},{7,6},{8,9},{9,8},{10,11... | collective-permute-start | bytes 4718600 | tf_op jit(solution)/shard_map/ppermute | solution.py:448
  169.0 39.7 %collective-permute-start.17 = (f32[384,1024]{1,0:T(8,128)S(1)}, f32[384,1024]{1,0:T(8,128)S(1)}, u32[]{:S(2)}, u32[]{:S(2)}) collective-permute-start(f32[384,1024]{1,0:T(8,128)S(1)} %add.158.p0), channel_id=1, source_target_pairs={{0,2},{1,3},{2,0},{3,1},{4,6},{5,7},{6,4},{7,5},{8,10},{9,11},{10,... | collective-permute-start | bytes 4718600 | tf_op jit(solution)/shard_map/ppermute | solution.py:452
  170.5 38.2 %collective-permute-start.18 = (f32[384,1024]{1,0:T(8,128)S(1)}, f32[384,1024]{1,0:T(8,128)S(1)}, u32[]{:S(2)}, u32[]{:S(2)}) collective-permute-start(f32[384,1024]{1,0:T(8,128)S(1)} %add.158.p0), channel_id=1, source_target_pairs={{0,1},{1,0},{2,3},{3,2},{4,5},{5,4},{6,7},{7,6},{8,9},{9,8},{10,11... | collective-permute-start | bytes 4718600 | tf_op jit(solution)/shard_map/ppermute | solution.py:448
  170.5 38.2 %collective-permute-start.19 = (f32[384,512]{1,0:T(8,128)}, f32[384,512]{1,0:T(8,128)}, u32[]{:S(2)}, u32[]{:S(2)}) collective-permute-start(f32[384,512]{1,0:T(8,128)} %get-tuple-element.220), channel_id=1, source_target_pairs={{0,16},{4,20},{8,24},{12,28},{16,0},{20,4},{24,8},{28,12},{1,17},{... | collective-permute-start | bytes 2359304 | tf_op jit(solution)/shard_map/ppermute | solution.py:745
  208.9 34.2 %collective-permute-start.23 = (f32[384,512]{1,0:T(8,128)}, f32[384,512]{1,0:T(8,128)}, u32[]{:S(2)}, u32[]{:S(2)}) collective-permute-start(f32[384,512]{1,0:T(8,128)} %get-tuple-element.220), channel_id=1, source_target_pairs={{0,24},{4,28},{8,0},{12,4},{16,8},{20,12},{24,16},{28,20},{1,25},{... | collective-permute-start | bytes 2359304 | tf_op jit(solution)/shard_map/ppermute | solution.py:745
  225.7 20.4 %collective-permute-start.24 = (f32[384,512]{1,0:T(8,128)}, f32[384,512]{1,0:T(8,128)}, u32[]{:S(2)}, u32[]{:S(2)}) collective-permute-start(f32[384,512]{1,0:T(8,128)} %get-tuple-element.221), channel_id=1, source_target_pairs={{0,24},{4,28},{8,0},{12,4},{16,8},{20,12},{24,16},{28,20},{1,25},{... | collective-permute-start | bytes 2359304 | tf_op jit(solution)/shard_map/ppermute | solution.py:745
  229.1 11.7 %collective-permute-start.22 = (f32[6,136,128]{2,1,0:T(8,128)}, f32[6,136,128]{2,1,0:T(8,128)}, u32[]{:S(2)}, u32[]{:S(2)}) collective-permute-start(f32[6,136,128]{2,1,0:T(8,128)} %slice_select_fusion), channel_id=1, source_target_pairs={{0,4},{4,0},{8,12},{12,8},{16,20},{20,16},{24,28},{28,24},{1,5},{5... | collective-permute-start | bytes 1253384 | tf_op jit(solution)/shard_map/ppermute | solution.py:423
  249.1 240.9 %all-reduce.3.cloned.1.call-start = ((), (), s32[]{:S(2)}) async-start(), calls=%async_computation.1 | async-start | bytes 12582912 | tf_op jit(solution)/shard_map/psum | solution.py:827
  251.2 13.2 %collective-permute-start.25 = (f32[6,136,128]{2,1,0:T(8,128)S(1)}, f32[6,136,128]{2,1,0:T(8,128)S(1)}, u32[]{:S(2)}, u32[]{:S(2)}) collective-permute-start(f32[6,136,128]{2,1,0:T(8,128)S(1)} %pad_maximum_fusion.9), channel_id=1, source_target_pairs={{8,0},{12,4},{16,8},{20,12},{24,16},{28,20},{9,1},{13,5},{17,9},{2... | collective-permute-start | bytes 1253384 | tf_op jit(solution)/shard_map/ppermute | solution.py:429
  253.1 33.7 %collective-permute-start.27 = (f32[384,512]{1,0:T(8,128)S(1)}, f32[384,512]{1,0:T(8,128)S(1)}, u32[]{:S(2)}, u32[]{:S(2)}) collective-permute-start(f32[384,512]{1,0:T(8,128)S(1)} %copy-done.7), channel_id=1, source_target_pairs={{0,4},{4,0},{8,12},{12,8},{16,20},{20,16},{24,28},{28,24},{1,5},{5... | collective-permute-start | bytes 2359304 | tf_op jit(solution)/shard_map/ppermute | solution.py:456
  253.7 33.1 %collective-permute-start.29 = (f32[384,512]{1,0:T(8,128)}, f32[384,512]{1,0:T(8,128)S(1)}, u32[]{:S(2)}, u32[]{:S(2)}) collective-permute-start(f32[384,512]{1,0:T(8,128)} %collective-permute-done.24), channel_id=1, source_target_pairs={{0,2},{1,3},{2,0},{3,1},{4,6},{5,7},{6,4},{7,5},{8,10},{9,11},{10,... | collective-permute-start | bytes 2359304 | tf_op jit(solution)/shard_map/ppermute | solution.py:452
  264.6 22.1 %collective-permute-start.26 = (f32[6,136,128]{2,1,0:T(8,128)S(1)}, f32[6,136,128]{2,1,0:T(8,128)S(1)}, u32[]{:S(2)}, u32[]{:S(2)}) collective-permute-start(f32[6,136,128]{2,1,0:T(8,128)S(1)} %pad_maximum_fusion.10), channel_id=1, source_target_pairs={{16,0},{20,4},{24,8},{28,12},{17,1},{21,5},{25,9},{29,13},{18,2},{... | collective-permute-start | bytes 1253384 | tf_op jit(solution)/shard_map/ppermute | solution.py:430
  265.9 20.9 %collective-permute-start.28 = (f32[384,256]{1,0:T(8,128)S(1)}, f32[384,256]{1,0:T(8,128)S(1)}, u32[]{:S(2)}, u32[]{:S(2)}) collective-permute-start(f32[384,256]{1,0:T(8,128)S(1)} %copy-done.37), channel_id=1, source_target_pairs={{0,4},{4,0},{8,12},{12,8},{16,20},{20,16},{24,28},{28,24},{1,5},{5... | collective-permute-start | bytes 1179656 | tf_op jit(solution)/shard_map/ppermute | solution.py:456
  288.1 15.8 %collective-permute-start.32 = (f32[1,2,384,512]{3,2,1,0:T(8,128)S(1)}, f32[1,2,384,512]{3,2,1,0:T(8,128)S(1)}, u32[]{:S(2)}, u32[]{:S(2)}) collective-permute-start(f32[1,2,384,512]{3,2,1,0:T(8,128)S(1)} %maximum_bitcast_fusion.2.here_ref), channel_id=1, source_target_pairs={{0,1},{1,0},{2,3},{3,2},{4,5},{5,4},{6,7},{7,6},{8,9},{9,8},{10,11... | collective-permute-start | bytes 4718600 | tf_op jit(solution)/shard_map/ppermute | solution.py:448
  288.3 11.6 %collective-permute-start.30 = (f32[6,128,128]{2,1,0:T(8,128)S(1)}, f32[6,128,128]{2,1,0:T(8,128)S(1)}, u32[]{:S(2)}, u32[]{:S(2)}) collective-permute-start(f32[6,128,128]{2,1,0:T(8,128)S(1)} %fusion.8), channel_id=1, source_target_pairs={{0,4},{4,0},{8,12},{12,8},{16,20},{20,16},{24,28},{28,24},{1,5},{5... | collective-permute-start | bytes 1179656 | tf_op jit(solution)/shard_map/ppermute | solution.py:438
  288.9 20.1 %collective-permute-start.31 = (f32[384,256]{1,0:T(8,128)S(1)}, f32[384,256]{1,0:T(8,128)S(1)}, u32[]{:S(2)}, u32[]{:S(2)}) collective-permute-start(f32[384,256]{1,0:T(8,128)S(1)} %collective-permute-done.28), channel_id=1, source_target_pairs={{0,2},{1,3},{2,0},{3,1},{4,6},{5,7},{6,4},{7,5},{8,10},{9,11},{10,... | collective-permute-start | bytes 1179656 | tf_op jit(solution)/shard_map/ppermute | solution.py:452
  309.1 3.9 collective-permute-start.35
  309.2 26.9 %collective-permute-start.34 = (f32[1,2,256,512]{3,2,1,0:T(8,128)}, f32[1,2,256,512]{3,2,1,0:T(8,128)}, u32[]{:S(2)}, u32[]{:S(2)}) collective-permute-start(f32[1,2,256,512]{3,2,1,0:T(8,128)} %get-tuple-element.250), channel_id=1, source_target_pairs={{0,8},{4,12},{8,0},{12,4},{16,24},{20,28},{24,16},{28,20},{1,9},{5... | collective-permute-start | bytes 3145736 | tf_op jit(solution)/shard_map/ppermute | solution.py:751
  311.7 48.9 %collective-permute-start.33 = (f32[2,384,512]{2,1,0:T(8,128)}, f32[2,384,512]{2,1,0:T(8,128)}, u32[]{:S(2)}, u32[]{:S(2)}) collective-permute-start(f32[2,384,512]{2,1,0:T(8,128)} %get-tuple-element.248), channel_id=1, source_target_pairs={{0,4},{4,0},{8,12},{12,8},{16,20},{20,16},{24,28},{28,24},{1,5},{5... | collective-permute-start | bytes 4718600 | tf_op jit(solution)/shard_map/ppermute | solution.py:456
  319.1 39.2 %collective-permute-start.36 = (f32[1,2,256,512]{3,2,1,0:T(8,128)}, f32[1,2,256,512]{3,2,1,0:T(8,128)}, u32[]{:S(2)}, u32[]{:S(2)}) collective-permute-start(f32[1,2,256,512]{3,2,1,0:T(8,128)} %get-tuple-element.256), channel_id=1, source_target_pairs={{0,8},{4,12},{8,0},{12,4},{16,24},{20,28},{24,16},{28,20},{1,9},{5... | collective-permute-start | bytes 3145736 | tf_op jit(solution)/shard_map/ppermute | solution.py:751
  366.1 71.2 %collective-permute-start.37 = (f32[2,2,256,512]{3,2,1,0:T(8,128)}, f32[2,2,256,512]{3,2,1,0:T(8,128)}, u32[]{:S(2)}, u32[]{:S(2)}) collective-permute-start(f32[2,2,256,512]{3,2,1,0:T(8,128)} %get-tuple-element.272), channel_id=1, source_target_pairs={{0,8},{4,12},{8,0},{12,4},{16,24},{20,28},{24,16},{28,20},{1,9},{5... | collective-permute-start | bytes 6291464 | tf_op jit(solution)/shard_map/ppermute | solution.py:751
  368.9 66.5 %collective-permute-start.38 = (f32[2,256,512]{2,1,0:T(8,128)}, f32[2,256,512]{2,1,0:T(8,128)}, u32[]{:S(2)}, u32[]{:S(2)}) collective-permute-start(f32[2,256,512]{2,1,0:T(8,128)} %pad_maximum_fusion.4), channel_id=1, source_target_pairs={{0,16},{4,20},{8,24},{12,28},{16,0},{20,4},{24,8},{28,12},{1,17},{... | collective-permute-start | bytes 3145736 | tf_op jit(solution)/shard_map/ppermute | solution.py:756
  371.2 31.3 %collective-permute-start.39 = (f32[384,512]{1,0:T(8,128)}, f32[384,512]{1,0:T(8,128)}, u32[]{:S(2)}, u32[]{:S(2)}) collective-permute-start(f32[384,512]{1,0:T(8,128)} %get-tuple-element.283.d0.refs_0_), channel_id=1, source_target_pairs={{0,4},{4,0},{8,12},{12,8},{16,20},{20,16},{24,28},{28,24},{1,5},{5... | collective-permute-start | bytes 2359304 | tf_op jit(solution)/shard_map/ppermute | solution.py:456
  402.5 38.4 %collective-permute-start.40 = (f32[3,256,512]{2,1,0:T(8,128)}, f32[3,256,512]{2,1,0:T(8,128)}, u32[]{:S(2)}, u32[]{:S(2)}) collective-permute-start(f32[3,256,512]{2,1,0:T(8,128)} %get-tuple-element.284), channel_id=1, source_target_pairs={{0,4},{4,0},{8,12},{12,8},{16,20},{20,16},{24,28},{28,24},{1,5},{5... | collective-permute-start | bytes 4718600 | tf_op jit(solution)/shard_map/ppermute | solution.py:456
  440.9 60.5 %collective-permute-start.41 = (f32[3,256,512]{2,1,0:T(8,128)}, f32[3,256,512]{2,1,0:T(8,128)}, u32[]{:S(2)}, u32[]{:S(2)}) collective-permute-start(f32[3,256,512]{2,1,0:T(8,128)} %get-tuple-element.290), channel_id=1, source_target_pairs={{0,4},{4,0},{8,12},{12,8},{16,20},{20,16},{24,28},{28,24},{1,5},{5... | collective-permute-start | bytes 4718600 | tf_op jit(solution)/shard_map/ppermute | solution.py:456
  442.0 55.8 %collective-permute-start.42 = (f32[1,2,256,512]{3,2,1,0:T(8,128)}, f32[1,2,256,512]{3,2,1,0:T(8,128)}, u32[]{:S(2)}, u32[]{:S(2)}) collective-permute-start(f32[1,2,256,512]{3,2,1,0:T(8,128)} %get-tuple-element.292), channel_id=1, source_target_pairs={{0,8},{4,12},{8,0},{12,4},{16,24},{20,28},{24,16},{28,20},{1,9},{5... | collective-permute-start | bytes 3145736 | tf_op jit(solution)/shard_map/ppermute | solution.py:751
  445.2 54.2 %collective-permute-start.43 = (f32[2,256,512]{2,1,0:T(8,128)}, f32[2,256,512]{2,1,0:T(8,128)}, u32[]{:S(2)}, u32[]{:S(2)}) collective-permute-start(f32[2,256,512]{2,1,0:T(8,128)} %get-tuple-element.295), channel_id=1, source_target_pairs={{0,16},{4,20},{8,24},{12,28},{16,0},{20,4},{24,8},{28,12},{1,17},{... | collective-permute-start | bytes 3145736 | tf_op jit(solution)/shard_map/ppermute | solution.py:756
  501.4 6.1 %collective-permute-start.44 = (f32[5120]{0:T(1024)S(1)}, f32[5120]{0:T(1024)S(1)}, u32[]{:S(2)}, u32[]{:S(2)}) collective-permute-start(f32[5120]{0:T(1024)S(1)} %pad_maximum_fusion.11), channel_id=1, source_target_pairs={{0,4},{4,0},{8,12},{12,8},{16,20},{20,16},{24,28},{28,24},{1,5},{5... | collective-permute-start | bytes 61448 | tf_op jit(solution)/shard_map/ppermute | solution.py:853
  504.5 27.4 %collective-permute-start.47 = (f32[1,256,512]{2,1,0:T(8,128)S(1)}, f32[1,256,512]{2,1,0:T(8,128)S(1)}, u32[]{:S(2)}, u32[]{:S(2)}) collective-permute-start(f32[1,256,512]{2,1,0:T(8,128)S(1)} %get-tuple-element.305), channel_id=1, source_target_pairs={{0,16},{4,20},{8,24},{12,28},{16,0},{20,4},{24,8},{28,12},{1,17},{... | collective-permute-start | bytes 1572872 | tf_op jit(solution)/shard_map/ppermute | solution.py:756
  506.9 26.9 %collective-permute-start.48 = (f32[3,256,384]{2,1,0:T(8,128)S(1)}, f32[3,256,384]{2,1,0:T(8,128)S(1)}, u32[]{:S(2)}, u32[]{:S(2)}) collective-permute-start(f32[3,256,384]{2,1,0:T(8,128)S(1)} %copy-done.62), channel_id=1, source_target_pairs={{0,4},{4,0},{8,12},{12,8},{16,20},{20,16},{24,28},{28,24},{1,5},{5... | collective-permute-start | bytes 3538952 | tf_op jit(solution)/shard_map/ppermute | solution.py:456
  507.5 10.6 %collective-permute-start.45 = (f32[5120]{0:T(1024)S(1)}, f32[5120]{0:T(1024)S(1)}, u32[]{:S(2)}, u32[]{:S(2)}) collective-permute-start(f32[5120]{0:T(1024)S(1)} %add.176), channel_id=1, source_target_pairs={{0,8},{4,12},{8,0},{12,4},{16,24},{20,28},{24,16},{28,20},{1,9},{5... | collective-permute-start | bytes 61448 | tf_op jit(solution)/shard_map/ppermute | solution.py:853
  518.1 12.6 %collective-permute-start.46 = (f32[5120]{0:T(1024)S(1)}, f32[5120]{0:T(1024)S(1)}, u32[]{:S(2)}, u32[]{:S(2)}) collective-permute-start(f32[5120]{0:T(1024)S(1)} %add.177), channel_id=1, source_target_pairs={{0,16},{4,20},{8,24},{12,28},{16,0},{20,4},{24,8},{28,12},{1,17},{... | collective-permute-start | bytes 61448 | tf_op jit(solution)/shard_map/ppermute | solution.py:853
  (66 other events, 587.9 us)
Sparse Core Ops, SparseCore 0:
  249.2 84.3 all-gather.2
  372.5 117.4 all-reduce.2

commit v4 on v3

--- a/solution.py
+++ b/solution.py
@@ -791,7 +791,8 @@
     xnl2 = shift(xn_quarter, 2)
     dy_all = assemble([(dy2, dy2_over)], dy_all, 2)
     xn1_turned = do.turn(seq_at, xn1, xn1_got)
-    dhalf, dover, dhalf_other, xnl2, xn_quarter, xnl1, dy_all, xn1_turned = tie(dhalf, dover, dhalf_other, xnl2, xn_quarter, xnl1, dy_all, xn1_turned)
+    dhalf, dover, dhalf_other, xnl2, xn_quarter, xnl1, dy_all, xn1_turned, ffn = tie(dhalf, dover, dhalf_other, xnl2, xn_quarter, xnl1, dy_all, xn1_turned, ffn)
+    ffn = lax.psum(ffn, "head")
 
     xnl3 = shift(xn_quarter, 3)
     dpre_gate, dmixed, part_gain, back, dhidden, dbranch, dbranch_away, part_norm_second = do.norm_back(
@@ -810,25 +811,29 @@
     dy3_over = y_swap(dy3)
     early, into, gate_got, dpre_query, dbranch_own, dy3_over = tie(early, into, gate_got, dpre_query, dbranch_own, dy3_over)
 
+    gate = do.mix_grad(xn1_turned, dpre_gate, gate_got)
+    early, into, gate, dbranch_own, dy3_over, ffn = tie(early, into, gate, dbranch_own, dy3_over, ffn)
+
+    near_gate = sum_near(*gate)
     dbranch_over = y_swap(dbranch_own)
-    gate = do.mix_grad(xn1_turned, dpre_gate, gate_got)
     carried = enter_states(early, into, do.state_shape, True)
     dy_all = assemble([(dy3, dy3_over)], dy_all, 3)
-    carried, gate = tie(carried, gate)
     dpre_fv, part_bound = do.state_back(seq_at, lengths, carried, states, ke, proj, cum, bound, dkeys, dvalues, dlogf)
-    dpre_fv, dpre_query, gate, dbranch_over, dy_all = tie(dpre_fv, dpre_query, gate, dbranch_over, dy_all)
+    dpre_fv, dpre_query, dbranch_over, dy_all = tie(dpre_fv, dpre_query, dbranch_over, dy_all)
 
     fv_got = x_swap(dpre_fv)
-    near_gate = sum_near(*gate)
-    dxn1 = do.first_grad((dpre_query, dpre_fv[0], dpre_fv[1], dpre_gate), mix_weight)
     down = do.mix_grad(do.turn(seq_at, dbranch, assemble([(dbranch_own, dbranch_over)])), gated, gated_got)
     near_down = sum_near(*down)
-    fv_got, near_gate, near_down, xn_all, dpre_query, xn_parts, dxn1, ffn = tie(fv_got, near_gate, near_down, xn_all, dpre_query, xn_parts, dxn1, ffn)
-    dxn1, ffn = lax.psum((dxn1, ffn), "head")
+    near_gate, down = tie(near_gate, down)
+    grad_gate = sum_far(near_gate)
+    dxn1 = do.first_grad((dpre_query, dpre_fv[0], dpre_fv[1], dpre_gate), mix_weight)
+    xn_parts, dxn1, ffn = tie(xn_parts, dxn1, ffn)
+    fv_got, grad_gate, near_down, xn_all, dpre_query, xn_parts = tie(fv_got, grad_gate, near_down, xn_all, dpre_query, xn_parts)
+    dxn1 = lax.psum(dxn1, "head")
 
     rows = jnp.stack([seq, seq ^ 1]).astype(jnp.int32)
     query_got = x_swap(dpre_query)
-    grad_early = sum_far(tuple(jax.tree.map(lambda a, b: jnp.concatenate([a, b]), near_gate, near_down)))
+    grad_w_out = sum_far(near_down)
     forget_values = do.mix_grad(xn1_turned, dpre_fv[0], fv_got[0], dpre_fv[1], fv_got[1])
     forget_values, xn_all, xn_parts = tie(forget_values, xn_all, xn_parts)
     near_fv = sum_near(*forget_values)
@@ -838,25 +843,26 @@
     got_a = x_swap(away_a)
     query = do.mix_grad(xn1_turned, dpre_query, query_got)
     mine_b, away_b = do.ffn_grad(rows, xn_all, dy_all, ffn_in, ffn_out, 2, 2)
-    near_fv, grad_early, got_a, query, away_b, xn_all = tie(near_fv, grad_early, got_a, query, away_b, xn_all)
+    near_fv, grad_w_out, got_a, query, away_b, xn_all, dhidden, hidden = tie(near_fv, grad_w_out, got_a, query, away_b, xn_all, dhidden, hidden)
 
     got_b = x_swap(away_b)
     near_query, grad_fv = sum_near(*query), sum_far(near_fv)
     grad_tokens, part_norm_first = do.first_back(dxn1, dhidden, tokens, norm_first)
     mine_c, away_c = do.ffn_grad(rows, xn_all, dy_all, ffn_in, ffn_out, 4, do.steps - 4)
     small = jnp.concatenate([part_norm_first[0], part_norm_second[0], part_bound[0], part_gain[0]])
-    got_b, near_query, grad_fv, small, away_c = tie(got_b, near_query, grad_fv, small, away_c)
+    small = small + lax.ppermute(small, "seq", flip(1))
+    output = (hidden + ffn).astype(BF16)
+    got_b, near_query, grad_fv, small, away_c, output = tie(got_b, near_query, grad_fv, small, away_c, output)
 
     got_c = x_swap(away_c)
     grad_query = sum_far(near_query)
-    for bit in (1, 2, 4):
+    for bit in (2, 4):
         small = small + lax.ppermute(small, "seq", flip(bit))
-    output = (hidden + ffn).astype(BF16)
     parts = ((mine_a, got_a), (mine_b, got_b), (mine_c, got_c))
     grad_in = jnp.concatenate([mine[:2] + got[:2] for mine, got in parts], axis=2)
     grad_out = jnp.concatenate([(mine[2] + got[2]).T for mine, got in parts], axis=0)
-    grad_mix = jnp.concatenate([grad_query, grad_fv, grad_early[:1]])
-    return output, grad_tokens, small, (grad_mix, grad_early[1].T, grad_in, grad_out)
+    grad_mix = jnp.concatenate([grad_query, grad_fv, grad_gate])
+    return output, grad_tokens, small, (grad_mix, grad_w_out[0].T, grad_in, grad_out)
 
 
 def weight_grads_whole(xn1, dproj, gated, dbranch, xn2, dy, ffn_in, ffn_out):

time: 556 us -> 563 us (1.013)
    ppermute x3 -> x4, waiting for transfers between devices: 6.34 us -> 45.1 us  [sum_far(): return a + b + lax.ppermute(far, 'seq', flip(4))]
    ppermute x4, waiting for transfers between devices: 24.6 us -> 4.99 us  [sum_near(): got = lax.ppermute(send, 'seq', flip(2))]
    psum x1 -> x2, waiting for transfers between devices: 18.1 us -> 0.01 us  [the longest x1 0.01 us: run_lines(): ffn = lax.psum(ffn, 'head')]
    unnamed x137 -> x155, local copies, waits for them, and re-layouts: 15.6 us -> 21.9 us
    ppermute x3 -> x2, waiting for transfers between devices: 16.6 us -> 17.2 us  [run_lines(): small = small + lax.ppermute(small, 'seq', flip(bit))]
  transfers between devices with their start and end apart: 51 -> 53, of which waited for: 23 -> 23; matrix products, arithmetic and copies ran while one was open for 8% -> 8% of each run, Pallas kernels for 30% -> 29%
where the time goes in v4:
time: 563 us; the launch traced here: 555 us
  waiting for transfers between devices  213 us (38%)
  Pallas kernels  171 us (30%)
  starting transfers between devices  77.9 us (14%)
  other arithmetic  51 us (9%)
  local copies, waits for them, and re-layouts  27.2 us (5%)
  between operations  15.2 us (3%)
    ppermute x6, waiting for transfers between devices, shift(): return lax.ppermute(a, 'seq', z_shift(k))  65.2 us
    pallas_call x3, Pallas kernels, ffn_grad(): call(functools.partial(ffn_grad_kernel, tail), 'ffn_grad', [out, out], [S...  62.1 us
    ppermute x4, waiting for transfers between devices, sum_far(): return a + b + lax.ppermute(far, 'seq', flip(4))  45.1 us
    ppermute x6, starting transfers between devices, shift(): return lax.ppermute(a, 'seq', z_shift(k))  23.6 us
    pallas_call x1, Pallas kernels, ffn_own(): call(ffn_own_kernel, 'ffn_own', [self.wide, self.half, self.half], [SMEM,...  22.9 us
    unnamed x155, local copies, waits for them, and re-layouts  21.9 us
    ppermute x2, waiting for transfers between devices, pair_states(): lax.ppermute(jnp.where(is_low, packed[half:], packed[:half]), 'seq', X_SWAP)  20.4 us
    ppermute x2, waiting for transfers between devices, pass_states(): further = lax.ppermute(join(before, pair), 'seq', z_line(2 * step))  18.6 us
  transfers between devices with their start and end apart: 53, of which 23 were waited for; matrix products, arithmetic and copies ran while one was open for 8% of the time, Pallas kernels for 29%

profile of v4, /device:TPU:0, one launch (start us, length us, event | category | flops | bytes accessed | tf_op | source)
XLA Modules:
  0.0 555.4 jit_solution(13300483022196674731)
XLA Ops:
  10.2 3.0 collective-permute-start.1
  13.2 11.8 %project.1 = (bf16[384,2048]{1,0:T(8,128)(2,1)S(1)}, f32[384,1024]{1,0:T(8,128)}, f32[4,384,512]{2,1,0:T(8,128)}, f32[384,512]{1,0:T(8,128)S(1)}, bf16[384,512]{...) custom-call(s32[1]{0:T(128)} %bitcast.4.pos.place, ...), custom_call_target="tpu_custom_call" | custom-call | flops 3221225472 | bytes 20000000 | tf_op jit(solution)/shard_map/project/pallas_call | solution.py:515
  26.6 9.6 %collective-permute-done = f32[6,136,128]{2,1,0:T(8,128)S(1)} collective-permute-done((f32[6,136,128]{2,1,0:T(8,128)S(1)}, f32[6,136,128]{2,1,0:T(8,128)S(1)}, u32[]{:S(2)}, u32[]{:S(2)}) %collective-permute-start) | collective-permute-done | bytes 417824 | tf_op jit(solution)/shard_map/ppermute | solution.py:423
  36.5 3.5 collective-permute-start.2
  41.6 6.1 %collective-permute-done.2 = f32[6,136,128]{2,1,0:T(8,128)S(1)} collective-permute-done((f32[6,136,128]{2,1,0:T(8,128)S(1)}, f32[6,136,128]{2,1,0:T(8,128)S(1)}, u32[]{:S(2)}, u32[]{:S(2)}) %collective-permute-start.2) | collective-permute-done | bytes 417824 | tf_op jit(solution)/shard_map/ppermute | solution.py:429
  47.8 5.4 collective-permute-start.3
  53.2 6.9 %collective-permute-done.3 = f32[6,136,128]{2,1,0:T(8,128)S(1)} collective-permute-done((f32[6,136,128]{2,1,0:T(8,128)S(1)}, f32[6,136,128]{2,1,0:T(8,128)S(1)}, u32[]{:S(2)}, u32[]{:S(2)}) %collective-permute-start.3) | collective-permute-done | bytes 417824 | tf_op jit(solution)/shard_map/ppermute | solution.py:430
  61.8 6.6 %collective-permute-done.5 = f32[6,128,128]{2,1,0:T(8,128)} collective-permute-done((f32[6,128,128]{2,1,0:T(8,128)S(1)}, f32[6,128,128]{2,1,0:T(8,128)}, u32[]{:S(2)}, u32[]{:S(2)}) %collective-permute-start.5) | collective-permute-done | bytes 393248 | tf_op jit(solution)/shard_map/ppermute | solution.py:438
  69.6 4.6 mixer_out.1
  74.2 3.6 collective-permute-done.6
  84.3 3.4 collective-permute-start.9
  87.8 2.8 assemble.4.refs_0_
  90.6 31.5 %collective-permute-done.9 = f32[384,512]{1,0:T(8,128)} collective-permute-done((f32[384,512]{1,0:T(8,128)}, f32[384,512]{1,0:T(8,128)}, u32[]{:S(2)}, u32[]{:S(2)}) %collective-permute-start.9) | collective-permute-done | bytes 786464 | tf_op jit(solution)/shard_map/ppermute | solution.py:745
  127.0 6.4 %second_norm.1 = (f32[384,2048]{1,0:T(8,128)}, bf16[1536,2048]{1,0:T(8,128)(2,1)}, f32[384,512]{1,0:T(8,128)}) custom-call(s32[3]{0:T(128)S(1)} %pad_add_fusion.place, bf16[384,2048]{1,0:T(8,128)(2,1)S(1)} %bitcast.132, f32[384,1024]{1,0:T(8,128)} %add.163.p0, f32[384,1024]{1,0:T(8,128)} %collective-permute-done.8.p1, ...), custom_call_target="tpu_custom_call" | custom-call | bytes 10000000 | tf_op jit(solution)/shard_map/second_norm/pallas_call | solution.py:577
  133.4 8.6 %collective-permute-start.14 = (f32[384,512]{1,0:T(8,128)}, f32[384,512]{1,0:T(8,128)S(1)}, u32[]{:S(2)}, u32[]{:S(2)}) collective-permute-start(f32[384,512]{1,0:T(8,128)} %get-tuple-element.230), channel_id=1, source_target_pairs={{0,8},{4,12},{8,16},{12,20},{16,24},{20,28},{24,0},{28,4},{1,9},{5... | collective-permute-start | bytes 2359304 | tf_op jit(solution)/shard_map/ppermute | solution.py:745
  142.0 22.9 %ffn_own.1 = (f32[384,2048]{1,0:T(8,128)}, f32[384,1024]{1,0:T(8,128)}, f32[384,1024]{1,0:T(8,128)}) custom-call(s32[1]{0:T(128)} %bitcast.core, bf16[1536,2048]{1,0:T(8,128)(2,1)} %get-tuple-element.288.xn_ref._, bf16[384,2048]{1,0:T(8,128)(2,1)} %bitcast.128, bf16[2,2048,1408]{2,1,0:T(8,128)(2,1)} %refs_2_.1, bf16[1408,2048]{1,0:T(8,128)(2,1)} %refs_3_.1, ...), custom_call_target="tpu_custom_call" | custom-call | flops 13287555072 | bytes 30000000 | tf_op jit(solution)/shard_map/ffn_own/pallas_call | solution.py:549
  170.6 3.4 collective-permute-start.19
  177.7 31.0 %collective-permute-done.19 = f32[384,512]{1,0:T(8,128)S(1)} collective-permute-done((f32[384,512]{1,0:T(8,128)}, f32[384,512]{1,0:T(8,128)S(1)}, u32[]{:S(2)}, u32[]{:S(2)}) %collective-permute-start.19) | collective-permute-done | bytes 786464 | tf_op jit(solution)/shard_map/ppermute | solution.py:745
  210.9 2.6 collective-permute-start.23
  216.9 10.4 %norm_back.1 = (f32[384,512]{1,0:T(8,128)S(1)}, bf16[384,512]{1,0:T(8,128)(2,1)S(1)}, f32[1,512]{1,0:T(1,128)S(1)}, f32[3,4,136,128]{3,2,1,0:T(8,128)S(1)}, f32[...) custom-call(s32[3]{0:T(128)S(1)} %pad_add_fusion.place, ...), custom_call_target="tpu_custom_call" | custom-call | flops 805306368 | bytes 10000000 | tf_op jit(solution)/shard_map/norm_back/pallas_call | solution.py:564
  229.2 2.6 collective-permute-start.24
  233.6 10.8 %collective-permute-done.22 = f32[6,136,128]{2,1,0:T(8,128)} collective-permute-done((f32[6,136,128]{2,1,0:T(8,128)}, f32[6,136,128]{2,1,0:T(8,128)}, u32[]{:S(2)}, u32[]{:S(2)}) %collective-permute-start.22) | collective-permute-done | bytes 417824 | tf_op jit(solution)/shard_map/ppermute | solution.py:423
  246.6 2.6 collective-permute-done.24
  249.3 2.8 pad_maximum_fusion.1
  258.8 8.3 %collective-permute-done.25 = f32[6,136,128]{2,1,0:T(8,128)S(1)} collective-permute-done((f32[6,136,128]{2,1,0:T(8,128)S(1)}, f32[6,136,128]{2,1,0:T(8,128)S(1)}, u32[]{:S(2)}, u32[]{:S(2)}) %collective-permute-start.25) | collective-permute-done | bytes 417824 | tf_op jit(solution)/shard_map/ppermute | solution.py:429
  269.6 6.0 %intra_back.1 = (f32[384,512]{1,0:T(8,128)}, f32[384,512]{1,0:T(8,128)S(1)}, f32[384,512]{1,0:T(8,128)S(1)}, f32[384,512]{1,0:T(8,128)S(1)}) custom-call(bf16[384,512]{1,0:T(8,128)(2,1)S(1)} %copy-done.33, bf16[384,512]{1,0:T(8,128)(2,1)S(1)} %get-tuple-element.170.qe_ref, bf16[384,512]{1,0:T(8,128)(2,1)S(1)} %get-tuple-element.236.ke_ref, ...), custom_call_target="tpu_custom_call" | custom-call | flops 352321536 | bytes 10000000 | tf_op jit(solution)/shard_map/intra_back/pallas_call | solution.py:612
  277.3 11.7 %collective-permute-done.26 = f32[6,136,128]{2,1,0:T(8,128)S(1)} collective-permute-done((f32[6,136,128]{2,1,0:T(8,128)S(1)}, f32[6,136,128]{2,1,0:T(8,128)S(1)}, u32[]{:S(2)}, u32[]{:S(2)}) %collective-permute-start.26) | collective-permute-done | bytes 417824 | tf_op jit(solution)/shard_map/ppermute | solution.py:430
  289.1 4.9 collective-permute-done.29
  302.1 2.5 collective-permute-start.34
  304.6 6.8 %collective-permute-done.30 = f32[6,128,128]{2,1,0:T(8,128)S(1)} collective-permute-done((f32[6,128,128]{2,1,0:T(8,128)S(1)}, f32[6,128,128]{2,1,0:T(8,128)S(1)}, u32[]{:S(2)}, u32[]{:S(2)}) %collective-permute-start.30) | collective-permute-done | bytes 393248 | tf_op jit(solution)/shard_map/ppermute | solution.py:438
  311.6 3.9 state_back.1
  333.0 8.0 %first_grad.1 = f32[384,2048]{1,0:T(8,128)} custom-call(f32[384,512]{1,0:T(8,128)} %get-tuple-element.291.d0.refs_0_, f32[384,512]{1,0:T(8,128)S(1)} %get-tuple-element.345.d1.refs_0_, f32[384,512]{1,0:T(8,128)S(1)} %get-tuple-element.344.d2.refs_2_, f32[384,512]{1,0:T(8,128)S(1)} %copy-done.8, bf16[4,2048,512]{2,1,0:T(8,128)(2,1)} %w_ref.7), custom_call_target="tpu_custom_call" | custom-call | flops 3221225472 | bytes 15000000 | tf_op jit(solution)/shard_map/first_grad/pallas_call | solution.py:589
  341.8 19.6 %collective-permute-done.36 = f32[1,256,512]{2,1,0:T(8,128)} collective-permute-done((f32[1,256,512]{2,1,0:T(8,128)}, f32[1,256,512]{2,1,0:T(8,128)}, u32[]{:S(2)}, u32[]{:S(2)}) %collective-permute-start.36) | collective-permute-done | bytes 524320 | tf_op jit(solution)/shard_map/ppermute | solution.py:756
  363.6 2.7 fusion.2
  367.9 3.8 mix_grad.6
  371.7 3.1 collective-permute-start.38
  376.2 6.9 %join.1.xn_ref = bf16[1536,2048]{1,0:T(8,128)(2,1)} custom-call(f32[4,1152,512]{2,1,0:T(8,128)} %bitcast.153, bf16[1536,2048]{1,0:T(8,128)(2,1)} %get-tuple-element.288.xn_ref._), custom_call_target="tpu_custom_call", output_to_operand_aliasing={{}: (1, {})} | custom-call | bytes 14155776 | tf_op jit(solution)/shard_map/join/pallas_call | solution.py:479
  383.1 20.8 %ffn_grad.3 = (f32[3,256,512]{2,1,0:T(8,128)}, f32[3,256,512]{2,1,0:T(8,128)}) custom-call(s32[2]{0:T(128)} %pad_add_fusion.3.rows, bf16[1536,2048]{1,0:T(8,128)(2,1)} %join.1.xn_ref, bf16[1536,2048]{1,0:T(8,128)(2,1)} %assemble.6.dy_ref, bf16[2,2048,1408]{2,1,0:T(8,128)(2,1)} %refs_2_.1, bf16[1408,2048]{1,0:T(8,128)(2,1)} %refs_3_.1), custom_call_target="tpu_custom_call" | custom-call | flops 12079595520 | bytes 20000000 | tf_op jit(solution)/shard_map/ffn_grad/pallas_call | solution.py:667
  406.9 24.1 %collective-permute-done.39 = f32[1,256,512]{2,1,0:T(8,128)} collective-permute-done((f32[1,256,512]{2,1,0:T(8,128)}, f32[1,256,512]{2,1,0:T(8,128)}, u32[]{:S(2)}, u32[]{:S(2)}) %collective-permute-start.39) | collective-permute-done | bytes 524320 | tf_op jit(solution)/shard_map/ppermute | solution.py:756
  433.0 2.6 mix_grad.7
  437.6 20.9 %ffn_grad.4 = (f32[3,256,512]{2,1,0:T(8,128)}, f32[3,256,512]{2,1,0:T(8,128)}) custom-call(s32[2]{0:T(128)} %pad_add_fusion.3.rows, bf16[1536,2048]{1,0:T(8,128)(2,1)} %join.1.xn_ref, bf16[1536,2048]{1,0:T(8,128)(2,1)} %assemble.6.dy_ref, bf16[2,2048,1408]{2,1,0:T(8,128)(2,1)} %refs_2_.1, bf16[1408,2048]{1,0:T(8,128)(2,1)} %refs_3_.1), custom_call_target="tpu_custom_call" | custom-call | flops 12079595520 | bytes 20000000 | tf_op jit(solution)/shard_map/ffn_grad/pallas_call | solution.py:667
  458.5 3.7 fusion
  468.5 5.5 first_back.1
  475.0 20.5 %ffn_grad.5 = (f32[3,256,384]{2,1,0:T(8,128)}, f32[3,256,384]{2,1,0:T(8,128)}) custom-call(s32[2]{0:T(128)} %pad_add_fusion.3.rows, bf16[1536,2048]{1,0:T(8,128)(2,1)} %join.1.xn_ref, bf16[1536,2048]{1,0:T(8,128)(2,1)} %assemble.6.dy_ref, bf16[2,2048,1408]{2,1,0:T(8,128)(2,1)} %refs_2_.1, bf16[1408,2048]{1,0:T(8,128)(2,1)} %refs_3_.1, ...), custom_call_target="tpu_custom_call" | custom-call | flops 9059696640 | bytes 20000000 | tf_op jit(solution)/shard_map/ffn_grad/pallas_call | solution.py:667
  495.5 4.5 add_convert_fusion
  505.6 4.0 collective-permute-done.43
  514.5 2.9 collective-permute-start.48
  521.1 17.2 %collective-permute-done.47 = f32[5120]{0:T(1024)S(1)} collective-permute-done((f32[5120]{0:T(1024)S(1)}, f32[5120]{0:T(1024)S(1)}, u32[]{:S(2)}, u32[]{:S(2)}) %collective-permute-start.47) | collective-permute-done | bytes 20512 | tf_op jit(solution)/shard_map/ppermute | solution.py:860
  (308 shorter events, 122.4 us)
Async XLA Ops:
  7.2 290.9 %all-reduce.3.cloned.1.call-start = ((), (), s32[]{:S(2)}) async-start(), calls=%async_computation | async-start | bytes 6291456 | tf_op jit(solution)/shard_map/psum | solution.py:795
  10.2 26.2 %collective-permute-start.1 = (f32[384,512]{1,0:T(8,128)}, f32[384,512]{1,0:T(8,128)}, u32[]{:S(2)}, u32[]{:S(2)}) collective-permute-start(f32[384,512]{1,0:T(8,128)} %get-tuple-element.231), channel_id=1, source_target_pairs={{0,8},{4,12},{8,16},{12,20},{16,24},{20,28},{24,0},{28,4},{1,9},{5... | collective-permute-start | bytes 2359304 | tf_op jit(solution)/shard_map/ppermute | solution.py:745
  25.1 11.2 %collective-permute-start = (f32[6,136,128]{2,1,0:T(8,128)S(1)}, f32[6,136,128]{2,1,0:T(8,128)S(1)}, u32[]{:S(2)}, u32[]{:S(2)}) collective-permute-start(f32[6,136,128]{2,1,0:T(8,128)S(1)} %slice_select_fusion.2), channel_id=1, source_target_pairs={{0,4},{4,0},{8,12},{12,8},{16,20},{20,16},{24,28},{28,24},{1,5},{5... | collective-permute-start | bytes 1253384 | tf_op jit(solution)/shard_map/ppermute | solution.py:423
  36.5 11.2 %collective-permute-start.2 = (f32[6,136,128]{2,1,0:T(8,128)S(1)}, f32[6,136,128]{2,1,0:T(8,128)S(1)}, u32[]{:S(2)}, u32[]{:S(2)}) collective-permute-start(f32[6,136,128]{2,1,0:T(8,128)S(1)} %pad_maximum_fusion.6), channel_id=1, source_target_pairs={{0,8},{4,12},{8,16},{12,20},{16,24},{20,28},{1,9},{5,13},{9,17},{1... | collective-permute-start | bytes 1253384 | tf_op jit(solution)/shard_map/ppermute | solution.py:429
  40.0 20.2 %collective-permute-start.4 = (f32[384,512]{1,0:T(8,128)}, f32[384,512]{1,0:T(8,128)}, u32[]{:S(2)}, u32[]{:S(2)}) collective-permute-start(f32[384,512]{1,0:T(8,128)} %collective-permute-done.1), channel_id=1, source_target_pairs={{0,2},{1,3},{2,0},{3,1},{4,6},{5,7},{6,4},{7,5},{8,10},{9,11},{10,... | collective-permute-start | bytes 2359304 | tf_op jit(solution)/shard_map/ppermute | solution.py:452
  47.8 12.3 %collective-permute-start.3 = (f32[6,136,128]{2,1,0:T(8,128)S(1)}, f32[6,136,128]{2,1,0:T(8,128)S(1)}, u32[]{:S(2)}, u32[]{:S(2)}) collective-permute-start(f32[6,136,128]{2,1,0:T(8,128)S(1)} %pad_maximum_fusion.7), channel_id=1, source_target_pairs={{0,16},{4,20},{8,24},{12,28},{1,17},{5,21},{9,25},{13,29},{2,18},{... | collective-permute-start | bytes 1253384 | tf_op jit(solution)/shard_map/ppermute | solution.py:430
  60.3 8.1 %collective-permute-start.5 = (f32[6,128,128]{2,1,0:T(8,128)S(1)}, f32[6,128,128]{2,1,0:T(8,128)}, u32[]{:S(2)}, u32[]{:S(2)}) collective-permute-start(f32[6,128,128]{2,1,0:T(8,128)S(1)} %fusion.9), channel_id=1, source_target_pairs={{0,4},{4,0},{8,12},{12,8},{16,20},{20,16},{24,28},{28,24},{1,5},{5... | collective-permute-start | bytes 1179656 | tf_op jit(solution)/shard_map/ppermute | solution.py:438
  80.8 7.0 %collective-permute-start.11 = (f32[1,2,384,512]{3,2,1,0:T(8,128)S(1)}, f32[1,2,384,512]{3,2,1,0:T(8,128)}, u32[]{:S(2)}, u32[]{:S(2)}) collective-permute-start(f32[1,2,384,512]{3,2,1,0:T(8,128)S(1)} %maximum_bitcast_fusion.here_ref), channel_id=1, source_target_pairs={{0,1},{1,0},{2,3},{3,2},{4,5},{5,4},{6,7},{7,6},{8,9},{9,8},{10,11... | collective-permute-start | bytes 4718600 | tf_op jit(solution)/shard_map/ppermute | solution.py:448
  81.0 41.2 %collective-permute-start.7 = (f32[384,1024]{1,0:T(8,128)}, f32[384,1024]{1,0:T(8,128)}, u32[]{:S(2)}, u32[]{:S(2)}) collective-permute-start(f32[384,1024]{1,0:T(8,128)} %add.163.p0), channel_id=1, source_target_pairs={{0,1},{1,0},{2,3},{3,2},{4,5},{5,4},{6,7},{7,6},{8,9},{9,8},{10,11... | collective-permute-start | bytes 4718600 | tf_op jit(solution)/shard_map/ppermute | solution.py:448
  81.3 40.8 %collective-permute-start.8 = (f32[384,1024]{1,0:T(8,128)}, f32[384,1024]{1,0:T(8,128)}, u32[]{:S(2)}, u32[]{:S(2)}) collective-permute-start(f32[384,1024]{1,0:T(8,128)} %add.163.p0), channel_id=1, source_target_pairs={{0,2},{1,3},{2,0},{3,1},{4,6},{5,7},{6,4},{7,5},{8,10},{9,11},{10,... | collective-permute-start | bytes 4718600 | tf_op jit(solution)/shard_map/ppermute | solution.py:452
  82.8 39.3 %collective-permute-start.10 = (f32[384,1024]{1,0:T(8,128)}, f32[384,1024]{1,0:T(8,128)}, u32[]{:S(2)}, u32[]{:S(2)}) collective-permute-start(f32[384,1024]{1,0:T(8,128)} %get-tuple-element.188), channel_id=1, source_target_pairs={{0,4},{4,0},{8,12},{12,8},{16,20},{20,16},{24,28},{28,24},{1,5},{5... | collective-permute-start | bytes 4718600 | tf_op jit(solution)/shard_map/ppermute | solution.py:456
  84.3 37.8 %collective-permute-start.9 = (f32[384,512]{1,0:T(8,128)}, f32[384,512]{1,0:T(8,128)}, u32[]{:S(2)}, u32[]{:S(2)}) collective-permute-start(f32[384,512]{1,0:T(8,128)} %get-tuple-element.231), channel_id=1, source_target_pairs={{0,16},{4,20},{8,24},{12,28},{16,0},{20,4},{24,8},{28,12},{1,17},{... | collective-permute-start | bytes 2359304 | tf_op jit(solution)/shard_map/ppermute | solution.py:745
  122.3 42.6 %collective-permute-start.13 = (f32[384,512]{1,0:T(8,128)}, f32[384,512]{1,0:T(8,128)}, u32[]{:S(2)}, u32[]{:S(2)}) collective-permute-start(f32[384,512]{1,0:T(8,128)} %collective-permute-done.9), channel_id=1, source_target_pairs={{0,2},{1,3},{2,0},{3,1},{4,6},{5,7},{6,4},{7,5},{8,10},{9,11},{10,... | collective-permute-start | bytes 2359304 | tf_op jit(solution)/shard_map/ppermute | solution.py:452
  122.9 42.1 %collective-permute-start.15 = (f32[384,512]{1,0:T(8,128)}, f32[384,512]{1,0:T(8,128)S(1)}, u32[]{:S(2)}, u32[]{:S(2)}) collective-permute-start(f32[384,512]{1,0:T(8,128)} %get-tuple-element.200), channel_id=1, source_target_pairs={{0,4},{4,0},{8,12},{12,8},{16,20},{20,16},{24,28},{28,24},{1,5},{5... | collective-permute-start | bytes 2359304 | tf_op jit(solution)/shard_map/ppermute | solution.py:456
  133.4 31.6 %collective-permute-start.14 = (f32[384,512]{1,0:T(8,128)}, f32[384,512]{1,0:T(8,128)S(1)}, u32[]{:S(2)}, u32[]{:S(2)}) collective-permute-start(f32[384,512]{1,0:T(8,128)} %get-tuple-element.230), channel_id=1, source_target_pairs={{0,8},{4,12},{8,16},{12,20},{16,24},{20,28},{24,0},{28,4},{1,9},{5... | collective-permute-start | bytes 2359304 | tf_op jit(solution)/shard_map/ppermute | solution.py:745
  167.1 8.7 %collective-permute-start.20 = (f32[1,2,384,512]{3,2,1,0:T(8,128)S(1)}, f32[1,2,384,512]{3,2,1,0:T(8,128)S(1)}, u32[]{:S(2)}, u32[]{:S(2)}) collective-permute-start(f32[1,2,384,512]{3,2,1,0:T(8,128)S(1)} %maximum_bitcast_fusion.1.here_ref), channel_id=1, source_target_pairs={{0,1},{1,0},{2,3},{3,2},{4,5},{5,4},{6,7},{7,6},{8,9},{9,8},{10,11... | collective-permute-start | bytes 4718600 | tf_op jit(solution)/shard_map/ppermute | solution.py:448
  169.0 39.7 %collective-permute-start.17 = (f32[384,1024]{1,0:T(8,128)S(1)}, f32[384,1024]{1,0:T(8,128)}, u32[]{:S(2)}, u32[]{:S(2)}) collective-permute-start(f32[384,1024]{1,0:T(8,128)S(1)} %add.164.p0), channel_id=1, source_target_pairs={{0,2},{1,3},{2,0},{3,1},{4,6},{5,7},{6,4},{7,5},{8,10},{9,11},{10,... | collective-permute-start | bytes 4718600 | tf_op jit(solution)/shard_map/ppermute | solution.py:452
  170.6 38.1 %collective-permute-start.18 = (f32[384,1024]{1,0:T(8,128)S(1)}, f32[384,1024]{1,0:T(8,128)S(1)}, u32[]{:S(2)}, u32[]{:S(2)}) collective-permute-start(f32[384,1024]{1,0:T(8,128)S(1)} %add.164.p0), channel_id=1, source_target_pairs={{0,1},{1,0},{2,3},{3,2},{4,5},{5,4},{6,7},{7,6},{8,9},{9,8},{10,11... | collective-permute-start | bytes 4718600 | tf_op jit(solution)/shard_map/ppermute | solution.py:448
  170.6 38.1 %collective-permute-start.19 = (f32[384,512]{1,0:T(8,128)}, f32[384,512]{1,0:T(8,128)S(1)}, u32[]{:S(2)}, u32[]{:S(2)}) collective-permute-start(f32[384,512]{1,0:T(8,128)} %get-tuple-element.230), channel_id=1, source_target_pairs={{0,16},{4,20},{8,24},{12,28},{16,0},{20,4},{24,8},{28,12},{1,17},{... | collective-permute-start | bytes 2359304 | tf_op jit(solution)/shard_map/ppermute | solution.py:745
  210.9 155.5 %all-gather.3.cloned.1.call-start = ((), (), s32[]{:S(2)}) async-start(), calls=%async_computation.2 | async-start | bytes 11796480 | tf_op jit(solution)/shard_map/all_gather | solution.py:806
  210.9 35.7 %collective-permute-start.23 = (f32[384,512]{1,0:T(8,128)}, f32[384,512]{1,0:T(8,128)}, u32[]{:S(2)}, u32[]{:S(2)}) collective-permute-start(f32[384,512]{1,0:T(8,128)} %get-tuple-element.230), channel_id=1, source_target_pairs={{0,24},{4,28},{8,0},{12,4},{16,8},{20,12},{24,16},{28,20},{1,25},{... | collective-permute-start | bytes 2359304 | tf_op jit(solution)/shard_map/ppermute | solution.py:745
  229.2 20.1 %collective-permute-start.24 = (f32[384,512]{1,0:T(8,128)}, f32[384,512]{1,0:T(8,128)}, u32[]{:S(2)}, u32[]{:S(2)}) collective-permute-start(f32[384,512]{1,0:T(8,128)} %get-tuple-element.231), channel_id=1, source_target_pairs={{0,24},{4,28},{8,0},{12,4},{16,8},{20,12},{24,16},{28,20},{1,25},{... | collective-permute-start | bytes 2359304 | tf_op jit(solution)/shard_map/ppermute | solution.py:745
  232.6 11.8 %collective-permute-start.22 = (f32[6,136,128]{2,1,0:T(8,128)}, f32[6,136,128]{2,1,0:T(8,128)}, u32[]{:S(2)}, u32[]{:S(2)}) collective-permute-start(f32[6,136,128]{2,1,0:T(8,128)} %slice_select_fusion), channel_id=1, source_target_pairs={{0,4},{4,0},{8,12},{12,8},{16,20},{20,16},{24,28},{28,24},{1,5},{5... | collective-permute-start | bytes 1253384 | tf_op jit(solution)/shard_map/ppermute | solution.py:423
  252.1 214.6 %all-reduce.5.cloned.1.call-start = ((), (), s32[]{:S(2)}) async-start(), calls=%async_computation.1 | async-start | bytes 6291456 | tf_op jit(solution)/shard_map/psum | solution.py:832
  254.2 12.9 %collective-permute-start.25 = (f32[6,136,128]{2,1,0:T(8,128)S(1)}, f32[6,136,128]{2,1,0:T(8,128)S(1)}, u32[]{:S(2)}, u32[]{:S(2)}) collective-permute-start(f32[6,136,128]{2,1,0:T(8,128)S(1)} %pad_maximum_fusion.8), channel_id=1, source_target_pairs={{8,0},{12,4},{16,8},{20,12},{24,16},{28,20},{9,1},{13,5},{17,9},{2... | collective-permute-start | bytes 1253384 | tf_op jit(solution)/shard_map/ppermute | solution.py:429
  256.1 33.0 %collective-permute-start.27 = (f32[384,512]{1,0:T(8,128)S(1)}, f32[384,512]{1,0:T(8,128)S(1)}, u32[]{:S(2)}, u32[]{:S(2)}) collective-permute-start(f32[384,512]{1,0:T(8,128)S(1)} %copy-done.7), channel_id=1, source_target_pairs={{0,4},{4,0},{8,12},{12,8},{16,20},{20,16},{24,28},{28,24},{1,5},{5... | collective-permute-start | bytes 2359304 | tf_op jit(solution)/shard_map/ppermute | solution.py:456
  257.2 36.8 %collective-permute-start.29 = (f32[384,512]{1,0:T(8,128)}, f32[384,512]{1,0:T(8,128)S(1)}, u32[]{:S(2)}, u32[]{:S(2)}) collective-permute-start(f32[384,512]{1,0:T(8,128)} %collective-permute-done.24), channel_id=1, source_target_pairs={{0,2},{1,3},{2,0},{3,1},{4,6},{5,7},{6,4},{7,5},{8,10},{9,11},{10,... | collective-permute-start | bytes 2359304 | tf_op jit(solution)/shard_map/ppermute | solution.py:452
  267.2 21.8 %collective-permute-start.26 = (f32[6,136,128]{2,1,0:T(8,128)S(1)}, f32[6,136,128]{2,1,0:T(8,128)S(1)}, u32[]{:S(2)}, u32[]{:S(2)}) collective-permute-start(f32[6,136,128]{2,1,0:T(8,128)S(1)} %pad_maximum_fusion.9), channel_id=1, source_target_pairs={{16,0},{20,4},{24,8},{28,12},{17,1},{21,5},{25,9},{29,13},{18,2},{... | collective-permute-start | bytes 1253384 | tf_op jit(solution)/shard_map/ppermute | solution.py:430
  268.6 20.5 %collective-permute-start.28 = (f32[384,256]{1,0:T(8,128)S(1)}, f32[384,256]{1,0:T(8,128)S(1)}, u32[]{:S(2)}, u32[]{:S(2)}) collective-permute-start(f32[384,256]{1,0:T(8,128)S(1)} %copy-done.46), channel_id=1, source_target_pairs={{0,4},{4,0},{8,12},{12,8},{16,20},{20,16},{24,28},{28,24},{1,5},{5... | collective-permute-start | bytes 1179656 | tf_op jit(solution)/shard_map/ppermute | solution.py:456
  299.6 15.9 %collective-permute-start.32 = (f32[1,2,384,512]{3,2,1,0:T(8,128)S(1)}, f32[1,2,384,512]{3,2,1,0:T(8,128)S(1)}, u32[]{:S(2)}, u32[]{:S(2)}) collective-permute-start(f32[1,2,384,512]{3,2,1,0:T(8,128)S(1)} %maximum_bitcast_fusion.2.here_ref), channel_id=1, source_target_pairs={{0,1},{1,0},{2,3},{3,2},{4,5},{5,4},{6,7},{7,6},{8,9},{9,8},{10,11... | collective-permute-start | bytes 4718600 | tf_op jit(solution)/shard_map/ppermute | solution.py:448
  299.8 11.6 %collective-permute-start.30 = (f32[6,128,128]{2,1,0:T(8,128)S(1)}, f32[6,128,128]{2,1,0:T(8,128)S(1)}, u32[]{:S(2)}, u32[]{:S(2)}) collective-permute-start(f32[6,128,128]{2,1,0:T(8,128)S(1)} %fusion.7), channel_id=1, source_target_pairs={{0,4},{4,0},{8,12},{12,8},{16,20},{20,16},{24,28},{28,24},{1,5},{5... | collective-permute-start | bytes 1179656 | tf_op jit(solution)/shard_map/ppermute | solution.py:438
  301.0 16.4 %collective-permute-start.31 = (f32[384,256]{1,0:T(8,128)S(1)}, f32[384,256]{1,0:T(8,128)S(1)}, u32[]{:S(2)}, u32[]{:S(2)}) collective-permute-start(f32[384,256]{1,0:T(8,128)S(1)} %copy-done.70), channel_id=1, source_target_pairs={{0,2},{1,3},{2,0},{3,1},{4,6},{5,7},{6,4},{7,5},{8,10},{9,11},{10,... | collective-permute-start | bytes 1179656 | tf_op jit(solution)/shard_map/ppermute | solution.py:452
  302.1 26.1 %collective-permute-start.34 = (f32[1,2,256,512]{3,2,1,0:T(8,128)}, f32[1,2,256,512]{3,2,1,0:T(8,128)}, u32[]{:S(2)}, u32[]{:S(2)}) collective-permute-start(f32[1,2,256,512]{3,2,1,0:T(8,128)} %get-tuple-element.261), channel_id=1, source_target_pairs={{0,8},{4,12},{8,0},{12,4},{16,24},{20,28},{24,16},{28,20},{1,9},{5... | collective-permute-start | bytes 3145736 | tf_op jit(solution)/shard_map/ppermute | solution.py:751
  318.2 48.1 %collective-permute-start.33 = (f32[2,384,512]{2,1,0:T(8,128)}, f32[2,384,512]{2,1,0:T(8,128)}, u32[]{:S(2)}, u32[]{:S(2)}) collective-permute-start(f32[2,384,512]{2,1,0:T(8,128)} %get-tuple-element.259), channel_id=1, source_target_pairs={{0,4},{4,0},{8,12},{12,8},{16,20},{20,16},{24,28},{28,24},{1,5},{5... | collective-permute-start | bytes 4718600 | tf_op jit(solution)/shard_map/ppermute | solution.py:456
  324.7 39.0 %collective-permute-start.37 = (f32[1,2,256,512]{3,2,1,0:T(8,128)}, f32[1,2,256,512]{3,2,1,0:T(8,128)}, u32[]{:S(2)}, u32[]{:S(2)}) collective-permute-start(f32[1,2,256,512]{3,2,1,0:T(8,128)} %get-tuple-element.267), channel_id=1, source_target_pairs={{0,8},{4,12},{8,0},{12,4},{16,24},{20,28},{24,16},{28,20},{1,9},{5... | collective-permute-start | bytes 3145736 | tf_op jit(solution)/shard_map/ppermute | solution.py:751
  330.5 30.9 %collective-permute-start.36 = (f32[1,256,512]{2,1,0:T(8,128)}, f32[1,256,512]{2,1,0:T(8,128)}, u32[]{:S(2)}, u32[]{:S(2)}) collective-permute-start(f32[1,256,512]{2,1,0:T(8,128)} %get-tuple-element.270), channel_id=1, source_target_pairs={{0,16},{4,20},{8,24},{12,28},{16,0},{20,4},{24,8},{28,12},{1,17},{... | collective-permute-start | bytes 1572872 | tf_op jit(solution)/shard_map/ppermute | solution.py:756
  371.7 86.8 %collective-permute-start.38 = (f32[2,2,256,512]{3,2,1,0:T(8,128)}, f32[2,2,256,512]{3,2,1,0:T(8,128)}, u32[]{:S(2)}, u32[]{:S(2)}) collective-permute-start(f32[2,2,256,512]{3,2,1,0:T(8,128)} %get-tuple-element.283), channel_id=1, source_target_pairs={{0,8},{4,12},{8,0},{12,4},{16,24},{20,28},{24,16},{28,20},{1,9},{5... | collective-permute-start | bytes 6291464 | tf_op jit(solution)/shard_map/ppermute | solution.py:751
  374.8 56.2 %collective-permute-start.39 = (f32[1,256,512]{2,1,0:T(8,128)}, f32[1,256,512]{2,1,0:T(8,128)}, u32[]{:S(2)}, u32[]{:S(2)}) collective-permute-start(f32[1,256,512]{2,1,0:T(8,128)} %get-tuple-element.286), channel_id=1, source_target_pairs={{0,16},{4,20},{8,24},{12,28},{16,0},{20,4},{24,8},{28,12},{1,17},{... | collective-permute-start | bytes 1572872 | tf_op jit(solution)/shard_map/ppermute | solution.py:756
  375.1 31.1 %collective-permute-start.40 = (f32[384,512]{1,0:T(8,128)}, f32[384,512]{1,0:T(8,128)}, u32[]{:S(2)}, u32[]{:S(2)}) collective-permute-start(f32[384,512]{1,0:T(8,128)} %get-tuple-element.291.d0.refs_0_), channel_id=1, source_target_pairs={{0,4},{4,0},{8,12},{12,8},{16,20},{20,16},{24,28},{28,24},{1,5},{5... | collective-permute-start | bytes 2359304 | tf_op jit(solution)/shard_map/ppermute | solution.py:456
  406.2 56.0 %collective-permute-start.41 = (f32[3,256,512]{2,1,0:T(8,128)}, f32[3,256,512]{2,1,0:T(8,128)}, u32[]{:S(2)}, u32[]{:S(2)}) collective-permute-start(f32[3,256,512]{2,1,0:T(8,128)} %get-tuple-element.292), channel_id=1, source_target_pairs={{0,4},{4,0},{8,12},{12,8},{16,20},{20,16},{24,28},{28,24},{1,5},{5... | collective-permute-start | bytes 4718600 | tf_op jit(solution)/shard_map/ppermute | solution.py:456
  462.2 51.7 %collective-permute-start.42 = (f32[3,256,512]{2,1,0:T(8,128)}, f32[3,256,512]{2,1,0:T(8,128)}, u32[]{:S(2)}, u32[]{:S(2)}) collective-permute-start(f32[3,256,512]{2,1,0:T(8,128)} %get-tuple-element.299), channel_id=1, source_target_pairs={{0,4},{4,0},{8,12},{12,8},{16,20},{20,16},{24,28},{28,24},{1,5},{5... | collective-permute-start | bytes 4718600 | tf_op jit(solution)/shard_map/ppermute | solution.py:456
  463.2 46.4 %collective-permute-start.43 = (f32[1,2,256,512]{3,2,1,0:T(8,128)S(1)}, f32[1,2,256,512]{3,2,1,0:T(8,128)}, u32[]{:S(2)}, u32[]{:S(2)}) collective-permute-start(f32[1,2,256,512]{3,2,1,0:T(8,128)S(1)} %copy-done.40), channel_id=1, source_target_pairs={{0,8},{4,12},{8,0},{12,4},{16,24},{20,28},{24,16},{28,20},{1,9},{5... | collective-permute-start | bytes 3145736 | tf_op jit(solution)/shard_map/ppermute | solution.py:751
  465.8 46.6 %collective-permute-start.44 = (f32[2,256,512]{2,1,0:T(8,128)}, f32[2,256,512]{2,1,0:T(8,128)}, u32[]{:S(2)}, u32[]{:S(2)}) collective-permute-start(f32[2,256,512]{2,1,0:T(8,128)} %get-tuple-element.304), channel_id=1, source_target_pairs={{0,16},{4,20},{8,24},{12,28},{16,0},{20,4},{24,8},{28,12},{1,17},{... | collective-permute-start | bytes 3145736 | tf_op jit(solution)/shard_map/ppermute | solution.py:756
  474.0 31.5 %collective-permute-start.45 = (f32[5120]{0:T(1024)S(1)}, f32[5120]{0:T(1024)S(1)}, u32[]{:S(2)}, u32[]{:S(2)}) collective-permute-start(f32[5120]{0:T(1024)S(1)} %pad_maximum_fusion.10), channel_id=1, source_target_pairs={{0,4},{4,0},{8,12},{12,8},{16,20},{20,16},{24,28},{28,24},{1,5},{5... | collective-permute-start | bytes 61448 | tf_op jit(solution)/shard_map/ppermute | solution.py:853
  513.9 5.9 %collective-permute-start.46 = (f32[5120]{0:T(1024)S(1)}, f32[5120]{0:T(1024)S(1)}, u32[]{:S(2)}, u32[]{:S(2)}) collective-permute-start(f32[5120]{0:T(1024)S(1)} %fusion.11), channel_id=1, source_target_pairs={{0,8},{4,12},{8,0},{12,4},{16,24},{20,28},{24,16},{28,20},{1,9},{5... | collective-permute-start | bytes 61448 | tf_op jit(solution)/shard_map/ppermute | solution.py:860
  514.5 25.1 %collective-permute-start.48 = (f32[1,256,512]{2,1,0:T(8,128)S(1)}, f32[1,256,512]{2,1,0:T(8,128)S(1)}, u32[]{:S(2)}, u32[]{:S(2)}) collective-permute-start(f32[1,256,512]{2,1,0:T(8,128)S(1)} %get-tuple-element.320), channel_id=1, source_target_pairs={{0,16},{4,20},{8,24},{12,28},{16,0},{20,4},{24,8},{28,12},{1,17},{... | collective-permute-start | bytes 1572872 | tf_op jit(solution)/shard_map/ppermute | solution.py:756
  517.3 23.9 %collective-permute-start.49 = (f32[3,256,384]{2,1,0:T(8,128)S(1)}, f32[3,256,384]{2,1,0:T(8,128)S(1)}, u32[]{:S(2)}, u32[]{:S(2)}) collective-permute-start(f32[3,256,384]{2,1,0:T(8,128)S(1)} %copy-done.71), channel_id=1, source_target_pairs={{0,4},{4,0},{8,12},{12,8},{16,20},{20,16},{24,28},{28,24},{1,5},{5... | collective-permute-start | bytes 3538952 | tf_op jit(solution)/shard_map/ppermute | solution.py:456
  519.8 18.5 %collective-permute-start.47 = (f32[5120]{0:T(1024)S(1)}, f32[5120]{0:T(1024)S(1)}, u32[]{:S(2)}, u32[]{:S(2)}) collective-permute-start(f32[5120]{0:T(1024)S(1)} %add.185), channel_id=1, source_target_pairs={{0,16},{4,20},{8,24},{12,28},{16,0},{20,4},{24,8},{28,12},{1,17},{... | collective-permute-start | bytes 61448 | tf_op jit(solution)/shard_map/ppermute | solution.py:860
  (77 other events, 531.0 us)
Sparse Core Ops, SparseCore 0:
  211.0 84.7 all-reduce.2
  297.9 66.6 all-gather.2
  376.3 67.6 all-reduce.4

commit v5 on v4

--- a/solution.py
+++ b/solution.py
@@ -752,8 +752,10 @@
         return (keep[:, 0], got[:, 0]), keep[:, 1] + got[:, 1]
 
     def sum_far(near):
-        (a, b), far = near
-        return a + b + lax.ppermute(far, "seq", flip(4))
+        return lax.ppermute(near[1], "seq", flip(4))
+
+    def summed(near, far):
+        return near[0][0] + near[0][1] + far
 
     dy_quarter, dy_all = do.widen(scalar(head), dy, 4)
     dy1 = shift(dy_quarter, 1)
@@ -825,15 +827,15 @@
     down = do.mix_grad(do.turn(seq_at, dbranch, assemble([(dbranch_own, dbranch_over)])), gated, gated_got)
     near_down = sum_near(*down)
     near_gate, down = tie(near_gate, down)
-    grad_gate = sum_far(near_gate)
+    gate_far = sum_far(near_gate)
     dxn1 = do.first_grad((dpre_query, dpre_fv[0], dpre_fv[1], dpre_gate), mix_weight)
     xn_parts, dxn1, ffn = tie(xn_parts, dxn1, ffn)
-    fv_got, grad_gate, near_down, xn_all, dpre_query, xn_parts = tie(fv_got, grad_gate, near_down, xn_all, dpre_query, xn_parts)
+    fv_got, gate_far, near_down, xn_all, dpre_query, xn_parts = tie(fv_got, gate_far, near_down, xn_all, dpre_query, xn_parts)
     dxn1 = lax.psum(dxn1, "head")
 
     rows = jnp.stack([seq, seq ^ 1]).astype(jnp.int32)
     query_got = x_swap(dpre_query)
-    grad_w_out = sum_far(near_down)
+    w_far = sum_far(near_down)
     forget_values = do.mix_grad(xn1_turned, dpre_fv[0], fv_got[0], dpre_fv[1], fv_got[1])
     forget_values, xn_all, xn_parts = tie(forget_values, xn_all, xn_parts)
     near_fv = sum_near(*forget_values)
@@ -843,25 +845,26 @@
     got_a = x_swap(away_a)
     query = do.mix_grad(xn1_turned, dpre_query, query_got)
     mine_b, away_b = do.ffn_grad(rows, xn_all, dy_all, ffn_in, ffn_out, 2, 2)
-    near_fv, grad_w_out, got_a, query, away_b, xn_all, dhidden, hidden = tie(near_fv, grad_w_out, got_a, query, away_b, xn_all, dhidden, hidden)
+    near_fv, w_far, got_a, query, away_b, xn_all, dhidden, hidden = tie(near_fv, w_far, got_a, query, away_b, xn_all, dhidden, hidden)
 
     got_b = x_swap(away_b)
-    near_query, grad_fv = sum_near(*query), sum_far(near_fv)
+    near_query, fv_far = sum_near(*query), sum_far(near_fv)
     grad_tokens, part_norm_first = do.first_back(dxn1, dhidden, tokens, norm_first)
     mine_c, away_c = do.ffn_grad(rows, xn_all, dy_all, ffn_in, ffn_out, 4, do.steps - 4)
     small = jnp.concatenate([part_norm_first[0], part_norm_second[0], part_bound[0], part_gain[0]])
     small = small + lax.ppermute(small, "seq", flip(1))
     output = (hidden + ffn).astype(BF16)
-    got_b, near_query, grad_fv, small, away_c, output = tie(got_b, near_query, grad_fv, small, away_c, output)
+    got_b, near_query, fv_far, small, away_c, output = tie(got_b, near_query, fv_far, small, away_c, output)
 
     got_c = x_swap(away_c)
-    grad_query = sum_far(near_query)
+    query_far = sum_far(near_query)
     for bit in (2, 4):
         small = small + lax.ppermute(small, "seq", flip(bit))
     parts = ((mine_a, got_a), (mine_b, got_b), (mine_c, got_c))
     grad_in = jnp.concatenate([mine[:2] + got[:2] for mine, got in parts], axis=2)
     grad_out = jnp.concatenate([(mine[2] + got[2]).T for mine, got in parts], axis=0)
-    grad_mix = jnp.concatenate([grad_query, grad_fv, grad_gate])
+    grad_mix = jnp.concatenate([summed(near_query, query_far), summed(near_fv, fv_far), summed(near_gate, gate_far)])
+    grad_w_out = summed(near_down, w_far)
     return output, grad_tokens, small, (grad_mix, grad_w_out[0].T, grad_in, grad_out)
 
 

time: 563 us -> 539 us (0.957)
  waiting for transfers between devices: 213 us -> 191 us
    ppermute x4, waiting for transfers between devices: 45.1 us -> 0.01 us  [sum_far(): return lax.ppermute(near[1], 'seq', flip(4))]
    ppermute x4, waiting for transfers between devices: 4.99 us -> 23 us  [sum_near(): got = lax.ppermute(send, 'seq', flip(2))]
  transfers between devices with their start and end apart: 53 -> 53, of which waited for: 23 -> 21; matrix products, arithmetic and copies ran while one was open for 8% -> 9% of each run, Pallas kernels for 29% -> 30%
where the time goes in v5:
time: 539 us; the launch traced here: 532 us
  waiting for transfers between devices  191 us (35%)
  Pallas kernels  172 us (32%)
  starting transfers between devices  76.3 us (14%)
  other arithmetic  48.1 us (9%)
  local copies, waits for them, and re-layouts  29 us (5%)
  between operations  15.2 us (3%)
    ppermute x6, waiting for transfers between devices, shift(): return lax.ppermute(a, 'seq', z_shift(k))  65.2 us
    pallas_call x3, Pallas kernels, ffn_grad(): call(functools.partial(ffn_grad_kernel, tail), 'ffn_grad', [out, out], [S...  62.3 us
    ppermute x6, starting transfers between devices, shift(): return lax.ppermute(a, 'seq', z_shift(k))  23.7 us
    ppermute x4, waiting for transfers between devices, sum_near(): got = lax.ppermute(send, 'seq', flip(2))  23 us
    pallas_call x1, Pallas kernels, ffn_own(): call(ffn_own_kernel, 'ffn_own', [self.wide, self.half, self.half], [SMEM,...  22.9 us
    unnamed x155, local copies, waits for them, and re-layouts  22 us
    ppermute x2, waiting for transfers between devices, pair_states(): lax.ppermute(jnp.where(is_low, packed[half:], packed[:half]), 'seq', X_SWAP)  20.4 us
    ppermute x2, waiting for transfers between devices, pass_states(): further = lax.ppermute(join(before, pair), 'seq', z_line(2 * step))  18.5 us
  transfers between devices with their start and end apart: 53, of which 21 were waited for; matrix products, arithmetic and copies ran while one was open for 9% of the time, Pallas kernels for 30%

profile of v5, /device:TPU:0, one launch (start us, length us, event | category | flops | bytes accessed | tf_op | source)
XLA Modules:
  0.0 531.7 jit_solution(15481699917695034205)
XLA Ops:
  10.2 3.0 collective-permute-start.1
  13.2 11.8 %project.1 = (bf16[384,2048]{1,0:T(8,128)(2,1)S(1)}, f32[384,1024]{1,0:T(8,128)}, f32[4,384,512]{2,1,0:T(8,128)}, f32[384,512]{1,0:T(8,128)S(1)}, bf16[384,512]{...) custom-call(s32[1]{0:T(128)} %bitcast.4.pos.place, ...), custom_call_target="tpu_custom_call" | custom-call | flops 3221225472 | bytes 20000000 | tf_op jit(solution)/shard_map/project/pallas_call | solution.py:515
  26.6 9.6 %collective-permute-done = f32[6,136,128]{2,1,0:T(8,128)S(1)} collective-permute-done((f32[6,136,128]{2,1,0:T(8,128)S(1)}, f32[6,136,128]{2,1,0:T(8,128)S(1)}, u32[]{:S(2)}, u32[]{:S(2)}) %collective-permute-start) | collective-permute-done | bytes 417824 | tf_op jit(solution)/shard_map/ppermute | solution.py:423
  36.5 3.5 collective-permute-start.2
  41.6 6.1 %collective-permute-done.2 = f32[6,136,128]{2,1,0:T(8,128)S(1)} collective-permute-done((f32[6,136,128]{2,1,0:T(8,128)S(1)}, f32[6,136,128]{2,1,0:T(8,128)S(1)}, u32[]{:S(2)}, u32[]{:S(2)}) %collective-permute-start.2) | collective-permute-done | bytes 417824 | tf_op jit(solution)/shard_map/ppermute | solution.py:429
  47.8 5.4 %collective-permute-start.3 = (f32[6,136,128]{2,1,0:T(8,128)S(1)}, f32[6,136,128]{2,1,0:T(8,128)S(1)}, u32[]{:S(2)}, u32[]{:S(2)}) collective-permute-start(f32[6,136,128]{2,1,0:T(8,128)S(1)} %pad_maximum_fusion.7), channel_id=1, source_target_pairs={{0,16},{4,20},{8,24},{12,28},{1,17},{5,21},{9,25},{13,29},{2,18},{... | collective-permute-start | bytes 1253384 | tf_op jit(solution)/shard_map/ppermute | solution.py:430
  53.3 6.9 %collective-permute-done.3 = f32[6,136,128]{2,1,0:T(8,128)S(1)} collective-permute-done((f32[6,136,128]{2,1,0:T(8,128)S(1)}, f32[6,136,128]{2,1,0:T(8,128)S(1)}, u32[]{:S(2)}, u32[]{:S(2)}) %collective-permute-start.3) | collective-permute-done | bytes 417824 | tf_op jit(solution)/shard_map/ppermute | solution.py:430
  61.9 6.5 %collective-permute-done.5 = f32[6,128,128]{2,1,0:T(8,128)S(1)} collective-permute-done((f32[6,128,128]{2,1,0:T(8,128)S(1)}, f32[6,128,128]{2,1,0:T(8,128)S(1)}, u32[]{:S(2)}, u32[]{:S(2)}) %collective-permute-start.5) | collective-permute-done | bytes 393248 | tf_op jit(solution)/shard_map/ppermute | solution.py:438
  68.5 4.7 mixer_out.1
  73.2 3.6 collective-permute-done.6
  83.4 3.4 collective-permute-start.9
  86.9 2.8 assemble.4.refs_0_
  89.7 31.5 %collective-permute-done.9 = f32[384,512]{1,0:T(8,128)} collective-permute-done((f32[384,512]{1,0:T(8,128)}, f32[384,512]{1,0:T(8,128)}, u32[]{:S(2)}, u32[]{:S(2)}) %collective-permute-start.9) | collective-permute-done | bytes 786464 | tf_op jit(solution)/shard_map/ppermute | solution.py:745
  126.1 6.4 %second_norm.1 = (f32[384,2048]{1,0:T(8,128)}, bf16[1536,2048]{1,0:T(8,128)(2,1)}, f32[384,512]{1,0:T(8,128)}) custom-call(s32[3]{0:T(128)S(1)} %pad_add_fusion.place, bf16[384,2048]{1,0:T(8,128)(2,1)S(1)} %bitcast.133, f32[384,1024]{1,0:T(8,128)} %add.163.p0, f32[384,1024]{1,0:T(8,128)} %collective-permute-done.8.p1, ...), custom_call_target="tpu_custom_call" | custom-call | bytes 10000000 | tf_op jit(solution)/shard_map/second_norm/pallas_call | solution.py:577
  132.5 8.7 %collective-permute-start.14 = (f32[384,512]{1,0:T(8,128)}, f32[384,512]{1,0:T(8,128)S(1)}, u32[]{:S(2)}, u32[]{:S(2)}) collective-permute-start(f32[384,512]{1,0:T(8,128)} %get-tuple-element.230), channel_id=1, source_target_pairs={{0,8},{4,12},{8,16},{12,20},{16,24},{20,28},{24,0},{28,4},{1,9},{5... | collective-permute-start | bytes 2359304 | tf_op jit(solution)/shard_map/ppermute | solution.py:745
  141.1 22.9 %ffn_own.1 = (f32[384,2048]{1,0:T(8,128)}, f32[384,1024]{1,0:T(8,128)}, f32[384,1024]{1,0:T(8,128)}) custom-call(s32[1]{0:T(128)} %bitcast.core, bf16[1536,2048]{1,0:T(8,128)(2,1)} %get-tuple-element.284.xn_ref._, bf16[384,2048]{1,0:T(8,128)(2,1)} %bitcast.129, bf16[2,2048,1408]{2,1,0:T(8,128)(2,1)} %refs_2_.1, bf16[1408,2048]{1,0:T(8,128)(2,1)} %refs_3_.1, ...), custom_call_target="tpu_custom_call" | custom-call | flops 13287555072 | bytes 30000000 | tf_op jit(solution)/shard_map/ffn_own/pallas_call | solution.py:549
  169.6 3.4 collective-permute-start.19
  176.8 31.0 %collective-permute-done.19 = f32[384,512]{1,0:T(8,128)S(1)} collective-permute-done((f32[384,512]{1,0:T(8,128)}, f32[384,512]{1,0:T(8,128)S(1)}, u32[]{:S(2)}, u32[]{:S(2)}) %collective-permute-start.19) | collective-permute-done | bytes 786464 | tf_op jit(solution)/shard_map/ppermute | solution.py:745
  209.9 2.6 collective-permute-start.23
  215.9 10.4 %norm_back.1 = (f32[384,512]{1,0:T(8,128)S(1)}, bf16[384,512]{1,0:T(8,128)(2,1)S(1)}, f32[1,512]{1,0:T(1,128)S(1)}, f32[3,4,136,128]{3,2,1,0:T(8,128)S(1)}, f32[...) custom-call(s32[3]{0:T(128)S(1)} %pad_add_fusion.place, ...), custom_call_target="tpu_custom_call" | custom-call | flops 805306368 | bytes 10000000 | tf_op jit(solution)/shard_map/norm_back/pallas_call | solution.py:564
  228.2 2.7 collective-permute-start.24
  232.6 10.8 %collective-permute-done.22 = f32[6,136,128]{2,1,0:T(8,128)} collective-permute-done((f32[6,136,128]{2,1,0:T(8,128)}, f32[6,136,128]{2,1,0:T(8,128)}, u32[]{:S(2)}, u32[]{:S(2)}) %collective-permute-start.22) | collective-permute-done | bytes 417824 | tf_op jit(solution)/shard_map/ppermute | solution.py:423
  245.7 2.6 collective-permute-done.24
  248.3 2.8 pad_maximum_fusion.1
  257.8 8.4 %collective-permute-done.25 = f32[6,136,128]{2,1,0:T(8,128)S(1)} collective-permute-done((f32[6,136,128]{2,1,0:T(8,128)S(1)}, f32[6,136,128]{2,1,0:T(8,128)S(1)}, u32[]{:S(2)}, u32[]{:S(2)}) %collective-permute-start.25) | collective-permute-done | bytes 417824 | tf_op jit(solution)/shard_map/ppermute | solution.py:429
  268.7 6.0 %intra_back.1 = (f32[384,512]{1,0:T(8,128)}, f32[384,512]{1,0:T(8,128)S(1)}, f32[384,512]{1,0:T(8,128)S(1)}, f32[384,512]{1,0:T(8,128)S(1)}) custom-call(bf16[384,512]{1,0:T(8,128)(2,1)S(1)} %copy-done.33, bf16[384,512]{1,0:T(8,128)(2,1)S(1)} %get-tuple-element.170.qe_ref, bf16[384,512]{1,0:T(8,128)(2,1)S(1)} %get-tuple-element.236.ke_ref, ...), custom_call_target="tpu_custom_call" | custom-call | flops 352321536 | bytes 10000000 | tf_op jit(solution)/shard_map/intra_back/pallas_call | solution.py:612
  276.4 11.7 %collective-permute-done.26 = f32[6,136,128]{2,1,0:T(8,128)S(1)} collective-permute-done((f32[6,136,128]{2,1,0:T(8,128)S(1)}, f32[6,136,128]{2,1,0:T(8,128)S(1)}, u32[]{:S(2)}, u32[]{:S(2)}) %collective-permute-start.26) | collective-permute-done | bytes 417824 | tf_op jit(solution)/shard_map/ppermute | solution.py:430
  288.1 4.9 collective-permute-done.29
  301.1 2.6 collective-permute-start.34
  303.6 6.8 %collective-permute-done.30 = f32[6,128,128]{2,1,0:T(8,128)S(1)} collective-permute-done((f32[6,128,128]{2,1,0:T(8,128)S(1)}, f32[6,128,128]{2,1,0:T(8,128)S(1)}, u32[]{:S(2)}, u32[]{:S(2)}) %collective-permute-start.30) | collective-permute-done | bytes 393248 | tf_op jit(solution)/shard_map/ppermute | solution.py:438
  310.6 3.9 state_back.1
  324.7 2.6 collective-permute-start.37
  334.2 7.9 %first_grad.1 = f32[384,2048]{1,0:T(8,128)} custom-call(f32[384,512]{1,0:T(8,128)} %get-tuple-element.287.d0.refs_0_, f32[384,512]{1,0:T(8,128)S(1)} %get-tuple-element.345.d1.refs_0_, f32[384,512]{1,0:T(8,128)S(1)} %get-tuple-element.344.d2.refs_2_, f32[384,512]{1,0:T(8,128)S(1)} %copy-done.8, bf16[4,2048,512]{2,1,0:T(8,128)(2,1)} %w_ref.7), custom_call_target="tpu_custom_call" | custom-call | flops 3221225472 | bytes 15000000 | tf_op jit(solution)/shard_map/first_grad/pallas_call | solution.py:589
  343.0 19.2 %collective-permute-done.37 = f32[1,2,256,512]{3,2,1,0:T(8,128)} collective-permute-done((f32[1,2,256,512]{3,2,1,0:T(8,128)}, f32[1,2,256,512]{3,2,1,0:T(8,128)}, u32[]{:S(2)}, u32[]{:S(2)}) %collective-permute-start.37) | collective-permute-done | bytes 1048608 | tf_op jit(solution)/shard_map/ppermute | solution.py:751
  362.2 2.8 fusion.2
  366.8 3.8 mix_grad.6
  371.7 2.9 collective-permute-start.39
  375.7 6.7 %join.1.xn_ref = bf16[1536,2048]{1,0:T(8,128)(2,1)} custom-call(f32[4,1152,512]{2,1,0:T(8,128)} %bitcast.154, bf16[1536,2048]{1,0:T(8,128)(2,1)} %get-tuple-element.284.xn_ref._), custom_call_target="tpu_custom_call", output_to_operand_aliasing={{}: (1, {})} | custom-call | bytes 14155776 | tf_op jit(solution)/shard_map/join/pallas_call | solution.py:479
  382.4 20.8 %ffn_grad.3 = (f32[3,256,512]{2,1,0:T(8,128)}, f32[3,256,512]{2,1,0:T(8,128)}) custom-call(s32[2]{0:T(128)} %pad_add_fusion.3.rows, bf16[1536,2048]{1,0:T(8,128)(2,1)} %join.1.xn_ref, bf16[1536,2048]{1,0:T(8,128)(2,1)} %assemble.6.dy_ref, bf16[2,2048,1408]{2,1,0:T(8,128)(2,1)} %refs_2_.1, bf16[1408,2048]{1,0:T(8,128)(2,1)} %refs_3_.1), custom_call_target="tpu_custom_call" | custom-call | flops 12079595520 | bytes 20000000 | tf_op jit(solution)/shard_map/ffn_grad/pallas_call | solution.py:667
  407.7 21.0 %ffn_grad.4 = (f32[3,256,512]{2,1,0:T(8,128)}, f32[3,256,512]{2,1,0:T(8,128)}) custom-call(s32[2]{0:T(128)} %pad_add_fusion.3.rows, bf16[1536,2048]{1,0:T(8,128)(2,1)} %join.1.xn_ref, bf16[1536,2048]{1,0:T(8,128)(2,1)} %assemble.6.dy_ref, bf16[2,2048,1408]{2,1,0:T(8,128)(2,1)} %refs_2_.1, bf16[1408,2048]{1,0:T(8,128)(2,1)} %refs_3_.1), custom_call_target="tpu_custom_call" | custom-call | flops 12079595520 | bytes 20000000 | tf_op jit(solution)/shard_map/ffn_grad/pallas_call | solution.py:667
  428.7 3.8 mix_grad.7
  432.5 3.6 fusion
  436.2 5.1 collective-permute-done.41
  445.2 5.5 %first_back.1 = (bf16[384,2048]{1,0:T(8,128)(2,1)}, f32[1,2048]{1,0:T(1,128)S(1)}) custom-call(f32[384,2048]{1,0:T(8,128)S(1)} %copy-done.11, f32[384,2048]{1,0:T(8,128)} %get-tuple-element.300.dhidden_ref, bf16[384,2048]{1,0:T(8,128)(2,1)S(1)} %bitcast.134, f32[1,2048]{1,0:T(1,128)S(1)} %bitcast.145), custom_call_target="tpu_custom_call" | custom-call | bytes 10000000 | tf_op jit(solution)/shard_map/first_back/pallas_call | solution.py:601
  451.7 20.5 %ffn_grad.5 = (f32[3,256,384]{2,1,0:T(8,128)}, f32[3,256,384]{2,1,0:T(8,128)}) custom-call(s32[2]{0:T(128)} %pad_add_fusion.3.rows, bf16[1536,2048]{1,0:T(8,128)(2,1)} %join.1.xn_ref, bf16[1536,2048]{1,0:T(8,128)(2,1)} %assemble.6.dy_ref, bf16[2,2048,1408]{2,1,0:T(8,128)(2,1)} %refs_2_.1, bf16[1408,2048]{1,0:T(8,128)(2,1)} %refs_3_.1, ...), custom_call_target="tpu_custom_call" | custom-call | flops 9059696640 | bytes 20000000 | tf_op jit(solution)/shard_map/ffn_grad/pallas_call | solution.py:667
  472.2 4.5 add_convert_fusion
  483.5 3.8 collective-permute-done.43
  498.1 16.5 %collective-permute-done.47 = f32[5120]{0:T(1024)S(1)} collective-permute-done((f32[5120]{0:T(1024)S(1)}, f32[5120]{0:T(1024)S(1)}, u32[]{:S(2)}, u32[]{:S(2)}) %collective-permute-start.47) | collective-permute-done | bytes 20512 | tf_op jit(solution)/shard_map/ppermute | solution.py:862
  (308 shorter events, 118.4 us)
Async XLA Ops:
  7.2 289.9 %all-reduce.3.cloned.1.call-start = ((), (), s32[]{:S(2)}) async-start(), calls=%async_computation | async-start | bytes 6291456 | tf_op jit(solution)/shard_map/psum | solution.py:797
  10.2 26.2 %collective-permute-start.1 = (f32[384,512]{1,0:T(8,128)}, f32[384,512]{1,0:T(8,128)}, u32[]{:S(2)}, u32[]{:S(2)}) collective-permute-start(f32[384,512]{1,0:T(8,128)} %get-tuple-element.231), channel_id=1, source_target_pairs={{0,8},{4,12},{8,16},{12,20},{16,24},{20,28},{24,0},{28,4},{1,9},{5... | collective-permute-start | bytes 2359304 | tf_op jit(solution)/shard_map/ppermute | solution.py:745
  25.1 11.2 %collective-permute-start = (f32[6,136,128]{2,1,0:T(8,128)S(1)}, f32[6,136,128]{2,1,0:T(8,128)S(1)}, u32[]{:S(2)}, u32[]{:S(2)}) collective-permute-start(f32[6,136,128]{2,1,0:T(8,128)S(1)} %slice_select_fusion.2), channel_id=1, source_target_pairs={{0,4},{4,0},{8,12},{12,8},{16,20},{20,16},{24,28},{28,24},{1,5},{5... | collective-permute-start | bytes 1253384 | tf_op jit(solution)/shard_map/ppermute | solution.py:423
  36.5 11.2 %collective-permute-start.2 = (f32[6,136,128]{2,1,0:T(8,128)S(1)}, f32[6,136,128]{2,1,0:T(8,128)S(1)}, u32[]{:S(2)}, u32[]{:S(2)}) collective-permute-start(f32[6,136,128]{2,1,0:T(8,128)S(1)} %pad_maximum_fusion.6), channel_id=1, source_target_pairs={{0,8},{4,12},{8,16},{12,20},{16,24},{20,28},{1,9},{5,13},{9,17},{1... | collective-permute-start | bytes 1253384 | tf_op jit(solution)/shard_map/ppermute | solution.py:429
  40.0 20.2 %collective-permute-start.4 = (f32[384,512]{1,0:T(8,128)}, f32[384,512]{1,0:T(8,128)}, u32[]{:S(2)}, u32[]{:S(2)}) collective-permute-start(f32[384,512]{1,0:T(8,128)} %collective-permute-done.1), channel_id=1, source_target_pairs={{0,2},{1,3},{2,0},{3,1},{4,6},{5,7},{6,4},{7,5},{8,10},{9,11},{10,... | collective-permute-start | bytes 2359304 | tf_op jit(solution)/shard_map/ppermute | solution.py:452
  47.8 12.3 %collective-permute-start.3 = (f32[6,136,128]{2,1,0:T(8,128)S(1)}, f32[6,136,128]{2,1,0:T(8,128)S(1)}, u32[]{:S(2)}, u32[]{:S(2)}) collective-permute-start(f32[6,136,128]{2,1,0:T(8,128)S(1)} %pad_maximum_fusion.7), channel_id=1, source_target_pairs={{0,16},{4,20},{8,24},{12,28},{1,17},{5,21},{9,25},{13,29},{2,18},{... | collective-permute-start | bytes 1253384 | tf_op jit(solution)/shard_map/ppermute | solution.py:430
  60.3 8.0 %collective-permute-start.5 = (f32[6,128,128]{2,1,0:T(8,128)S(1)}, f32[6,128,128]{2,1,0:T(8,128)S(1)}, u32[]{:S(2)}, u32[]{:S(2)}) collective-permute-start(f32[6,128,128]{2,1,0:T(8,128)S(1)} %fusion.9), channel_id=1, source_target_pairs={{0,4},{4,0},{8,12},{12,8},{16,20},{20,16},{24,28},{28,24},{1,5},{5... | collective-permute-start | bytes 1179656 | tf_op jit(solution)/shard_map/ppermute | solution.py:438
  79.8 7.1 %collective-permute-start.11 = (f32[1,2,384,512]{3,2,1,0:T(8,128)S(1)}, f32[1,2,384,512]{3,2,1,0:T(8,128)}, u32[]{:S(2)}, u32[]{:S(2)}) collective-permute-start(f32[1,2,384,512]{3,2,1,0:T(8,128)S(1)} %maximum_bitcast_fusion.here_ref), channel_id=1, source_target_pairs={{0,1},{1,0},{2,3},{3,2},{4,5},{5,4},{6,7},{7,6},{8,9},{9,8},{10,11... | collective-permute-start | bytes 4718600 | tf_op jit(solution)/shard_map/ppermute | solution.py:448
  80.0 41.2 %collective-permute-start.7 = (f32[384,1024]{1,0:T(8,128)}, f32[384,1024]{1,0:T(8,128)}, u32[]{:S(2)}, u32[]{:S(2)}) collective-permute-start(f32[384,1024]{1,0:T(8,128)} %add.163.p0), channel_id=1, source_target_pairs={{0,1},{1,0},{2,3},{3,2},{4,5},{5,4},{6,7},{7,6},{8,9},{9,8},{10,11... | collective-permute-start | bytes 4718600 | tf_op jit(solution)/shard_map/ppermute | solution.py:448
  80.4 40.9 %collective-permute-start.8 = (f32[384,1024]{1,0:T(8,128)}, f32[384,1024]{1,0:T(8,128)}, u32[]{:S(2)}, u32[]{:S(2)}) collective-permute-start(f32[384,1024]{1,0:T(8,128)} %add.163.p0), channel_id=1, source_target_pairs={{0,2},{1,3},{2,0},{3,1},{4,6},{5,7},{6,4},{7,5},{8,10},{9,11},{10,... | collective-permute-start | bytes 4718600 | tf_op jit(solution)/shard_map/ppermute | solution.py:452
  81.9 39.3 %collective-permute-start.10 = (f32[384,1024]{1,0:T(8,128)}, f32[384,1024]{1,0:T(8,128)}, u32[]{:S(2)}, u32[]{:S(2)}) collective-permute-start(f32[384,1024]{1,0:T(8,128)} %get-tuple-element.188), channel_id=1, source_target_pairs={{0,4},{4,0},{8,12},{12,8},{16,20},{20,16},{24,28},{28,24},{1,5},{5... | collective-permute-start | bytes 4718600 | tf_op jit(solution)/shard_map/ppermute | solution.py:456
  83.4 37.8 %collective-permute-start.9 = (f32[384,512]{1,0:T(8,128)}, f32[384,512]{1,0:T(8,128)}, u32[]{:S(2)}, u32[]{:S(2)}) collective-permute-start(f32[384,512]{1,0:T(8,128)} %get-tuple-element.231), channel_id=1, source_target_pairs={{0,16},{4,20},{8,24},{12,28},{16,0},{20,4},{24,8},{28,12},{1,17},{... | collective-permute-start | bytes 2359304 | tf_op jit(solution)/shard_map/ppermute | solution.py:745
  121.4 42.6 %collective-permute-start.13 = (f32[384,512]{1,0:T(8,128)}, f32[384,512]{1,0:T(8,128)}, u32[]{:S(2)}, u32[]{:S(2)}) collective-permute-start(f32[384,512]{1,0:T(8,128)} %collective-permute-done.9), channel_id=1, source_target_pairs={{0,2},{1,3},{2,0},{3,1},{4,6},{5,7},{6,4},{7,5},{8,10},{9,11},{10,... | collective-permute-start | bytes 2359304 | tf_op jit(solution)/shard_map/ppermute | solution.py:452
  121.9 42.1 %collective-permute-start.15 = (f32[384,512]{1,0:T(8,128)}, f32[384,512]{1,0:T(8,128)S(1)}, u32[]{:S(2)}, u32[]{:S(2)}) collective-permute-start(f32[384,512]{1,0:T(8,128)} %get-tuple-element.200), channel_id=1, source_target_pairs={{0,4},{4,0},{8,12},{12,8},{16,20},{20,16},{24,28},{28,24},{1,5},{5... | collective-permute-start | bytes 2359304 | tf_op jit(solution)/shard_map/ppermute | solution.py:456
  132.5 31.6 %collective-permute-start.14 = (f32[384,512]{1,0:T(8,128)}, f32[384,512]{1,0:T(8,128)S(1)}, u32[]{:S(2)}, u32[]{:S(2)}) collective-permute-start(f32[384,512]{1,0:T(8,128)} %get-tuple-element.230), channel_id=1, source_target_pairs={{0,8},{4,12},{8,16},{12,20},{16,24},{20,28},{24,0},{28,4},{1,9},{5... | collective-permute-start | bytes 2359304 | tf_op jit(solution)/shard_map/ppermute | solution.py:745
  166.2 8.7 %collective-permute-start.20 = (f32[1,2,384,512]{3,2,1,0:T(8,128)S(1)}, f32[1,2,384,512]{3,2,1,0:T(8,128)S(1)}, u32[]{:S(2)}, u32[]{:S(2)}) collective-permute-start(f32[1,2,384,512]{3,2,1,0:T(8,128)S(1)} %maximum_bitcast_fusion.1.here_ref), channel_id=1, source_target_pairs={{0,1},{1,0},{2,3},{3,2},{4,5},{5,4},{6,7},{7,6},{8,9},{9,8},{10,11... | collective-permute-start | bytes 4718600 | tf_op jit(solution)/shard_map/ppermute | solution.py:448
  168.1 39.6 %collective-permute-start.17 = (f32[384,1024]{1,0:T(8,128)S(1)}, f32[384,1024]{1,0:T(8,128)}, u32[]{:S(2)}, u32[]{:S(2)}) collective-permute-start(f32[384,1024]{1,0:T(8,128)S(1)} %add.164.p0), channel_id=1, source_target_pairs={{0,2},{1,3},{2,0},{3,1},{4,6},{5,7},{6,4},{7,5},{8,10},{9,11},{10,... | collective-permute-start | bytes 4718600 | tf_op jit(solution)/shard_map/ppermute | solution.py:452
  169.6 38.1 %collective-permute-start.18 = (f32[384,1024]{1,0:T(8,128)S(1)}, f32[384,1024]{1,0:T(8,128)S(1)}, u32[]{:S(2)}, u32[]{:S(2)}) collective-permute-start(f32[384,1024]{1,0:T(8,128)S(1)} %add.164.p0), channel_id=1, source_target_pairs={{0,1},{1,0},{2,3},{3,2},{4,5},{5,4},{6,7},{7,6},{8,9},{9,8},{10,11... | collective-permute-start | bytes 4718600 | tf_op jit(solution)/shard_map/ppermute | solution.py:448
  169.6 38.1 %collective-permute-start.19 = (f32[384,512]{1,0:T(8,128)}, f32[384,512]{1,0:T(8,128)S(1)}, u32[]{:S(2)}, u32[]{:S(2)}) collective-permute-start(f32[384,512]{1,0:T(8,128)} %get-tuple-element.230), channel_id=1, source_target_pairs={{0,16},{4,20},{8,24},{12,28},{16,0},{20,4},{24,8},{28,12},{1,17},{... | collective-permute-start | bytes 2359304 | tf_op jit(solution)/shard_map/ppermute | solution.py:745
  209.9 155.1 %all-gather.3.cloned.1.call-start = ((), (), s32[]{:S(2)}) async-start(), calls=%async_computation.2 | async-start | bytes 11796480 | tf_op jit(solution)/shard_map/all_gather | solution.py:808
  209.9 35.7 %collective-permute-start.23 = (f32[384,512]{1,0:T(8,128)}, f32[384,512]{1,0:T(8,128)}, u32[]{:S(2)}, u32[]{:S(2)}) collective-permute-start(f32[384,512]{1,0:T(8,128)} %get-tuple-element.230), channel_id=1, source_target_pairs={{0,24},{4,28},{8,0},{12,4},{16,8},{20,12},{24,16},{28,20},{1,25},{... | collective-permute-start | bytes 2359304 | tf_op jit(solution)/shard_map/ppermute | solution.py:745
  228.2 20.1 %collective-permute-start.24 = (f32[384,512]{1,0:T(8,128)}, f32[384,512]{1,0:T(8,128)}, u32[]{:S(2)}, u32[]{:S(2)}) collective-permute-start(f32[384,512]{1,0:T(8,128)} %get-tuple-element.231), channel_id=1, source_target_pairs={{0,24},{4,28},{8,0},{12,4},{16,8},{20,12},{24,16},{28,20},{1,25},{... | collective-permute-start | bytes 2359304 | tf_op jit(solution)/shard_map/ppermute | solution.py:745
  231.7 11.7 %collective-permute-start.22 = (f32[6,136,128]{2,1,0:T(8,128)}, f32[6,136,128]{2,1,0:T(8,128)}, u32[]{:S(2)}, u32[]{:S(2)}) collective-permute-start(f32[6,136,128]{2,1,0:T(8,128)} %slice_select_fusion), channel_id=1, source_target_pairs={{0,4},{4,0},{8,12},{12,8},{16,20},{20,16},{24,28},{28,24},{1,5},{5... | collective-permute-start | bytes 1253384 | tf_op jit(solution)/shard_map/ppermute | solution.py:423
  251.1 192.2 %all-reduce.5.cloned.1.call-start = ((), (), s32[]{:S(2)}) async-start(), calls=%async_computation.1 | async-start | bytes 6291456 | tf_op jit(solution)/shard_map/psum | solution.py:834
  253.3 12.9 %collective-permute-start.25 = (f32[6,136,128]{2,1,0:T(8,128)S(1)}, f32[6,136,128]{2,1,0:T(8,128)S(1)}, u32[]{:S(2)}, u32[]{:S(2)}) collective-permute-start(f32[6,136,128]{2,1,0:T(8,128)S(1)} %pad_maximum_fusion.8), channel_id=1, source_target_pairs={{8,0},{12,4},{16,8},{20,12},{24,16},{28,20},{9,1},{13,5},{17,9},{2... | collective-permute-start | bytes 1253384 | tf_op jit(solution)/shard_map/ppermute | solution.py:429
  255.2 33.0 %collective-permute-start.27 = (f32[384,512]{1,0:T(8,128)S(1)}, f32[384,512]{1,0:T(8,128)S(1)}, u32[]{:S(2)}, u32[]{:S(2)}) collective-permute-start(f32[384,512]{1,0:T(8,128)S(1)} %copy-done.7), channel_id=1, source_target_pairs={{0,4},{4,0},{8,12},{12,8},{16,20},{20,16},{24,28},{28,24},{1,5},{5... | collective-permute-start | bytes 2359304 | tf_op jit(solution)/shard_map/ppermute | solution.py:456
  256.2 36.8 %collective-permute-start.29 = (f32[384,512]{1,0:T(8,128)}, f32[384,512]{1,0:T(8,128)S(1)}, u32[]{:S(2)}, u32[]{:S(2)}) collective-permute-start(f32[384,512]{1,0:T(8,128)} %collective-permute-done.24), channel_id=1, source_target_pairs={{0,2},{1,3},{2,0},{3,1},{4,6},{5,7},{6,4},{7,5},{8,10},{9,11},{10,... | collective-permute-start | bytes 2359304 | tf_op jit(solution)/shard_map/ppermute | solution.py:452
  266.3 21.8 %collective-permute-start.26 = (f32[6,136,128]{2,1,0:T(8,128)S(1)}, f32[6,136,128]{2,1,0:T(8,128)S(1)}, u32[]{:S(2)}, u32[]{:S(2)}) collective-permute-start(f32[6,136,128]{2,1,0:T(8,128)S(1)} %pad_maximum_fusion.9), channel_id=1, source_target_pairs={{16,0},{20,4},{24,8},{28,12},{17,1},{21,5},{25,9},{29,13},{18,2},{... | collective-permute-start | bytes 1253384 | tf_op jit(solution)/shard_map/ppermute | solution.py:430
  267.6 20.5 %collective-permute-start.28 = (f32[384,256]{1,0:T(8,128)S(1)}, f32[384,256]{1,0:T(8,128)S(1)}, u32[]{:S(2)}, u32[]{:S(2)}) collective-permute-start(f32[384,256]{1,0:T(8,128)S(1)} %copy-done.44), channel_id=1, source_target_pairs={{0,4},{4,0},{8,12},{12,8},{16,20},{20,16},{24,28},{28,24},{1,5},{5... | collective-permute-start | bytes 1179656 | tf_op jit(solution)/shard_map/ppermute | solution.py:456
  298.7 15.9 %collective-permute-start.32 = (f32[1,2,384,512]{3,2,1,0:T(8,128)S(1)}, f32[1,2,384,512]{3,2,1,0:T(8,128)S(1)}, u32[]{:S(2)}, u32[]{:S(2)}) collective-permute-start(f32[1,2,384,512]{3,2,1,0:T(8,128)S(1)} %maximum_bitcast_fusion.2.here_ref), channel_id=1, source_target_pairs={{0,1},{1,0},{2,3},{3,2},{4,5},{5,4},{6,7},{7,6},{8,9},{9,8},{10,11... | collective-permute-start | bytes 4718600 | tf_op jit(solution)/shard_map/ppermute | solution.py:448
  298.9 11.6 %collective-permute-start.30 = (f32[6,128,128]{2,1,0:T(8,128)S(1)}, f32[6,128,128]{2,1,0:T(8,128)S(1)}, u32[]{:S(2)}, u32[]{:S(2)}) collective-permute-start(f32[6,128,128]{2,1,0:T(8,128)S(1)} %fusion.7), channel_id=1, source_target_pairs={{0,4},{4,0},{8,12},{12,8},{16,20},{20,16},{24,28},{28,24},{1,5},{5... | collective-permute-start | bytes 1179656 | tf_op jit(solution)/shard_map/ppermute | solution.py:438
  300.0 16.4 %collective-permute-start.31 = (f32[384,256]{1,0:T(8,128)S(1)}, f32[384,256]{1,0:T(8,128)S(1)}, u32[]{:S(2)}, u32[]{:S(2)}) collective-permute-start(f32[384,256]{1,0:T(8,128)S(1)} %copy-done.70), channel_id=1, source_target_pairs={{0,2},{1,3},{2,0},{3,1},{4,6},{5,7},{6,4},{7,5},{8,10},{9,11},{10,... | collective-permute-start | bytes 1179656 | tf_op jit(solution)/shard_map/ppermute | solution.py:452
  301.1 26.7 %collective-permute-start.34 = (f32[1,2,256,512]{3,2,1,0:T(8,128)}, f32[1,2,256,512]{3,2,1,0:T(8,128)}, u32[]{:S(2)}, u32[]{:S(2)}) collective-permute-start(f32[1,2,256,512]{3,2,1,0:T(8,128)} %get-tuple-element.261), channel_id=1, source_target_pairs={{0,8},{4,12},{8,0},{12,4},{16,24},{20,28},{24,16},{28,20},{1,9},{5... | collective-permute-start | bytes 3145736 | tf_op jit(solution)/shard_map/ppermute | solution.py:751
  316.5 48.5 %collective-permute-start.33 = (f32[2,384,512]{2,1,0:T(8,128)}, f32[2,384,512]{2,1,0:T(8,128)}, u32[]{:S(2)}, u32[]{:S(2)}) collective-permute-start(f32[2,384,512]{2,1,0:T(8,128)} %get-tuple-element.259), channel_id=1, source_target_pairs={{0,4},{4,0},{8,12},{12,8},{16,20},{20,16},{24,28},{28,24},{1,5},{5... | collective-permute-start | bytes 4718600 | tf_op jit(solution)/shard_map/ppermute | solution.py:456
  324.7 37.6 %collective-permute-start.37 = (f32[1,2,256,512]{3,2,1,0:T(8,128)}, f32[1,2,256,512]{3,2,1,0:T(8,128)}, u32[]{:S(2)}, u32[]{:S(2)}) collective-permute-start(f32[1,2,256,512]{3,2,1,0:T(8,128)} %get-tuple-element.267), channel_id=1, source_target_pairs={{0,8},{4,12},{8,0},{12,4},{16,24},{20,28},{24,16},{28,20},{1,9},{5... | collective-permute-start | bytes 3145736 | tf_op jit(solution)/shard_map/ppermute | solution.py:751
  331.8 33.2 %collective-permute-start.36 = (f32[1,256,512]{2,1,0:T(8,128)}, f32[1,256,512]{2,1,0:T(8,128)S(1)}, u32[]{:S(2)}, u32[]{:S(2)}) collective-permute-start(f32[1,256,512]{2,1,0:T(8,128)} %get-tuple-element.268), channel_id=1, source_target_pairs={{0,16},{4,20},{8,24},{12,28},{16,0},{20,4},{24,8},{28,12},{1,17},{... | collective-permute-start | bytes 1572872 | tf_op jit(solution)/shard_map/ppermute | solution.py:755
  370.6 61.9 %collective-permute-start.38 = (f32[2,2,256,512]{3,2,1,0:T(8,128)}, f32[2,2,256,512]{3,2,1,0:T(8,128)}, u32[]{:S(2)}, u32[]{:S(2)}) collective-permute-start(f32[2,2,256,512]{3,2,1,0:T(8,128)} %get-tuple-element.281), channel_id=1, source_target_pairs={{0,8},{4,12},{8,0},{12,4},{16,24},{20,28},{24,16},{28,20},{1,9},{5... | collective-permute-start | bytes 6291464 | tf_op jit(solution)/shard_map/ppermute | solution.py:751
  371.7 64.4 %collective-permute-start.39 = (f32[1,256,512]{2,1,0:T(8,128)}, f32[1,256,512]{2,1,0:T(8,128)}, u32[]{:S(2)}, u32[]{:S(2)}) collective-permute-start(f32[1,256,512]{2,1,0:T(8,128)} %get-tuple-element.282), channel_id=1, source_target_pairs={{0,16},{4,20},{8,24},{12,28},{16,0},{20,4},{24,8},{28,12},{1,17},{... | collective-permute-start | bytes 1572872 | tf_op jit(solution)/shard_map/ppermute | solution.py:755
  374.6 31.0 %collective-permute-start.40 = (f32[384,512]{1,0:T(8,128)}, f32[384,512]{1,0:T(8,128)}, u32[]{:S(2)}, u32[]{:S(2)}) collective-permute-start(f32[384,512]{1,0:T(8,128)} %get-tuple-element.287.d0.refs_0_), channel_id=1, source_target_pairs={{0,4},{4,0},{8,12},{12,8},{16,20},{20,16},{24,28},{28,24},{1,5},{5... | collective-permute-start | bytes 2359304 | tf_op jit(solution)/shard_map/ppermute | solution.py:456
  405.6 35.6 %collective-permute-start.41 = (f32[3,256,512]{2,1,0:T(8,128)}, f32[3,256,512]{2,1,0:T(8,128)}, u32[]{:S(2)}, u32[]{:S(2)}) collective-permute-start(f32[3,256,512]{2,1,0:T(8,128)} %get-tuple-element.288), channel_id=1, source_target_pairs={{0,4},{4,0},{8,12},{12,8},{16,20},{20,16},{24,28},{28,24},{1,5},{5... | collective-permute-start | bytes 4718600 | tf_op jit(solution)/shard_map/ppermute | solution.py:456
  441.3 47.5 %collective-permute-start.42 = (f32[3,256,512]{2,1,0:T(8,128)}, f32[3,256,512]{2,1,0:T(8,128)}, u32[]{:S(2)}, u32[]{:S(2)}) collective-permute-start(f32[3,256,512]{2,1,0:T(8,128)} %get-tuple-element.295), channel_id=1, source_target_pairs={{0,4},{4,0},{8,12},{12,8},{16,20},{20,16},{24,28},{28,24},{1,5},{5... | collective-permute-start | bytes 4718600 | tf_op jit(solution)/shard_map/ppermute | solution.py:456
  442.1 45.2 %collective-permute-start.43 = (f32[1,2,256,512]{3,2,1,0:T(8,128)}, f32[1,2,256,512]{3,2,1,0:T(8,128)}, u32[]{:S(2)}, u32[]{:S(2)}) collective-permute-start(f32[1,2,256,512]{3,2,1,0:T(8,128)} %get-tuple-element.297), channel_id=1, source_target_pairs={{0,8},{4,12},{8,0},{12,4},{16,24},{20,28},{24,16},{28,20},{1,9},{5... | collective-permute-start | bytes 3145736 | tf_op jit(solution)/shard_map/ppermute | solution.py:751
  442.2 46.5 %collective-permute-start.44 = (f32[2,256,512]{2,1,0:T(8,128)}, f32[2,256,512]{2,1,0:T(8,128)}, u32[]{:S(2)}, u32[]{:S(2)}) collective-permute-start(f32[2,256,512]{2,1,0:T(8,128)} %get-tuple-element.298), channel_id=1, source_target_pairs={{0,16},{4,20},{8,24},{12,28},{16,0},{20,4},{24,8},{28,12},{1,17},{... | collective-permute-start | bytes 3145736 | tf_op jit(solution)/shard_map/ppermute | solution.py:755
  450.7 32.8 %collective-permute-start.45 = (f32[5120]{0:T(1024)S(1)}, f32[5120]{0:T(1024)S(1)}, u32[]{:S(2)}, u32[]{:S(2)}) collective-permute-start(f32[5120]{0:T(1024)S(1)} %pad_maximum_fusion.10), channel_id=1, source_target_pairs={{0,4},{4,0},{8,12},{12,8},{16,20},{20,16},{24,28},{28,24},{1,5},{5... | collective-permute-start | bytes 61448 | tf_op jit(solution)/shard_map/ppermute | solution.py:855
  488.8 7.7 %collective-permute-start.46 = (f32[5120]{0:T(1024)S(1)}, f32[5120]{0:T(1024)S(1)}, u32[]{:S(2)}, u32[]{:S(2)}) collective-permute-start(f32[5120]{0:T(1024)S(1)} %fusion.11), channel_id=1, source_target_pairs={{0,8},{4,12},{8,0},{12,4},{16,24},{20,28},{24,16},{28,20},{1,9},{5... | collective-permute-start | bytes 61448 | tf_op jit(solution)/shard_map/ppermute | solution.py:862
  489.2 26.7 %collective-permute-start.48 = (f32[1,256,512]{2,1,0:T(8,128)S(1)}, f32[1,256,512]{2,1,0:T(8,128)S(1)}, u32[]{:S(2)}, u32[]{:S(2)}) collective-permute-start(f32[1,256,512]{2,1,0:T(8,128)S(1)} %get-tuple-element.314), channel_id=1, source_target_pairs={{0,16},{4,20},{8,24},{12,28},{16,0},{20,4},{24,8},{28,12},{1,17},{... | collective-permute-start | bytes 1572872 | tf_op jit(solution)/shard_map/ppermute | solution.py:755
  491.6 25.9 %collective-permute-start.49 = (f32[3,256,384]{2,1,0:T(8,128)S(1)}, f32[3,256,384]{2,1,0:T(8,128)S(1)}, u32[]{:S(2)}, u32[]{:S(2)}) collective-permute-start(f32[3,256,384]{2,1,0:T(8,128)S(1)} %copy-done.71), channel_id=1, source_target_pairs={{0,4},{4,0},{8,12},{12,8},{16,20},{20,16},{24,28},{28,24},{1,5},{5... | collective-permute-start | bytes 3538952 | tf_op jit(solution)/shard_map/ppermute | solution.py:456
  496.5 18.2 %collective-permute-start.47 = (f32[5120]{0:T(1024)S(1)}, f32[5120]{0:T(1024)S(1)}, u32[]{:S(2)}, u32[]{:S(2)}) collective-permute-start(f32[5120]{0:T(1024)S(1)} %add.179), channel_id=1, source_target_pairs={{0,16},{4,20},{8,24},{12,28},{16,0},{20,4},{24,8},{28,12},{1,17},{... | collective-permute-start | bytes 61448 | tf_op jit(solution)/shard_map/ppermute | solution.py:862
  (77 other events, 480.7 us)
Sparse Core Ops, SparseCore 0:
  210.0 84.7 all-reduce.2
  296.9 66.6 all-gather.2
  375.8 65.7 all-reduce.4

commit v6 on v5

--- a/solution.py
+++ b/solution.py
@@ -811,7 +811,7 @@
     dpre_query, dkeys, dvalues, dlogf = do.intra_back(dmixed, qe, ke, proj, cum, states)
     gate_got = x_swap(dpre_gate)
     dy3_over = y_swap(dy3)
-    early, into, gate_got, dpre_query, dbranch_own, dy3_over = tie(early, into, gate_got, dpre_query, dbranch_own, dy3_over)
+    early, into, gate_got, dpre_query = tie(early, into, gate_got, dpre_query)
 
     gate = do.mix_grad(xn1_turned, dpre_gate, gate_got)
     early, into, gate, dbranch_own, dy3_over, ffn = tie(early, into, gate, dbranch_own, dy3_over, ffn)

time: 539 us -> 537 us (level)
    unnamed x155 -> x145, local copies, waits for them, and re-layouts: 22 us -> 20.4 us
  transfers between devices with their start and end apart: 53 -> 53, of which waited for: 21 -> 22; matrix products, arithmetic and copies ran while one was open for 9% -> 9% of each run, Pallas kernels for 30% -> 30%
where the time goes in v6:
time: 537 us; the launch traced here: 529 us
  waiting for transfers between devices  191 us (36%)
  Pallas kernels  171 us (32%)
  starting transfers between devices  76 us (14%)
  other arithmetic  49 us (9%)
  local copies, waits for them, and re-layouts  27.3 us (5%)
  between operations  15.1 us (3%)
    ppermute x6, waiting for transfers between devices, shift(): return lax.ppermute(a, 'seq', z_shift(k))  65.3 us
    pallas_call x3, Pallas kernels, ffn_grad(): call(functools.partial(ffn_grad_kernel, tail), 'ffn_grad', [out, out], [S...  62.3 us
    ppermute x6, starting transfers between devices, shift(): return lax.ppermute(a, 'seq', z_shift(k))  23.7 us
    pallas_call x1, Pallas kernels, ffn_own(): call(ffn_own_kernel, 'ffn_own', [self.wide, self.half, self.half], [SMEM,...  22.9 us
    ppermute x4, waiting for transfers between devices, sum_near(): got = lax.ppermute(send, 'seq', flip(2))  22.3 us
    ppermute x2, waiting for transfers between devices, pair_states(): lax.ppermute(jnp.where(is_low, packed[half:], packed[:half]), 'seq', X_SWAP)  20.4 us
    unnamed x145, local copies, waits for them, and re-layouts  20.4 us
    ppermute x2, waiting for transfers between devices, pass_states(): further = lax.ppermute(join(before, pair), 'seq', z_line(2 * step))  18.5 us
  transfers between devices with their start and end apart: 53, of which 22 were waited for; matrix products, arithmetic and copies ran while one was open for 9% of the time, Pallas kernels for 30%

profile of v6, /device:TPU:0, one launch (start us, length us, event | category | flops | bytes accessed | tf_op | source)
XLA Modules:
  0.0 529.4 jit_solution(464459655945607554)
XLA Ops:
  10.2 3.0 collective-permute-start.1
  13.2 11.8 %project.1 = (bf16[384,2048]{1,0:T(8,128)(2,1)S(1)}, f32[384,1024]{1,0:T(8,128)}, f32[4,384,512]{2,1,0:T(8,128)}, f32[384,512]{1,0:T(8,128)S(1)}, bf16[384,512]{...) custom-call(s32[1]{0:T(128)} %bitcast.4.pos.place, ...), custom_call_target="tpu_custom_call" | custom-call | flops 3221225472 | bytes 20000000 | tf_op jit(solution)/shard_map/project/pallas_call | solution.py:515
  26.6 9.6 %collective-permute-done = f32[6,136,128]{2,1,0:T(8,128)S(1)} collective-permute-done((f32[6,136,128]{2,1,0:T(8,128)S(1)}, f32[6,136,128]{2,1,0:T(8,128)S(1)}, u32[]{:S(2)}, u32[]{:S(2)}) %collective-permute-start) | collective-permute-done | bytes 417824 | tf_op jit(solution)/shard_map/ppermute | solution.py:423
  36.5 3.5 collective-permute-start.2
  41.6 6.1 %collective-permute-done.2 = f32[6,136,128]{2,1,0:T(8,128)S(1)} collective-permute-done((f32[6,136,128]{2,1,0:T(8,128)S(1)}, f32[6,136,128]{2,1,0:T(8,128)S(1)}, u32[]{:S(2)}, u32[]{:S(2)}) %collective-permute-start.2) | collective-permute-done | bytes 417824 | tf_op jit(solution)/shard_map/ppermute | solution.py:429
  47.8 5.4 %collective-permute-start.3 = (f32[6,136,128]{2,1,0:T(8,128)S(1)}, f32[6,136,128]{2,1,0:T(8,128)S(1)}, u32[]{:S(2)}, u32[]{:S(2)}) collective-permute-start(f32[6,136,128]{2,1,0:T(8,128)S(1)} %pad_maximum_fusion.7), channel_id=1, source_target_pairs={{0,16},{4,20},{8,24},{12,28},{1,17},{5,21},{9,25},{13,29},{2,18},{... | collective-permute-start | bytes 1253384 | tf_op jit(solution)/shard_map/ppermute | solution.py:430
  53.2 6.9 %collective-permute-done.3 = f32[6,136,128]{2,1,0:T(8,128)S(1)} collective-permute-done((f32[6,136,128]{2,1,0:T(8,128)S(1)}, f32[6,136,128]{2,1,0:T(8,128)S(1)}, u32[]{:S(2)}, u32[]{:S(2)}) %collective-permute-start.3) | collective-permute-done | bytes 417824 | tf_op jit(solution)/shard_map/ppermute | solution.py:430
  61.8 6.5 %collective-permute-done.5 = f32[6,128,128]{2,1,0:T(8,128)S(1)} collective-permute-done((f32[6,128,128]{2,1,0:T(8,128)S(1)}, f32[6,128,128]{2,1,0:T(8,128)S(1)}, u32[]{:S(2)}, u32[]{:S(2)}) %collective-permute-start.5) | collective-permute-done | bytes 393248 | tf_op jit(solution)/shard_map/ppermute | solution.py:438
  68.5 4.7 mixer_out.1
  73.2 3.6 collective-permute-done.6
  83.4 3.4 collective-permute-start.9
  86.8 2.8 assemble.4.refs_0_
  89.7 31.5 %collective-permute-done.9 = f32[384,512]{1,0:T(8,128)} collective-permute-done((f32[384,512]{1,0:T(8,128)}, f32[384,512]{1,0:T(8,128)}, u32[]{:S(2)}, u32[]{:S(2)}) %collective-permute-start.9) | collective-permute-done | bytes 786464 | tf_op jit(solution)/shard_map/ppermute | solution.py:745
  122.4 2.5 collective-permute-done.12.p3
  126.0 6.4 %second_norm.1 = (f32[384,2048]{1,0:T(8,128)}, bf16[1536,2048]{1,0:T(8,128)(2,1)}, f32[384,512]{1,0:T(8,128)}) custom-call(s32[3]{0:T(128)S(1)} %pad_add_fusion.place, bf16[384,2048]{1,0:T(8,128)(2,1)S(1)} %bitcast.133, f32[384,1024]{1,0:T(8,128)} %add.163.p0, f32[384,1024]{1,0:T(8,128)} %collective-permute-done.8.p1, ...), custom_call_target="tpu_custom_call" | custom-call | bytes 10000000 | tf_op jit(solution)/shard_map/second_norm/pallas_call | solution.py:577
  132.4 8.7 %collective-permute-start.14 = (f32[384,512]{1,0:T(8,128)}, f32[384,512]{1,0:T(8,128)S(1)}, u32[]{:S(2)}, u32[]{:S(2)}) collective-permute-start(f32[384,512]{1,0:T(8,128)} %get-tuple-element.228), channel_id=1, source_target_pairs={{0,8},{4,12},{8,16},{12,20},{16,24},{20,28},{24,0},{28,4},{1,9},{5... | collective-permute-start | bytes 2359304 | tf_op jit(solution)/shard_map/ppermute | solution.py:745
  141.0 22.9 %ffn_own.1 = (f32[384,2048]{1,0:T(8,128)}, f32[384,1024]{1,0:T(8,128)}, f32[384,1024]{1,0:T(8,128)}) custom-call(s32[1]{0:T(128)} %bitcast.core, bf16[1536,2048]{1,0:T(8,128)(2,1)} %get-tuple-element.280.xn_ref._, bf16[384,2048]{1,0:T(8,128)(2,1)} %bitcast.129, bf16[2,2048,1408]{2,1,0:T(8,128)(2,1)} %refs_2_.1, bf16[1408,2048]{1,0:T(8,128)(2,1)} %refs_3_.1, ...), custom_call_target="tpu_custom_call" | custom-call | flops 13287555072 | bytes 30000000 | tf_op jit(solution)/shard_map/ffn_own/pallas_call | solution.py:549
  169.6 3.4 collective-permute-start.19
  176.7 31.0 %collective-permute-done.19 = f32[384,512]{1,0:T(8,128)S(1)} collective-permute-done((f32[384,512]{1,0:T(8,128)}, f32[384,512]{1,0:T(8,128)S(1)}, u32[]{:S(2)}, u32[]{:S(2)}) %collective-permute-start.19) | collective-permute-done | bytes 786464 | tf_op jit(solution)/shard_map/ppermute | solution.py:745
  209.9 2.6 collective-permute-start.23
  215.9 9.9 %norm_back.1 = (f32[384,512]{1,0:T(8,128)S(1)}, bf16[384,512]{1,0:T(8,128)(2,1)S(1)}, f32[1,512]{1,0:T(1,128)S(1)}, f32[3,4,136,128]{3,2,1,0:T(8,128)S(1)}, f32[...) custom-call(s32[3]{0:T(128)S(1)} %pad_add_fusion.place, ...), custom_call_target="tpu_custom_call" | custom-call | flops 805306368 | bytes 10000000 | tf_op jit(solution)/shard_map/norm_back/pallas_call | solution.py:564
  226.9 2.6 collective-permute-start.24
  231.3 10.8 %collective-permute-done.22 = f32[6,136,128]{2,1,0:T(8,128)} collective-permute-done((f32[6,136,128]{2,1,0:T(8,128)}, f32[6,136,128]{2,1,0:T(8,128)}, u32[]{:S(2)}, u32[]{:S(2)}) %collective-permute-start.22) | collective-permute-done | bytes 417824 | tf_op jit(solution)/shard_map/ppermute | solution.py:423
  244.4 2.7 collective-permute-done.24
  247.1 2.7 pad_maximum_fusion.1
  256.0 9.1 %collective-permute-done.25 = f32[6,136,128]{2,1,0:T(8,128)S(1)} collective-permute-done((f32[6,136,128]{2,1,0:T(8,128)S(1)}, f32[6,136,128]{2,1,0:T(8,128)S(1)}, u32[]{:S(2)}, u32[]{:S(2)}) %collective-permute-start.25) | collective-permute-done | bytes 417824 | tf_op jit(solution)/shard_map/ppermute | solution.py:429
  267.8 5.9 %intra_back.1 = (f32[384,512]{1,0:T(8,128)}, f32[384,512]{1,0:T(8,128)S(1)}, f32[384,512]{1,0:T(8,128)S(1)}, f32[384,512]{1,0:T(8,128)S(1)}) custom-call(bf16[384,512]{1,0:T(8,128)(2,1)S(1)} %copy-done.33, bf16[384,512]{1,0:T(8,128)(2,1)S(1)} %get-tuple-element.168.qe_ref, bf16[384,512]{1,0:T(8,128)(2,1)S(1)} %get-tuple-element.234.ke_ref, ...), custom_call_target="tpu_custom_call" | custom-call | flops 352321536 | bytes 10000000 | tf_op jit(solution)/shard_map/intra_back/pallas_call | solution.py:612
  275.5 11.7 %collective-permute-done.26 = f32[6,136,128]{2,1,0:T(8,128)S(1)} collective-permute-done((f32[6,136,128]{2,1,0:T(8,128)S(1)}, f32[6,136,128]{2,1,0:T(8,128)S(1)}, u32[]{:S(2)}, u32[]{:S(2)}) %collective-permute-start.26) | collective-permute-done | bytes 417824 | tf_op jit(solution)/shard_map/ppermute | solution.py:430
  290.4 4.3 all-reduce.3.cloned.1.call-done
  300.2 7.9 %collective-permute-done.30 = f32[6,128,128]{2,1,0:T(8,128)S(1)} collective-permute-done((f32[6,128,128]{2,1,0:T(8,128)S(1)}, f32[6,128,128]{2,1,0:T(8,128)S(1)}, u32[]{:S(2)}, u32[]{:S(2)}) %collective-permute-start.30) | collective-permute-done | bytes 393248 | tf_op jit(solution)/shard_map/ppermute | solution.py:438
  308.2 4.1 state_back.1
  330.3 2.5 collective-permute-start.36
  332.8 8.0 %first_grad.1 = f32[384,2048]{1,0:T(8,128)} custom-call(f32[384,512]{1,0:T(8,128)} %get-tuple-element.283.d0.refs_0_, f32[384,512]{1,0:T(8,128)S(1)} %get-tuple-element.341.d1.refs_0_, f32[384,512]{1,0:T(8,128)S(1)} %get-tuple-element.340.d2.refs_2_, f32[384,512]{1,0:T(8,128)S(1)} %copy-done.8, bf16[4,2048,512]{2,1,0:T(8,128)(2,1)} %w_ref.7), custom_call_target="tpu_custom_call" | custom-call | flops 3221225472 | bytes 15000000 | tf_op jit(solution)/shard_map/first_grad/pallas_call | solution.py:589
  341.7 19.0 %collective-permute-done.37 = f32[1,2,256,512]{3,2,1,0:T(8,128)} collective-permute-done((f32[1,2,256,512]{3,2,1,0:T(8,128)}, f32[1,2,256,512]{3,2,1,0:T(8,128)}, u32[]{:S(2)}, u32[]{:S(2)}) %collective-permute-start.37) | collective-permute-done | bytes 1048608 | tf_op jit(solution)/shard_map/ppermute | solution.py:751
  360.7 2.7 fusion.2
  365.2 3.8 mix_grad.6
  369.0 4.1 collective-permute-start.39
  374.2 6.1 %join.1.xn_ref = bf16[1536,2048]{1,0:T(8,128)(2,1)} custom-call(f32[4,1152,512]{2,1,0:T(8,128)} %bitcast.154, bf16[1536,2048]{1,0:T(8,128)(2,1)} %get-tuple-element.280.xn_ref._), custom_call_target="tpu_custom_call", output_to_operand_aliasing={{}: (1, {})} | custom-call | bytes 14155776 | tf_op jit(solution)/shard_map/join/pallas_call | solution.py:479
  380.3 20.8 %ffn_grad.3 = (f32[3,256,512]{2,1,0:T(8,128)}, f32[3,256,512]{2,1,0:T(8,128)}) custom-call(s32[2]{0:T(128)} %pad_add_fusion.3.rows, bf16[1536,2048]{1,0:T(8,128)(2,1)} %join.1.xn_ref, bf16[1536,2048]{1,0:T(8,128)(2,1)} %assemble.6.dy_ref, bf16[2,2048,1408]{2,1,0:T(8,128)(2,1)} %refs_2_.1, bf16[1408,2048]{1,0:T(8,128)(2,1)} %refs_3_.1), custom_call_target="tpu_custom_call" | custom-call | flops 12079595520 | bytes 20000000 | tf_op jit(solution)/shard_map/ffn_grad/pallas_call | solution.py:667
  406.1 21.1 %ffn_grad.4 = (f32[3,256,512]{2,1,0:T(8,128)}, f32[3,256,512]{2,1,0:T(8,128)}) custom-call(s32[2]{0:T(128)} %pad_add_fusion.3.rows, bf16[1536,2048]{1,0:T(8,128)(2,1)} %join.1.xn_ref, bf16[1536,2048]{1,0:T(8,128)(2,1)} %assemble.6.dy_ref, bf16[2,2048,1408]{2,1,0:T(8,128)(2,1)} %refs_2_.1, bf16[1408,2048]{1,0:T(8,128)(2,1)} %refs_3_.1), custom_call_target="tpu_custom_call" | custom-call | flops 12079595520 | bytes 20000000 | tf_op jit(solution)/shard_map/ffn_grad/pallas_call | solution.py:667
  427.3 3.8 mix_grad.7
  431.1 3.6 fusion
  434.7 4.7 collective-permute-done.41
  443.7 5.5 %first_back.1 = (bf16[384,2048]{1,0:T(8,128)(2,1)}, f32[1,2048]{1,0:T(1,128)S(1)}) custom-call(f32[384,2048]{1,0:T(8,128)S(1)} %copy-done.11, f32[384,2048]{1,0:T(8,128)} %get-tuple-element.296.dhidden_ref, bf16[384,2048]{1,0:T(8,128)(2,1)S(1)} %bitcast.134, f32[1,2048]{1,0:T(1,128)S(1)} %bitcast.145), custom_call_target="tpu_custom_call" | custom-call | bytes 10000000 | tf_op jit(solution)/shard_map/first_back/pallas_call | solution.py:601
  449.9 20.4 %ffn_grad.5 = (f32[3,256,384]{2,1,0:T(8,128)}, f32[3,256,384]{2,1,0:T(8,128)}) custom-call(s32[2]{0:T(128)} %pad_add_fusion.3.rows, bf16[1536,2048]{1,0:T(8,128)(2,1)} %join.1.xn_ref, bf16[1536,2048]{1,0:T(8,128)(2,1)} %assemble.6.dy_ref, bf16[2,2048,1408]{2,1,0:T(8,128)(2,1)} %refs_2_.1, bf16[1408,2048]{1,0:T(8,128)(2,1)} %refs_3_.1, ...), custom_call_target="tpu_custom_call" | custom-call | flops 9059696640 | bytes 20000000 | tf_op jit(solution)/shard_map/ffn_grad/pallas_call | solution.py:667
  470.2 4.5 add_convert_fusion
  481.6 3.3 collective-permute-done.43
  496.5 15.9 %collective-permute-done.47 = f32[5120]{0:T(1024)S(1)} collective-permute-done((f32[5120]{0:T(1024)S(1)}, f32[5120]{0:T(1024)S(1)}, u32[]{:S(2)}, u32[]{:S(2)}) %collective-permute-start.47) | collective-permute-done | bytes 20512 | tf_op jit(solution)/shard_map/ppermute | solution.py:862
  (298 shorter events, 116.4 us)
Async XLA Ops:
  7.2 287.5 %all-reduce.3.cloned.1.call-start = ((), (), s32[]{:S(2)}) async-start(), calls=%async_computation | async-start | bytes 6291456 | tf_op jit(solution)/shard_map/psum | solution.py:797
  10.2 26.2 %collective-permute-start.1 = (f32[384,512]{1,0:T(8,128)}, f32[384,512]{1,0:T(8,128)}, u32[]{:S(2)}, u32[]{:S(2)}) collective-permute-start(f32[384,512]{1,0:T(8,128)} %get-tuple-element.229), channel_id=1, source_target_pairs={{0,8},{4,12},{8,16},{12,20},{16,24},{20,28},{24,0},{28,4},{1,9},{5... | collective-permute-start | bytes 2359304 | tf_op jit(solution)/shard_map/ppermute | solution.py:745
  25.1 11.2 %collective-permute-start = (f32[6,136,128]{2,1,0:T(8,128)S(1)}, f32[6,136,128]{2,1,0:T(8,128)S(1)}, u32[]{:S(2)}, u32[]{:S(2)}) collective-permute-start(f32[6,136,128]{2,1,0:T(8,128)S(1)} %slice_select_fusion.2), channel_id=1, source_target_pairs={{0,4},{4,0},{8,12},{12,8},{16,20},{20,16},{24,28},{28,24},{1,5},{5... | collective-permute-start | bytes 1253384 | tf_op jit(solution)/shard_map/ppermute | solution.py:423
  36.5 11.2 %collective-permute-start.2 = (f32[6,136,128]{2,1,0:T(8,128)S(1)}, f32[6,136,128]{2,1,0:T(8,128)S(1)}, u32[]{:S(2)}, u32[]{:S(2)}) collective-permute-start(f32[6,136,128]{2,1,0:T(8,128)S(1)} %pad_maximum_fusion.6), channel_id=1, source_target_pairs={{0,8},{4,12},{8,16},{12,20},{16,24},{20,28},{1,9},{5,13},{9,17},{1... | collective-permute-start | bytes 1253384 | tf_op jit(solution)/shard_map/ppermute | solution.py:429
  40.0 20.2 %collective-permute-start.4 = (f32[384,512]{1,0:T(8,128)}, f32[384,512]{1,0:T(8,128)}, u32[]{:S(2)}, u32[]{:S(2)}) collective-permute-start(f32[384,512]{1,0:T(8,128)} %collective-permute-done.1), channel_id=1, source_target_pairs={{0,2},{1,3},{2,0},{3,1},{4,6},{5,7},{6,4},{7,5},{8,10},{9,11},{10,... | collective-permute-start | bytes 2359304 | tf_op jit(solution)/shard_map/ppermute | solution.py:452
  47.8 12.3 %collective-permute-start.3 = (f32[6,136,128]{2,1,0:T(8,128)S(1)}, f32[6,136,128]{2,1,0:T(8,128)S(1)}, u32[]{:S(2)}, u32[]{:S(2)}) collective-permute-start(f32[6,136,128]{2,1,0:T(8,128)S(1)} %pad_maximum_fusion.7), channel_id=1, source_target_pairs={{0,16},{4,20},{8,24},{12,28},{1,17},{5,21},{9,25},{13,29},{2,18},{... | collective-permute-start | bytes 1253384 | tf_op jit(solution)/shard_map/ppermute | solution.py:430
  60.3 8.0 %collective-permute-start.5 = (f32[6,128,128]{2,1,0:T(8,128)S(1)}, f32[6,128,128]{2,1,0:T(8,128)S(1)}, u32[]{:S(2)}, u32[]{:S(2)}) collective-permute-start(f32[6,128,128]{2,1,0:T(8,128)S(1)} %fusion.9), channel_id=1, source_target_pairs={{0,4},{4,0},{8,12},{12,8},{16,20},{20,16},{24,28},{28,24},{1,5},{5... | collective-permute-start | bytes 1179656 | tf_op jit(solution)/shard_map/ppermute | solution.py:438
  79.8 7.0 %collective-permute-start.11 = (f32[1,2,384,512]{3,2,1,0:T(8,128)S(1)}, f32[1,2,384,512]{3,2,1,0:T(8,128)}, u32[]{:S(2)}, u32[]{:S(2)}) collective-permute-start(f32[1,2,384,512]{3,2,1,0:T(8,128)S(1)} %maximum_bitcast_fusion.here_ref), channel_id=1, source_target_pairs={{0,1},{1,0},{2,3},{3,2},{4,5},{5,4},{6,7},{7,6},{8,9},{9,8},{10,11... | collective-permute-start | bytes 4718600 | tf_op jit(solution)/shard_map/ppermute | solution.py:448
  80.0 41.2 %collective-permute-start.7 = (f32[384,1024]{1,0:T(8,128)}, f32[384,1024]{1,0:T(8,128)}, u32[]{:S(2)}, u32[]{:S(2)}) collective-permute-start(f32[384,1024]{1,0:T(8,128)} %add.163.p0), channel_id=1, source_target_pairs={{0,1},{1,0},{2,3},{3,2},{4,5},{5,4},{6,7},{7,6},{8,9},{9,8},{10,11... | collective-permute-start | bytes 4718600 | tf_op jit(solution)/shard_map/ppermute | solution.py:448
  80.4 40.8 %collective-permute-start.8 = (f32[384,1024]{1,0:T(8,128)}, f32[384,1024]{1,0:T(8,128)}, u32[]{:S(2)}, u32[]{:S(2)}) collective-permute-start(f32[384,1024]{1,0:T(8,128)} %add.163.p0), channel_id=1, source_target_pairs={{0,2},{1,3},{2,0},{3,1},{4,6},{5,7},{6,4},{7,5},{8,10},{9,11},{10,... | collective-permute-start | bytes 4718600 | tf_op jit(solution)/shard_map/ppermute | solution.py:452
  81.9 39.3 %collective-permute-start.10 = (f32[384,1024]{1,0:T(8,128)}, f32[384,1024]{1,0:T(8,128)}, u32[]{:S(2)}, u32[]{:S(2)}) collective-permute-start(f32[384,1024]{1,0:T(8,128)} %get-tuple-element.186), channel_id=1, source_target_pairs={{0,4},{4,0},{8,12},{12,8},{16,20},{20,16},{24,28},{28,24},{1,5},{5... | collective-permute-start | bytes 4718600 | tf_op jit(solution)/shard_map/ppermute | solution.py:456
  83.4 37.8 %collective-permute-start.9 = (f32[384,512]{1,0:T(8,128)}, f32[384,512]{1,0:T(8,128)}, u32[]{:S(2)}, u32[]{:S(2)}) collective-permute-start(f32[384,512]{1,0:T(8,128)} %get-tuple-element.229), channel_id=1, source_target_pairs={{0,16},{4,20},{8,24},{12,28},{16,0},{20,4},{24,8},{28,12},{1,17},{... | collective-permute-start | bytes 2359304 | tf_op jit(solution)/shard_map/ppermute | solution.py:745
  121.4 42.6 %collective-permute-start.13 = (f32[384,512]{1,0:T(8,128)}, f32[384,512]{1,0:T(8,128)}, u32[]{:S(2)}, u32[]{:S(2)}) collective-permute-start(f32[384,512]{1,0:T(8,128)} %collective-permute-done.9), channel_id=1, source_target_pairs={{0,2},{1,3},{2,0},{3,1},{4,6},{5,7},{6,4},{7,5},{8,10},{9,11},{10,... | collective-permute-start | bytes 2359304 | tf_op jit(solution)/shard_map/ppermute | solution.py:452
  121.9 42.1 %collective-permute-start.15 = (f32[384,512]{1,0:T(8,128)}, f32[384,512]{1,0:T(8,128)S(1)}, u32[]{:S(2)}, u32[]{:S(2)}) collective-permute-start(f32[384,512]{1,0:T(8,128)} %get-tuple-element.198), channel_id=1, source_target_pairs={{0,4},{4,0},{8,12},{12,8},{16,20},{20,16},{24,28},{28,24},{1,5},{5... | collective-permute-start | bytes 2359304 | tf_op jit(solution)/shard_map/ppermute | solution.py:456
  132.4 31.6 %collective-permute-start.14 = (f32[384,512]{1,0:T(8,128)}, f32[384,512]{1,0:T(8,128)S(1)}, u32[]{:S(2)}, u32[]{:S(2)}) collective-permute-start(f32[384,512]{1,0:T(8,128)} %get-tuple-element.228), channel_id=1, source_target_pairs={{0,8},{4,12},{8,16},{12,20},{16,24},{20,28},{24,0},{28,4},{1,9},{5... | collective-permute-start | bytes 2359304 | tf_op jit(solution)/shard_map/ppermute | solution.py:745
  166.1 8.7 %collective-permute-start.20 = (f32[1,2,384,512]{3,2,1,0:T(8,128)S(1)}, f32[1,2,384,512]{3,2,1,0:T(8,128)S(1)}, u32[]{:S(2)}, u32[]{:S(2)}) collective-permute-start(f32[1,2,384,512]{3,2,1,0:T(8,128)S(1)} %maximum_bitcast_fusion.1.here_ref), channel_id=1, source_target_pairs={{0,1},{1,0},{2,3},{3,2},{4,5},{5,4},{6,7},{7,6},{8,9},{9,8},{10,11... | collective-permute-start | bytes 4718600 | tf_op jit(solution)/shard_map/ppermute | solution.py:448
  168.1 39.6 %collective-permute-start.17 = (f32[384,1024]{1,0:T(8,128)S(1)}, f32[384,1024]{1,0:T(8,128)}, u32[]{:S(2)}, u32[]{:S(2)}) collective-permute-start(f32[384,1024]{1,0:T(8,128)S(1)} %add.164.p0), channel_id=1, source_target_pairs={{0,2},{1,3},{2,0},{3,1},{4,6},{5,7},{6,4},{7,5},{8,10},{9,11},{10,... | collective-permute-start | bytes 4718600 | tf_op jit(solution)/shard_map/ppermute | solution.py:452
  169.6 38.1 %collective-permute-start.18 = (f32[384,1024]{1,0:T(8,128)S(1)}, f32[384,1024]{1,0:T(8,128)S(1)}, u32[]{:S(2)}, u32[]{:S(2)}) collective-permute-start(f32[384,1024]{1,0:T(8,128)S(1)} %add.164.p0), channel_id=1, source_target_pairs={{0,1},{1,0},{2,3},{3,2},{4,5},{5,4},{6,7},{7,6},{8,9},{9,8},{10,11... | collective-permute-start | bytes 4718600 | tf_op jit(solution)/shard_map/ppermute | solution.py:448
  169.6 38.1 %collective-permute-start.19 = (f32[384,512]{1,0:T(8,128)}, f32[384,512]{1,0:T(8,128)S(1)}, u32[]{:S(2)}, u32[]{:S(2)}) collective-permute-start(f32[384,512]{1,0:T(8,128)} %get-tuple-element.228), channel_id=1, source_target_pairs={{0,16},{4,20},{8,24},{12,28},{16,0},{20,4},{24,8},{28,12},{1,17},{... | collective-permute-start | bytes 2359304 | tf_op jit(solution)/shard_map/ppermute | solution.py:745
  209.8 153.5 %all-gather.3.cloned.1.call-start = ((), (), s32[]{:S(2)}) async-start(), calls=%async_computation.2 | async-start | bytes 11796480 | tf_op jit(solution)/shard_map/all_gather | solution.py:808
  209.9 34.5 %collective-permute-start.23 = (f32[384,512]{1,0:T(8,128)}, f32[384,512]{1,0:T(8,128)}, u32[]{:S(2)}, u32[]{:S(2)}) collective-permute-start(f32[384,512]{1,0:T(8,128)} %get-tuple-element.228), channel_id=1, source_target_pairs={{0,24},{4,28},{8,0},{12,4},{16,8},{20,12},{24,16},{28,20},{1,25},{... | collective-permute-start | bytes 2359304 | tf_op jit(solution)/shard_map/ppermute | solution.py:745
  226.9 20.2 %collective-permute-start.24 = (f32[384,512]{1,0:T(8,128)}, f32[384,512]{1,0:T(8,128)}, u32[]{:S(2)}, u32[]{:S(2)}) collective-permute-start(f32[384,512]{1,0:T(8,128)} %get-tuple-element.229), channel_id=1, source_target_pairs={{0,24},{4,28},{8,0},{12,4},{16,8},{20,12},{24,16},{28,20},{1,25},{... | collective-permute-start | bytes 2359304 | tf_op jit(solution)/shard_map/ppermute | solution.py:745
  230.4 11.8 %collective-permute-start.22 = (f32[6,136,128]{2,1,0:T(8,128)}, f32[6,136,128]{2,1,0:T(8,128)}, u32[]{:S(2)}, u32[]{:S(2)}) collective-permute-start(f32[6,136,128]{2,1,0:T(8,128)} %slice_select_fusion), channel_id=1, source_target_pairs={{0,4},{4,0},{8,12},{12,8},{16,20},{20,16},{24,28},{28,24},{1,5},{5... | collective-permute-start | bytes 1253384 | tf_op jit(solution)/shard_map/ppermute | solution.py:423
  249.9 191.9 %all-reduce.5.cloned.1.call-start = ((), (), s32[]{:S(2)}) async-start(), calls=%async_computation.1 | async-start | bytes 6291456 | tf_op jit(solution)/shard_map/psum | solution.py:834
  252.1 13.0 %collective-permute-start.25 = (f32[6,136,128]{2,1,0:T(8,128)S(1)}, f32[6,136,128]{2,1,0:T(8,128)S(1)}, u32[]{:S(2)}, u32[]{:S(2)}) collective-permute-start(f32[6,136,128]{2,1,0:T(8,128)S(1)} %pad_maximum_fusion.8), channel_id=1, source_target_pairs={{8,0},{12,4},{16,8},{20,12},{24,16},{28,20},{9,1},{13,5},{17,9},{2... | collective-permute-start | bytes 1253384 | tf_op jit(solution)/shard_map/ppermute | solution.py:429
  253.5 33.7 %collective-permute-start.27 = (f32[384,512]{1,0:T(8,128)S(1)}, f32[384,512]{1,0:T(8,128)S(1)}, u32[]{:S(2)}, u32[]{:S(2)}) collective-permute-start(f32[384,512]{1,0:T(8,128)S(1)} %copy-done.7), channel_id=1, source_target_pairs={{0,4},{4,0},{8,12},{12,8},{16,20},{20,16},{24,28},{28,24},{1,5},{5... | collective-permute-start | bytes 2359304 | tf_op jit(solution)/shard_map/ppermute | solution.py:456
  254.5 40.3 %collective-permute-start.29 = (f32[384,512]{1,0:T(8,128)}, f32[384,512]{1,0:T(8,128)}, u32[]{:S(2)}, u32[]{:S(2)}) collective-permute-start(f32[384,512]{1,0:T(8,128)} %collective-permute-done.24), channel_id=1, source_target_pairs={{0,2},{1,3},{2,0},{3,1},{4,6},{5,7},{6,4},{7,5},{8,10},{9,11},{10,... | collective-permute-start | bytes 2359304 | tf_op jit(solution)/shard_map/ppermute | solution.py:452
  265.2 21.9 %collective-permute-start.26 = (f32[6,136,128]{2,1,0:T(8,128)S(1)}, f32[6,136,128]{2,1,0:T(8,128)S(1)}, u32[]{:S(2)}, u32[]{:S(2)}) collective-permute-start(f32[6,136,128]{2,1,0:T(8,128)S(1)} %pad_maximum_fusion.9), channel_id=1, source_target_pairs={{16,0},{20,4},{24,8},{28,12},{17,1},{21,5},{25,9},{29,13},{18,2},{... | collective-permute-start | bytes 1253384 | tf_op jit(solution)/shard_map/ppermute | solution.py:430
  266.9 27.8 %collective-permute-start.28 = (f32[384,256]{1,0:T(8,128)}, f32[384,256]{1,0:T(8,128)}, u32[]{:S(2)}, u32[]{:S(2)}) collective-permute-start(f32[384,256]{1,0:T(8,128)} %get-tuple-element.242), channel_id=1, source_target_pairs={{0,4},{4,0},{8,12},{12,8},{16,20},{20,16},{24,28},{28,24},{1,5},{5... | collective-permute-start | bytes 1179656 | tf_op jit(solution)/shard_map/ppermute | solution.py:456
  296.3 16.1 %collective-permute-start.32 = (f32[1,2,384,512]{3,2,1,0:T(8,128)S(1)}, f32[1,2,384,512]{3,2,1,0:T(8,128)S(1)}, u32[]{:S(2)}, u32[]{:S(2)}) collective-permute-start(f32[1,2,384,512]{3,2,1,0:T(8,128)S(1)} %maximum_bitcast_fusion.2.here_ref), channel_id=1, source_target_pairs={{0,1},{1,0},{2,3},{3,2},{4,5},{5,4},{6,7},{7,6},{8,9},{9,8},{10,11... | collective-permute-start | bytes 4718600 | tf_op jit(solution)/shard_map/ppermute | solution.py:448
  296.5 11.6 %collective-permute-start.30 = (f32[6,128,128]{2,1,0:T(8,128)S(1)}, f32[6,128,128]{2,1,0:T(8,128)S(1)}, u32[]{:S(2)}, u32[]{:S(2)}) collective-permute-start(f32[6,128,128]{2,1,0:T(8,128)S(1)} %fusion.7), channel_id=1, source_target_pairs={{0,4},{4,0},{8,12},{12,8},{16,20},{20,16},{24,28},{28,24},{1,5},{5... | collective-permute-start | bytes 1179656 | tf_op jit(solution)/shard_map/ppermute | solution.py:438
  298.0 16.2 %collective-permute-start.31 = (f32[384,256]{1,0:T(8,128)}, f32[384,256]{1,0:T(8,128)S(1)}, u32[]{:S(2)}, u32[]{:S(2)}) collective-permute-start(f32[384,256]{1,0:T(8,128)} %collective-permute-done.28), channel_id=1, source_target_pairs={{0,2},{1,3},{2,0},{3,1},{4,6},{5,7},{6,4},{7,5},{8,10},{9,11},{10,... | collective-permute-start | bytes 1179656 | tf_op jit(solution)/shard_map/ppermute | solution.py:452
  298.7 27.5 %collective-permute-start.34 = (f32[1,2,256,512]{3,2,1,0:T(8,128)}, f32[1,2,256,512]{3,2,1,0:T(8,128)}, u32[]{:S(2)}, u32[]{:S(2)}) collective-permute-start(f32[1,2,256,512]{3,2,1,0:T(8,128)} %get-tuple-element.257), channel_id=1, source_target_pairs={{0,8},{4,12},{8,0},{12,4},{16,24},{20,28},{24,16},{28,20},{1,9},{5... | collective-permute-start | bytes 3145736 | tf_op jit(solution)/shard_map/ppermute | solution.py:751
  315.4 48.0 %collective-permute-start.33 = (f32[2,384,512]{2,1,0:T(8,128)}, f32[2,384,512]{2,1,0:T(8,128)}, u32[]{:S(2)}, u32[]{:S(2)}) collective-permute-start(f32[2,384,512]{2,1,0:T(8,128)} %get-tuple-element.255), channel_id=1, source_target_pairs={{0,4},{4,0},{8,12},{12,8},{16,20},{20,16},{24,28},{28,24},{1,5},{5... | collective-permute-start | bytes 4718600 | tf_op jit(solution)/shard_map/ppermute | solution.py:456
  323.4 37.2 %collective-permute-start.37 = (f32[1,2,256,512]{3,2,1,0:T(8,128)}, f32[1,2,256,512]{3,2,1,0:T(8,128)}, u32[]{:S(2)}, u32[]{:S(2)}) collective-permute-start(f32[1,2,256,512]{3,2,1,0:T(8,128)} %get-tuple-element.263), channel_id=1, source_target_pairs={{0,8},{4,12},{8,0},{12,4},{16,24},{20,28},{24,16},{28,20},{1,9},{5... | collective-permute-start | bytes 3145736 | tf_op jit(solution)/shard_map/ppermute | solution.py:751
  330.3 33.1 %collective-permute-start.36 = (f32[1,256,512]{2,1,0:T(8,128)}, f32[1,256,512]{2,1,0:T(8,128)S(1)}, u32[]{:S(2)}, u32[]{:S(2)}) collective-permute-start(f32[1,256,512]{2,1,0:T(8,128)} %get-tuple-element.264), channel_id=1, source_target_pairs={{0,16},{4,20},{8,24},{12,28},{16,0},{20,4},{24,8},{28,12},{1,17},{... | collective-permute-start | bytes 1572872 | tf_op jit(solution)/shard_map/ppermute | solution.py:755
  369.0 62.0 %collective-permute-start.38 = (f32[2,2,256,512]{3,2,1,0:T(8,128)}, f32[2,2,256,512]{3,2,1,0:T(8,128)}, u32[]{:S(2)}, u32[]{:S(2)}) collective-permute-start(f32[2,2,256,512]{3,2,1,0:T(8,128)} %get-tuple-element.277), channel_id=1, source_target_pairs={{0,8},{4,12},{8,0},{12,4},{16,24},{20,28},{24,16},{28,20},{1,9},{5... | collective-permute-start | bytes 6291464 | tf_op jit(solution)/shard_map/ppermute | solution.py:751
  369.0 65.7 %collective-permute-start.39 = (f32[1,256,512]{2,1,0:T(8,128)}, f32[1,256,512]{2,1,0:T(8,128)}, u32[]{:S(2)}, u32[]{:S(2)}) collective-permute-start(f32[1,256,512]{2,1,0:T(8,128)} %get-tuple-element.278), channel_id=1, source_target_pairs={{0,16},{4,20},{8,24},{12,28},{16,0},{20,4},{24,8},{28,12},{1,17},{... | collective-permute-start | bytes 1572872 | tf_op jit(solution)/shard_map/ppermute | solution.py:755
  373.1 30.4 %collective-permute-start.40 = (f32[384,512]{1,0:T(8,128)}, f32[384,512]{1,0:T(8,128)}, u32[]{:S(2)}, u32[]{:S(2)}) collective-permute-start(f32[384,512]{1,0:T(8,128)} %get-tuple-element.283.d0.refs_0_), channel_id=1, source_target_pairs={{0,4},{4,0},{8,12},{12,8},{16,20},{20,16},{24,28},{28,24},{1,5},{5... | collective-permute-start | bytes 2359304 | tf_op jit(solution)/shard_map/ppermute | solution.py:456
  403.6 35.9 %collective-permute-start.41 = (f32[3,256,512]{2,1,0:T(8,128)}, f32[3,256,512]{2,1,0:T(8,128)}, u32[]{:S(2)}, u32[]{:S(2)}) collective-permute-start(f32[3,256,512]{2,1,0:T(8,128)} %get-tuple-element.284), channel_id=1, source_target_pairs={{0,4},{4,0},{8,12},{12,8},{16,20},{20,16},{24,28},{28,24},{1,5},{5... | collective-permute-start | bytes 4718600 | tf_op jit(solution)/shard_map/ppermute | solution.py:456
  439.4 47.4 %collective-permute-start.42 = (f32[3,256,512]{2,1,0:T(8,128)}, f32[3,256,512]{2,1,0:T(8,128)}, u32[]{:S(2)}, u32[]{:S(2)}) collective-permute-start(f32[3,256,512]{2,1,0:T(8,128)} %get-tuple-element.291), channel_id=1, source_target_pairs={{0,4},{4,0},{8,12},{12,8},{16,20},{20,16},{24,28},{28,24},{1,5},{5... | collective-permute-start | bytes 4718600 | tf_op jit(solution)/shard_map/ppermute | solution.py:456
  440.5 44.4 %collective-permute-start.43 = (f32[1,2,256,512]{3,2,1,0:T(8,128)}, f32[1,2,256,512]{3,2,1,0:T(8,128)}, u32[]{:S(2)}, u32[]{:S(2)}) collective-permute-start(f32[1,2,256,512]{3,2,1,0:T(8,128)} %get-tuple-element.293), channel_id=1, source_target_pairs={{0,8},{4,12},{8,0},{12,4},{16,24},{20,28},{24,16},{28,20},{1,9},{5... | collective-permute-start | bytes 3145736 | tf_op jit(solution)/shard_map/ppermute | solution.py:751
  440.5 46.3 %collective-permute-start.44 = (f32[2,256,512]{2,1,0:T(8,128)}, f32[2,256,512]{2,1,0:T(8,128)}, u32[]{:S(2)}, u32[]{:S(2)}) collective-permute-start(f32[2,256,512]{2,1,0:T(8,128)} %get-tuple-element.294), channel_id=1, source_target_pairs={{0,16},{4,20},{8,24},{12,28},{16,0},{20,4},{24,8},{28,12},{1,17},{... | collective-permute-start | bytes 3145736 | tf_op jit(solution)/shard_map/ppermute | solution.py:755
  449.1 32.5 %collective-permute-start.45 = (f32[5120]{0:T(1024)S(1)}, f32[5120]{0:T(1024)S(1)}, u32[]{:S(2)}, u32[]{:S(2)}) collective-permute-start(f32[5120]{0:T(1024)S(1)} %pad_maximum_fusion.10), channel_id=1, source_target_pairs={{0,4},{4,0},{8,12},{12,8},{16,20},{20,16},{24,28},{28,24},{1,5},{5... | collective-permute-start | bytes 61448 | tf_op jit(solution)/shard_map/ppermute | solution.py:855
  486.9 7.5 %collective-permute-start.46 = (f32[5120]{0:T(1024)S(1)}, f32[5120]{0:T(1024)S(1)}, u32[]{:S(2)}, u32[]{:S(2)}) collective-permute-start(f32[5120]{0:T(1024)S(1)} %fusion.11), channel_id=1, source_target_pairs={{0,8},{4,12},{8,0},{12,4},{16,24},{20,28},{24,16},{28,20},{1,9},{5... | collective-permute-start | bytes 61448 | tf_op jit(solution)/shard_map/ppermute | solution.py:862
  486.9 26.7 %collective-permute-start.48 = (f32[1,256,512]{2,1,0:T(8,128)S(1)}, f32[1,256,512]{2,1,0:T(8,128)S(1)}, u32[]{:S(2)}, u32[]{:S(2)}) collective-permute-start(f32[1,256,512]{2,1,0:T(8,128)S(1)} %get-tuple-element.310), channel_id=1, source_target_pairs={{0,16},{4,20},{8,24},{12,28},{16,0},{20,4},{24,8},{28,12},{1,17},{... | collective-permute-start | bytes 1572872 | tf_op jit(solution)/shard_map/ppermute | solution.py:755
  489.0 26.2 %collective-permute-start.49 = (f32[3,256,384]{2,1,0:T(8,128)S(1)}, f32[3,256,384]{2,1,0:T(8,128)S(1)}, u32[]{:S(2)}, u32[]{:S(2)}) collective-permute-start(f32[3,256,384]{2,1,0:T(8,128)S(1)} %copy-done.66), channel_id=1, source_target_pairs={{0,4},{4,0},{8,12},{12,8},{16,20},{20,16},{24,28},{28,24},{1,5},{5... | collective-permute-start | bytes 3538952 | tf_op jit(solution)/shard_map/ppermute | solution.py:456
  494.3 18.0 %collective-permute-start.47 = (f32[5120]{0:T(1024)S(1)}, f32[5120]{0:T(1024)S(1)}, u32[]{:S(2)}, u32[]{:S(2)}) collective-permute-start(f32[5120]{0:T(1024)S(1)} %add.179), channel_id=1, source_target_pairs={{0,16},{4,20},{8,24},{12,28},{16,0},{20,4},{24,8},{28,12},{1,17},{... | collective-permute-start | bytes 61448 | tf_op jit(solution)/shard_map/ppermute | solution.py:862
  (72 other events, 450.8 us)
Sparse Core Ops, SparseCore 0:
  210.0 84.7 all-reduce.2
  296.9 64.9 all-gather.2
  374.3 65.1 all-reduce.4
